TPU v7x, 512 devices: a whole 4x4x16 slice. The times are simulated.
512 devices in a mesh: row: 16 (over z), col: 32 (over x, y, core).
Axes of the slice: x: 4, y: 4, z: 16, core: 2. Of those that a mesh axis runs over, the one named last changes fastest.
Arguments:
- activations: bfloat16 [2048, 6144], P('row', 'col'), may hold values from -6 to 6
- out_grad: bfloat16 [2048, 49152], P('row', 'col'), may hold values from -6 to 6
- weight_slots: bfloat16 [32, 16, 512, 512], P('col', 'row'), may hold values from -0.15625 to 0.15625
- block_mask: int32 [96, 12], replicated, may hold values from 0 to 1, as said below
- block_owner: int32 [96, 12], replicated, may hold values from 0 to 15, as said below
Outputs:
- outputs: bfloat16 [2048, 49152], P('row', 'col')
- in_grad: bfloat16 [2048, 6144], P('row', 'col')
- weight_grad: bfloat16 [32, 16, 512, 512], P('col', 'row')
Inputs may be any that keep to these rules, and one draw needn't show every extreme that they name: `block_mask`: in each group of block rows (3 rows of 12 blocks) exactly a quarter of the blocks are nonzero. `block_owner`: among the nonzero blocks of one group, no index of row owns more than 1, and some index owns exactly 1.
All inputs are finite; a program needn't handle non-finite values.
Results may differ from a plain program's by a relative error of at most 0.005.
Values may be sent and summed in bfloat16 or wider, within the bound.
No kernel may reach another device: no remote copies, remote signals or barrier semaphores. Data moves between devices by JAX's collectives and lax.ppermute only.
A program may use at most 64 MiB of HBM per device.

v0:
```python
import math

import jax
import jax.numpy as jnp
from jax import lax
from jax.sharding import PartitionSpec as P


def per_device(activations, out_grad, weight_slots, block_mask, block_owner):
    block_size = weight_slots.shape[2]
    slot_count = weight_slots.shape[1]
    owner_count = lax.axis_size("row")
    group_index = lax.axis_index("col")
    owner_index = lax.axis_index("row")
    tok_rows = activations.shape[0]
    group_rows = out_grad.shape[1] // block_size
    model_blocks = block_mask.shape[1]
    group_size = group_rows * model_blocks
    group_mask = lax.dynamic_slice_in_dim(
        block_mask, group_index * group_rows, group_rows, 0
    ).reshape(group_size)
    group_owner = lax.dynamic_slice_in_dim(
        block_owner, group_index * group_rows, group_rows, 0
    ).reshape(group_size)
    owner_ids = jnp.arange(owner_count, dtype=jnp.int32)
    chosen = ((group_mask[None, :] == 1) & (group_owner[None, :] == owner_ids[:, None])).astype(
        jnp.int32
    )
    rank_list = jnp.cumsum(chosen, axis=1) - 1
    slot_range = jnp.arange(slot_count, dtype=jnp.int32)
    picked = chosen[:, None, :] * (rank_list[:, None, :] == slot_range[None, :, None]).astype(
        jnp.int32
    )
    filled = jnp.sum(picked, axis=2)
    block_ids = jnp.sum(picked * jnp.arange(group_size, dtype=jnp.int32)[None, None, :], axis=2)
    hidden_index = block_ids // model_blocks
    model_index = block_ids % model_blocks
    hidden_onehot = (
        (hidden_index[:, :, None] == jnp.arange(group_rows, dtype=jnp.int32)[None, None, :]).astype(
            jnp.int32
        )
        * filled[:, :, None]
    ).astype(jnp.bfloat16)
    model_onehot = (
        (
            model_index[:, :, None] == jnp.arange(model_blocks, dtype=jnp.int32)[None, None, :]
        ).astype(jnp.int32)
        * filled[:, :, None]
    ).astype(jnp.bfloat16)
    own_filled = lax.dynamic_index_in_dim(filled, owner_index, 0, keepdims=False)
    own_hidden = lax.dynamic_index_in_dim(hidden_index, owner_index, 0, keepdims=False)
    whole_rows = lax.all_gather(activations, "col", axis=1, tiled=True)
    model_panels = whole_rows.reshape(tok_rows, model_blocks, block_size)
    act_send = jnp.take(model_panels, model_index.reshape(-1), axis=1).reshape(
        tok_rows, owner_count, slot_count, block_size
    )
    weights = weight_slots[0]
    act_recv = lax.all_to_all(act_send, "row", split_axis=1, concat_axis=1, tiled=True)
    piece_rows = lax.all_gather(out_grad, "row", axis=0, tiled=True)
    gathered = jnp.take(
        piece_rows.reshape(piece_rows.shape[0], group_rows, block_size), own_hidden, axis=1
    )
    grad_recv = gathered.reshape(owner_count, tok_rows, slot_count, block_size)
    grad_form = "atso"
    partial_out = jnp.einsum(
        "tasi,soi->taso", act_recv, weights, preferred_element_type=jnp.float32
    ).astype(jnp.bfloat16)
    partial_in = jnp.einsum(
        grad_form + ",soi->tasi", grad_recv, weights, preferred_element_type=jnp.float32
    ).astype(jnp.bfloat16)
    weight_sum = jnp.einsum(
        grad_form + ",tasi->soi", grad_recv, act_recv, preferred_element_type=jnp.float32
    )
    grad_scale = 1.0 / math.sqrt(tok_rows * owner_count)
    weight_grad = (weight_sum * grad_scale * own_filled.astype(jnp.float32)[:, None, None]).astype(
        jnp.bfloat16
    )[None]
    out_back, in_back = (
        lax.all_to_all(partial_out, "row", split_axis=1, concat_axis=1, tiled=True),
        lax.all_to_all(partial_in, "row", split_axis=1, concat_axis=1, tiled=True),
    )
    outputs = jnp.einsum(
        "taso,asf->tfo", out_back, hidden_onehot, preferred_element_type=jnp.float32
    )
    outputs = outputs.reshape(tok_rows, group_rows * block_size).astype(jnp.bfloat16)
    rows_sum = jnp.einsum(
        "tasi,asd->tdi", in_back, model_onehot, preferred_element_type=jnp.float32
    )
    rows_sum = rows_sum.reshape(tok_rows, model_blocks * block_size)
    in_grad = lax.psum_scatter(rows_sum, "col", scatter_dimension=1, tiled=True).astype(
        jnp.bfloat16
    )
    return (outputs, in_grad, weight_grad)


def solution(mesh):
    placed = (P("row", "col"), P("row", "col"), P("col", "row", None, None), P(), P())
    return jax.shard_map(
        per_device,
        mesh=mesh,
        in_specs=placed,
        out_specs=(P("row", "col"), P("row", "col"), P("col", "row", None, None)),
        check_vma=False,
    )
```

profile of v0, /device:TPU:1, one launch (start us, length us, event | category | flops | bytes accessed | tf_op | source)
XLA Modules:
  0.0 509.0 jit_solution(14227515447452860769)
XLA Ops:
  8.0 1.9 copy.57
  9.9 0.8 constant_dynamic-slice_fusion.1
  10.9 0.8 dynamic-slice_compare_fusion
  12.2 63.2 %all-gather.3.cloned.1.call-done = bf16[128,6144]{0,1:T(8,128)(2,1)} async-done(((bf16[128,192]{0,1:T(8,128)(2,1)}), bf16[128,6144]{0,1:T(8,128)(2,1)}) %all-gather.3.cloned.1.call-update) | async-done | bytes 1572880 | tf_op jit(solution)/shard_map/all_gather | solution.py:52
  75.5 1.7 copy.52
  77.2 2.1 gather_fusion
  79.3 3.3 fusion
  82.5 12.0 %all-to-all-start = ((bf16[128,16,1,512]{3,0,2,1:T(8,128)(2,1)}), bf16[128,16,1,512]{3,0,2,1:T(8,128)(2,1)S(1)}, u32[]{:S(2)}, u32[]{:S(2)}) async-start(bf16[128,16,1,512]{3,0,2,1:T(8,128)(2,1)} %fusion), calls=%async_computation | async-start | bytes 4194304 | tf_op jit(solution)/shard_map/all_to_all | solution.py:58
  97.1 168.9 %all-gather.5.cloned.1.call-done = bf16[2048,1536]{0,1:T(8,128)(2,1)} async-done(((bf16[128,1536]{0,1:T(8,128)(2,1)}), bf16[2048,1536]{0,1:T(8,128)(2,1)}) %all-gather.5.cloned.1.call-update) | async-done | bytes 6291472 | tf_op jit(solution)/shard_map/all_gather | solution.py:59
  266.0 3.1 dynamic-slice_select_fusion
  269.1 4.0 copy.58
  273.0 4.2 convert_bitcast_fusion
  277.2 6.9 %all-to-all-start.2 = ((bf16[128,16,1,512]{3,0,2,1:T(8,128)(2,1)}), bf16[128,16,1,512]{3,0,2,1:T(8,128)(2,1)}, u32[]{:S(2)}, u32[]{:S(2)}) async-start(bf16[128,16,1,512]{3,0,2,1:T(8,128)(2,1)} %convert_bitcast_fusion), calls=%async_computation.2 | async-start | bytes 4194304 | tf_op jit(solution)/shard_map/all_to_all | solution.py:80
  284.2 2.6 convert_bitcast_fusion.1
  286.8 88.4 %all-to-all-done.2 = bf16[128,16,1,512]{3,0,2,1:T(8,128)(2,1)} async-done(((bf16[128,16,1,512]{3,0,2,1:T(8,128)(2,1)}), bf16[128,16,1,512]{3,0,2,1:T(8,128)(2,1)}, u32[]{:S(2)}, u32[]{:S(2)}) %all-to-all-start.2) | async-done | bytes 2097184 | tf_op jit(solution)/shard_map/all_to_all | solution.py:80
  375.2 11.0 %all-to-all-start.1 = ((bf16[128,16,1,512]{3,0,2,1:T(8,128)(2,1)}), bf16[128,16,1,512]{3,0,2,1:T(8,128)(2,1)}, u32[]{:S(2)}, u32[]{:S(2)}) async-start(bf16[128,16,1,512]{3,0,2,1:T(8,128)(2,1)} %convert_bitcast_fusion.1), calls=%async_computation.1 | async-start | bytes 4194304 | tf_op jit(solution)/shard_map/all_to_all | solution.py:79
  386.2 4.9 convolution_bitcast_fusion
  391.1 4.9 copy.61
  397.2 3.7 fusion.24
  400.9 77.1 %all-to-all-done.1 = bf16[128,16,1,512]{3,0,2,1:T(8,128)(2,1)} async-done(((bf16[128,16,1,512]{3,0,2,1:T(8,128)(2,1)}), bf16[128,16,1,512]{3,0,2,1:T(8,128)(2,1)}, u32[]{:S(2)}, u32[]{:S(2)}) %all-to-all-start.1) | async-done | bytes 2097184 | tf_op jit(solution)/shard_map/all_to_all | solution.py:79
  478.0 2.9 fusion.27
  481.3 0.9 copy.63
  482.2 18.7 %reduce-scatter.2.cloned.1.call-done = f32[128,192]{0,1:T(8,128)} async-done(((f32[128,6144]{0,1:T(8,128)}), f32[128,192]{0,1:T(8,128)}) %reduce-scatter.2.cloned.1.call-update) | async-done | bytes 98320 | tf_op jit(solution)/shard_map/reduce_scatter | solution.py:90
  500.9 1.5 convert_element_type.113
  (23 shorter events, 3.1 us)
Async XLA Ops:
  7.2 265.9 %copy-start = (bf16[1,1,512,512]{3,2,1,0:T(8,128)(2,1)S(1)}, bf16[1,1,512,512]{3,2,1,0:T(8,128)(2,1)}, u32[]{:S(2)}) copy-start(bf16[1,1,512,512]{3,2,1,0:T(8,128)(2,1)} %param.7) | copy-start | bytes 1572868
  7.2 68.3 %all-gather.3.cloned.1.call-start = ((), (), s32[]{:S(2)}) async-start(), calls=%async_computation.4 | async-start | bytes 1622016 | tf_op jit(solution)/shard_map/all_gather | solution.py:52
  7.9 258.1 %all-gather.5.cloned.1.call-start = ((), (), s32[]{:S(2)}) async-start(), calls=%async_computation.5 | async-start | bytes 6684672 | tf_op jit(solution)/shard_map/all_gather | solution.py:59
  82.5 194.7 %all-to-all-start = ((bf16[128,16,1,512]{3,0,2,1:T(8,128)(2,1)}), bf16[128,16,1,512]{3,0,2,1:T(8,128)(2,1)S(1)}, u32[]{:S(2)}, u32[]{:S(2)}) async-start(bf16[128,16,1,512]{3,0,2,1:T(8,128)(2,1)} %fusion), calls=%async_computation | async-start | bytes 4194304 | tf_op jit(solution)/shard_map/all_to_all | solution.py:58
  277.2 97.9 %all-to-all-start.2 = ((bf16[128,16,1,512]{3,0,2,1:T(8,128)(2,1)}), bf16[128,16,1,512]{3,0,2,1:T(8,128)(2,1)}, u32[]{:S(2)}, u32[]{:S(2)}) async-start(bf16[128,16,1,512]{3,0,2,1:T(8,128)(2,1)} %convert_bitcast_fusion), calls=%async_computation.2 | async-start | bytes 4194304 | tf_op jit(solution)/shard_map/all_to_all | solution.py:80
  375.2 102.9 %all-to-all-start.1 = ((bf16[128,16,1,512]{3,0,2,1:T(8,128)(2,1)}), bf16[128,16,1,512]{3,0,2,1:T(8,128)(2,1)}, u32[]{:S(2)}, u32[]{:S(2)}) async-start(bf16[128,16,1,512]{3,0,2,1:T(8,128)(2,1)} %convert_bitcast_fusion.1), calls=%async_computation.1 | async-start | bytes 4194304 | tf_op jit(solution)/shard_map/all_to_all | solution.py:79
  386.1 114.8 %reduce-scatter.2.cloned.1.call-start = ((), (), s32[]{:S(2)}) async-start(), calls=%async_computation.6 | async-start | bytes 3244032 | tf_op jit(solution)/shard_map/reduce_scatter | solution.py:90
Sparse Core Ops, SparseCore 0:
  11.1 64.2 all-gather.2
  78.0 187.8 all-gather.4
  396.1 104.7 reduce-scatter.1
where the time goes:
time: 510 us; the launch traced here: 509 us
  waiting for transfers between devices  417 us (82%)
  starting transfers between devices  30 us (6%)
  local copies, waits for them, and re-layouts  18.2 us (4%)
  matrix products  18.2 us (4%)
  between operations  16.4 us (3%)
  other arithmetic  9.05 us (2%)
    all_gather x1, waiting for transfers between devices, per_device(): piece_rows = lax.all_gather(out_grad, 'row', axis=0, tiled=True)  169 us
    all_to_all x1, waiting for transfers between devices, per_device(): lax.all_to_all(partial_in, 'row', split_axis=1, concat_axis=1, tiled=True)  88.4 us
    all_to_all x1, waiting for transfers between devices, per_device(): lax.all_to_all(partial_out, 'row', split_axis=1, concat_axis=1, tiled=True)  77.1 us
    all_gather x1, waiting for transfers between devices, per_device(): whole_rows = lax.all_gather(activations, 'col', axis=1, tiled=True)  63.2 us
    reduce_scatter x1, waiting for transfers between devices, per_device(): lax.psum_scatter(rows_sum, 'col', scatter_dimension=1, tiled=True)  18.7 us
    all_to_all x1, starting transfers between devices, per_device(): lax.all_to_all(act_send, 'row', split_axis=1, concat_axis=1, tiled=True)  12 us
    all_to_all x1, starting transfers between devices, per_device(): lax.all_to_all(partial_out, 'row', split_axis=1, concat_axis=1, tiled=True)  11 us
  transfers between devices with their start and end apart: 6, of which 5 were waited for; matrix products, arithmetic and copies ran while one was open for 9% of the time, Pallas kernels for 0%

commit v1 on v0

v1 whole, which is shorter than its diff:
```python
import functools
import math

import jax
import jax.numpy as jnp
from jax import lax
from jax.experimental import pallas as pl
from jax.experimental.pallas import tpu as pltpu
from jax.sharding import PartitionSpec as P

BF = jnp.bfloat16
F32 = jnp.float32
NX, NY, NC = 4, 4, 2
VMEM_BYTES = 48 * 1024 * 1024


def col_of(x, y, c):
    return (x * NY + y) * NC + c


X_GROUPS = [[col_of(x, y, c) for x in range(NX)] for y in range(NY) for c in range(NC)]
Y_GROUPS = [[col_of(x, y, c) for y in range(NY)] for x in range(NX) for c in range(NC)]
CORE_SWAP = [(i, i ^ 1) for i in range(NX * NY * NC)]


def tokens_kernel(meta, act_ref, grad_ref, w_ref, out_ref, in_ref, out_acc, in_acc, *, blk):
    step = pl.program_id(0)

    @pl.when(step == 0)
    def _():
        out_acc[...] = jnp.zeros_like(out_acc)
        in_acc[...] = jnp.zeros_like(in_acc)

    hid = pl.ds(pl.multiple_of(meta[1, step] * blk, blk), blk)
    mod = pl.ds(pl.multiple_of(meta[2, step] * blk, blk), blk)
    w = w_ref[0]
    out_acc[hid, :] += jnp.dot(w, act_ref[mod, :], preferred_element_type=F32)
    in_acc[:, mod] += jnp.dot(grad_ref[:, hid], w, preferred_element_type=F32)

    @pl.when(step == pl.num_programs(0) - 1)
    def _():
        out_ref[...] = out_acc[...].T.astype(BF)
        in_ref[...] = in_acc[...].T.astype(BF)


def tokens_step(meta, act_t, grad, w_all):
    blk = w_all.shape[1]
    feats, toks = act_t.shape
    hidden = grad.shape[1]
    whole = lambda k, m: (0, 0)
    return pl.pallas_call(
        functools.partial(tokens_kernel, blk=blk),
        grid_spec=pltpu.PrefetchScalarGridSpec(
            num_scalar_prefetch=1,
            grid=(meta.shape[1],),
            in_specs=[
                pl.BlockSpec((feats, toks), whole),
                pl.BlockSpec((toks, hidden), whole),
                pl.BlockSpec((1, blk, blk), lambda k, m: (m[0, k], 0, 0)),
            ],
            out_specs=[
                pl.BlockSpec((toks, hidden), whole),
                pl.BlockSpec((feats, toks), whole),
            ],
            scratch_shapes=[pltpu.VMEM((hidden, toks), F32), pltpu.VMEM((toks, feats), F32)],
        ),
        out_shape=[
            jax.ShapeDtypeStruct((toks, hidden), BF),
            jax.ShapeDtypeStruct((feats, toks), BF),
        ],
        compiler_params=pltpu.CompilerParams(vmem_limit_bytes=VMEM_BYTES),
        name="tokens_step",
    )(meta, act_t, grad, w_all)


def wgrad_kernel(core, grad_ref, own_ref, oth_ref, out_ref, a_buf, b_buf, *, scale):
    n_x, n_z, rows, toks = grad_ref.shape
    piece = own_ref.shape[2]

    @pl.when(pl.program_id(0) == 0)
    def _():
        for x in range(n_x):
            for z in range(n_z):
                a_buf[x * rows : (x + 1) * rows, z * toks : (z + 1) * toks] = grad_ref[x, z]

    own_rows = pl.ds(pl.multiple_of(core[0] * piece, piece), piece)
    oth_rows = pl.ds(pl.multiple_of((1 - core[0]) * piece, piece), piece)
    for z in range(n_z):
        b_buf[own_rows, z * toks : (z + 1) * toks] = own_ref[0, z]
        b_buf[oth_rows, z * toks : (z + 1) * toks] = oth_ref[0, z]
    prod = lax.dot_general(
        a_buf[...], b_buf[...], (((1,), (1,)), ((), ())), preferred_element_type=F32
    )
    out_ref[...] = (prod * scale).astype(BF)


def wgrad_products(core, grad_x, act_own, act_oth, scale):
    n_x, n_z, rows, toks = grad_x.shape
    n_y, _, piece, _ = act_own.shape
    span = NC * piece
    block = pl.BlockSpec((1, n_z, piece, toks), lambda y, m: (y, 0, 0, 0))
    return pl.pallas_call(
        functools.partial(wgrad_kernel, scale=scale),
        grid_spec=pltpu.PrefetchScalarGridSpec(
            num_scalar_prefetch=1,
            grid=(n_y,),
            in_specs=[
                pl.BlockSpec((n_x, n_z, rows, toks), lambda y, m: (0, 0, 0, 0)),
                block,
                block,
            ],
            out_specs=pl.BlockSpec((n_x * rows, span), lambda y, m: (0, y)),
            scratch_shapes=[
                pltpu.VMEM((n_x * rows, n_z * toks), BF),
                pltpu.VMEM((span, n_z * toks), BF),
            ],
        ),
        out_shape=jax.ShapeDtypeStruct((n_x * rows, n_y * span), BF),
        compiler_params=pltpu.CompilerParams(vmem_limit_bytes=VMEM_BYTES),
        name="wgrad_products",
    )(core, grad_x, act_own, act_oth)


def slots_kernel(meta, prod_ref, out_ref, *, chunk, blk, per_x):
    for s in range(out_ref.shape[0]):
        hid, mod, full = meta[0, s], meta[1, s], meta[2, s]
        rows = pl.ds(pl.multiple_of(hid * chunk, chunk), chunk)
        cols = pl.ds(pl.multiple_of(lax.rem(mod, per_x) * blk, blk), blk)
        part = prod_ref[lax.div(mod, per_x), rows, cols]
        out_ref[s] = jnp.where(full > 0, part, jnp.zeros_like(part))


def pick_slots(meta, prods, chunk, blk):
    owners = meta.shape[1]
    return pl.pallas_call(
        functools.partial(slots_kernel, chunk=chunk, blk=blk, per_x=prods.shape[2] // blk),
        in_specs=[
            pl.BlockSpec(memory_space=pltpu.SMEM),
            pl.BlockSpec(memory_space=pltpu.VMEM),
        ],
        out_specs=pl.BlockSpec(memory_space=pltpu.VMEM),
        out_shape=jax.ShapeDtypeStruct((owners, chunk, blk), BF),
        compiler_params=pltpu.CompilerParams(vmem_limit_bytes=VMEM_BYTES),
        name="pick_slots",
    )(meta, prods)


def layout_tables(block_mask, block_owner, group, n_groups, owners):
    per_group = block_mask.shape[0] // n_groups
    model_blocks = block_mask.shape[1]
    size = per_group * model_blocks
    mask = lax.dynamic_slice_in_dim(block_mask, group * per_group, per_group, 0).reshape(size)
    owner = lax.dynamic_slice_in_dim(block_owner, group * per_group, per_group, 0).reshape(size)
    ids = jnp.arange(size, dtype=jnp.int32)
    before = jnp.sum(jnp.where(ids[:, None] < ids[None, :], mask[:, None], 0), axis=0)
    count = size // 4
    ranked = jnp.where(
        (before[None, :] == jnp.arange(count, dtype=jnp.int32)[:, None]) & (mask[None, :] == 1), 1, 0
    )
    id_of = jnp.sum(ranked * ids[None, :], axis=1)
    owner_of = jnp.sum(ranked * owner[None, :], axis=1)
    listed = jnp.stack([owner_of, id_of // model_blocks, id_of % model_blocks])
    held = jnp.where(
        (owner[None, :] == jnp.arange(owners, dtype=jnp.int32)[:, None]) & (mask[None, :] == 1), 1, 0
    )
    full = jnp.sum(held, axis=1)
    id_at = jnp.sum(held * ids[None, :], axis=1)
    slots = jnp.stack([id_at // model_blocks, id_at % model_blocks, full])
    return listed, slots


def share(x, groups):
    n = len(groups[0])
    wide = jnp.broadcast_to(x[None], (n, *x.shape))
    return lax.all_to_all(wide, "col", 0, 0, tiled=True, axis_index_groups=groups)


def per_device(activations, out_grad, weight_slots, block_mask, block_owner):
    blk = weight_slots.shape[2]
    owners, groups = lax.axis_size("row"), lax.axis_size("col")
    group = lax.axis_index("col")
    toks, piece = activations.shape
    hidden = out_grad.shape[1]
    hid_blocks = hidden // blk
    chunk = blk // owners
    listed, slots = layout_tables(block_mask, block_owner, group, groups, owners)

    w_all = lax.all_gather(weight_slots[0, 0], "row", axis=0)
    act_t = activations.T
    grad_t = out_grad.T

    act_z = lax.all_gather(act_t, "row", axis=0)
    grad_send = grad_t.reshape(hid_blocks, owners, chunk, toks).transpose(1, 0, 2, 3)
    grad_z = lax.all_to_all(
        grad_send.reshape(owners, hid_blocks * chunk, toks), "row", 0, 0, tiled=True
    )
    act_own = share(act_z, Y_GROUPS).reshape(NY, owners, piece, toks)
    act_oth = lax.ppermute(act_own, "col", CORE_SWAP)
    grad_x = share(grad_z, X_GROUPS).reshape(NX, owners, hid_blocks * chunk, toks)
    core = lax.rem(group, NC).reshape(1).astype(jnp.int32)
    scale = 1.0 / math.sqrt(toks * owners)
    prods = wgrad_products(core, grad_x, act_own, act_oth, scale)
    prods = lax.all_to_all(
        prods.reshape(NX, hid_blocks * chunk, -1),
        "col",
        0,
        0,
        tiled=True,
        axis_index_groups=X_GROUPS,
    )
    slot_parts = pick_slots(slots, prods, chunk, blk)
    weight_grad = lax.all_to_all(slot_parts, "row", 0, 0, tiled=True).reshape(1, 1, blk, blk)

    act_all = lax.all_to_all(
        jnp.broadcast_to(act_t[None], (groups, piece, toks)), "col", 0, 0, tiled=True
    ).reshape(groups * piece, toks)
    outputs, in_part = tokens_step(listed, act_all, out_grad, w_all)
    in_recv = lax.all_to_all(in_part.reshape(groups, piece, toks), "col", 0, 0, tiled=True)
    in_grad = jnp.sum(in_recv.astype(F32), axis=0).astype(BF).T
    return outputs, in_grad, weight_grad


def solution(mesh):
    placed = (P("row", "col"), P("row", "col"), P("col", "row", None, None), P(), P())
    return jax.shard_map(
        per_device,
        mesh=mesh,
        in_specs=placed,
        out_specs=(P("row", "col"), P("row", "col"), P("col", "row", None, None)),
        check_vma=False,
    )
```

time: 510 us -> 280 us (0.55)
  waiting for transfers between devices: 417 us -> 74.6 us
  blocking collectives: 0 us -> 117 us
  Pallas kernels: 0 us -> 19.4 us
  matrix products: 18.2 us -> 0 us
  starting transfers between devices: 30 us -> 45.9 us
  local copies, waits for them, and re-layouts: 18.2 us -> 6.89 us
  other arithmetic: 9.05 us -> 1.24 us
    all_gather x2 -> x1, waiting for transfers between devices: 232 us -> 0.02 us  [per_device(): w_all = lax.all_gather(weight_slots[0, 0], 'row', axis=0)]
    all_to_all x3 -> x4, waiting for transfers between devices: 166 us -> 73.9 us  [the longest x1 22.8 us: per_device(): lax.all_to_all(in_part.reshape(groups, piece, toks), 'col', 0, 0, tiled=T...]
    all_to_all x0 -> x3, blocking collectives: none -> 79.8 us  [the longest x1 33.6 us: share(): lax.all_to_all(wide, 'col', 0, 0, tiled=True, axis_index_groups=groups)]
    all_gather x0 -> x1, blocking collectives: none -> 36.8 us  [per_device(): act_z = lax.all_gather(act_t, 'row', axis=0)]
    pallas_call x0 -> x3, Pallas kernels: none -> 19.4 us  [the longest x1 9.97 us: tokens_step(): pl.pallas_call(functools.partial(tokens_kernel, blk=blk), grid_spec=pltpu...]
    reduce_scatter x1 -> x0, waiting for transfers between devices: 18.7 us -> none  [per_device(): lax.psum_scatter(rows_sum, 'col', scatter_dimension=1, tiled=True)]
    dot_general x5 -> x0, matrix products: 18.2 us -> none  [the longest x1 4.87 us: per_device(): jnp.einsum('tasi,asd->tdi', in_back, model_onehot, preferred_element_type...]
    ppermute x0 -> x1, starting transfers between devices: none -> 11.5 us  [per_device(): act_oth = lax.ppermute(act_own, 'col', CORE_SWAP)]
  transfers between devices with their start and end apart: 6 -> 6, of which waited for: 5 -> 4; matrix products, arithmetic and copies ran while one was open for 9% -> 2% of each run, Pallas kernels for 0% -> 7%
where the time goes in v1:
time: 280 us; the launch traced here: 279 us
  blocking collectives  117 us (42%)
  waiting for transfers between devices  74.6 us (27%)
  starting transfers between devices  45.9 us (16%)
  Pallas kernels  19.4 us (7%)
  between operations  14.2 us (5%)
  local copies, waits for them, and re-layouts  6.89 us (2%)
    all_gather x1, blocking collectives, per_device(): act_z = lax.all_gather(act_t, 'row', axis=0)  36.8 us
    all_to_all x1, blocking collectives, share(): lax.all_to_all(wide, 'col', 0, 0, tiled=True, axis_index_groups=groups)  33.6 us
    all_to_all x1, blocking collectives, per_device(): lax.all_to_all(grad_send.reshape(owners, hid_blocks * chunk, toks), 'row'...  31 us
    all_to_all x1, waiting for transfers between devices, per_device(): lax.all_to_all(in_part.reshape(groups, piece, toks), 'col', 0, 0, tiled=T...  22.8 us
    all_to_all x1, waiting for transfers between devices, per_device(): lax.all_to_all(jnp.broadcast_to(act_t[None], (groups, piece, toks)), 'col...  20.7 us
    all_to_all x1, waiting for transfers between devices, share(): lax.all_to_all(wide, 'col', 0, 0, tiled=True, axis_index_groups=groups)  17.9 us
    all_to_all x1, blocking collectives, per_device(): lax.all_to_all(prods.reshape(NX, hid_blocks * chunk, -1), 'col', 0, 0, ti...  15.3 us
    all_to_all x1, waiting for transfers between devices, per_device(): lax.all_to_all(slot_parts, 'row', 0, 0, tiled=True).reshape(1, 1, blk, blk)  12.6 us
  transfers between devices with their start and end apart: 6, of which 4 were waited for; matrix products, arithmetic and copies ran while one was open for 2% of the time, Pallas kernels for 7%

profile of v1, /device:TPU:1, one launch (start us, length us, event | category | flops | bytes accessed | tf_op | source)
XLA Modules:
  0.0 278.9 jit_solution(7636871880264857906)
XLA Ops:
  7.2 0.7 all-gather.4.cloned.1.call-update
  7.9 36.8 %all-gather.1 = bf16[3072,128]{1,0:T(8,128)(2,1)S(1)} all-gather(bf16[192,128]{1,0:T(8,128)(2,1)} %bitcast.42), channel_id=3, replica_groups=mesh['row'=16,'col'=32] {'row'}, dimensions={0}, use_global_device_ids=true | all-gather | bytes 835584 | tf_op jit(solution)/shard_map/all_gather | solution.py:192
  44.7 0.7 broadcast_in_dim.67
  45.5 33.6 %all_to_all.35.own_ref = bf16[4,16,192,128]{3,2,1,0:T(8,128)(2,1)S(1)} all-to-all(bf16[4,16,192,128]{3,2,1,0:T(8,128)(2,1)S(1)} %broadcast_in_dim.67), channel_id=1, replica_groups={{0,2,4,6},{1,3,5,7},{8,10,12,14},{9,11,13,15},{16,18,20,22},{17,19,21,2..., dimensions={0} | all-to-all | bytes 6291456 | tf_op jit(solution)/shard_map/all_to_all | solution.py:175
  79.1 11.5 %collective-permute-start = (bf16[4,16,192,128]{3,2,1,0:T(8,128)(2,1)S(1)}, bf16[4,16,192,128]{3,2,1,0:T(8,128)(2,1)}, u32[]{:S(2)}, u32[]{:S(2)}) collective-permute-start(bf16[4,16,192,128]{3,2,1,0:T(8,128)(2,1)S(1)} %all_to_all.35.own_ref), channel_id=1, source_target_pairs={{0,1},{1,0},{2,3},{3,2},{4,5},{5,4},{6,7},{7,6},{8,9},{9,8},{10,11... | collective-permute-start | bytes 9437192 | tf_op jit(solution)/shard_map/ppermute | solution.py:198
  90.7 0.9 copy.27
  91.6 1.0 copy.28
  92.6 31.0 %all_to_all.36 = bf16[16,96,128]{2,1,0:T(8,128)(2,1)S(1)} all-to-all(bf16[16,96,128]{2,1,0:T(8,128)(2,1)S(1)} %bitcast.40), channel_id=1, replica_groups=mesh['row'=16,'col'=32] {'row'}, dimensions={0} | all-to-all | bytes 786432 | tf_op jit(solution)/shard_map/all_to_all | solution.py:194
  123.6 1.4 broadcast_in_dim.65
  124.9 4.3 %all-to-all-start.3 = ((bf16[4,16,96,128]{3,2,1,0:T(8,128)(2,1)}), bf16[4,16,96,128]{3,2,1,0:T(8,128)(2,1)}, u32[]{:S(2)}, u32[]{:S(2)}) async-start(bf16[4,16,96,128]{3,2,1,0:T(8,128)(2,1)} %broadcast_in_dim.65), calls=%async_computation.3 | async-start | bytes 3145728 | tf_op jit(solution)/shard_map/all_to_all | solution.py:175
  129.3 17.9 %all-to-all-done.3.grad_ref = bf16[4,16,96,128]{3,2,1,0:T(8,128)(2,1)} async-done(((bf16[4,16,96,128]{3,2,1,0:T(8,128)(2,1)}), bf16[4,16,96,128]{3,2,1,0:T(8,128)(2,1)}, u32[]{:S(2)}, u32[]{:S(2)}) %all-to-all-start.3) | async-done | bytes 1572896 | tf_op jit(solution)/shard_map/all_to_all | solution.py:175
  147.2 8.0 %wgrad_products.1 = bf16[384,1536]{1,0:T(8,128)(2,1)S(1)} custom-call(s32[1]{0:T(128)} %bitcast.13.core, bf16[4,16,96,128]{3,2,1,0:T(8,128)(2,1)} %all-to-all-done.3.grad_ref, bf16[4,16,192,128]{3,2,1,0:T(8,128)(2,1)S(1)} %all_to_all.35.own_ref, bf16[4,16,192,128]{3,2,1,0:T(8,128)(2,1)} %collective-permute-done.oth_ref), custom_call_target="tpu_custom_call" | custom-call | tf_op jit(solution)/shard_map/wgrad_products/pallas_call | solution.py:102
  155.2 15.3 %all_to_all.37.prod_ref = bf16[4,96,1536]{2,1,0:T(8,128)(2,1)S(1)} all-to-all(bf16[4,96,1536]{2,1,0:T(8,128)(2,1)S(1)} %bitcast.36), channel_id=1, replica_groups={{0,8,16,24},{1,9,17,25},{2,10,18,26},{3,11,19,27},{4,12,20,28},{5,13,21..., dimensions={0} | all-to-all | bytes 2359296 | tf_op jit(solution)/shard_map/all_to_all | solution.py:203
  170.4 1.6 broadcast_in_dim.62
  172.0 8.5 %all-to-all-start = ((bf16[32,192,128]{2,1,0:T(8,128)(2,1)}), bf16[32,192,128]{2,1,0:T(8,128)(2,1)S(1)}, u32[]{:S(2)}, u32[]{:S(2)}) async-start(bf16[32,192,128]{2,1,0:T(8,128)(2,1)} %broadcast_in_dim.62), calls=%async_computation | async-start | bytes 3145728 | tf_op jit(solution)/shard_map/all_to_all | solution.py:214
  181.1 1.5 pick_slots.1
  182.6 20.7 %all-to-all-done = bf16[32,192,128]{2,1,0:T(8,128)(2,1)S(1)} async-done(((bf16[32,192,128]{2,1,0:T(8,128)(2,1)}), bf16[32,192,128]{2,1,0:T(8,128)(2,1)S(1)}, u32[]{:S(2)}, u32[]{:S(2)}) %all-to-all-start) | async-done | bytes 1572896 | tf_op jit(solution)/shard_map/all_to_all | solution.py:214
  203.3 10.7 %all-to-all-start.6 = ((bf16[16,32,512]{2,1,0:T(8,128)(2,1)}), bf16[16,32,512]{2,1,0:T(8,128)(2,1)S(1)}, u32[]{:S(2)}, u32[]{:S(2)}) async-start(bf16[16,32,512]{2,1,0:T(8,128)(2,1)} %pick_slots.1), calls=%async_computation.6 | async-start | bytes 1048576 | tf_op jit(solution)/shard_map/all_to_all | solution.py:212
  214.2 10.0 %tokens_step.1 = (bf16[128,1536]{1,0:T(8,128)(2,1)}, bf16[6144,128]{1,0:T(8,128)(2,1)}) custom-call(s32[3,9]{1,0:T(4,128)S(1)} %pad_add_fusion.meta, bf16[6144,128]{1,0:T(8,128)(2,1)S(1)} %bitcast.35, bf16[128,1536]{1,0:T(8,128)(2,1)S(1)} %copy-done, bf16[16,512,512]{2,1,0:T(8,128)(2,1)} %bitcast.37), custom_call_target="tpu_custom_call" | custom-call | tf_op jit(solution)/shard_map/tokens_step/pallas_call | solution.py:51
  224.2 12.6 %all-to-all-done.6 = bf16[16,32,512]{2,1,0:T(8,128)(2,1)S(1)} async-done(((bf16[16,32,512]{2,1,0:T(8,128)(2,1)}), bf16[16,32,512]{2,1,0:T(8,128)(2,1)S(1)}, u32[]{:S(2)}, u32[]{:S(2)}) %all-to-all-start.6) | async-done | bytes 524320 | tf_op jit(solution)/shard_map/all_to_all | solution.py:212
  236.8 10.8 %all-to-all-start.1 = ((bf16[32,192,128]{2,1,0:T(8,128)(2,1)}), bf16[32,192,128]{2,1,0:T(8,128)(2,1)S(1)}, u32[]{:S(2)}, u32[]{:S(2)}) async-start(bf16[32,192,128]{2,1,0:T(8,128)(2,1)} %bitcast.7), calls=%async_computation.1 | async-start | bytes 3145728 | tf_op jit(solution)/shard_map/all_to_all | solution.py:218
  247.6 22.8 %all-to-all-done.1 = bf16[32,192,128]{2,1,0:T(8,128)(2,1)S(1)} async-done(((bf16[32,192,128]{2,1,0:T(8,128)(2,1)}), bf16[32,192,128]{2,1,0:T(8,128)(2,1)S(1)}, u32[]{:S(2)}, u32[]{:S(2)}) %all-to-all-start.1) | async-done | bytes 1572896 | tf_op jit(solution)/shard_map/all_to_all | solution.py:218
  270.4 0.8 reduce_sum.60
  271.3 0.8 copy.30
  (24 shorter events, 0.9 us)
Async XLA Ops:
  7.2 207.1 %all-gather.4.cloned.1.call-start = ((), (), s32[]{:S(2)}) async-start(), calls=%async_computation.7 | async-start | bytes 8912896 | tf_op jit(solution)/shard_map/all_gather | solution.py:188
  45.5 45.2 %copy-start = (bf16[128,1536]{1,0:T(8,128)(2,1)S(1)}, bf16[128,1536]{1,0:T(8,128)(2,1)}, u32[]{:S(2)}) copy-start(bf16[128,1536]{1,0:T(8,128)(2,1)} %grad_ref.1) | copy-start | bytes 1179652
  79.1 68.0 %collective-permute-start = (bf16[4,16,192,128]{3,2,1,0:T(8,128)(2,1)S(1)}, bf16[4,16,192,128]{3,2,1,0:T(8,128)(2,1)}, u32[]{:S(2)}, u32[]{:S(2)}) collective-permute-start(bf16[4,16,192,128]{3,2,1,0:T(8,128)(2,1)S(1)} %all_to_all.35.own_ref), channel_id=1, source_target_pairs={{0,1},{1,0},{2,3},{3,2},{4,5},{5,4},{6,7},{7,6},{8,9},{9,8},{10,11... | collective-permute-start | bytes 9437192 | tf_op jit(solution)/shard_map/ppermute | solution.py:198
  124.9 22.2 %all-to-all-start.3 = ((bf16[4,16,96,128]{3,2,1,0:T(8,128)(2,1)}), bf16[4,16,96,128]{3,2,1,0:T(8,128)(2,1)}, u32[]{:S(2)}, u32[]{:S(2)}) async-start(bf16[4,16,96,128]{3,2,1,0:T(8,128)(2,1)} %broadcast_in_dim.65), calls=%async_computation.3 | async-start | bytes 3145728 | tf_op jit(solution)/shard_map/all_to_all | solution.py:175
  155.1 15.3 %copy-start.1 = (bf16[128,192]{0,1:T(8,128)(2,1)S(1)}, bf16[128,192]{0,1:T(8,128)(2,1)}, u32[]{:S(2)}) copy-start(bf16[128,192]{0,1:T(8,128)(2,1)} %param.5) | copy-start | bytes 147460
  172.0 8.5 %copy-start.2 = (s32[96,12]{0,1:T(8,128)S(1)}, s32[96,12]{0,1:T(8,128)}, u32[]{:S(2)}) copy-start(s32[96,12]{0,1:T(8,128)} %param.9) | copy-start | bytes 13828
  172.0 8.5 %copy-start.3 = (s32[96,12]{0,1:T(8,128)S(1)}, s32[96,12]{0,1:T(8,128)}, u32[]{:S(2)}) copy-start(s32[96,12]{0,1:T(8,128)} %param.8) | copy-start | bytes 13828
  172.0 31.3 %all-to-all-start = ((bf16[32,192,128]{2,1,0:T(8,128)(2,1)}), bf16[32,192,128]{2,1,0:T(8,128)(2,1)S(1)}, u32[]{:S(2)}, u32[]{:S(2)}) async-start(bf16[32,192,128]{2,1,0:T(8,128)(2,1)} %broadcast_in_dim.62), calls=%async_computation | async-start | bytes 3145728 | tf_op jit(solution)/shard_map/all_to_all | solution.py:214
  203.3 33.5 %all-to-all-start.6 = ((bf16[16,32,512]{2,1,0:T(8,128)(2,1)}), bf16[16,32,512]{2,1,0:T(8,128)(2,1)S(1)}, u32[]{:S(2)}, u32[]{:S(2)}) async-start(bf16[16,32,512]{2,1,0:T(8,128)(2,1)} %pick_slots.1), calls=%async_computation.6 | async-start | bytes 1048576 | tf_op jit(solution)/shard_map/all_to_all | solution.py:212
  236.8 33.6 %all-to-all-start.1 = ((bf16[32,192,128]{2,1,0:T(8,128)(2,1)}), bf16[32,192,128]{2,1,0:T(8,128)(2,1)S(1)}, u32[]{:S(2)}, u32[]{:S(2)}) async-start(bf16[32,192,128]{2,1,0:T(8,128)(2,1)} %bitcast.7), calls=%async_computation.1 | async-start | bytes 3145728 | tf_op jit(solution)/shard_map/all_to_all | solution.py:218
Sparse Core Ops, SparseCore 0:
  10.1 131.5 all-gather.3

commit v2 on v1

v2 whole, which is shorter than its diff:
```python
import functools
import math

import jax
import jax.numpy as jnp
from jax import lax
from jax.experimental import pallas as pl
from jax.experimental.pallas import tpu as pltpu
from jax.sharding import PartitionSpec as P

BF = jnp.bfloat16
F32 = jnp.float32
NX, NY, NC = 4, 4, 2
PARAMS = pltpu.CompilerParams(vmem_limit_bytes=48 * 1024 * 1024)


def col_of(x, y, c):
    return (x * NY + y) * NC + c


PLANE = [(x, y, c) for x in range(NX) for y in range(NY) for c in range(NC)]
XC_GROUPS = [[col_of(x, y, c) for x in range(NX) for c in range(NC)] for y in range(NY)]
Y_GROUPS = [[col_of(x, y, c) for y in range(NY)] for x in range(NX) for c in range(NC)]
CORE_SWAP = [(col_of(x, y, c), col_of(x, y, 1 - c)) for x, y, c in PLANE]
X_SHIFTS = {s: [(col_of(x, y, c), col_of((x + s) % NX, y, c)) for x, y, c in PLANE] for s in range(1, NX)}


def aligned(start, size, step):
    return pl.ds(pl.multiple_of(start, step), size)


def tokens_kernel(meta, place, own_ref, oth_ref, grad_ref, w_ref, out_ref, in_ref, act, out_acc, in_acc, *, blk):
    step = pl.program_id(0)

    @pl.when(step == 0)
    def _():
        out_acc[...] = jnp.zeros_like(out_acc)
        in_acc[...] = jnp.zeros_like(in_acc)
        piece = own_ref.shape[2]
        x, core = place[0], place[1]
        for s in range(NX):
            line = lax.rem(x - s + NX, NX) * NY
            for y in range(NY):
                act[aligned(((line + y) * NC + core) * piece, piece, 64), :] = own_ref[s, y]
                act[aligned(((line + y) * NC + 1 - core) * piece, piece, 64), :] = oth_ref[s, y]

    hid = aligned(meta[1, step] * blk, blk, blk)
    mod = aligned(meta[2, step] * blk, blk, blk)
    w = w_ref[0]
    out_acc[hid, :] += jnp.dot(w, act[mod, :], preferred_element_type=F32)
    in_acc[:, mod] += jnp.dot(grad_ref[:, hid], w, preferred_element_type=F32)

    @pl.when(step == pl.num_programs(0) - 1)
    def _():
        out_ref[...] = out_acc[...].T.astype(BF)
        in_ref[...] = in_acc[...].T.astype(BF)


def tokens_step(meta, place, act_own, act_oth, grad, w_all):
    blk = w_all.shape[1]
    piece, toks = act_own.shape[2:]
    feats = NX * NY * NC * piece
    hidden = grad.shape[1]
    lines = pl.BlockSpec((NX, NY, piece, toks), lambda k, m, p: (0, 0, 0, 0))
    whole = lambda k, m, p: (0, 0)
    return pl.pallas_call(
        functools.partial(tokens_kernel, blk=blk),
        grid_spec=pltpu.PrefetchScalarGridSpec(
            num_scalar_prefetch=2,
            grid=(meta.shape[1],),
            in_specs=[
                lines,
                lines,
                pl.BlockSpec((toks, hidden), whole),
                pl.BlockSpec((1, blk, blk), lambda k, m, p: (m[0, k], 0, 0)),
            ],
            out_specs=[
                pl.BlockSpec((toks, hidden), whole),
                pl.BlockSpec((feats, toks), whole),
            ],
            scratch_shapes=[
                pltpu.VMEM((feats, toks), BF),
                pltpu.VMEM((hidden, toks), F32),
                pltpu.VMEM((toks, feats), F32),
            ],
        ),
        out_shape=[
            jax.ShapeDtypeStruct((toks, hidden), BF),
            jax.ShapeDtypeStruct((feats, toks), BF),
        ],
        compiler_params=PARAMS,
        name="tokens_step",
    )(meta, place, act_own, act_oth, grad, w_all)


def wgrad_kernel(place, own_ref, oth_ref, act_ref, out_ref, a_buf, b_buf, *, scale):
    n_x, n_z, rows, toks = own_ref.shape
    n_y, _, piece, _ = act_ref.shape
    x, core = place[0], place[1]

    @pl.when(pl.program_id(0) == 0)
    def _():
        for s in range(n_x):
            line = lax.rem(x - s + n_x, n_x) * NC
            for z in range(n_z):
                a_buf[aligned((line + core) * rows, rows, rows), z * toks : (z + 1) * toks] = own_ref[s, z]
                a_buf[aligned((line + 1 - core) * rows, rows, rows), z * toks : (z + 1) * toks] = oth_ref[s, z]

    for y in range(n_y):
        for z in range(n_z):
            b_buf[y * piece : (y + 1) * piece, z * toks : (z + 1) * toks] = act_ref[y, z]
    prod = lax.dot_general(
        a_buf[...], b_buf[...], (((1,), (1,)), ((), ())), preferred_element_type=F32
    )
    out_ref[...] = (prod * scale).astype(BF)


def wgrad_products(place, grad_own, grad_oth, act_own, scale):
    n_x, n_z, rows, toks = grad_own.shape
    n_y, _, piece, _ = act_own.shape
    step_y = 2
    span = step_y * piece
    lines = pl.BlockSpec((n_x, n_z, rows, toks), lambda y, p: (0, 0, 0, 0))
    return pl.pallas_call(
        functools.partial(wgrad_kernel, scale=scale),
        grid_spec=pltpu.PrefetchScalarGridSpec(
            num_scalar_prefetch=1,
            grid=(n_y // step_y,),
            in_specs=[
                lines,
                lines,
                pl.BlockSpec((step_y, n_z, piece, toks), lambda y, p: (y, 0, 0, 0)),
            ],
            out_specs=pl.BlockSpec((n_x * NC * rows, span), lambda y, p: (0, y)),
            scratch_shapes=[
                pltpu.VMEM((n_x * NC * rows, n_z * toks), BF),
                pltpu.VMEM((span, n_z * toks), BF),
            ],
        ),
        out_shape=jax.ShapeDtypeStruct((n_x * NC * rows, n_y * piece), BF),
        compiler_params=PARAMS,
        name="wgrad_products",
    )(place, grad_own, grad_oth, act_own)


def slots_kernel(meta, prod_ref, out_ref, line_buf, *, chunk, blk):
    piece = prod_ref.shape[2] // NY
    for x in range(NX):
        for y in range(NY):
            for c in range(NC):
                at = (y * NC + c) * piece
                line_buf[x, :, at : at + piece] = prod_ref[x * NC + c, :, y * piece : (y + 1) * piece]
    per_x = line_buf.shape[2] // blk
    for s in range(out_ref.shape[0]):
        hid, mod, full = meta[0, s], meta[1, s], meta[2, s]
        rows = aligned(hid * chunk, chunk, chunk)
        cols = aligned(lax.rem(mod, per_x) * blk, blk, blk)
        part = line_buf[lax.div(mod, per_x), rows, cols]
        out_ref[s] = jnp.where(full > 0, part, jnp.zeros_like(part))


def pick_slots(meta, prods, chunk, blk):
    owners = meta.shape[1]
    _, rows, cols = prods.shape
    return pl.pallas_call(
        functools.partial(slots_kernel, chunk=chunk, blk=blk),
        in_specs=[
            pl.BlockSpec(memory_space=pltpu.SMEM),
            pl.BlockSpec(memory_space=pltpu.VMEM),
        ],
        out_specs=pl.BlockSpec(memory_space=pltpu.VMEM),
        out_shape=jax.ShapeDtypeStruct((owners, chunk, blk), BF),
        scratch_shapes=[pltpu.VMEM((NX, rows, NC * cols), BF)],
        compiler_params=PARAMS,
        name="pick_slots",
    )(meta, prods)


def sum_kernel(parts_ref, out_ref):
    out_ref[...] = jnp.sum(parts_ref[...].astype(F32), axis=0).astype(BF)


def sum_groups(parts):
    return pl.pallas_call(
        sum_kernel,
        in_specs=[pl.BlockSpec(memory_space=pltpu.VMEM)],
        out_specs=pl.BlockSpec(memory_space=pltpu.VMEM),
        out_shape=jax.ShapeDtypeStruct(parts.shape[1:], BF),
        compiler_params=PARAMS,
        name="sum_groups",
    )(parts)


def layout_tables(block_mask, block_owner, group, n_groups, owners):
    per_group = block_mask.shape[0] // n_groups
    model_blocks = block_mask.shape[1]
    size = per_group * model_blocks
    mask = lax.dynamic_slice_in_dim(block_mask, group * per_group, per_group, 0).reshape(size)
    owner = lax.dynamic_slice_in_dim(block_owner, group * per_group, per_group, 0).reshape(size)
    ids = jnp.arange(size, dtype=jnp.int32)
    before = jnp.sum(jnp.where(ids[:, None] < ids[None, :], mask[:, None], 0), axis=0)
    count = size // 4
    ranked = jnp.where(
        (before[None, :] == jnp.arange(count, dtype=jnp.int32)[:, None]) & (mask[None, :] == 1), 1, 0
    )
    id_of = jnp.sum(ranked * ids[None, :], axis=1)
    owner_of = jnp.sum(ranked * owner[None, :], axis=1)
    listed = jnp.stack([owner_of, id_of // model_blocks, id_of % model_blocks])
    held = jnp.where(
        (owner[None, :] == jnp.arange(owners, dtype=jnp.int32)[:, None]) & (mask[None, :] == 1), 1, 0
    )
    full = jnp.sum(held, axis=1)
    id_at = jnp.sum(held * ids[None, :], axis=1)
    slots = jnp.stack([id_at // model_blocks, id_at % model_blocks, full])
    return listed, slots


def share_x(x):
    own = jnp.stack([x] + [lax.ppermute(x, "col", X_SHIFTS[s]) for s in range(1, NX)])
    return own, lax.ppermute(own, "col", CORE_SWAP)


def per_device(activations, out_grad, weight_slots, block_mask, block_owner):
    blk = weight_slots.shape[2]
    owners, groups = lax.axis_size("row"), lax.axis_size("col")
    group = lax.axis_index("col")
    toks, piece = activations.shape
    hidden = out_grad.shape[1]
    hid_blocks = hidden // blk
    chunk = blk // owners
    listed, slots = layout_tables(block_mask, block_owner, group, groups, owners)
    place = jnp.stack([group // (NY * NC), group % NC]).astype(jnp.int32)

    w_all = lax.all_gather(weight_slots[0, 0], "row", axis=0)

    grad_send = out_grad.T.reshape(hid_blocks, owners, chunk, toks).transpose(1, 0, 2, 3)
    grad_z = lax.all_to_all(
        grad_send.reshape(owners, hid_blocks * chunk, toks), "row", 0, 0, tiled=True
    )
    act_z = lax.all_gather(activations.T, "row", axis=0)
    act_z, grad_z = lax.optimization_barrier((act_z, grad_z))
    act_y = lax.all_to_all(
        jnp.broadcast_to(act_z[None], (NY, *act_z.shape)),
        "col",
        0,
        0,
        tiled=True,
        axis_index_groups=Y_GROUPS,
    ).reshape(NY, owners, piece, toks)
    grad_own, grad_oth = share_x(grad_z)
    scale = 1.0 / math.sqrt(toks * owners)
    prods = wgrad_products(place, grad_own, grad_oth, act_y, scale)
    prods = lax.all_to_all(
        prods.reshape(NX * NC, hid_blocks * chunk, NY * piece),
        "col",
        0,
        0,
        tiled=True,
        axis_index_groups=XC_GROUPS,
    )
    slot_parts = pick_slots(slots, prods, chunk, blk)
    weight_grad = lax.all_to_all(slot_parts, "row", 0, 0, tiled=True).reshape(1, 1, blk, blk)

    act_here = lax.dynamic_index_in_dim(act_y, lax.axis_index("row"), 1, keepdims=False)
    act_own, act_oth = share_x(act_here)
    outputs, in_part = tokens_step(listed, place, act_own, act_oth, out_grad, w_all)
    in_recv = lax.all_to_all(in_part.reshape(groups, piece, toks), "col", 0, 0, tiled=True)
    return outputs, sum_groups(in_recv).T, weight_grad


def solution(mesh):
    placed = (P("row", "col"), P("row", "col"), P("col", "row", None, None), P(), P())
    return jax.shard_map(
        per_device,
        mesh=mesh,
        in_specs=placed,
        out_specs=(P("row", "col"), P("row", "col"), P("col", "row", None, None)),
        check_vma=False,
    )
```

time: 280 us -> 237 us (0.85)
  blocking collectives: 117 us -> 55.4 us
  starting transfers between devices: 45.9 us -> 79.7 us
  waiting for transfers between devices: 74.6 us -> 58.6 us
    all_to_all x3 -> x0, blocking collectives: 79.8 us -> none  [the longest x1 33.6 us: share(): lax.all_to_all(wide, 'col', 0, 0, tiled=True, axis_index_groups=groups)]
    all_to_all x2 -> x3, waiting for transfers between devices: 38.5 us -> 16.6 us  [the longest x1 15.9 us: per_device(): lax.all_to_all(prods.reshape(NX * NC, hid_blocks * chunk, NY * piece), 'c...]
    ppermute x1 -> x8, starting transfers between devices: 11.5 us -> 32.3 us  [the longest x6 19 us: share_x(): lax.ppermute(x, 'col', X_SHIFTS[s])]
    all_to_all x2 -> x3, starting transfers between devices: 12.9 us -> 32.1 us  [the longest x1 15.7 us: per_device(): lax.all_to_all(grad_send.reshape(owners, hid_blocks * chunk, toks), 'row'...]
    ppermute x1 -> x8, waiting for transfers between devices: 0.01 us -> 18.7 us  [the longest x6 14.1 us: share_x(): lax.ppermute(x, 'col', X_SHIFTS[s])]
    all_gather x1, blocking collectives: 36.8 us -> 55.4 us  [per_device(): act_z = lax.all_gather(activations.T, 'row', axis=0)]
    all_to_all x1, waiting for transfers between devices: 12.6 us -> 0.01 us  [per_device(): lax.all_to_all(slot_parts, 'row', 0, 0, tiled=True).reshape(1, 1, blk, blk)]
    all_to_all x1, starting transfers between devices: 10.8 us -> 5.08 us  [per_device(): lax.all_to_all(in_part.reshape(groups, piece, toks), 'col', 0, 0, tiled=T...]
  transfers between devices with their start and end apart: 6 -> 14, of which waited for: 4 -> 9; matrix products, arithmetic and copies ran while one was open for 2% -> 3% of each run, Pallas kernels for 7% -> 8%
where the time goes in v2:
time: 237 us; the launch traced here: 236 us
  starting transfers between devices  79.7 us (34%)
  waiting for transfers between devices  58.6 us (25%)
  blocking collectives  55.4 us (23%)
  Pallas kernels  20.4 us (9%)
  between operations  14.2 us (6%)
  local copies, waits for them, and re-layouts  6.71 us (3%)
    all_gather x1, blocking collectives, per_device(): act_z = lax.all_gather(activations.T, 'row', axis=0)  55.4 us
    all_to_all x1, waiting for transfers between devices, per_device(): lax.all_to_all(in_part.reshape(groups, piece, toks), 'col', 0, 0, tiled=T...  22.7 us
    ppermute x6, starting transfers between devices, share_x(): lax.ppermute(x, 'col', X_SHIFTS[s])  19 us
    all_to_all x1, waiting for transfers between devices, per_device(): lax.all_to_all(prods.reshape(NX * NC, hid_blocks * chunk, NY * piece), 'c...  15.9 us
    all_to_all x1, starting transfers between devices, per_device(): lax.all_to_all(grad_send.reshape(owners, hid_blocks * chunk, toks), 'row'...  15.7 us
    ppermute x6, waiting for transfers between devices, share_x(): lax.ppermute(x, 'col', X_SHIFTS[s])  14.1 us
    ppermute x2, starting transfers between devices, share_x(): return (own, lax.ppermute(own, 'col', CORE_SWAP))  13.3 us
    all_to_all x1, starting transfers between devices, per_device(): lax.all_to_all(prods.reshape(NX * NC, hid_blocks * chunk, NY * piece), 'c...  11.7 us
  transfers between devices with their start and end apart: 14, of which 9 were waited for; matrix products, arithmetic and copies ran while one was open for 3% of the time, Pallas kernels for 8%

profile of v2, /device:TPU:1, one launch (start us, length us, event | category | flops | bytes accessed | tf_op | source)
XLA Modules:
  0.0 235.8 jit_solution(525249382563751931)
XLA Ops:
  9.9 15.7 %all-to-all-start = ((bf16[16,96,128]{2,1,0:T(8,128)(2,1)}), bf16[16,96,128]{2,1,0:T(8,128)(2,1)S(1)}, u32[]{:S(2)}, u32[]{:S(2)}) async-start(bf16[16,96,128]{2,1,0:T(8,128)(2,1)} %bitcast.11), calls=%async_computation | async-start | bytes 786432 | tf_op jit(solution)/shard_map/all_to_all | solution.py:237
  25.7 55.4 %all-gather = bf16[3072,128]{1,0:T(8,128)(2,1)S(1)} all-gather(bf16[192,128]{1,0:T(8,128)(2,1)S(1)} %bitcast.58), channel_id=2, replica_groups=mesh['row'=16,'col'=32] {'row'}, dimensions={0}, use_global_device_ids=true | all-gather | bytes 835584 | tf_op jit(solution)/shard_map/all_gather | solution.py:240
  81.0 2.5 %broadcast_in_dim.48 = bf16[4,16,192,128]{3,2,1,0:T(8,128)(2,1)} broadcast(bf16[16,192,128]{2,1,0:T(8,128)(2,1)S(1)} %bitcast.47), dimensions={1,2,3} | broadcast | bytes 3932160 | tf_op jit(solution)/shard_map/broadcast_in_dim | solution.py:243
  83.5 4.7 %all-to-all-start.1 = ((bf16[4,16,192,128]{3,2,1,0:T(8,128)(2,1)}), bf16[4,16,192,128]{3,2,1,0:T(8,128)(2,1)}, u32[]{:S(2)}, u32[]{:S(2)}) async-start(bf16[4,16,192,128]{3,2,1,0:T(8,128)(2,1)} %broadcast_in_dim.48), calls=%async_computation.1 | async-start | bytes 6291456 | tf_op jit(solution)/shard_map/all_to_all | solution.py:242
  88.3 3.1 %collective-permute-start.4 = (bf16[16,96,128]{2,1,0:T(8,128)(2,1)S(1)}, bf16[16,96,128]{2,1,0:T(8,128)(2,1)S(1)}, u32[]{:S(2)}, u32[]{:S(2)}) collective-permute-start(bf16[16,96,128]{2,1,0:T(8,128)(2,1)S(1)} %all-to-all-done), channel_id=1, source_target_pairs={{0,8},{1,9},{2,10},{3,11},{4,12},{5,13},{6,14},{7,15},{8,16},{9,17... | collective-permute-start | bytes 1179656 | tf_op jit(solution)/shard_map/ppermute | solution.py:219
  91.4 4.4 %collective-permute-start.5 = (bf16[16,96,128]{2,1,0:T(8,128)(2,1)S(1)}, bf16[16,96,128]{2,1,0:T(8,128)(2,1)S(1)}, u32[]{:S(2)}, u32[]{:S(2)}) collective-permute-start(bf16[16,96,128]{2,1,0:T(8,128)(2,1)S(1)} %all-to-all-done), channel_id=1, source_target_pairs={{0,16},{1,17},{2,18},{3,19},{4,20},{5,21},{6,22},{7,23},{8,24},{9,... | collective-permute-start | bytes 1179656 | tf_op jit(solution)/shard_map/ppermute | solution.py:219
  95.8 3.1 %collective-permute-start.6 = (bf16[16,96,128]{2,1,0:T(8,128)(2,1)S(1)}, bf16[16,96,128]{2,1,0:T(8,128)(2,1)S(1)}, u32[]{:S(2)}, u32[]{:S(2)}) collective-permute-start(bf16[16,96,128]{2,1,0:T(8,128)(2,1)S(1)} %all-to-all-done), channel_id=1, source_target_pairs={{0,24},{1,25},{2,26},{3,27},{4,28},{5,29},{6,30},{7,31},{8,0},{9,1... | collective-permute-start | bytes 1179656 | tf_op jit(solution)/shard_map/ppermute | solution.py:219
  98.9 6.0 %collective-permute-done.5 = bf16[16,96,128]{2,1,0:T(8,128)(2,1)S(1)} collective-permute-done((bf16[16,96,128]{2,1,0:T(8,128)(2,1)S(1)}, bf16[16,96,128]{2,1,0:T(8,128)(2,1)S(1)}, u32[]{:S(2)}, u32[]{:S(2)}) %collective-permute-start.5) | collective-permute-done | bytes 393248 | tf_op jit(solution)/shard_map/ppermute | solution.py:219
  106.6 9.3 %collective-permute-start.7 = (bf16[4,16,96,128]{3,2,1,0:T(8,128)(2,1)S(1)}, bf16[4,16,96,128]{3,2,1,0:T(8,128)(2,1)S(1)}, u32[]{:S(2)}, u32[]{:S(2)}) collective-permute-start(bf16[4,16,96,128]{3,2,1,0:T(8,128)(2,1)S(1)} %pad_maximum_fusion.own_ref), channel_id=1, source_target_pairs={{0,1},{1,0},{2,3},{3,2},{4,5},{5,4},{6,7},{7,6},{8,9},{9,8},{10,11... | collective-permute-start | bytes 4718600 | tf_op jit(solution)/shard_map/ppermute | solution.py:220
  116.0 2.9 %collective-permute-done.7.oth_ref = bf16[4,16,96,128]{3,2,1,0:T(8,128)(2,1)S(1)} collective-permute-done((bf16[4,16,96,128]{3,2,1,0:T(8,128)(2,1)S(1)}, bf16[4,16,96,128]{3,2,1,0:T(8,128)(2,1)S(1)}, u32[]{:S(2)}, u32[]{:S(2)}) %collective-permute-start.7) | collective-permute-done | bytes 1572896 | tf_op jit(solution)/shard_map/ppermute | solution.py:220
  119.6 7.8 %wgrad_products.1 = bf16[768,768]{1,0:T(8,128)(2,1)} custom-call(s32[2]{0:T(128)S(1)} %pad_add_fusion.2.place, bf16[4,16,96,128]{3,2,1,0:T(8,128)(2,1)S(1)} %pad_maximum_fusion.own_ref, bf16[4,16,96,128]{3,2,1,0:T(8,128)(2,1)S(1)} %collective-permute-done.7.oth_ref, bf16[4,16,192,128]{3,2,1,0:T(8,128)(2,1)} %all-to-all-done.1.act_ref), custom_call_target="tpu_custom_call" | custom-call | tf_op jit(solution)/shard_map/wgrad_products/pallas_call | solution.py:124
  127.4 11.7 %all-to-all-start.3 = ((bf16[8,96,768]{2,1,0:T(8,128)(2,1)}), bf16[8,96,768]{2,1,0:T(8,128)(2,1)S(1)}, u32[]{:S(2)}, u32[]{:S(2)}) async-start(bf16[8,96,768]{2,1,0:T(8,128)(2,1)} %bitcast.28), calls=%async_computation.3 | async-start | bytes 2359296 | tf_op jit(solution)/shard_map/all_to_all | solution.py:253
  139.7 15.9 %all-to-all-done.3.prod_ref = bf16[8,96,768]{2,1,0:T(8,128)(2,1)S(1)} async-done(((bf16[8,96,768]{2,1,0:T(8,128)(2,1)}), bf16[8,96,768]{2,1,0:T(8,128)(2,1)S(1)}, u32[]{:S(2)}, u32[]{:S(2)}) %all-to-all-start.3) | async-done | bytes 1179680 | tf_op jit(solution)/shard_map/all_to_all | solution.py:253
  155.6 1.7 pick_slots.1
  157.3 10.2 %all-to-all-start.4 = ((bf16[16,32,512]{2,1,0:T(8,128)(2,1)}), bf16[16,32,512]{2,1,0:T(8,128)(2,1)S(1)}, u32[]{:S(2)}, u32[]{:S(2)}) async-start(bf16[16,32,512]{2,1,0:T(8,128)(2,1)} %pick_slots.1), calls=%async_computation.4 | async-start | bytes 1048576 | tf_op jit(solution)/shard_map/all_to_all | solution.py:262
  168.5 2.2 collective-permute-start
  170.7 3.7 %collective-permute-start.1 = (bf16[4,192,128]{2,1,0:T(8,128)(2,1)S(1)}, bf16[4,192,128]{2,1,0:T(8,128)(2,1)S(1)}, u32[]{:S(2)}, u32[]{:S(2)}) collective-permute-start(bf16[4,192,128]{2,1,0:T(8,128)(2,1)S(1)} %get-tuple-element.16), channel_id=1, source_target_pairs={{0,16},{1,17},{2,18},{3,19},{4,20},{5,21},{6,22},{7,23},{8,24},{9,... | collective-permute-start | bytes 589832 | tf_op jit(solution)/shard_map/ppermute | solution.py:219
  174.4 2.5 %collective-permute-start.2 = (bf16[4,192,128]{2,1,0:T(8,128)(2,1)S(1)}, bf16[4,192,128]{2,1,0:T(8,128)(2,1)S(1)}, u32[]{:S(2)}, u32[]{:S(2)}) collective-permute-start(bf16[4,192,128]{2,1,0:T(8,128)(2,1)S(1)} %get-tuple-element.16), channel_id=1, source_target_pairs={{0,24},{1,25},{2,26},{3,27},{4,28},{5,29},{6,30},{7,31},{8,0},{9,1... | collective-permute-start | bytes 589832 | tf_op jit(solution)/shard_map/ppermute | solution.py:219
  176.9 4.2 %collective-permute-done.1 = bf16[4,192,128]{2,1,0:T(8,128)(2,1)S(1)} collective-permute-done((bf16[4,192,128]{2,1,0:T(8,128)(2,1)S(1)}, bf16[4,192,128]{2,1,0:T(8,128)(2,1)S(1)}, u32[]{:S(2)}, u32[]{:S(2)}) %collective-permute-start.1) | collective-permute-done | bytes 196640 | tf_op jit(solution)/shard_map/ppermute | solution.py:219
  181.1 2.4 %collective-permute-done.2 = bf16[4,192,128]{2,1,0:T(8,128)(2,1)S(1)} collective-permute-done((bf16[4,192,128]{2,1,0:T(8,128)(2,1)S(1)}, bf16[4,192,128]{2,1,0:T(8,128)(2,1)S(1)}, u32[]{:S(2)}, u32[]{:S(2)}) %collective-permute-start.2) | collective-permute-done | bytes 196640 | tf_op jit(solution)/shard_map/ppermute | solution.py:219
  183.6 4.0 %collective-permute-start.3 = (bf16[4,4,192,128]{3,2,1,0:T(8,128)(2,1)S(1)}, bf16[4,4,192,128]{3,2,1,0:T(8,128)(2,1)S(1)}, u32[]{:S(2)}, u32[]{:S(2)}) collective-permute-start(bf16[4,4,192,128]{3,2,1,0:T(8,128)(2,1)S(1)} %pad_maximum_fusion.1.own_ref), channel_id=1, source_target_pairs={{0,1},{1,0},{2,3},{3,2},{4,5},{5,4},{6,7},{7,6},{8,9},{9,8},{10,11... | collective-permute-start | bytes 2359304 | tf_op jit(solution)/shard_map/ppermute | solution.py:220
  189.5 10.1 %tokens_step.1 = (bf16[128,1536]{1,0:T(8,128)(2,1)}, bf16[6144,128]{1,0:T(8,128)(2,1)}) custom-call(s32[3,9]{1,0:T(4,128)S(1)} %pad_add_fusion.meta, s32[2]{0:T(128)S(1)} %pad_add_fusion.2.place, bf16[4,4,192,128]{3,2,1,0:T(8,128)(2,1)S(1)} %pad_maximum_fusion.1.own_ref, bf16[4,4,192,128]{3,2,1,0:T(8,128)(2,1)S(1)} %collective-permute-done.3.oth_ref, ...), custom_call_target="tpu_custom_call" | custom-call | tf_op jit(solution)/shard_map/tokens_step/pallas_call | solution.py:66
  199.6 5.1 %all-to-all-start.2 = ((bf16[32,192,128]{2,1,0:T(8,128)(2,1)}), bf16[32,192,128]{2,1,0:T(8,128)(2,1)S(1)}, u32[]{:S(2)}, u32[]{:S(2)}) async-start(bf16[32,192,128]{2,1,0:T(8,128)(2,1)} %bitcast.18), calls=%async_computation.2 | async-start | bytes 3145728 | tf_op jit(solution)/shard_map/all_to_all | solution.py:267
  204.7 22.7 %all-to-all-done.2.parts_ref = bf16[32,192,128]{2,1,0:T(8,128)(2,1)S(1)} async-done(((bf16[32,192,128]{2,1,0:T(8,128)(2,1)}), bf16[32,192,128]{2,1,0:T(8,128)(2,1)S(1)}, u32[]{:S(2)}, u32[]{:S(2)}) %all-to-all-start.2) | async-done | bytes 1572896 | tf_op jit(solution)/shard_map/all_to_all | solution.py:267
  (39 shorter events, 10.4 us)
Async XLA Ops:
  7.2 18.5 %copy-start.1 = (bf16[128,192]{0,1:T(8,128)(2,1)S(1)}, bf16[128,192]{0,1:T(8,128)(2,1)}, u32[]{:S(2)}) copy-start(bf16[128,192]{0,1:T(8,128)(2,1)} %param.5) | copy-start | bytes 147460
  7.2 182.3 %all-gather.4.cloned.1.call-start = ((), (), s32[]{:S(2)}) async-start(), calls=%async_computation.5 | async-start | bytes 8912896 | tf_op jit(solution)/shard_map/all_gather | solution.py:234
  9.9 71.1 %all-to-all-start = ((bf16[16,96,128]{2,1,0:T(8,128)(2,1)}), bf16[16,96,128]{2,1,0:T(8,128)(2,1)S(1)}, u32[]{:S(2)}, u32[]{:S(2)}) async-start(bf16[16,96,128]{2,1,0:T(8,128)(2,1)} %bitcast.11), calls=%async_computation | async-start | bytes 786432 | tf_op jit(solution)/shard_map/all_to_all | solution.py:237
  83.5 36.1 %all-to-all-start.1 = ((bf16[4,16,192,128]{3,2,1,0:T(8,128)(2,1)}), bf16[4,16,192,128]{3,2,1,0:T(8,128)(2,1)}, u32[]{:S(2)}, u32[]{:S(2)}) async-start(bf16[4,16,192,128]{3,2,1,0:T(8,128)(2,1)} %broadcast_in_dim.48), calls=%async_computation.1 | async-start | bytes 6291456 | tf_op jit(solution)/shard_map/all_to_all | solution.py:242
  88.3 10.6 %collective-permute-start.4 = (bf16[16,96,128]{2,1,0:T(8,128)(2,1)S(1)}, bf16[16,96,128]{2,1,0:T(8,128)(2,1)S(1)}, u32[]{:S(2)}, u32[]{:S(2)}) collective-permute-start(bf16[16,96,128]{2,1,0:T(8,128)(2,1)S(1)} %all-to-all-done), channel_id=1, source_target_pairs={{0,8},{1,9},{2,10},{3,11},{4,12},{5,13},{6,14},{7,15},{8,16},{9,17... | collective-permute-start | bytes 1179656 | tf_op jit(solution)/shard_map/ppermute | solution.py:219
  91.4 13.5 %collective-permute-start.5 = (bf16[16,96,128]{2,1,0:T(8,128)(2,1)S(1)}, bf16[16,96,128]{2,1,0:T(8,128)(2,1)S(1)}, u32[]{:S(2)}, u32[]{:S(2)}) collective-permute-start(bf16[16,96,128]{2,1,0:T(8,128)(2,1)S(1)} %all-to-all-done), channel_id=1, source_target_pairs={{0,16},{1,17},{2,18},{3,19},{4,20},{5,21},{6,22},{7,23},{8,24},{9,... | collective-permute-start | bytes 1179656 | tf_op jit(solution)/shard_map/ppermute | solution.py:219
  95.8 10.6 %collective-permute-start.6 = (bf16[16,96,128]{2,1,0:T(8,128)(2,1)S(1)}, bf16[16,96,128]{2,1,0:T(8,128)(2,1)S(1)}, u32[]{:S(2)}, u32[]{:S(2)}) collective-permute-start(bf16[16,96,128]{2,1,0:T(8,128)(2,1)S(1)} %all-to-all-done), channel_id=1, source_target_pairs={{0,24},{1,25},{2,26},{3,27},{4,28},{5,29},{6,30},{7,31},{8,0},{9,1... | collective-permute-start | bytes 1179656 | tf_op jit(solution)/shard_map/ppermute | solution.py:219
  106.6 12.3 %collective-permute-start.7 = (bf16[4,16,96,128]{3,2,1,0:T(8,128)(2,1)S(1)}, bf16[4,16,96,128]{3,2,1,0:T(8,128)(2,1)S(1)}, u32[]{:S(2)}, u32[]{:S(2)}) collective-permute-start(bf16[4,16,96,128]{3,2,1,0:T(8,128)(2,1)S(1)} %pad_maximum_fusion.own_ref), channel_id=1, source_target_pairs={{0,1},{1,0},{2,3},{3,2},{4,5},{5,4},{6,7},{7,6},{8,9},{9,8},{10,11... | collective-permute-start | bytes 4718600 | tf_op jit(solution)/shard_map/ppermute | solution.py:220
  127.4 11.7 %copy-start.2 = (s32[96,12]{0,1:T(8,128)S(1)}, s32[96,12]{0,1:T(8,128)}, u32[]{:S(2)}) copy-start(s32[96,12]{0,1:T(8,128)} %param.9) | copy-start | bytes 13828
  127.4 11.7 %copy-start.3 = (s32[96,12]{0,1:T(8,128)S(1)}, s32[96,12]{0,1:T(8,128)}, u32[]{:S(2)}) copy-start(s32[96,12]{0,1:T(8,128)} %param.8) | copy-start | bytes 13828
  127.4 28.2 %all-to-all-start.3 = ((bf16[8,96,768]{2,1,0:T(8,128)(2,1)}), bf16[8,96,768]{2,1,0:T(8,128)(2,1)S(1)}, u32[]{:S(2)}, u32[]{:S(2)}) async-start(bf16[8,96,768]{2,1,0:T(8,128)(2,1)} %bitcast.28), calls=%async_computation.3 | async-start | bytes 2359296 | tf_op jit(solution)/shard_map/all_to_all | solution.py:253
  157.3 32.2 %copy-start = (bf16[128,1536]{1,0:T(8,128)(2,1)S(1)}, bf16[128,1536]{1,0:T(8,128)(2,1)}, u32[]{:S(2)}) copy-start(bf16[128,1536]{1,0:T(8,128)(2,1)} %grad_ref.1) | copy-start | bytes 1179652
  157.3 42.3 %all-to-all-start.4 = ((bf16[16,32,512]{2,1,0:T(8,128)(2,1)}), bf16[16,32,512]{2,1,0:T(8,128)(2,1)S(1)}, u32[]{:S(2)}, u32[]{:S(2)}) async-start(bf16[16,32,512]{2,1,0:T(8,128)(2,1)} %pick_slots.1), calls=%async_computation.4 | async-start | bytes 1048576 | tf_op jit(solution)/shard_map/all_to_all | solution.py:262
  168.5 8.4 %collective-permute-start = (bf16[4,192,128]{2,1,0:T(8,128)(2,1)S(1)}, bf16[4,192,128]{2,1,0:T(8,128)(2,1)S(1)}, u32[]{:S(2)}, u32[]{:S(2)}) collective-permute-start(bf16[4,192,128]{2,1,0:T(8,128)(2,1)S(1)} %get-tuple-element.16), channel_id=1, source_target_pairs={{0,8},{1,9},{2,10},{3,11},{4,12},{5,13},{6,14},{7,15},{8,16},{9,17... | collective-permute-start | bytes 589832 | tf_op jit(solution)/shard_map/ppermute | solution.py:219
  170.7 10.4 %collective-permute-start.1 = (bf16[4,192,128]{2,1,0:T(8,128)(2,1)S(1)}, bf16[4,192,128]{2,1,0:T(8,128)(2,1)S(1)}, u32[]{:S(2)}, u32[]{:S(2)}) collective-permute-start(bf16[4,192,128]{2,1,0:T(8,128)(2,1)S(1)} %get-tuple-element.16), channel_id=1, source_target_pairs={{0,16},{1,17},{2,18},{3,19},{4,20},{5,21},{6,22},{7,23},{8,24},{9,... | collective-permute-start | bytes 589832 | tf_op jit(solution)/shard_map/ppermute | solution.py:219
  174.4 9.1 %collective-permute-start.2 = (bf16[4,192,128]{2,1,0:T(8,128)(2,1)S(1)}, bf16[4,192,128]{2,1,0:T(8,128)(2,1)S(1)}, u32[]{:S(2)}, u32[]{:S(2)}) collective-permute-start(bf16[4,192,128]{2,1,0:T(8,128)(2,1)S(1)} %get-tuple-element.16), channel_id=1, source_target_pairs={{0,24},{1,25},{2,26},{3,27},{4,28},{5,29},{6,30},{7,31},{8,0},{9,1... | collective-permute-start | bytes 589832 | tf_op jit(solution)/shard_map/ppermute | solution.py:219
  183.6 5.9 %collective-permute-start.3 = (bf16[4,4,192,128]{3,2,1,0:T(8,128)(2,1)S(1)}, bf16[4,4,192,128]{3,2,1,0:T(8,128)(2,1)S(1)}, u32[]{:S(2)}, u32[]{:S(2)}) collective-permute-start(bf16[4,4,192,128]{3,2,1,0:T(8,128)(2,1)S(1)} %pad_maximum_fusion.1.own_ref), channel_id=1, source_target_pairs={{0,1},{1,0},{2,3},{3,2},{4,5},{5,4},{6,7},{7,6},{8,9},{9,8},{10,11... | collective-permute-start | bytes 2359304 | tf_op jit(solution)/shard_map/ppermute | solution.py:220
  199.6 27.8 %all-to-all-start.2 = ((bf16[32,192,128]{2,1,0:T(8,128)(2,1)}), bf16[32,192,128]{2,1,0:T(8,128)(2,1)S(1)}, u32[]{:S(2)}, u32[]{:S(2)}) async-start(bf16[32,192,128]{2,1,0:T(8,128)(2,1)} %bitcast.18), calls=%async_computation.2 | async-start | bytes 3145728 | tf_op jit(solution)/shard_map/all_to_all | solution.py:267
Sparse Core Ops, SparseCore 0:
  10.1 129.9 all-gather.3

commit v3 on v2

--- a/solution.py
+++ b/solution.py
@@ -143,7 +143,9 @@
     )(place, grad_own, grad_oth, act_own)
 
 
-def slots_kernel(meta, prod_ref, out_ref, line_buf, *, chunk, blk):
+def slots_kernel(meta, at_z, prod_ref, *refs, chunk, blk):
+    out_refs, line_buf = refs[:-1], refs[-1]
+    owners = len(out_refs)
     piece = prod_ref.shape[2] // NY
     for x in range(NX):
         for y in range(NY):
@@ -151,29 +153,52 @@
                 at = (y * NC + c) * piece
                 line_buf[x, :, at : at + piece] = prod_ref[x * NC + c, :, y * piece : (y + 1) * piece]
     per_x = line_buf.shape[2] // blk
-    for s in range(out_ref.shape[0]):
-        hid, mod, full = meta[0, s], meta[1, s], meta[2, s]
+    for s in range(owners):
+        owner = lax.rem(at_z[0] + s, owners)
+        hid, mod, full = meta[0, owner], meta[1, owner], meta[2, owner]
         rows = aligned(hid * chunk, chunk, chunk)
         cols = aligned(lax.rem(mod, per_x) * blk, blk, blk)
         part = line_buf[lax.div(mod, per_x), rows, cols]
-        out_ref[s] = jnp.where(full > 0, part, jnp.zeros_like(part))
-
-
-def pick_slots(meta, prods, chunk, blk):
+        out_refs[s][...] = jnp.where(full > 0, part, jnp.zeros_like(part))
+
+
+def pick_slots(meta, at_z, prods, chunk, blk):
     owners = meta.shape[1]
     _, rows, cols = prods.shape
     return pl.pallas_call(
         functools.partial(slots_kernel, chunk=chunk, blk=blk),
         in_specs=[
             pl.BlockSpec(memory_space=pltpu.SMEM),
+            pl.BlockSpec(memory_space=pltpu.SMEM),
             pl.BlockSpec(memory_space=pltpu.VMEM),
         ],
+        out_specs=[pl.BlockSpec(memory_space=pltpu.VMEM)] * owners,
+        out_shape=[jax.ShapeDtypeStruct((chunk, blk), BF)] * owners,
+        scratch_shapes=[pltpu.VMEM((NX, rows, NC * cols), BF)],
+        compiler_params=PARAMS,
+        name="pick_slots",
+    )(meta, at_z, prods)
+
+
+def join_kernel(at_z, *refs):
+    part_refs, out_ref = refs[:-1], refs[-1]
+    owners = len(part_refs)
+    chunk = part_refs[0].shape[0]
+    for s in range(owners):
+        source = lax.rem(at_z[0] - s + owners, owners)
+        out_ref[aligned(source * chunk, chunk, chunk), :] = part_refs[s][...]
+
+
+def join_rows(at_z, parts):
+    chunk, blk = parts[0].shape
+    return pl.pallas_call(
+        join_kernel,
+        in_specs=[pl.BlockSpec(memory_space=pltpu.SMEM)] + [pl.BlockSpec(memory_space=pltpu.VMEM)] * len(parts),
         out_specs=pl.BlockSpec(memory_space=pltpu.VMEM),
-        out_shape=jax.ShapeDtypeStruct((owners, chunk, blk), BF),
-        scratch_shapes=[pltpu.VMEM((NX, rows, NC * cols), BF)],
-        compiler_params=PARAMS,
-        name="pick_slots",
-    )(meta, prods)
+        out_shape=jax.ShapeDtypeStruct((chunk * len(parts), blk), BF),
+        compiler_params=PARAMS,
+        name="join_rows",
+    )(at_z, *parts)
 
 
 def sum_kernel(parts_ref, out_ref):
@@ -258,8 +283,13 @@
         tiled=True,
         axis_index_groups=XC_GROUPS,
     )
-    slot_parts = pick_slots(slots, prods, chunk, blk)
-    weight_grad = lax.all_to_all(slot_parts, "row", 0, 0, tiled=True).reshape(1, 1, blk, blk)
+    at_z = lax.axis_index("row").reshape(1).astype(jnp.int32)
+    slot_parts = pick_slots(slots, at_z, prods, chunk, blk)
+    slot_parts = [slot_parts[0]] + [
+        lax.ppermute(slot_parts[s], "row", [(z, (z + s) % owners) for z in range(owners)])
+        for s in range(1, owners)
+    ]
+    weight_grad = join_rows(at_z, slot_parts)[None, None]
 
     act_here = lax.dynamic_index_in_dim(act_y, lax.axis_index("row"), 1, keepdims=False)
     act_own, act_oth = share_x(act_here)

time: 237 us -> 266 us (1.12); the launches traced: 236 us -> 261 us
  starting transfers between devices: 79.7 us -> 145 us
  waiting for transfers between devices: 58.6 us -> 16.7 us
    ppermute x0 -> x15, starting transfers between devices: none -> 74.9 us  [per_device(): lax.ppermute(slot_parts[s], 'row', [(z, (z + s) % owners) for z in range(...]
    all_to_all x1, waiting for transfers between devices: 22.7 us -> 0.01 us  [per_device(): lax.all_to_all(in_part.reshape(groups, piece, toks), 'col', 0, 0, tiled=T...]
    all_to_all x1, waiting for transfers between devices: 15.9 us -> 0.11 us  [per_device(): lax.all_to_all(prods.reshape(NX * NC, hid_blocks * chunk, NY * piece), 'c...]
    all_to_all x1 -> x0, starting transfers between devices: 10.2 us -> none  [per_device(): lax.all_to_all(slot_parts, 'row', 0, 0, tiled=True).reshape(1, 1, blk, blk)]
    ppermute x6, waiting for transfers between devices: 14.1 us -> 7.57 us  [share_x(): lax.ppermute(x, 'col', X_SHIFTS[s])]
    all_to_all x1, waiting for transfers between devices: 0.66 us -> 3.65 us  [per_device(): lax.all_to_all(jnp.broadcast_to(act_z[None], (NY, *act_z.shape)), 'col',...]
    ppermute x0 -> x15, waiting for transfers between devices: none -> 2.76 us  [per_device(): lax.ppermute(slot_parts[s], 'row', [(z, (z + s) % owners) for z in range(...]
    ppermute x2, waiting for transfers between devices: 4.56 us -> 1.89 us  [share_x(): return (own, lax.ppermute(own, 'col', CORE_SWAP))]
  transfers between devices with their start and end apart: 14 -> 28, of which waited for: 9 -> 6; matrix products, arithmetic and copies ran while one was open for 3% -> 3% of each run, Pallas kernels for 8% -> 7%
where the time goes in v3:
time: 266 us; the launch traced here: 261 us
  starting transfers between devices  145 us (55%)
  blocking collectives  55.4 us (21%)
  Pallas kernels  19.1 us (7%)
  waiting for transfers between devices  16.7 us (6%)
  between operations  14.5 us (5%)
  local copies, waits for them, and re-layouts  8.76 us (3%)
    ppermute x15, starting transfers between devices, per_device(): lax.ppermute(slot_parts[s], 'row', [(z, (z + s) % owners) for z in range(...  74.9 us
    all_gather x1, blocking collectives, per_device(): act_z = lax.all_gather(activations.T, 'row', axis=0)  55.4 us
    ppermute x6, starting transfers between devices, share_x(): lax.ppermute(x, 'col', X_SHIFTS[s])  21.1 us
    all_to_all x1, starting transfers between devices, per_device(): lax.all_to_all(grad_send.reshape(owners, hid_blocks * chunk, toks), 'row'...  15.7 us
    all_to_all x1, starting transfers between devices, per_device(): lax.all_to_all(prods.reshape(NX * NC, hid_blocks * chunk, NY * piece), 'c...  11.6 us
    ppermute x2, starting transfers between devices, share_x(): return (own, lax.ppermute(own, 'col', CORE_SWAP))  11.3 us
    pallas_call x1, Pallas kernels, tokens_step(): pl.pallas_call(functools.partial(tokens_kernel, blk=blk), grid_spec=pltpu...  9.46 us
    ppermute x6, waiting for transfers between devices, share_x(): lax.ppermute(x, 'col', X_SHIFTS[s])  7.57 us
  transfers between devices with their start and end apart: 28, of which 6 were waited for; matrix products, arithmetic and copies ran while one was open for 3% of the time, Pallas kernels for 7%

profile of v3, /device:TPU:1, one launch (start us, length us, event | category | flops | bytes accessed | tf_op | source)
XLA Modules:
  0.0 261.2 jit_solution(7200678153095015708)
XLA Ops:
  9.9 15.7 %all-to-all-start = ((bf16[16,96,128]{2,1,0:T(8,128)(2,1)}), bf16[16,96,128]{2,1,0:T(8,128)(2,1)S(1)}, u32[]{:S(2)}, u32[]{:S(2)}) async-start(bf16[16,96,128]{2,1,0:T(8,128)(2,1)} %bitcast.11), calls=%async_computation | async-start | bytes 786432 | tf_op jit(solution)/shard_map/all_to_all | solution.py:262
  25.7 55.4 %all-gather = bf16[3072,128]{1,0:T(8,128)(2,1)S(1)} all-gather(bf16[192,128]{1,0:T(8,128)(2,1)S(1)} %bitcast.59), channel_id=2, replica_groups=mesh['row'=16,'col'=32] {'row'}, dimensions={0}, use_global_device_ids=true | all-gather | bytes 835584 | tf_op jit(solution)/shard_map/all_gather | solution.py:265
  83.5 4.7 %all-to-all-start.1 = ((bf16[4,16,192,128]{3,2,1,0:T(8,128)(2,1)}), bf16[4,16,192,128]{3,2,1,0:T(8,128)(2,1)}, u32[]{:S(2)}, u32[]{:S(2)}) async-start(bf16[4,16,192,128]{3,2,1,0:T(8,128)(2,1)} %broadcast_in_dim.51), calls=%async_computation.1 | async-start | bytes 6291456 | tf_op jit(solution)/shard_map/all_to_all | solution.py:267
  91.3 4.4 %collective-permute-start.5 = (bf16[16,96,128]{2,1,0:T(8,128)(2,1)S(1)}, bf16[16,96,128]{2,1,0:T(8,128)(2,1)S(1)}, u32[]{:S(2)}, u32[]{:S(2)}) collective-permute-start(bf16[16,96,128]{2,1,0:T(8,128)(2,1)S(1)} %all-to-all-done), channel_id=1, source_target_pairs={{0,16},{1,17},{2,18},{3,19},{4,20},{5,21},{6,22},{7,23},{8,24},{9,... | collective-permute-start | bytes 1179656 | tf_op jit(solution)/shard_map/ppermute | solution.py:244
  98.8 6.0 %collective-permute-done.5 = bf16[16,96,128]{2,1,0:T(8,128)(2,1)S(1)} collective-permute-done((bf16[16,96,128]{2,1,0:T(8,128)(2,1)S(1)}, bf16[16,96,128]{2,1,0:T(8,128)(2,1)S(1)}, u32[]{:S(2)}, u32[]{:S(2)}) %collective-permute-start.5) | collective-permute-done | bytes 393248 | tf_op jit(solution)/shard_map/ppermute | solution.py:244
  106.5 9.3 %collective-permute-start.7 = (bf16[4,16,96,128]{3,2,1,0:T(8,128)(2,1)S(1)}, bf16[4,16,96,128]{3,2,1,0:T(8,128)(2,1)S(1)}, u32[]{:S(2)}, u32[]{:S(2)}) collective-permute-start(bf16[4,16,96,128]{3,2,1,0:T(8,128)(2,1)S(1)} %pad_maximum_fusion.own_ref), channel_id=1, source_target_pairs={{0,1},{1,0},{2,3},{3,2},{4,5},{5,4},{6,7},{7,6},{8,9},{9,8},{10,11... | collective-permute-start | bytes 4718600 | tf_op jit(solution)/shard_map/ppermute | solution.py:245
  115.9 3.7 %all-to-all-done.1.act_ref = bf16[4,16,192,128]{3,2,1,0:T(8,128)(2,1)} async-done(((bf16[4,16,192,128]{3,2,1,0:T(8,128)(2,1)}), bf16[4,16,192,128]{3,2,1,0:T(8,128)(2,1)}, u32[]{:S(2)}, u32[]{:S(2)}) %all-to-all-start.1) | async-done | bytes 3145760 | tf_op jit(solution)/shard_map/all_to_all | solution.py:267
  121.2 3.2 %collective-permute-start = (bf16[4,192,128]{2,1,0:T(8,128)(2,1)}, bf16[4,192,128]{2,1,0:T(8,128)(2,1)S(1)}, u32[]{:S(2)}, u32[]{:S(2)}) collective-permute-start(bf16[4,192,128]{2,1,0:T(8,128)(2,1)} %get-tuple-element.48), channel_id=1, source_target_pairs={{0,8},{1,9},{2,10},{3,11},{4,12},{5,13},{6,14},{7,15},{8,16},{9,17... | collective-permute-start | bytes 589832 | tf_op jit(solution)/shard_map/ppermute | solution.py:244
  124.4 4.3 %collective-permute-start.1 = (bf16[4,192,128]{2,1,0:T(8,128)(2,1)}, bf16[4,192,128]{2,1,0:T(8,128)(2,1)}, u32[]{:S(2)}, u32[]{:S(2)}) collective-permute-start(bf16[4,192,128]{2,1,0:T(8,128)(2,1)} %get-tuple-element.48), channel_id=1, source_target_pairs={{0,16},{1,17},{2,18},{3,19},{4,20},{5,21},{6,22},{7,23},{8,24},{9,... | collective-permute-start | bytes 589832 | tf_op jit(solution)/shard_map/ppermute | solution.py:244
  131.9 7.0 %wgrad_products.1 = bf16[768,768]{1,0:T(8,128)(2,1)S(1)} custom-call(s32[2]{0:T(128)S(1)} %pad_add_fusion.2.place, bf16[4,16,96,128]{3,2,1,0:T(8,128)(2,1)S(1)} %pad_maximum_fusion.own_ref, bf16[4,16,96,128]{3,2,1,0:T(8,128)(2,1)S(1)} %collective-permute-done.7.oth_ref, bf16[4,16,192,128]{3,2,1,0:T(8,128)(2,1)} %all-to-all-done.1.act_ref), custom_call_target="tpu_custom_call" | custom-call | tf_op jit(solution)/shard_map/wgrad_products/pallas_call | solution.py:124
  139.9 11.6 %all-to-all-start.3 = ((bf16[8,96,768]{2,1,0:T(8,128)(2,1)}), bf16[8,96,768]{2,1,0:T(8,128)(2,1)S(1)}, u32[]{:S(2)}, u32[]{:S(2)}) async-start(bf16[8,96,768]{2,1,0:T(8,128)(2,1)} %bitcast.47), calls=%async_computation.3 | async-start | bytes 2359296 | tf_op jit(solution)/shard_map/all_to_all | solution.py:278
  157.3 9.5 %tokens_step.1 = (bf16[128,1536]{1,0:T(8,128)(2,1)}, bf16[6144,128]{1,0:T(8,128)(2,1)S(1)}) custom-call(s32[3,9]{1,0:T(4,128)S(1)} %pad_add_fusion.meta, s32[2]{0:T(128)S(1)} %pad_add_fusion.2.place, bf16[4,4,192,128]{3,2,1,0:T(8,128)(2,1)S(1)} %pad_maximum_fusion.1.own_ref, bf16[4,4,192,128]{3,2,1,0:T(8,128)(2,1)S(1)} %collective-permute-done.3.oth_ref, ...), custom_call_target="tpu_custom_call" | custom-call | tf_op jit(solution)/shard_map/tokens_step/pallas_call | solution.py:66
  168.1 5.5 %all-to-all-start.2 = ((bf16[32,192,128]{2,1,0:T(8,128)(2,1)}), bf16[32,192,128]{2,1,0:T(8,128)(2,1)S(1)}, u32[]{:S(2)}, u32[]{:S(2)}) async-start(bf16[32,192,128]{2,1,0:T(8,128)(2,1)} %bitcast.48), calls=%async_computation.2 | async-start | bytes 3145728 | tf_op jit(solution)/shard_map/all_to_all | solution.py:297
  174.7 4.3 %collective-permute-start.10 = (bf16[32,512]{1,0:T(8,128)(2,1)S(1)}, bf16[32,512]{1,0:T(8,128)(2,1)S(1)}, u32[]{:S(2)}, u32[]{:S(2)}) collective-permute-start(bf16[32,512]{1,0:T(8,128)(2,1)S(1)} %get-tuple-element.30), channel_id=1, source_target_pairs={{0,96},{32,128},{64,160},{96,192},{128,224},{160,256},{192,288},{2... | collective-permute-start | bytes 98312 | tf_op jit(solution)/shard_map/ppermute | solution.py:289
  179.0 6.5 %collective-permute-start.11 = (bf16[32,512]{1,0:T(8,128)(2,1)S(1)}, bf16[32,512]{1,0:T(8,128)(2,1)S(1)}, u32[]{:S(2)}, u32[]{:S(2)}) collective-permute-start(bf16[32,512]{1,0:T(8,128)(2,1)S(1)} %get-tuple-element.31), channel_id=1, source_target_pairs={{0,128},{32,160},{64,192},{96,224},{128,256},{160,288},{192,320},{... | collective-permute-start | bytes 98312 | tf_op jit(solution)/shard_map/ppermute | solution.py:289
  185.5 5.3 %collective-permute-start.12 = (bf16[32,512]{1,0:T(8,128)(2,1)S(1)}, bf16[32,512]{1,0:T(8,128)(2,1)S(1)}, u32[]{:S(2)}, u32[]{:S(2)}) collective-permute-start(bf16[32,512]{1,0:T(8,128)(2,1)S(1)} %get-tuple-element.32), channel_id=1, source_target_pairs={{0,160},{32,192},{64,224},{96,256},{128,288},{160,320},{192,352},{... | collective-permute-start | bytes 98312 | tf_op jit(solution)/shard_map/ppermute | solution.py:289
  190.8 3.6 %collective-permute-start.13 = (bf16[32,512]{1,0:T(8,128)(2,1)S(1)}, bf16[32,512]{1,0:T(8,128)(2,1)S(1)}, u32[]{:S(2)}, u32[]{:S(2)}) collective-permute-start(bf16[32,512]{1,0:T(8,128)(2,1)S(1)} %get-tuple-element.33), channel_id=1, source_target_pairs={{0,192},{32,224},{64,256},{96,288},{128,320},{160,352},{192,384},{... | collective-permute-start | bytes 98312 | tf_op jit(solution)/shard_map/ppermute | solution.py:289
  194.4 9.4 %collective-permute-start.14 = (bf16[32,512]{1,0:T(8,128)(2,1)S(1)}, bf16[32,512]{1,0:T(8,128)(2,1)S(1)}, u32[]{:S(2)}, u32[]{:S(2)}) collective-permute-start(bf16[32,512]{1,0:T(8,128)(2,1)S(1)} %get-tuple-element.34), channel_id=1, source_target_pairs={{0,224},{32,256},{64,288},{96,320},{128,352},{160,384},{192,416},{... | collective-permute-start | bytes 98312 | tf_op jit(solution)/shard_map/ppermute | solution.py:289
  203.8 3.8 %collective-permute-start.15 = (bf16[32,512]{1,0:T(8,128)(2,1)S(1)}, bf16[32,512]{1,0:T(8,128)(2,1)S(1)}, u32[]{:S(2)}, u32[]{:S(2)}) collective-permute-start(bf16[32,512]{1,0:T(8,128)(2,1)S(1)} %get-tuple-element.35), channel_id=1, source_target_pairs={{0,256},{32,288},{64,320},{96,352},{128,384},{160,416},{192,448},{... | collective-permute-start | bytes 98312 | tf_op jit(solution)/shard_map/ppermute | solution.py:289
  207.6 9.0 %collective-permute-start.16 = (bf16[32,512]{1,0:T(8,128)(2,1)S(1)}, bf16[32,512]{1,0:T(8,128)(2,1)S(1)}, u32[]{:S(2)}, u32[]{:S(2)}) collective-permute-start(bf16[32,512]{1,0:T(8,128)(2,1)S(1)} %get-tuple-element.36), channel_id=1, source_target_pairs={{0,288},{32,320},{64,352},{96,384},{128,416},{160,448},{192,480},{... | collective-permute-start | bytes 98312 | tf_op jit(solution)/shard_map/ppermute | solution.py:289
  216.6 6.4 %collective-permute-start.17 = (bf16[32,512]{1,0:T(8,128)(2,1)S(1)}, bf16[32,512]{1,0:T(8,128)(2,1)S(1)}, u32[]{:S(2)}, u32[]{:S(2)}) collective-permute-start(bf16[32,512]{1,0:T(8,128)(2,1)S(1)} %get-tuple-element.37), channel_id=1, source_target_pairs={{0,320},{32,352},{64,384},{96,416},{128,448},{160,480},{192,0},{22... | collective-permute-start | bytes 98312 | tf_op jit(solution)/shard_map/ppermute | solution.py:289
  226.0 6.0 %collective-permute-start.19 = (bf16[32,512]{1,0:T(8,128)(2,1)S(1)}, bf16[32,512]{1,0:T(8,128)(2,1)S(1)}, u32[]{:S(2)}, u32[]{:S(2)}) collective-permute-start(bf16[32,512]{1,0:T(8,128)(2,1)S(1)} %get-tuple-element.39), channel_id=1, source_target_pairs={{0,384},{32,416},{64,448},{96,480},{128,0},{160,32},{192,64},{224,... | collective-permute-start | bytes 98312 | tf_op jit(solution)/shard_map/ppermute | solution.py:289
  232.0 6.3 %collective-permute-start.20 = (bf16[32,512]{1,0:T(8,128)(2,1)S(1)}, bf16[32,512]{1,0:T(8,128)(2,1)S(1)}, u32[]{:S(2)}, u32[]{:S(2)}) collective-permute-start(bf16[32,512]{1,0:T(8,128)(2,1)S(1)} %get-tuple-element.40), channel_id=1, source_target_pairs={{0,416},{32,448},{64,480},{96,0},{128,32},{160,64},{192,96},{224,1... | collective-permute-start | bytes 98312 | tf_op jit(solution)/shard_map/ppermute | solution.py:289
  245.6 4.3 %collective-permute-start.9 = (bf16[32,512]{1,0:T(8,128)(2,1)S(1)}, bf16[32,512]{1,0:T(8,128)(2,1)S(1)}, u32[]{:S(2)}, u32[]{:S(2)}) collective-permute-start(bf16[32,512]{1,0:T(8,128)(2,1)S(1)} %get-tuple-element.29), channel_id=1, source_target_pairs={{0,64},{32,96},{64,128},{96,160},{128,192},{160,224},{192,256},{22... | collective-permute-start | bytes 98312 | tf_op jit(solution)/shard_map/ppermute | solution.py:289
  (71 shorter events, 41.7 us)
Async XLA Ops:
  7.2 150.2 %all-gather.4.cloned.1.call-start = ((), (), s32[]{:S(2)}) async-start(), calls=%async_computation.4 | async-start | bytes 8912896 | tf_op jit(solution)/shard_map/all_gather | solution.py:259
  9.9 71.1 %all-to-all-start = ((bf16[16,96,128]{2,1,0:T(8,128)(2,1)}), bf16[16,96,128]{2,1,0:T(8,128)(2,1)S(1)}, u32[]{:S(2)}, u32[]{:S(2)}) async-start(bf16[16,96,128]{2,1,0:T(8,128)(2,1)} %bitcast.11), calls=%async_computation | async-start | bytes 786432 | tf_op jit(solution)/shard_map/all_to_all | solution.py:262
  83.5 36.1 %all-to-all-start.1 = ((bf16[4,16,192,128]{3,2,1,0:T(8,128)(2,1)}), bf16[4,16,192,128]{3,2,1,0:T(8,128)(2,1)}, u32[]{:S(2)}, u32[]{:S(2)}) async-start(bf16[4,16,192,128]{3,2,1,0:T(8,128)(2,1)} %broadcast_in_dim.51), calls=%async_computation.1 | async-start | bytes 6291456 | tf_op jit(solution)/shard_map/all_to_all | solution.py:267
  88.2 10.6 %collective-permute-start.4 = (bf16[16,96,128]{2,1,0:T(8,128)(2,1)S(1)}, bf16[16,96,128]{2,1,0:T(8,128)(2,1)S(1)}, u32[]{:S(2)}, u32[]{:S(2)}) collective-permute-start(bf16[16,96,128]{2,1,0:T(8,128)(2,1)S(1)} %all-to-all-done), channel_id=1, source_target_pairs={{0,8},{1,9},{2,10},{3,11},{4,12},{5,13},{6,14},{7,15},{8,16},{9,17... | collective-permute-start | bytes 1179656 | tf_op jit(solution)/shard_map/ppermute | solution.py:244
  91.3 13.5 %collective-permute-start.5 = (bf16[16,96,128]{2,1,0:T(8,128)(2,1)S(1)}, bf16[16,96,128]{2,1,0:T(8,128)(2,1)S(1)}, u32[]{:S(2)}, u32[]{:S(2)}) collective-permute-start(bf16[16,96,128]{2,1,0:T(8,128)(2,1)S(1)} %all-to-all-done), channel_id=1, source_target_pairs={{0,16},{1,17},{2,18},{3,19},{4,20},{5,21},{6,22},{7,23},{8,24},{9,... | collective-permute-start | bytes 1179656 | tf_op jit(solution)/shard_map/ppermute | solution.py:244
  95.7 10.6 %collective-permute-start.6 = (bf16[16,96,128]{2,1,0:T(8,128)(2,1)S(1)}, bf16[16,96,128]{2,1,0:T(8,128)(2,1)S(1)}, u32[]{:S(2)}, u32[]{:S(2)}) collective-permute-start(bf16[16,96,128]{2,1,0:T(8,128)(2,1)S(1)} %all-to-all-done), channel_id=1, source_target_pairs={{0,24},{1,25},{2,26},{3,27},{4,28},{5,29},{6,30},{7,31},{8,0},{9,1... | collective-permute-start | bytes 1179656 | tf_op jit(solution)/shard_map/ppermute | solution.py:244
  106.5 25.3 %collective-permute-start.7 = (bf16[4,16,96,128]{3,2,1,0:T(8,128)(2,1)S(1)}, bf16[4,16,96,128]{3,2,1,0:T(8,128)(2,1)S(1)}, u32[]{:S(2)}, u32[]{:S(2)}) collective-permute-start(bf16[4,16,96,128]{3,2,1,0:T(8,128)(2,1)S(1)} %pad_maximum_fusion.own_ref), channel_id=1, source_target_pairs={{0,1},{1,0},{2,3},{3,2},{4,5},{5,4},{6,7},{7,6},{8,9},{9,8},{10,11... | collective-permute-start | bytes 4718600 | tf_op jit(solution)/shard_map/ppermute | solution.py:245
  121.2 30.8 %collective-permute-start = (bf16[4,192,128]{2,1,0:T(8,128)(2,1)}, bf16[4,192,128]{2,1,0:T(8,128)(2,1)S(1)}, u32[]{:S(2)}, u32[]{:S(2)}) collective-permute-start(bf16[4,192,128]{2,1,0:T(8,128)(2,1)} %get-tuple-element.48), channel_id=1, source_target_pairs={{0,8},{1,9},{2,10},{3,11},{4,12},{5,13},{6,14},{7,15},{8,16},{9,17... | collective-permute-start | bytes 589832 | tf_op jit(solution)/shard_map/ppermute | solution.py:244
  124.4 27.7 %collective-permute-start.1 = (bf16[4,192,128]{2,1,0:T(8,128)(2,1)}, bf16[4,192,128]{2,1,0:T(8,128)(2,1)}, u32[]{:S(2)}, u32[]{:S(2)}) collective-permute-start(bf16[4,192,128]{2,1,0:T(8,128)(2,1)} %get-tuple-element.48), channel_id=1, source_target_pairs={{0,16},{1,17},{2,18},{3,19},{4,20},{5,21},{6,22},{7,23},{8,24},{9,... | collective-permute-start | bytes 589832 | tf_op jit(solution)/shard_map/ppermute | solution.py:244
  128.7 23.3 %collective-permute-start.2 = (bf16[4,192,128]{2,1,0:T(8,128)(2,1)}, bf16[4,192,128]{2,1,0:T(8,128)(2,1)}, u32[]{:S(2)}, u32[]{:S(2)}) collective-permute-start(bf16[4,192,128]{2,1,0:T(8,128)(2,1)} %get-tuple-element.48), channel_id=1, source_target_pairs={{0,24},{1,25},{2,26},{3,27},{4,28},{5,29},{6,30},{7,31},{8,0},{9,1... | collective-permute-start | bytes 589832 | tf_op jit(solution)/shard_map/ppermute | solution.py:244
  139.9 28.1 %all-to-all-start.3 = ((bf16[8,96,768]{2,1,0:T(8,128)(2,1)}), bf16[8,96,768]{2,1,0:T(8,128)(2,1)S(1)}, u32[]{:S(2)}, u32[]{:S(2)}) async-start(bf16[8,96,768]{2,1,0:T(8,128)(2,1)} %bitcast.47), calls=%async_computation.3 | async-start | bytes 2359296 | tf_op jit(solution)/shard_map/all_to_all | solution.py:278
  168.1 85.4 %all-to-all-start.2 = ((bf16[32,192,128]{2,1,0:T(8,128)(2,1)}), bf16[32,192,128]{2,1,0:T(8,128)(2,1)S(1)}, u32[]{:S(2)}, u32[]{:S(2)}) async-start(bf16[32,192,128]{2,1,0:T(8,128)(2,1)} %bitcast.48), calls=%async_computation.2 | async-start | bytes 3145728 | tf_op jit(solution)/shard_map/all_to_all | solution.py:297
  174.7 29.1 %collective-permute-start.10 = (bf16[32,512]{1,0:T(8,128)(2,1)S(1)}, bf16[32,512]{1,0:T(8,128)(2,1)S(1)}, u32[]{:S(2)}, u32[]{:S(2)}) collective-permute-start(bf16[32,512]{1,0:T(8,128)(2,1)S(1)} %get-tuple-element.30), channel_id=1, source_target_pairs={{0,96},{32,128},{64,160},{96,192},{128,224},{160,256},{192,288},{2... | collective-permute-start | bytes 98312 | tf_op jit(solution)/shard_map/ppermute | solution.py:289
  179.0 28.6 %collective-permute-start.11 = (bf16[32,512]{1,0:T(8,128)(2,1)S(1)}, bf16[32,512]{1,0:T(8,128)(2,1)S(1)}, u32[]{:S(2)}, u32[]{:S(2)}) collective-permute-start(bf16[32,512]{1,0:T(8,128)(2,1)S(1)} %get-tuple-element.31), channel_id=1, source_target_pairs={{0,128},{32,160},{64,192},{96,224},{128,256},{160,288},{192,320},{... | collective-permute-start | bytes 98312 | tf_op jit(solution)/shard_map/ppermute | solution.py:289
  185.5 31.1 %collective-permute-start.12 = (bf16[32,512]{1,0:T(8,128)(2,1)S(1)}, bf16[32,512]{1,0:T(8,128)(2,1)S(1)}, u32[]{:S(2)}, u32[]{:S(2)}) collective-permute-start(bf16[32,512]{1,0:T(8,128)(2,1)S(1)} %get-tuple-element.32), channel_id=1, source_target_pairs={{0,160},{32,192},{64,224},{96,256},{128,288},{160,320},{192,352},{... | collective-permute-start | bytes 98312 | tf_op jit(solution)/shard_map/ppermute | solution.py:289
  190.8 32.2 %collective-permute-start.13 = (bf16[32,512]{1,0:T(8,128)(2,1)S(1)}, bf16[32,512]{1,0:T(8,128)(2,1)S(1)}, u32[]{:S(2)}, u32[]{:S(2)}) collective-permute-start(bf16[32,512]{1,0:T(8,128)(2,1)S(1)} %get-tuple-element.33), channel_id=1, source_target_pairs={{0,192},{32,224},{64,256},{96,288},{128,320},{160,352},{192,384},{... | collective-permute-start | bytes 98312 | tf_op jit(solution)/shard_map/ppermute | solution.py:289
  194.4 31.6 %collective-permute-start.14 = (bf16[32,512]{1,0:T(8,128)(2,1)S(1)}, bf16[32,512]{1,0:T(8,128)(2,1)S(1)}, u32[]{:S(2)}, u32[]{:S(2)}) collective-permute-start(bf16[32,512]{1,0:T(8,128)(2,1)S(1)} %get-tuple-element.34), channel_id=1, source_target_pairs={{0,224},{32,256},{64,288},{96,320},{128,352},{160,384},{192,416},{... | collective-permute-start | bytes 98312 | tf_op jit(solution)/shard_map/ppermute | solution.py:289
  203.8 28.2 %collective-permute-start.15 = (bf16[32,512]{1,0:T(8,128)(2,1)S(1)}, bf16[32,512]{1,0:T(8,128)(2,1)S(1)}, u32[]{:S(2)}, u32[]{:S(2)}) collective-permute-start(bf16[32,512]{1,0:T(8,128)(2,1)S(1)} %get-tuple-element.35), channel_id=1, source_target_pairs={{0,256},{32,288},{64,320},{96,352},{128,384},{160,416},{192,448},{... | collective-permute-start | bytes 98312 | tf_op jit(solution)/shard_map/ppermute | solution.py:289
  207.6 30.7 %collective-permute-start.16 = (bf16[32,512]{1,0:T(8,128)(2,1)S(1)}, bf16[32,512]{1,0:T(8,128)(2,1)S(1)}, u32[]{:S(2)}, u32[]{:S(2)}) collective-permute-start(bf16[32,512]{1,0:T(8,128)(2,1)S(1)} %get-tuple-element.36), channel_id=1, source_target_pairs={{0,288},{32,320},{64,352},{96,384},{128,416},{160,448},{192,480},{... | collective-permute-start | bytes 98312 | tf_op jit(solution)/shard_map/ppermute | solution.py:289
  216.6 23.7 %collective-permute-start.17 = (bf16[32,512]{1,0:T(8,128)(2,1)S(1)}, bf16[32,512]{1,0:T(8,128)(2,1)S(1)}, u32[]{:S(2)}, u32[]{:S(2)}) collective-permute-start(bf16[32,512]{1,0:T(8,128)(2,1)S(1)} %get-tuple-element.37), channel_id=1, source_target_pairs={{0,320},{32,352},{64,384},{96,416},{128,448},{160,480},{192,0},{22... | collective-permute-start | bytes 98312 | tf_op jit(solution)/shard_map/ppermute | solution.py:289
  223.0 19.5 %collective-permute-start.18 = (bf16[32,512]{1,0:T(8,128)(2,1)S(1)}, bf16[32,512]{1,0:T(8,128)(2,1)S(1)}, u32[]{:S(2)}, u32[]{:S(2)}) collective-permute-start(bf16[32,512]{1,0:T(8,128)(2,1)S(1)} %get-tuple-element.38), channel_id=1, source_target_pairs={{0,352},{32,384},{64,416},{96,448},{128,480},{160,0},{192,32},{224... | collective-permute-start | bytes 98312 | tf_op jit(solution)/shard_map/ppermute | solution.py:289
  226.0 19.6 %collective-permute-start.19 = (bf16[32,512]{1,0:T(8,128)(2,1)S(1)}, bf16[32,512]{1,0:T(8,128)(2,1)S(1)}, u32[]{:S(2)}, u32[]{:S(2)}) collective-permute-start(bf16[32,512]{1,0:T(8,128)(2,1)S(1)} %get-tuple-element.39), channel_id=1, source_target_pairs={{0,384},{32,416},{64,448},{96,480},{128,0},{160,32},{192,64},{224,... | collective-permute-start | bytes 98312 | tf_op jit(solution)/shard_map/ppermute | solution.py:289
  232.0 17.9 %collective-permute-start.20 = (bf16[32,512]{1,0:T(8,128)(2,1)S(1)}, bf16[32,512]{1,0:T(8,128)(2,1)S(1)}, u32[]{:S(2)}, u32[]{:S(2)}) collective-permute-start(bf16[32,512]{1,0:T(8,128)(2,1)S(1)} %get-tuple-element.40), channel_id=1, source_target_pairs={{0,416},{32,448},{64,480},{96,0},{128,32},{160,64},{192,96},{224,1... | collective-permute-start | bytes 98312 | tf_op jit(solution)/shard_map/ppermute | solution.py:289
  238.3 11.5 %collective-permute-start.21 = (bf16[32,512]{1,0:T(8,128)(2,1)S(1)}, bf16[32,512]{1,0:T(8,128)(2,1)S(1)}, u32[]{:S(2)}, u32[]{:S(2)}) collective-permute-start(bf16[32,512]{1,0:T(8,128)(2,1)S(1)} %get-tuple-element.41), channel_id=1, source_target_pairs={{0,448},{32,480},{64,0},{96,32},{128,64},{160,96},{192,128},{224,1... | collective-permute-start | bytes 98312 | tf_op jit(solution)/shard_map/ppermute | solution.py:289
  (10 other events, 89.6 us)
Sparse Core Ops, SparseCore 0:
  10.1 129.9 all-gather.3

commit v4 on v2

--- a/solution.py
+++ b/solution.py
@@ -23,26 +23,28 @@
 Y_GROUPS = [[col_of(x, y, c) for y in range(NY)] for x in range(NX) for c in range(NC)]
 CORE_SWAP = [(col_of(x, y, c), col_of(x, y, 1 - c)) for x, y, c in PLANE]
 X_SHIFTS = {s: [(col_of(x, y, c), col_of((x + s) % NX, y, c)) for x, y, c in PLANE] for s in range(1, NX)}
+Y_SHIFTS = {s: [(col_of(x, y, c), col_of(x, (y + s) % NY, c)) for x, y, c in PLANE] for s in range(1, NY)}
 
 
 def aligned(start, size, step):
     return pl.ds(pl.multiple_of(start, step), size)
 
 
-def tokens_kernel(meta, place, own_ref, oth_ref, grad_ref, w_ref, out_ref, in_ref, act, out_acc, in_acc, *, blk):
+def tokens_kernel(meta, place, own_ref, oth_ref, grad_ref, w_ref, out_ref, *refs, blk):
+    in_refs, (act, out_acc, in_acc, in_rows) = refs[:NY], refs[NY:]
     step = pl.program_id(0)
+    piece = own_ref.shape[2]
+    x, y, core = place[0], place[1], place[2]
 
     @pl.when(step == 0)
     def _():
         out_acc[...] = jnp.zeros_like(out_acc)
         in_acc[...] = jnp.zeros_like(in_acc)
-        piece = own_ref.shape[2]
-        x, core = place[0], place[1]
         for s in range(NX):
             line = lax.rem(x - s + NX, NX) * NY
-            for y in range(NY):
-                act[aligned(((line + y) * NC + core) * piece, piece, 64), :] = own_ref[s, y]
-                act[aligned(((line + y) * NC + 1 - core) * piece, piece, 64), :] = oth_ref[s, y]
+            for j in range(NY):
+                act[aligned(((line + j) * NC + core) * piece, piece, 64), :] = own_ref[s, j]
+                act[aligned(((line + j) * NC + 1 - core) * piece, piece, 64), :] = oth_ref[s, j]
 
     hid = aligned(meta[1, step] * blk, blk, blk)
     mod = aligned(meta[2, step] * blk, blk, blk)
@@ -53,7 +55,12 @@
     @pl.when(step == pl.num_programs(0) - 1)
     def _():
         out_ref[...] = out_acc[...].T.astype(BF)
-        in_ref[...] = in_acc[...].T.astype(BF)
+        in_rows[...] = in_acc[...].T.astype(BF)
+        for s in range(NY):
+            for t in range(NX):
+                chip = (lax.rem(x + t, NX) * NY + lax.rem(y + s, NY)) * NC
+                in_refs[s][t, 0] = in_rows[aligned((chip + core) * piece, piece, 64), :]
+                in_refs[s][t, 1] = in_rows[aligned((chip + 1 - core) * piece, piece, 64), :]
 
 
 def tokens_step(meta, place, act_own, act_oth, grad, w_all):
@@ -74,20 +81,17 @@
                 pl.BlockSpec((toks, hidden), whole),
                 pl.BlockSpec((1, blk, blk), lambda k, m, p: (m[0, k], 0, 0)),
             ],
-            out_specs=[
-                pl.BlockSpec((toks, hidden), whole),
-                pl.BlockSpec((feats, toks), whole),
-            ],
+            out_specs=[pl.BlockSpec((toks, hidden), whole)]
+            + [pl.BlockSpec((NX, NC, piece, toks), lambda k, m, p: (0, 0, 0, 0))] * NY,
             scratch_shapes=[
                 pltpu.VMEM((feats, toks), BF),
                 pltpu.VMEM((hidden, toks), F32),
                 pltpu.VMEM((toks, feats), F32),
+                pltpu.VMEM((feats, toks), BF),
             ],
         ),
-        out_shape=[
-            jax.ShapeDtypeStruct((toks, hidden), BF),
-            jax.ShapeDtypeStruct((feats, toks), BF),
-        ],
+        out_shape=[jax.ShapeDtypeStruct((toks, hidden), BF)]
+        + [jax.ShapeDtypeStruct((NX, NC, piece, toks), BF)] * NY,
         compiler_params=PARAMS,
         name="tokens_step",
     )(meta, place, act_own, act_oth, grad, w_all)
@@ -96,7 +100,7 @@
 def wgrad_kernel(place, own_ref, oth_ref, act_ref, out_ref, a_buf, b_buf, *, scale):
     n_x, n_z, rows, toks = own_ref.shape
     n_y, _, piece, _ = act_ref.shape
-    x, core = place[0], place[1]
+    x, core = place[0], place[2]
 
     @pl.when(pl.program_id(0) == 0)
     def _():
@@ -176,19 +180,43 @@
     )(meta, prods)
 
 
-def sum_kernel(parts_ref, out_ref):
-    out_ref[...] = jnp.sum(parts_ref[...].astype(F32), axis=0).astype(BF)
-
-
-def sum_groups(parts):
+def sum_y_kernel(*refs):
+    parts, out_refs = refs[:NY], refs[NY:]
+    for t in range(NX):
+        out_refs[t][...] = sum(part[t].astype(F32) for part in parts)
+
+
+def sum_x_kernel(*refs):
+    parts, (own_ref, oth_ref) = refs[:NX], refs[NX:]
+    own_ref[...] = sum(part[0] for part in parts)
+    oth_ref[...] = sum(part[1] for part in parts)
+
+
+def sum_core_kernel(own_ref, oth_ref, out_ref):
+    out_ref[...] = (own_ref[...] + oth_ref[...]).astype(BF)
+
+
+def small_call(kernel, name, outs, *args):
     return pl.pallas_call(
-        sum_kernel,
-        in_specs=[pl.BlockSpec(memory_space=pltpu.VMEM)],
-        out_specs=pl.BlockSpec(memory_space=pltpu.VMEM),
-        out_shape=jax.ShapeDtypeStruct(parts.shape[1:], BF),
+        kernel,
+        in_specs=[pl.BlockSpec(memory_space=pltpu.VMEM)] * len(args),
+        out_specs=[pl.BlockSpec(memory_space=pltpu.VMEM)] * len(outs),
+        out_shape=outs,
         compiler_params=PARAMS,
-        name="sum_groups",
-    )(parts)
+        name=name,
+    )(*args)
+
+
+def sum_groups(in_parts):
+    _, _, piece, toks = in_parts[0].shape
+    got = [in_parts[0]] + [lax.ppermute(in_parts[s], "col", Y_SHIFTS[s]) for s in range(1, NY)]
+    pair = jax.ShapeDtypeStruct((NC, piece, toks), F32)
+    one = jax.ShapeDtypeStruct((piece, toks), F32)
+    by_x = small_call(sum_y_kernel, "sum_y", [pair] * NX, *got)
+    got = [by_x[0]] + [lax.ppermute(by_x[t], "col", X_SHIFTS[t]) for t in range(1, NX)]
+    own, oth = small_call(sum_x_kernel, "sum_x", [one] * NC, *got)
+    last = jax.ShapeDtypeStruct((piece, toks), BF)
+    return small_call(sum_core_kernel, "sum_core", [last], own, lax.ppermute(oth, "col", CORE_SWAP))[0]
 
 
 def layout_tables(block_mask, block_owner, group, n_groups, owners):
@@ -229,7 +257,7 @@
     hid_blocks = hidden // blk
     chunk = blk // owners
     listed, slots = layout_tables(block_mask, block_owner, group, groups, owners)
-    place = jnp.stack([group // (NY * NC), group % NC]).astype(jnp.int32)
+    place = jnp.stack([group // (NY * NC), group // NC % NY, group % NC]).astype(jnp.int32)
 
     w_all = lax.all_gather(weight_slots[0, 0], "row", axis=0)
 
@@ -250,6 +278,7 @@
     grad_own, grad_oth = share_x(grad_z)
     scale = 1.0 / math.sqrt(toks * owners)
     prods = wgrad_products(place, grad_own, grad_oth, act_y, scale)
+    prods, w_all = lax.optimization_barrier((prods, w_all))
     prods = lax.all_to_all(
         prods.reshape(NX * NC, hid_blocks * chunk, NY * piece),
         "col",
@@ -259,13 +288,13 @@
         axis_index_groups=XC_GROUPS,
     )
     slot_parts = pick_slots(slots, prods, chunk, blk)
-    weight_grad = lax.all_to_all(slot_parts, "row", 0, 0, tiled=True).reshape(1, 1, blk, blk)
 
     act_here = lax.dynamic_index_in_dim(act_y, lax.axis_index("row"), 1, keepdims=False)
     act_own, act_oth = share_x(act_here)
-    outputs, in_part = tokens_step(listed, place, act_own, act_oth, out_grad, w_all)
-    in_recv = lax.all_to_all(in_part.reshape(groups, piece, toks), "col", 0, 0, tiled=True)
-    return outputs, sum_groups(in_recv).T, weight_grad
+    outputs, *in_parts = tokens_step(listed, place, act_own, act_oth, out_grad, w_all)
+    slot_parts, in_parts = lax.optimization_barrier((slot_parts, in_parts))
+    weight_grad = lax.all_to_all(slot_parts, "row", 0, 0, tiled=True).reshape(1, 1, blk, blk)
+    return outputs, sum_groups(in_parts).T, weight_grad
 
 
 def solution(mesh):

time: 237 us -> 232 us (0.979)
  waiting for transfers between devices: 58.6 us -> 40 us
  starting transfers between devices: 79.7 us -> 92.6 us
    all_to_all x1 -> x0, waiting for transfers between devices: 22.7 us -> none  [per_device(): lax.all_to_all(in_part.reshape(groups, piece, toks), 'col', 0, 0, tiled=T...]
    ppermute x0 -> x7, waiting for transfers between devices: none -> 22.1 us  [the longest x3 15.5 us: sum_groups(): lax.ppermute(in_parts[s], 'col', Y_SHIFTS[s])]
    ppermute x0 -> x7, starting transfers between devices: none -> 22 us  [the longest x3 9.36 us: sum_groups(): lax.ppermute(by_x[t], 'col', X_SHIFTS[t])]
    all_to_all x1, waiting for transfers between devices: 15.9 us -> 1.33 us  [per_device(): lax.all_to_all(prods.reshape(NX * NC, hid_blocks * chunk, NY * piece), 'c...]
    all_to_all x1 -> x0, starting transfers between devices: 5.08 us -> none  [per_device(): lax.all_to_all(in_part.reshape(groups, piece, toks), 'col', 0, 0, tiled=T...]
    ppermute x6, waiting for transfers between devices: 14.1 us -> 11.2 us  [share_x(): lax.ppermute(x, 'col', X_SHIFTS[s])]
    ppermute x2, waiting for transfers between devices: 4.56 us -> 1.95 us  [share_x(): return (own, lax.ppermute(own, 'col', CORE_SWAP))]
  transfers between devices with their start and end apart: 14 -> 20, of which waited for: 9 -> 13; matrix products, arithmetic and copies ran while one was open for 3% -> 4% of each run, Pallas kernels for 8% -> 8%
where the time goes in v4:
time: 232 us; the launch traced here: 231 us
  starting transfers between devices  92.6 us (40%)
  blocking collectives  55.4 us (24%)
  waiting for transfers between devices  40 us (17%)
  Pallas kernels  19.9 us (9%)
  between operations  14.3 us (6%)
  local copies, waits for them, and re-layouts  7.38 us (3%)
    all_gather x1, blocking collectives, per_device(): act_z = lax.all_gather(activations.T, 'row', axis=0)  55.4 us
    ppermute x6, starting transfers between devices, share_x(): lax.ppermute(x, 'col', X_SHIFTS[s])  18.7 us
    all_to_all x1, starting transfers between devices, per_device(): lax.all_to_all(grad_send.reshape(owners, hid_blocks * chunk, toks), 'row'...  15.7 us
    ppermute x3, waiting for transfers between devices, sum_groups(): lax.ppermute(in_parts[s], 'col', Y_SHIFTS[s])  15.5 us
    ppermute x6, waiting for transfers between devices, share_x(): lax.ppermute(x, 'col', X_SHIFTS[s])  11.2 us
    ppermute x2, starting transfers between devices, share_x(): return (own, lax.ppermute(own, 'col', CORE_SWAP))  11.1 us
    all_to_all x1, starting transfers between devices, per_device(): lax.all_to_all(prods.reshape(NX * NC, hid_blocks * chunk, NY * piece), 'c...  10.2 us
    all_to_all x1, starting transfers between devices, per_device(): lax.all_to_all(slot_parts, 'row', 0, 0, tiled=True).reshape(1, 1, blk, blk)  10.1 us
  transfers between devices with their start and end apart: 20, of which 13 were waited for; matrix products, arithmetic and copies ran while one was open for 4% of the time, Pallas kernels for 8%

profile of v4, /device:TPU:1, one launch (start us, length us, event | category | flops | bytes accessed | tf_op | source)
XLA Modules:
  0.0 231.3 jit_solution(18325722063163485549)
XLA Ops:
  9.9 15.7 %all-to-all-start = ((bf16[16,96,128]{2,1,0:T(8,128)(2,1)}), bf16[16,96,128]{2,1,0:T(8,128)(2,1)S(1)}, u32[]{:S(2)}, u32[]{:S(2)}) async-start(bf16[16,96,128]{2,1,0:T(8,128)(2,1)} %bitcast.12), calls=%async_computation | async-start | bytes 786432 | tf_op jit(solution)/shard_map/all_to_all | solution.py:265
  25.7 55.4 %all-gather = bf16[3072,128]{1,0:T(8,128)(2,1)S(1)} all-gather(bf16[192,128]{1,0:T(8,128)(2,1)S(1)} %bitcast.55), channel_id=2, replica_groups=mesh['row'=16,'col'=32] {'row'}, dimensions={0}, use_global_device_ids=true | all-gather | bytes 835584 | tf_op jit(solution)/shard_map/all_gather | solution.py:268
  83.5 4.7 %all-to-all-start.1 = ((bf16[4,16,192,128]{3,2,1,0:T(8,128)(2,1)}), bf16[4,16,192,128]{3,2,1,0:T(8,128)(2,1)}, u32[]{:S(2)}, u32[]{:S(2)}) async-start(bf16[4,16,192,128]{3,2,1,0:T(8,128)(2,1)} %broadcast_in_dim.48), calls=%async_computation.1 | async-start | bytes 6291456 | tf_op jit(solution)/shard_map/all_to_all | solution.py:270
  88.3 4.4 %collective-permute-start.6 = (bf16[16,96,128]{2,1,0:T(8,128)(2,1)S(1)}, bf16[16,96,128]{2,1,0:T(8,128)(2,1)S(1)}, u32[]{:S(2)}, u32[]{:S(2)}) collective-permute-start(bf16[16,96,128]{2,1,0:T(8,128)(2,1)S(1)} %all-to-all-done), channel_id=1, source_target_pairs={{0,24},{1,25},{2,26},{3,27},{4,28},{5,29},{6,30},{7,31},{8,0},{9,1... | collective-permute-start | bytes 1179656 | tf_op jit(solution)/shard_map/ppermute | solution.py:247
  95.1 2.5 %collective-permute-start.4 = (bf16[16,96,128]{2,1,0:T(8,128)(2,1)S(1)}, bf16[16,96,128]{2,1,0:T(8,128)(2,1)S(1)}, u32[]{:S(2)}, u32[]{:S(2)}) collective-permute-start(bf16[16,96,128]{2,1,0:T(8,128)(2,1)S(1)} %all-to-all-done), channel_id=1, source_target_pairs={{0,8},{1,9},{2,10},{3,11},{4,12},{5,13},{6,14},{7,15},{8,16},{9,17... | collective-permute-start | bytes 1179656 | tf_op jit(solution)/shard_map/ppermute | solution.py:247
  97.6 4.3 %collective-permute-done.6 = bf16[16,96,128]{2,1,0:T(8,128)(2,1)S(1)} collective-permute-done((bf16[16,96,128]{2,1,0:T(8,128)(2,1)S(1)}, bf16[16,96,128]{2,1,0:T(8,128)(2,1)S(1)}, u32[]{:S(2)}, u32[]{:S(2)}) %collective-permute-start.6) | collective-permute-done | bytes 393248 | tf_op jit(solution)/shard_map/ppermute | solution.py:247
  102.8 6.0 %collective-permute-done.4 = bf16[16,96,128]{2,1,0:T(8,128)(2,1)S(1)} collective-permute-done((bf16[16,96,128]{2,1,0:T(8,128)(2,1)S(1)}, bf16[16,96,128]{2,1,0:T(8,128)(2,1)S(1)}, u32[]{:S(2)}, u32[]{:S(2)}) %collective-permute-start.4) | collective-permute-done | bytes 393248 | tf_op jit(solution)/shard_map/ppermute | solution.py:247
  109.0 9.1 %collective-permute-start.7 = (bf16[4,16,96,128]{3,2,1,0:T(8,128)(2,1)S(1)}, bf16[4,16,96,128]{3,2,1,0:T(8,128)(2,1)S(1)}, u32[]{:S(2)}, u32[]{:S(2)}) collective-permute-start(bf16[4,16,96,128]{3,2,1,0:T(8,128)(2,1)S(1)} %pad_maximum_fusion.own_ref), channel_id=1, source_target_pairs={{0,1},{1,0},{2,3},{3,2},{4,5},{5,4},{6,7},{7,6},{8,9},{9,8},{10,11... | collective-permute-start | bytes 4718600 | tf_op jit(solution)/shard_map/ppermute | solution.py:248
  121.3 4.4 %collective-permute-start.2 = (bf16[4,192,128]{2,1,0:T(8,128)(2,1)}, bf16[4,192,128]{2,1,0:T(8,128)(2,1)S(1)}, u32[]{:S(2)}, u32[]{:S(2)}) collective-permute-start(bf16[4,192,128]{2,1,0:T(8,128)(2,1)} %get-tuple-element.48), channel_id=1, source_target_pairs={{0,24},{1,25},{2,26},{3,27},{4,28},{5,29},{6,30},{7,31},{8,0},{9,1... | collective-permute-start | bytes 589832 | tf_op jit(solution)/shard_map/ppermute | solution.py:247
  128.1 2.5 %collective-permute-start = (bf16[4,192,128]{2,1,0:T(8,128)(2,1)}, bf16[4,192,128]{2,1,0:T(8,128)(2,1)}, u32[]{:S(2)}, u32[]{:S(2)}) collective-permute-start(bf16[4,192,128]{2,1,0:T(8,128)(2,1)} %get-tuple-element.48), channel_id=1, source_target_pairs={{0,8},{1,9},{2,10},{3,11},{4,12},{5,13},{6,14},{7,15},{8,16},{9,17... | collective-permute-start | bytes 589832 | tf_op jit(solution)/shard_map/ppermute | solution.py:247
  130.8 7.8 %wgrad_products.1 = bf16[768,768]{1,0:T(8,128)(2,1)} custom-call(s32[3]{0:T(128)S(1)} %pad_add_fusion.2.place, bf16[4,16,96,128]{3,2,1,0:T(8,128)(2,1)S(1)} %pad_maximum_fusion.own_ref, bf16[4,16,96,128]{3,2,1,0:T(8,128)(2,1)S(1)} %collective-permute-done.7.oth_ref, bf16[4,16,192,128]{3,2,1,0:T(8,128)(2,1)} %all-to-all-done.1.act_ref), custom_call_target="tpu_custom_call" | custom-call | tf_op jit(solution)/shard_map/wgrad_products/pallas_call | solution.py:128
  140.1 10.2 %all-to-all-start.2 = ((bf16[8,96,768]{2,1,0:T(8,128)(2,1)}), bf16[8,96,768]{2,1,0:T(8,128)(2,1)S(1)}, u32[]{:S(2)}, u32[]{:S(2)}) async-start(bf16[8,96,768]{2,1,0:T(8,128)(2,1)} %bitcast.27), calls=%async_computation.2 | async-start | bytes 2359296 | tf_op jit(solution)/shard_map/all_to_all | solution.py:282
  155.9 9.6 %tokens_step.1 = (bf16[128,1536]{1,0:T(8,128)(2,1)}, bf16[4,2,192,128]{3,2,1,0:T(8,128)(2,1)S(1)}, bf16[4,2,192,128]{3,2,1,0:T(8,128)(2,1)S(1)}, bf16[4,2,192,12...) custom-call(s32[3,9]{1,0:T(4,128)S(1)} %pad_add_fusion.meta, s32[3]{0:T(128)S(1)} %pad_add_fusion.2.place, ...), custom_call_target="tpu_custom_call" | custom-call | tf_op jit(solution)/shard_map/tokens_step/pallas_call | solution.py:73
  168.5 10.1 %all-to-all-start.3 = ((bf16[16,32,512]{2,1,0:T(8,128)(2,1)}), bf16[16,32,512]{2,1,0:T(8,128)(2,1)S(1)}, u32[]{:S(2)}, u32[]{:S(2)}) async-start(bf16[16,32,512]{2,1,0:T(8,128)(2,1)} %pick_slots.1), calls=%async_computation.3 | async-start | bytes 1048576 | tf_op jit(solution)/shard_map/all_to_all | solution.py:296
  180.9 3.6 %collective-permute-start.9 = (bf16[4,2,192,128]{3,2,1,0:T(8,128)(2,1)S(1)}, bf16[4,2,192,128]{3,2,1,0:T(8,128)(2,1)S(1)}, u32[]{:S(2)}, u32[]{:S(2)}) collective-permute-start(bf16[4,2,192,128]{3,2,1,0:T(8,128)(2,1)S(1)} %get-tuple-element.34), channel_id=1, source_target_pairs={{0,4},{1,5},{2,6},{3,7},{4,0},{5,1},{6,2},{7,3},{8,12},{9,13},{10,... | collective-permute-start | bytes 1179656 | tf_op jit(solution)/shard_map/ppermute | solution.py:212
  184.5 2.7 %collective-permute-start.10 = (bf16[4,2,192,128]{3,2,1,0:T(8,128)(2,1)S(1)}, bf16[4,2,192,128]{3,2,1,0:T(8,128)(2,1)S(1)}, u32[]{:S(2)}, u32[]{:S(2)}) collective-permute-start(bf16[4,2,192,128]{3,2,1,0:T(8,128)(2,1)S(1)} %get-tuple-element.35), channel_id=1, source_target_pairs={{0,6},{1,7},{2,0},{3,1},{4,2},{5,3},{6,4},{7,5},{8,14},{9,15},{10,... | collective-permute-start | bytes 1179656 | tf_op jit(solution)/shard_map/ppermute | solution.py:212
  187.1 4.6 %collective-permute-done.8.refs_1_ = bf16[4,2,192,128]{3,2,1,0:T(8,128)(2,1)S(1)} collective-permute-done((bf16[4,2,192,128]{3,2,1,0:T(8,128)(2,1)S(1)}, bf16[4,2,192,128]{3,2,1,0:T(8,128)(2,1)S(1)}, u32[]{:S(2)}, u32[]{:S(2)}) %collective-permute-start.8) | collective-permute-done | bytes 393248 | tf_op jit(solution)/shard_map/ppermute | solution.py:212
  191.8 7.3 %collective-permute-done.9.refs_2_ = bf16[4,2,192,128]{3,2,1,0:T(8,128)(2,1)S(1)} collective-permute-done((bf16[4,2,192,128]{3,2,1,0:T(8,128)(2,1)S(1)}, bf16[4,2,192,128]{3,2,1,0:T(8,128)(2,1)S(1)}, u32[]{:S(2)}, u32[]{:S(2)}) %collective-permute-start.9) | collective-permute-done | bytes 393248 | tf_op jit(solution)/shard_map/ppermute | solution.py:212
  199.0 3.6 %collective-permute-done.10.refs_3_ = bf16[4,2,192,128]{3,2,1,0:T(8,128)(2,1)S(1)} collective-permute-done((bf16[4,2,192,128]{3,2,1,0:T(8,128)(2,1)S(1)}, bf16[4,2,192,128]{3,2,1,0:T(8,128)(2,1)S(1)}, u32[]{:S(2)}, u32[]{:S(2)}) %collective-permute-start.10) | collective-permute-done | bytes 393248 | tf_op jit(solution)/shard_map/ppermute | solution.py:212
  205.0 4.1 %collective-permute-start.12 = (f32[2,192,128]{2,1,0:T(8,128)S(1)}, f32[2,192,128]{2,1,0:T(8,128)S(1)}, u32[]{:S(2)}, u32[]{:S(2)}) collective-permute-start(f32[2,192,128]{2,1,0:T(8,128)S(1)} %get-tuple-element.38), channel_id=1, source_target_pairs={{0,16},{1,17},{2,18},{3,19},{4,20},{5,21},{6,22},{7,23},{8,24},{9,... | collective-permute-start | bytes 589832 | tf_op jit(solution)/shard_map/ppermute | solution.py:216
  209.1 3.1 %collective-permute-start.13 = (f32[2,192,128]{2,1,0:T(8,128)S(1)}, f32[2,192,128]{2,1,0:T(8,128)S(1)}, u32[]{:S(2)}, u32[]{:S(2)}) collective-permute-start(f32[2,192,128]{2,1,0:T(8,128)S(1)} %get-tuple-element.39), channel_id=1, source_target_pairs={{0,24},{1,25},{2,26},{3,27},{4,28},{5,29},{6,30},{7,31},{8,0},{9,1... | collective-permute-start | bytes 589832 | tf_op jit(solution)/shard_map/ppermute | solution.py:216
  212.2 3.1 %collective-permute-done.12.refs_2_ = f32[2,192,128]{2,1,0:T(8,128)S(1)} collective-permute-done((f32[2,192,128]{2,1,0:T(8,128)S(1)}, f32[2,192,128]{2,1,0:T(8,128)S(1)}, u32[]{:S(2)}, u32[]{:S(2)}) %collective-permute-start.12) | collective-permute-done | bytes 196640 | tf_op jit(solution)/shard_map/ppermute | solution.py:216
  215.3 2.6 %collective-permute-done.13.refs_3_ = f32[2,192,128]{2,1,0:T(8,128)S(1)} collective-permute-done((f32[2,192,128]{2,1,0:T(8,128)S(1)}, f32[2,192,128]{2,1,0:T(8,128)S(1)}, u32[]{:S(2)}, u32[]{:S(2)}) %collective-permute-start.13) | collective-permute-done | bytes 196640 | tf_op jit(solution)/shard_map/ppermute | solution.py:216
  218.0 4.1 %collective-permute-start.14 = (f32[192,128]{1,0:T(8,128)S(1)}, f32[192,128]{1,0:T(8,128)S(1)}, u32[]{:S(2)}, u32[]{:S(2)}) collective-permute-start(f32[192,128]{1,0:T(8,128)S(1)} %get-tuple-element.41), channel_id=1, source_target_pairs={{0,1},{1,0},{2,3},{3,2},{4,5},{5,4},{6,7},{7,6},{8,9},{9,8},{10,11... | collective-permute-start | bytes 294920 | tf_op jit(solution)/shard_map/ppermute | solution.py:219
  (57 shorter events, 31.6 us)
Async XLA Ops:
  7.2 18.5 %copy-start.1 = (bf16[128,192]{0,1:T(8,128)(2,1)S(1)}, bf16[128,192]{0,1:T(8,128)(2,1)}, u32[]{:S(2)}) copy-start(bf16[128,192]{0,1:T(8,128)(2,1)} %param.5) | copy-start | bytes 147460
  7.2 133.0 %all-gather.4.cloned.1.call-start = ((), (), s32[]{:S(2)}) async-start(), calls=%async_computation.4 | async-start | bytes 8912896 | tf_op jit(solution)/shard_map/all_gather | solution.py:262
  9.9 71.1 %all-to-all-start = ((bf16[16,96,128]{2,1,0:T(8,128)(2,1)}), bf16[16,96,128]{2,1,0:T(8,128)(2,1)S(1)}, u32[]{:S(2)}, u32[]{:S(2)}) async-start(bf16[16,96,128]{2,1,0:T(8,128)(2,1)} %bitcast.12), calls=%async_computation | async-start | bytes 786432 | tf_op jit(solution)/shard_map/all_to_all | solution.py:265
  83.5 36.1 %all-to-all-start.1 = ((bf16[4,16,192,128]{3,2,1,0:T(8,128)(2,1)}), bf16[4,16,192,128]{3,2,1,0:T(8,128)(2,1)}, u32[]{:S(2)}, u32[]{:S(2)}) async-start(bf16[4,16,192,128]{3,2,1,0:T(8,128)(2,1)} %broadcast_in_dim.48), calls=%async_computation.1 | async-start | bytes 6291456 | tf_op jit(solution)/shard_map/all_to_all | solution.py:270
  88.3 13.6 %collective-permute-start.6 = (bf16[16,96,128]{2,1,0:T(8,128)(2,1)S(1)}, bf16[16,96,128]{2,1,0:T(8,128)(2,1)S(1)}, u32[]{:S(2)}, u32[]{:S(2)}) collective-permute-start(bf16[16,96,128]{2,1,0:T(8,128)(2,1)S(1)} %all-to-all-done), channel_id=1, source_target_pairs={{0,24},{1,25},{2,26},{3,27},{4,28},{5,29},{6,30},{7,31},{8,0},{9,1... | collective-permute-start | bytes 1179656 | tf_op jit(solution)/shard_map/ppermute | solution.py:247
  92.7 10.1 %collective-permute-start.5 = (bf16[16,96,128]{2,1,0:T(8,128)(2,1)S(1)}, bf16[16,96,128]{2,1,0:T(8,128)(2,1)S(1)}, u32[]{:S(2)}, u32[]{:S(2)}) collective-permute-start(bf16[16,96,128]{2,1,0:T(8,128)(2,1)S(1)} %all-to-all-done), channel_id=1, source_target_pairs={{0,16},{1,17},{2,18},{3,19},{4,20},{5,21},{6,22},{7,23},{8,24},{9,... | collective-permute-start | bytes 1179656 | tf_op jit(solution)/shard_map/ppermute | solution.py:247
  95.1 13.7 %collective-permute-start.4 = (bf16[16,96,128]{2,1,0:T(8,128)(2,1)S(1)}, bf16[16,96,128]{2,1,0:T(8,128)(2,1)S(1)}, u32[]{:S(2)}, u32[]{:S(2)}) collective-permute-start(bf16[16,96,128]{2,1,0:T(8,128)(2,1)S(1)} %all-to-all-done), channel_id=1, source_target_pairs={{0,8},{1,9},{2,10},{3,11},{4,12},{5,13},{6,14},{7,15},{8,16},{9,17... | collective-permute-start | bytes 1179656 | tf_op jit(solution)/shard_map/ppermute | solution.py:247
  109.0 21.8 %collective-permute-start.7 = (bf16[4,16,96,128]{3,2,1,0:T(8,128)(2,1)S(1)}, bf16[4,16,96,128]{3,2,1,0:T(8,128)(2,1)S(1)}, u32[]{:S(2)}, u32[]{:S(2)}) collective-permute-start(bf16[4,16,96,128]{3,2,1,0:T(8,128)(2,1)S(1)} %pad_maximum_fusion.own_ref), channel_id=1, source_target_pairs={{0,1},{1,0},{2,3},{3,2},{4,5},{5,4},{6,7},{7,6},{8,9},{9,8},{10,11... | collective-permute-start | bytes 4718600 | tf_op jit(solution)/shard_map/ppermute | solution.py:248
  118.5 12.2 %copy-start.4 = (s32[36]{0:T(128)}, s32[36]{0:T(128)S(1)}, u32[]{:S(2)}) copy-start(s32[36]{0:T(128)S(1)} %broadcast_in_dim.43) | copy-start | bytes 436
  121.3 29.3 %collective-permute-start.2 = (bf16[4,192,128]{2,1,0:T(8,128)(2,1)}, bf16[4,192,128]{2,1,0:T(8,128)(2,1)S(1)}, u32[]{:S(2)}, u32[]{:S(2)}) collective-permute-start(bf16[4,192,128]{2,1,0:T(8,128)(2,1)} %get-tuple-element.48), channel_id=1, source_target_pairs={{0,24},{1,25},{2,26},{3,27},{4,28},{5,29},{6,30},{7,31},{8,0},{9,1... | collective-permute-start | bytes 589832 | tf_op jit(solution)/shard_map/ppermute | solution.py:247
  125.7 24.9 %collective-permute-start.1 = (bf16[4,192,128]{2,1,0:T(8,128)(2,1)}, bf16[4,192,128]{2,1,0:T(8,128)(2,1)}, u32[]{:S(2)}, u32[]{:S(2)}) collective-permute-start(bf16[4,192,128]{2,1,0:T(8,128)(2,1)} %get-tuple-element.48), channel_id=1, source_target_pairs={{0,16},{1,17},{2,18},{3,19},{4,20},{5,21},{6,22},{7,23},{8,24},{9,... | collective-permute-start | bytes 589832 | tf_op jit(solution)/shard_map/ppermute | solution.py:247
  128.1 22.4 %collective-permute-start = (bf16[4,192,128]{2,1,0:T(8,128)(2,1)}, bf16[4,192,128]{2,1,0:T(8,128)(2,1)}, u32[]{:S(2)}, u32[]{:S(2)}) collective-permute-start(bf16[4,192,128]{2,1,0:T(8,128)(2,1)} %get-tuple-element.48), channel_id=1, source_target_pairs={{0,8},{1,9},{2,10},{3,11},{4,12},{5,13},{6,14},{7,15},{8,16},{9,17... | collective-permute-start | bytes 589832 | tf_op jit(solution)/shard_map/ppermute | solution.py:247
  138.5 11.8 %copy-start.5 = (s32[36]{0:T(128)S(1)}, s32[36]{0:T(128)}, u32[]{:S(2)}) copy-start(s32[36]{0:T(128)} %copy-done.4) | copy-start | bytes 436
  140.1 15.8 %copy-start = (bf16[128,1536]{1,0:T(8,128)(2,1)S(1)}, bf16[128,1536]{1,0:T(8,128)(2,1)}, u32[]{:S(2)}) copy-start(bf16[128,1536]{1,0:T(8,128)(2,1)} %grad_ref.1) | copy-start | bytes 1179652
  140.1 26.7 %all-to-all-start.2 = ((bf16[8,96,768]{2,1,0:T(8,128)(2,1)}), bf16[8,96,768]{2,1,0:T(8,128)(2,1)S(1)}, u32[]{:S(2)}, u32[]{:S(2)}) async-start(bf16[8,96,768]{2,1,0:T(8,128)(2,1)} %bitcast.27), calls=%async_computation.2 | async-start | bytes 2359296 | tf_op jit(solution)/shard_map/all_to_all | solution.py:282
  151.7 4.2 %collective-permute-start.3 = (bf16[4,4,192,128]{3,2,1,0:T(8,128)(2,1)S(1)}, bf16[4,4,192,128]{3,2,1,0:T(8,128)(2,1)S(1)}, u32[]{:S(2)}, u32[]{:S(2)}) collective-permute-start(bf16[4,4,192,128]{3,2,1,0:T(8,128)(2,1)S(1)} %pad_maximum_fusion.1.own_ref), channel_id=1, source_target_pairs={{0,1},{1,0},{2,3},{3,2},{4,5},{5,4},{6,7},{7,6},{8,9},{9,8},{10,11... | collective-permute-start | bytes 2359304 | tf_op jit(solution)/shard_map/ppermute | solution.py:248
  168.5 55.1 %all-to-all-start.3 = ((bf16[16,32,512]{2,1,0:T(8,128)(2,1)}), bf16[16,32,512]{2,1,0:T(8,128)(2,1)S(1)}, u32[]{:S(2)}, u32[]{:S(2)}) async-start(bf16[16,32,512]{2,1,0:T(8,128)(2,1)} %pick_slots.1), calls=%async_computation.3 | async-start | bytes 1048576 | tf_op jit(solution)/shard_map/all_to_all | solution.py:296
  178.6 13.2 %collective-permute-start.8 = (bf16[4,2,192,128]{3,2,1,0:T(8,128)(2,1)S(1)}, bf16[4,2,192,128]{3,2,1,0:T(8,128)(2,1)S(1)}, u32[]{:S(2)}, u32[]{:S(2)}) collective-permute-start(bf16[4,2,192,128]{3,2,1,0:T(8,128)(2,1)S(1)} %get-tuple-element.33), channel_id=1, source_target_pairs={{0,2},{1,3},{2,4},{3,5},{4,6},{5,7},{6,0},{7,1},{8,10},{9,11},{10,... | collective-permute-start | bytes 1179656 | tf_op jit(solution)/shard_map/ppermute | solution.py:212
  180.9 18.1 %collective-permute-start.9 = (bf16[4,2,192,128]{3,2,1,0:T(8,128)(2,1)S(1)}, bf16[4,2,192,128]{3,2,1,0:T(8,128)(2,1)S(1)}, u32[]{:S(2)}, u32[]{:S(2)}) collective-permute-start(bf16[4,2,192,128]{3,2,1,0:T(8,128)(2,1)S(1)} %get-tuple-element.34), channel_id=1, source_target_pairs={{0,4},{1,5},{2,6},{3,7},{4,0},{5,1},{6,2},{7,3},{8,12},{9,13},{10,... | collective-permute-start | bytes 1179656 | tf_op jit(solution)/shard_map/ppermute | solution.py:212
  184.5 18.1 %collective-permute-start.10 = (bf16[4,2,192,128]{3,2,1,0:T(8,128)(2,1)S(1)}, bf16[4,2,192,128]{3,2,1,0:T(8,128)(2,1)S(1)}, u32[]{:S(2)}, u32[]{:S(2)}) collective-permute-start(bf16[4,2,192,128]{3,2,1,0:T(8,128)(2,1)S(1)} %get-tuple-element.35), channel_id=1, source_target_pairs={{0,6},{1,7},{2,0},{3,1},{4,2},{5,3},{6,4},{7,5},{8,14},{9,15},{10,... | collective-permute-start | bytes 1179656 | tf_op jit(solution)/shard_map/ppermute | solution.py:212
  202.8 9.4 %collective-permute-start.11 = (f32[2,192,128]{2,1,0:T(8,128)S(1)}, f32[2,192,128]{2,1,0:T(8,128)S(1)}, u32[]{:S(2)}, u32[]{:S(2)}) collective-permute-start(f32[2,192,128]{2,1,0:T(8,128)S(1)} %get-tuple-element.37), channel_id=1, source_target_pairs={{0,8},{1,9},{2,10},{3,11},{4,12},{5,13},{6,14},{7,15},{8,16},{9,17... | collective-permute-start | bytes 589832 | tf_op jit(solution)/shard_map/ppermute | solution.py:216
  205.0 10.3 %collective-permute-start.12 = (f32[2,192,128]{2,1,0:T(8,128)S(1)}, f32[2,192,128]{2,1,0:T(8,128)S(1)}, u32[]{:S(2)}, u32[]{:S(2)}) collective-permute-start(f32[2,192,128]{2,1,0:T(8,128)S(1)} %get-tuple-element.38), channel_id=1, source_target_pairs={{0,16},{1,17},{2,18},{3,19},{4,20},{5,21},{6,22},{7,23},{8,24},{9,... | collective-permute-start | bytes 589832 | tf_op jit(solution)/shard_map/ppermute | solution.py:216
  209.1 8.8 %collective-permute-start.13 = (f32[2,192,128]{2,1,0:T(8,128)S(1)}, f32[2,192,128]{2,1,0:T(8,128)S(1)}, u32[]{:S(2)}, u32[]{:S(2)}) collective-permute-start(f32[2,192,128]{2,1,0:T(8,128)S(1)} %get-tuple-element.39), channel_id=1, source_target_pairs={{0,24},{1,25},{2,26},{3,27},{4,28},{5,29},{6,30},{7,31},{8,0},{9,1... | collective-permute-start | bytes 589832 | tf_op jit(solution)/shard_map/ppermute | solution.py:216
  218.0 5.1 %collective-permute-start.14 = (f32[192,128]{1,0:T(8,128)S(1)}, f32[192,128]{1,0:T(8,128)S(1)}, u32[]{:S(2)}, u32[]{:S(2)}) collective-permute-start(f32[192,128]{1,0:T(8,128)S(1)} %get-tuple-element.41), channel_id=1, source_target_pairs={{0,1},{1,0},{2,3},{3,2},{4,5},{5,4},{6,7},{7,6},{8,9},{9,8},{10,11... | collective-permute-start | bytes 294920 | tf_op jit(solution)/shard_map/ppermute | solution.py:219
  (2 other events, 18.8 us)
Sparse Core Ops, SparseCore 0:
  10.1 129.9 all-gather.3

commit v5 on v4

v5 whole, which is shorter than its diff:
```python
import functools
import math

import jax
import jax.numpy as jnp
from jax import lax
from jax.experimental import pallas as pl
from jax.experimental.pallas import tpu as pltpu
from jax.sharding import PartitionSpec as P

BF = jnp.bfloat16
F32 = jnp.float32
NX, NY, NC = 4, 4, 2
PAD = 64
PARAMS = pltpu.CompilerParams(vmem_limit_bytes=48 * 1024 * 1024)


def col_of(x, y, c):
    return (x * NY + y) * NC + c


PLANE = [(x, y, c) for x in range(NX) for y in range(NY) for c in range(NC)]
XC_GROUPS = [[col_of(x, y, c) for x in range(NX) for c in range(NC)] for y in range(NY)]
Y_GROUPS = [[col_of(x, y, c) for y in range(NY)] for x in range(NX) for c in range(NC)]
CORE_SWAP = [(col_of(x, y, c), col_of(x, y, 1 - c)) for x, y, c in PLANE]
X_SHIFTS = {s: [(col_of(x, y, c), col_of((x + s) % NX, y, c)) for x, y, c in PLANE] for s in range(1, NX)}
Y_SHIFTS = {s: [(col_of(x, y, c), col_of(x, (y + s) % NY, c)) for x, y, c in PLANE] for s in range(1, NY)}


def aligned(start, size, step):
    return pl.ds(pl.multiple_of(start, step), size)


def tokens_kernel(meta, place, own_ref, oth_ref, grad_ref, w_ref, out_ref, *refs, blk):
    (in_own, in_oth), (act, out_acc, in_acc, in_rows) = refs[:NC], refs[NC:]
    step = pl.program_id(0)
    piece = own_ref.shape[2]
    x, y, core = place[0], place[1], place[2]

    @pl.when(step == 0)
    def _():
        out_acc[...] = jnp.zeros_like(out_acc)
        in_acc[...] = jnp.zeros_like(in_acc)
        for t in range(NX):
            for s in range(NY):
                chip = (lax.rem(x - t + NX, NX) * NY + lax.rem(y - s + NY, NY)) * NC
                act[aligned((chip + core) * piece, piece, 64), :] = own_ref[t, s]
                act[aligned((chip + 1 - core) * piece, piece, 64), :] = oth_ref[t, s]

    hid = aligned(meta[1, step] * blk, blk, blk)
    mod = aligned(meta[2, step] * blk, blk, blk)
    w = w_ref[:, 0].reshape(blk, blk)
    out_acc[hid, :] += jnp.dot(w, act[mod, :], preferred_element_type=F32)
    in_acc[:, mod] += jnp.dot(grad_ref[:, hid], w, preferred_element_type=F32)

    @pl.when(step == pl.num_programs(0) - 1)
    def _():
        out_ref[...] = out_acc[...].T.astype(BF)
        in_rows[...] = in_acc[...].T.astype(BF)
        for s in range(NY):
            for t in range(NX):
                chip = (lax.rem(x + t, NX) * NY + lax.rem(y + s, NY)) * NC
                in_own[s, t] = in_rows[aligned((chip + core) * piece, piece, 64), :]
                in_oth[s, t] = in_rows[aligned((chip + 1 - core) * piece, piece, 64), :]


def tokens_step(meta, place, act_own, act_oth, grad, w_all):
    parts, _, rows, blk = w_all.shape
    piece, toks = act_own.shape[2:]
    feats = NX * NY * NC * piece
    hidden = grad.shape[1]
    lines = pl.BlockSpec((NX, NY, piece, toks), lambda k, m, p: (0, 0, 0, 0))
    whole = lambda k, m, p: (0, 0)
    return pl.pallas_call(
        functools.partial(tokens_kernel, blk=blk),
        grid_spec=pltpu.PrefetchScalarGridSpec(
            num_scalar_prefetch=2,
            grid=(meta.shape[1],),
            in_specs=[
                lines,
                lines,
                pl.BlockSpec((toks, hidden), whole),
                pl.BlockSpec((parts, 1, rows, blk), lambda k, m, p: (0, k, 0, 0)),
            ],
            out_specs=[pl.BlockSpec((toks, hidden), whole)]
            + [pl.BlockSpec((NY, NX, piece, toks), lambda k, m, p: (0, 0, 0, 0))] * NC,
            scratch_shapes=[
                pltpu.VMEM((feats, toks), BF),
                pltpu.VMEM((hidden, toks), F32),
                pltpu.VMEM((toks, feats), F32),
                pltpu.VMEM((feats, toks), BF),
            ],
        ),
        out_shape=[jax.ShapeDtypeStruct((toks, hidden), BF)]
        + [jax.ShapeDtypeStruct((NY, NX, piece, toks), BF)] * NC,
        compiler_params=PARAMS,
        name="tokens_step",
    )(meta, place, act_own, act_oth, grad, w_all)


def keep_kernel(meta, parts_ref, out_ref):
    for k in range(out_ref.shape[0]):
        out_ref[k] = parts_ref[meta[0, k]]


def keep_filled(meta, parts):
    return pl.pallas_call(
        keep_kernel,
        in_specs=[
            pl.BlockSpec(memory_space=pltpu.SMEM),
            pl.BlockSpec(memory_space=pltpu.VMEM),
        ],
        out_specs=pl.BlockSpec(memory_space=pltpu.VMEM),
        out_shape=jax.ShapeDtypeStruct((meta.shape[1], *parts.shape[1:]), BF),
        compiler_params=PARAMS,
        name="keep_filled",
    )(meta, parts)


def wgrad_kernel(place, own_ref, oth_ref, here, before, far_lo, far_hi, after, out_ref, a_buf, b_buf, *, scale):
    _, n_z, rows, toks = own_ref.shape
    piece = b_buf.shape[0] // NY
    x, y, core = place[0], place[1], place[2]
    step = pl.program_id(0)
    half = n_z // 2

    @pl.when(step == 0)
    def _():
        for s, parts in enumerate(((here,), (before,), (far_lo, far_hi), (after,))):
            at = aligned(lax.rem(y - s + NY, NY) * piece, piece, 64)
            for z in range(n_z):
                src = parts[0][z] if len(parts) == 1 else parts[z // half][z % half]
                b_buf[at, z * toks : (z + 1) * toks] = src[:piece]

    for z in range(n_z):
        a_buf[:rows, z * toks : (z + 1) * toks] = own_ref[0, z]
        a_buf[rows:, z * toks : (z + 1) * toks] = oth_ref[0, z]
    prod = lax.dot_general(
        a_buf[...], b_buf[...], (((1,), (1,)), ((), ())), preferred_element_type=F32
    )
    prod = (prod * scale).astype(BF)
    line = lax.rem(x - step + NX, NX) * NC
    out_ref[line + core] = prod[:rows]
    out_ref[line + 1 - core] = prod[rows:]


def wgrad_products(place, grad_own, grad_oth, act_y, piece, scale):
    n_x, n_z, rows, toks = grad_own.shape
    line = pl.BlockSpec((1, n_z, rows, toks), lambda s, p: (s, 0, 0, 0))
    return pl.pallas_call(
        functools.partial(wgrad_kernel, scale=scale),
        grid_spec=pltpu.PrefetchScalarGridSpec(
            num_scalar_prefetch=1,
            grid=(n_x,),
            in_specs=[line, line] + [pl.BlockSpec(a.shape, lambda s, p: (0, 0, 0)) for a in act_y],
            out_specs=pl.BlockSpec((n_x * NC, rows, NY * piece), lambda s, p: (0, 0, 0)),
            scratch_shapes=[
                pltpu.VMEM((NC * rows, n_z * toks), BF),
                pltpu.VMEM((NY * piece, n_z * toks), BF),
            ],
        ),
        out_shape=jax.ShapeDtypeStruct((n_x * NC, rows, NY * piece), BF),
        compiler_params=PARAMS,
        name="wgrad_products",
    )(place, grad_own, grad_oth, *act_y)


def slots_kernel(meta, prod_ref, out_ref, line_buf, *, chunk, blk):
    piece = prod_ref.shape[2] // NY
    for x in range(NX):
        for y in range(NY):
            for c in range(NC):
                at = (y * NC + c) * piece
                line_buf[x, :, at : at + piece] = prod_ref[x * NC + c, :, y * piece : (y + 1) * piece]
    per_x = line_buf.shape[2] // blk
    for s in range(out_ref.shape[0]):
        hid, mod, full = meta[0, s], meta[1, s], meta[2, s]
        rows = aligned(hid * chunk, chunk, chunk)
        cols = aligned(lax.rem(mod, per_x) * blk, blk, blk)
        part = line_buf[lax.div(mod, per_x), rows, cols]
        out_ref[s] = jnp.where(full > 0, part, jnp.zeros_like(part))


def pick_slots(meta, prods, chunk, blk):
    owners = meta.shape[1]
    _, rows, cols = prods.shape
    return pl.pallas_call(
        functools.partial(slots_kernel, chunk=chunk, blk=blk),
        in_specs=[
            pl.BlockSpec(memory_space=pltpu.SMEM),
            pl.BlockSpec(memory_space=pltpu.VMEM),
        ],
        out_specs=pl.BlockSpec(memory_space=pltpu.VMEM),
        out_shape=jax.ShapeDtypeStruct((owners, chunk, blk), BF),
        scratch_shapes=[pltpu.VMEM((NX, rows, NC * cols), BF)],
        compiler_params=PARAMS,
        name="pick_slots",
    )(meta, prods)


def sum_core_kernel(own_ref, oth_ref, *out_refs):
    for s in range(NY):
        out_refs[s][...] = (own_ref[s].astype(F32) + oth_ref[s].astype(F32)).astype(out_refs[s].dtype)


def sum_y_kernel(*refs):
    parts, out_refs = refs[:NY], refs[NY:]
    for t in range(NX):
        out_refs[t][...] = sum(part[t].astype(F32) for part in parts)


def sum_x_kernel(*refs):
    parts, out_ref = refs[:NX], refs[NX]
    out_ref[...] = sum(part[...] for part in parts).astype(BF)


def small_call(kernel, name, outs, *args):
    return pl.pallas_call(
        kernel,
        in_specs=[pl.BlockSpec(memory_space=pltpu.VMEM)] * len(args),
        out_specs=[pl.BlockSpec(memory_space=pltpu.VMEM)] * len(outs),
        out_shape=outs,
        compiler_params=PARAMS,
        name=name,
    )(*args)


def sum_groups(in_own, in_oth):
    _, _, piece, toks = in_own.shape
    got = lax.ppermute(in_oth, "col", CORE_SWAP)
    line = lambda dtype: jax.ShapeDtypeStruct((NX, piece, toks), dtype)
    by_y = small_call(sum_core_kernel, "sum_core", [line(F32)] + [line(BF)] * (NY - 1), in_own, got)
    got = [by_y[0]] + [lax.ppermute(by_y[s], "col", Y_SHIFTS[s]) for s in range(1, NY)]
    by_x = small_call(sum_y_kernel, "sum_y", [jax.ShapeDtypeStruct((piece, toks), F32)] * NX, *got)
    got = [by_x[0]] + [lax.ppermute(by_x[t], "col", X_SHIFTS[t]) for t in range(1, NX)]
    return small_call(sum_x_kernel, "sum_x", [jax.ShapeDtypeStruct((piece, toks), BF)], *got)[0]


def layout_tables(block_mask, block_owner, group, n_groups, owners):
    per_group = block_mask.shape[0] // n_groups
    model_blocks = block_mask.shape[1]
    size = per_group * model_blocks
    mask = lax.dynamic_slice_in_dim(block_mask, group * per_group, per_group, 0).reshape(size)
    owner = lax.dynamic_slice_in_dim(block_owner, group * per_group, per_group, 0).reshape(size)
    ids = jnp.arange(size, dtype=jnp.int32)
    before = jnp.sum(jnp.where(ids[:, None] < ids[None, :], mask[:, None], 0), axis=0)
    count = size // 4
    ranked = jnp.where(
        (before[None, :] == jnp.arange(count, dtype=jnp.int32)[:, None]) & (mask[None, :] == 1), 1, 0
    )
    id_of = jnp.sum(ranked * ids[None, :], axis=1)
    owner_of = jnp.sum(ranked * owner[None, :], axis=1)
    listed = jnp.stack([owner_of, id_of // model_blocks, id_of % model_blocks])
    held = jnp.where(
        (owner[None, :] == jnp.arange(owners, dtype=jnp.int32)[:, None]) & (mask[None, :] == 1), 1, 0
    )
    full = jnp.sum(held, axis=1)
    id_at = jnp.sum(held * ids[None, :], axis=1)
    slots = jnp.stack([id_at // model_blocks, id_at % model_blocks, full])
    return listed, slots


def line_x(x):
    return jnp.stack([x] + [lax.ppermute(x, "col", X_SHIFTS[t]) for t in range(1, NX)])


def share_y(x):
    half = x.shape[0] // 2
    before = lax.ppermute(x, "col", Y_SHIFTS[1])
    after = lax.ppermute(x, "col", Y_SHIFTS[NY - 1])
    far_lo = lax.ppermute(before[:half], "col", Y_SHIFTS[1])
    far_hi = lax.ppermute(after[half:], "col", Y_SHIFTS[NY - 1])
    return x, before, far_lo, far_hi, after


def per_device(activations, out_grad, weight_slots, block_mask, block_owner):
    blk = weight_slots.shape[2]
    owners, groups = lax.axis_size("row"), lax.axis_size("col")
    group, at_z = lax.axis_index("col"), lax.axis_index("row")
    toks, piece = activations.shape
    hidden = out_grad.shape[1]
    hid_blocks = hidden // blk
    chunk = blk // owners
    listed, slots = layout_tables(block_mask, block_owner, group, groups, owners)
    place = jnp.stack([group // (NY * NC), group // NC % NY, group % NC]).astype(jnp.int32)

    w_parts = lax.all_to_all(weight_slots[0, 0].reshape(owners, chunk, blk), "row", 0, 0, tiled=True)
    act_t = activations.T
    act_z = lax.all_gather(jnp.pad(act_t, ((0, PAD), (0, 0))), "row", axis=0)
    line_y = [act_t] + [lax.ppermute(act_t, "col", Y_SHIFTS[s]) for s in range(1, NY)]
    act_own = line_x(jnp.stack(line_y))
    grad_send = out_grad.T.reshape(hid_blocks, owners, chunk, toks).transpose(1, 0, 2, 3)
    grad_send = grad_send.reshape(owners, hid_blocks * chunk, toks)
    grad_send, w_parts, act_own = lax.optimization_barrier((grad_send, w_parts, act_own))
    w_all = lax.all_gather(keep_filled(listed, w_parts), "row", axis=0)
    grad_z = lax.all_to_all(grad_send, "row", 0, 0, tiled=True)
    act_oth = lax.ppermute(act_own, "col", CORE_SWAP)
    act_y = share_y(act_z[:, :piece])
    grad_z, act_y, act_oth = lax.optimization_barrier((grad_z, act_y, act_oth))

    grad_own = line_x(grad_z)
    grad_oth = lax.ppermute(grad_own, "col", CORE_SWAP)
    scale = 1.0 / math.sqrt(toks * owners)
    prods = wgrad_products(place, grad_own, grad_oth, act_y, piece, scale)
    prods = lax.all_to_all(prods, "col", 0, 0, tiled=True, axis_index_groups=XC_GROUPS)
    slot_parts = pick_slots(slots, prods, chunk, blk)
    weight_grad = lax.all_to_all(slot_parts, "row", 0, 0, tiled=True).reshape(1, 1, blk, blk)

    outputs, in_own, in_oth = tokens_step(listed, place, act_own, act_oth, out_grad, w_all)
    return outputs, sum_groups(in_own, in_oth).T, weight_grad


def solution(mesh):
    placed = (P("row", "col"), P("row", "col"), P("col", "row", None, None), P(), P())
    return jax.shard_map(
        per_device,
        mesh=mesh,
        in_specs=placed,
        out_specs=(P("row", "col"), P("row", "col"), P("col", "row", None, None)),
        check_vma=False,
    )
```

time: 232 us -> 259 us (1.12); the launches traced: 231 us -> 256 us
  blocking collectives: 55.4 us -> 0 us
  waiting for transfers between devices: 40 us -> 77.8 us
  starting transfers between devices: 92.6 us -> 127 us
  local copies, waits for them, and re-layouts: 7.38 us -> 12.4 us
    all_gather x1 -> x0, blocking collectives: 55.4 us -> none  [per_device(): act_z = lax.all_gather(activations.T, 'row', axis=0)]
    ppermute x12 -> x19, starting transfers between devices: 42.4 us -> 79 us  [the longest x6 20.5 us: line_x(): lax.ppermute(x, 'col', X_SHIFTS[t])]
    all_gather x1 -> x2, waiting for transfers between devices: 1.6 us -> 32 us  [the longest x1 32 us: per_device(): act_z = lax.all_gather(jnp.pad(act_t, ((0, PAD), (0, 0))), 'row', axis=0)]
    all_to_all x3, waiting for transfers between devices: 2.49 us -> 16.4 us  [the longest x1 16.3 us: per_device(): lax.all_to_all(prods, 'col', 0, 0, tiled=True, axis_index_groups=XC_GROUPS)]
    unnamed x14 -> x24, local copies, waits for them, and re-layouts: 2.03 us -> 7.77 us
    ppermute x12 -> x19, waiting for transfers between devices: 29.5 us -> 25.7 us  [the longest x6 11.1 us: line_x(): lax.ppermute(x, 'col', X_SHIFTS[t])]
    all_to_all x1, starting transfers between devices: 10.1 us -> 7.08 us  [per_device(): lax.all_to_all(slot_parts, 'row', 0, 0, tiled=True).reshape(1, 1, blk, blk)]
  transfers between devices with their start and end apart: 20 -> 28, of which waited for: 13 -> 16; matrix products, arithmetic and copies ran while one was open for 4% -> 3% of each run, Pallas kernels for 8% -> 8%
where the time goes in v5:
time: 259 us; the launch traced here: 256 us
  starting transfers between devices  127 us (49%)
  waiting for transfers between devices  77.8 us (30%)
  Pallas kernels  21.7 us (8%)
  between operations  14.5 us (6%)
  local copies, waits for them, and re-layouts  12.4 us (5%)
  other arithmetic  2.59 us (1%)
    all_gather x1, waiting for transfers between devices, per_device(): act_z = lax.all_gather(jnp.pad(act_t, ((0, PAD), (0, 0))), 'row', axis=0)  32 us
    ppermute x6, starting transfers between devices, line_x(): lax.ppermute(x, 'col', X_SHIFTS[t])  20.5 us
    all_to_all x1, waiting for transfers between devices, per_device(): lax.all_to_all(prods, 'col', 0, 0, tiled=True, axis_index_groups=XC_GROUPS)  16.3 us
    all_to_all x1, starting transfers between devices, per_device(): lax.all_to_all(weight_slots[0, 0].reshape(owners, chunk, blk), 'row', 0,...  15.9 us
    all_to_all x1, starting transfers between devices, per_device(): grad_z = lax.all_to_all(grad_send, 'row', 0, 0, tiled=True)  11.9 us
    ppermute x6, waiting for transfers between devices, line_x(): lax.ppermute(x, 'col', X_SHIFTS[t])  11.1 us
    ppermute x3, starting transfers between devices, sum_groups(): lax.ppermute(by_y[s], 'col', Y_SHIFTS[s])  11 us
    ppermute x1, starting transfers between devices, per_device(): grad_oth = lax.ppermute(grad_own, 'col', CORE_SWAP)  10.9 us
  transfers between devices with their start and end apart: 28, of which 16 were waited for; matrix products, arithmetic and copies ran while one was open for 3% of the time, Pallas kernels for 8%

profile of v5, /device:TPU:1, one launch (start us, length us, event | category | flops | bytes accessed | tf_op | source)
XLA Modules:
  0.0 255.6 jit_solution(4558381277860371316)
XLA Ops:
  7.2 15.9 %all-to-all-start = ((bf16[16,32,512]{2,1,0:T(8,128)(2,1)}), bf16[16,32,512]{2,1,0:T(8,128)(2,1)S(1)}, u32[]{:S(2)}, u32[]{:S(2)}) async-start(bf16[16,32,512]{2,1,0:T(8,128)(2,1)} %bitcast.53), calls=%async_computation | async-start | bytes 1048576 | tf_op jit(solution)/shard_map/all_to_all | solution.py:287
  24.6 3.2 %collective-permute-start = (bf16[192,128]{1,0:T(8,128)(2,1)}, bf16[192,128]{1,0:T(8,128)(2,1)S(1)}, u32[]{:S(2)}, u32[]{:S(2)}) collective-permute-start(bf16[192,128]{1,0:T(8,128)(2,1)} %bitcast.61), channel_id=1, source_target_pairs={{0,2},{1,3},{2,4},{3,5},{4,6},{5,7},{6,0},{7,1},{8,10},{9,11},{10,... | collective-permute-start | bytes 147464 | tf_op jit(solution)/shard_map/ppermute | solution.py:290
  27.8 4.5 %collective-permute-start.1 = (bf16[192,128]{1,0:T(8,128)(2,1)}, bf16[192,128]{1,0:T(8,128)(2,1)S(1)}, u32[]{:S(2)}, u32[]{:S(2)}) collective-permute-start(bf16[192,128]{1,0:T(8,128)(2,1)} %bitcast.62), channel_id=1, source_target_pairs={{0,4},{1,5},{2,6},{3,7},{4,0},{5,1},{6,2},{7,3},{8,12},{9,13},{10,... | collective-permute-start | bytes 147464 | tf_op jit(solution)/shard_map/ppermute | solution.py:290
  38.6 3.1 %collective-permute-start.3 = (bf16[4,192,128]{2,1,0:T(8,128)(2,1)S(1)}, bf16[4,192,128]{2,1,0:T(8,128)(2,1)S(1)}, u32[]{:S(2)}, u32[]{:S(2)}) collective-permute-start(bf16[4,192,128]{2,1,0:T(8,128)(2,1)S(1)} %get-tuple-element.50), channel_id=1, source_target_pairs={{0,8},{1,9},{2,10},{3,11},{4,12},{5,13},{6,14},{7,15},{8,16},{9,17... | collective-permute-start | bytes 589832 | tf_op jit(solution)/shard_map/ppermute | solution.py:264
  41.7 4.4 %collective-permute-start.4 = (bf16[4,192,128]{2,1,0:T(8,128)(2,1)S(1)}, bf16[4,192,128]{2,1,0:T(8,128)(2,1)S(1)}, u32[]{:S(2)}, u32[]{:S(2)}) collective-permute-start(bf16[4,192,128]{2,1,0:T(8,128)(2,1)S(1)} %get-tuple-element.50), channel_id=1, source_target_pairs={{0,16},{1,17},{2,18},{3,19},{4,20},{5,21},{6,22},{7,23},{8,24},{9,... | collective-permute-start | bytes 589832 | tf_op jit(solution)/shard_map/ppermute | solution.py:264
  55.7 11.9 %all-to-all-start.1 = ((bf16[16,96,128]{2,1,0:T(8,128)(2,1)}), bf16[16,96,128]{2,1,0:T(8,128)(2,1)}, u32[]{:S(2)}, u32[]{:S(2)}) async-start(bf16[16,96,128]{2,1,0:T(8,128)(2,1)} %bitcast.10), calls=%async_computation.1 | async-start | bytes 786432 | tf_op jit(solution)/shard_map/all_to_all | solution.py:296
  67.6 32.0 %all-gather.5.cloned.1.call-done = bf16[4096,128]{1,0:T(8,128)(2,1)} async-done(((bf16[256,128]{1,0:T(8,128)(2,1)}), bf16[4096,128]{1,0:T(8,128)(2,1)}) %all-gather.5.cloned.1.call-update) | async-done | bytes 1048592 | tf_op jit(solution)/shard_map/all_gather | solution.py:289
  102.9 4.5 %collective-permute-start.8 = (bf16[16,192,128]{2,1,0:T(8,128)(2,1)S(1)}, bf16[16,192,128]{2,1,0:T(8,128)(2,1)S(1)}, u32[]{:S(2)}, u32[]{:S(2)}) collective-permute-start(bf16[16,192,128]{2,1,0:T(8,128)(2,1)S(1)} %slice.12.here), channel_id=1, source_target_pairs={{0,6},{1,7},{2,0},{3,1},{4,2},{5,3},{6,4},{7,5},{8,14},{9,15},{10,... | collective-permute-start | bytes 2359304 | tf_op jit(solution)/shard_map/ppermute | solution.py:270
  107.3 9.8 %collective-permute-start.10 = (bf16[4,4,192,128]{3,2,1,0:T(8,128)(2,1)S(1)}, bf16[4,4,192,128]{3,2,1,0:T(8,128)(2,1)S(1)}, u32[]{:S(2)}, u32[]{:S(2)}) collective-permute-start(bf16[4,4,192,128]{3,2,1,0:T(8,128)(2,1)S(1)} %pad_maximum_fusion.1.own_ref), channel_id=1, source_target_pairs={{0,1},{1,0},{2,3},{3,2},{4,5},{5,4},{6,7},{7,6},{8,9},{9,8},{10,11... | collective-permute-start | bytes 2359304 | tf_op jit(solution)/shard_map/ppermute | solution.py:297
  119.2 4.6 %collective-permute-start.9 = (bf16[8,192,128]{2,1,0:T(8,128)(2,1)S(1)}, bf16[8,192,128]{2,1,0:T(8,128)(2,1)S(1)}, u32[]{:S(2)}, u32[]{:S(2)}) collective-permute-start(bf16[8,192,128]{2,1,0:T(8,128)(2,1)S(1)} %slice.14), channel_id=1, source_target_pairs={{0,6},{1,7},{2,0},{3,1},{4,2},{5,3},{6,4},{7,5},{8,14},{9,15},{10,... | collective-permute-start | bytes 1179656 | tf_op jit(solution)/shard_map/ppermute | solution.py:272
  124.7 3.1 %collective-permute-done.7.far_lo = bf16[8,192,128]{2,1,0:T(8,128)(2,1)S(1)} collective-permute-done((bf16[8,192,128]{2,1,0:T(8,128)(2,1)S(1)}, bf16[8,192,128]{2,1,0:T(8,128)(2,1)S(1)}, u32[]{:S(2)}, u32[]{:S(2)}) %collective-permute-start.7) | collective-permute-done | bytes 393248 | tf_op jit(solution)/shard_map/ppermute | solution.py:271
  130.1 3.6 %collective-permute-start.18 = (bf16[16,96,128]{2,1,0:T(8,128)(2,1)}, bf16[16,96,128]{2,1,0:T(8,128)(2,1)S(1)}, u32[]{:S(2)}, u32[]{:S(2)}) collective-permute-start(bf16[16,96,128]{2,1,0:T(8,128)(2,1)} %all-to-all-done.1), channel_id=1, source_target_pairs={{0,8},{1,9},{2,10},{3,11},{4,12},{5,13},{6,14},{7,15},{8,16},{9,17... | collective-permute-start | bytes 1179656 | tf_op jit(solution)/shard_map/ppermute | solution.py:264
  133.7 3.3 %collective-permute-start.19 = (bf16[16,96,128]{2,1,0:T(8,128)(2,1)}, bf16[16,96,128]{2,1,0:T(8,128)(2,1)S(1)}, u32[]{:S(2)}, u32[]{:S(2)}) collective-permute-start(bf16[16,96,128]{2,1,0:T(8,128)(2,1)} %all-to-all-done.1), channel_id=1, source_target_pairs={{0,16},{1,17},{2,18},{3,19},{4,20},{5,21},{6,22},{7,23},{8,24},{9,... | collective-permute-start | bytes 1179656 | tf_op jit(solution)/shard_map/ppermute | solution.py:264
  140.2 4.6 %collective-permute-done.19 = bf16[16,96,128]{2,1,0:T(8,128)(2,1)S(1)} collective-permute-done((bf16[16,96,128]{2,1,0:T(8,128)(2,1)}, bf16[16,96,128]{2,1,0:T(8,128)(2,1)S(1)}, u32[]{:S(2)}, u32[]{:S(2)}) %collective-permute-start.19) | collective-permute-done | bytes 393248 | tf_op jit(solution)/shard_map/ppermute | solution.py:264
  148.3 10.9 %collective-permute-start.21 = (bf16[4,16,96,128]{3,2,1,0:T(8,128)(2,1)S(1)}, bf16[4,16,96,128]{3,2,1,0:T(8,128)(2,1)}, u32[]{:S(2)}, u32[]{:S(2)}) collective-permute-start(bf16[4,16,96,128]{3,2,1,0:T(8,128)(2,1)S(1)} %pad_maximum_fusion.own_ref), channel_id=1, source_target_pairs={{0,1},{1,0},{2,3},{3,2},{4,5},{5,4},{6,7},{7,6},{8,9},{9,8},{10,11... | collective-permute-start | bytes 4718600 | tf_op jit(solution)/shard_map/ppermute | solution.py:302
  166.7 8.2 %wgrad_products.1 = bf16[8,96,768]{2,1,0:T(8,128)(2,1)} custom-call(s32[3]{0:T(128)S(1)} %pad_add_fusion.2.place, bf16[4,16,96,128]{3,2,1,0:T(8,128)(2,1)S(1)} %pad_maximum_fusion.own_ref, bf16[4,16,96,128]{3,2,1,0:T(8,128)(2,1)} %collective-permute-done.21.oth_ref, bf16[16,192,128]{2,1,0:T(8,128)(2,1)S(1)} %slice.12.here, ...), custom_call_target="tpu_custom_call" | custom-call | tf_op jit(solution)/shard_map/wgrad_products/pallas_call | solution.py:150
  174.9 4.3 %all-to-all-start.2 = ((bf16[8,96,768]{2,1,0:T(8,128)(2,1)}), bf16[8,96,768]{2,1,0:T(8,128)(2,1)S(1)}, u32[]{:S(2)}, u32[]{:S(2)}) async-start(bf16[8,96,768]{2,1,0:T(8,128)(2,1)} %wgrad_products.1), calls=%async_computation.2 | async-start | bytes 2359296 | tf_op jit(solution)/shard_map/all_to_all | solution.py:305
  179.4 16.3 %all-to-all-done.2.prod_ref = bf16[8,96,768]{2,1,0:T(8,128)(2,1)S(1)} async-done(((bf16[8,96,768]{2,1,0:T(8,128)(2,1)}), bf16[8,96,768]{2,1,0:T(8,128)(2,1)S(1)}, u32[]{:S(2)}, u32[]{:S(2)}) %all-to-all-start.2) | async-done | bytes 1179680 | tf_op jit(solution)/shard_map/all_to_all | solution.py:305
  197.4 7.1 %all-to-all-start.3 = ((bf16[16,32,512]{2,1,0:T(8,128)(2,1)}), bf16[16,32,512]{2,1,0:T(8,128)(2,1)S(1)}, u32[]{:S(2)}, u32[]{:S(2)}) async-start(bf16[16,32,512]{2,1,0:T(8,128)(2,1)} %pick_slots.1), calls=%async_computation.3 | async-start | bytes 1048576 | tf_op jit(solution)/shard_map/all_to_all | solution.py:307
  204.5 9.6 %tokens_step.1 = (bf16[128,1536]{1,0:T(8,128)(2,1)}, bf16[4,4,192,128]{3,2,1,0:T(8,128)(2,1)S(1)}, bf16[4,4,192,128]{3,2,1,0:T(8,128)(2,1)S(1)}) custom-call(s32[3,9]{1,0:T(4,128)S(1)} %pad_add_fusion.meta, s32[3]{0:T(128)S(1)} %pad_add_fusion.2.place, bf16[4,4,192,128]{3,2,1,0:T(8,128)(2,1)S(1)} %pad_maximum_fusion.1.own_ref, ...), custom_call_target="tpu_custom_call" | custom-call | tf_op jit(solution)/shard_map/tokens_step/pallas_call | solution.py:74
  219.3 3.1 %collective-permute-start.12 = (bf16[4,192,128]{2,1,0:T(8,128)(2,1)S(1)}, bf16[4,192,128]{2,1,0:T(8,128)(2,1)S(1)}, u32[]{:S(2)}, u32[]{:S(2)}) collective-permute-start(bf16[4,192,128]{2,1,0:T(8,128)(2,1)S(1)} %get-tuple-element.32), channel_id=1, source_target_pairs={{0,2},{1,3},{2,4},{3,5},{4,6},{5,7},{6,0},{7,1},{8,10},{9,11},{10,... | collective-permute-start | bytes 589832 | tf_op jit(solution)/shard_map/ppermute | solution.py:233
  222.4 4.9 %collective-permute-start.13 = (bf16[4,192,128]{2,1,0:T(8,128)(2,1)S(1)}, bf16[4,192,128]{2,1,0:T(8,128)(2,1)S(1)}, u32[]{:S(2)}, u32[]{:S(2)}) collective-permute-start(bf16[4,192,128]{2,1,0:T(8,128)(2,1)S(1)} %get-tuple-element.33), channel_id=1, source_target_pairs={{0,4},{1,5},{2,6},{3,7},{4,0},{5,1},{6,2},{7,3},{8,12},{9,13},{10,... | collective-permute-start | bytes 589832 | tf_op jit(solution)/shard_map/ppermute | solution.py:233
  230.3 3.9 %collective-permute-done.13.refs_2_ = bf16[4,192,128]{2,1,0:T(8,128)(2,1)S(1)} collective-permute-done((bf16[4,192,128]{2,1,0:T(8,128)(2,1)S(1)}, bf16[4,192,128]{2,1,0:T(8,128)(2,1)S(1)}, u32[]{:S(2)}, u32[]{:S(2)}) %collective-permute-start.13) | collective-permute-done | bytes 196640 | tf_op jit(solution)/shard_map/ppermute | solution.py:233
  237.4 3.7 %collective-permute-start.16 = (f32[192,128]{1,0:T(8,128)S(1)}, f32[192,128]{1,0:T(8,128)S(1)}, u32[]{:S(2)}, u32[]{:S(2)}) collective-permute-start(f32[192,128]{1,0:T(8,128)S(1)} %get-tuple-element.37), channel_id=1, source_target_pairs={{0,16},{1,17},{2,18},{3,19},{4,20},{5,21},{6,22},{7,23},{8,24},{9,... | collective-permute-start | bytes 294920 | tf_op jit(solution)/shard_map/ppermute | solution.py:235
  (87 shorter events, 60.7 us)
Async XLA Ops:
  7.2 47.2 %all-to-all-start = ((bf16[16,32,512]{2,1,0:T(8,128)(2,1)}), bf16[16,32,512]{2,1,0:T(8,128)(2,1)S(1)}, u32[]{:S(2)}, u32[]{:S(2)}) async-start(bf16[16,32,512]{2,1,0:T(8,128)(2,1)} %bitcast.53), calls=%async_computation | async-start | bytes 1048576 | tf_op jit(solution)/shard_map/all_to_all | solution.py:287
  23.1 76.6 %all-gather.5.cloned.1.call-start = ((), (), s32[]{:S(2)}) async-start(), calls=%async_computation.4 | async-start | bytes 1114112 | tf_op jit(solution)/shard_map/all_gather | solution.py:289
  24.6 179.9 %all-gather.7.cloned.1.call-start = ((), (), s32[]{:S(2)}) async-start(), calls=%async_computation.5 | async-start | bytes 5013504 | tf_op jit(solution)/shard_map/all_gather | solution.py:295
  24.6 12.1 %collective-permute-start = (bf16[192,128]{1,0:T(8,128)(2,1)}, bf16[192,128]{1,0:T(8,128)(2,1)S(1)}, u32[]{:S(2)}, u32[]{:S(2)}) collective-permute-start(bf16[192,128]{1,0:T(8,128)(2,1)} %bitcast.61), channel_id=1, source_target_pairs={{0,2},{1,3},{2,4},{3,5},{4,6},{5,7},{6,0},{7,1},{8,10},{9,11},{10,... | collective-permute-start | bytes 147464 | tf_op jit(solution)/shard_map/ppermute | solution.py:290
  27.8 8.9 %collective-permute-start.1 = (bf16[192,128]{1,0:T(8,128)(2,1)}, bf16[192,128]{1,0:T(8,128)(2,1)S(1)}, u32[]{:S(2)}, u32[]{:S(2)}) collective-permute-start(bf16[192,128]{1,0:T(8,128)(2,1)} %bitcast.62), channel_id=1, source_target_pairs={{0,4},{1,5},{2,6},{3,7},{4,0},{5,1},{6,2},{7,3},{8,12},{9,13},{10,... | collective-permute-start | bytes 147464 | tf_op jit(solution)/shard_map/ppermute | solution.py:290
  38.6 11.6 %collective-permute-start.3 = (bf16[4,192,128]{2,1,0:T(8,128)(2,1)S(1)}, bf16[4,192,128]{2,1,0:T(8,128)(2,1)S(1)}, u32[]{:S(2)}, u32[]{:S(2)}) collective-permute-start(bf16[4,192,128]{2,1,0:T(8,128)(2,1)S(1)} %get-tuple-element.50), channel_id=1, source_target_pairs={{0,8},{1,9},{2,10},{3,11},{4,12},{5,13},{6,14},{7,15},{8,16},{9,17... | collective-permute-start | bytes 589832 | tf_op jit(solution)/shard_map/ppermute | solution.py:264
  41.7 10.0 %collective-permute-start.4 = (bf16[4,192,128]{2,1,0:T(8,128)(2,1)S(1)}, bf16[4,192,128]{2,1,0:T(8,128)(2,1)S(1)}, u32[]{:S(2)}, u32[]{:S(2)}) collective-permute-start(bf16[4,192,128]{2,1,0:T(8,128)(2,1)S(1)} %get-tuple-element.50), channel_id=1, source_target_pairs={{0,16},{1,17},{2,18},{3,19},{4,20},{5,21},{6,22},{7,23},{8,24},{9,... | collective-permute-start | bytes 589832 | tf_op jit(solution)/shard_map/ppermute | solution.py:264
  46.1 8.2 %collective-permute-start.5 = (bf16[4,192,128]{2,1,0:T(8,128)(2,1)S(1)}, bf16[4,192,128]{2,1,0:T(8,128)(2,1)S(1)}, u32[]{:S(2)}, u32[]{:S(2)}) collective-permute-start(bf16[4,192,128]{2,1,0:T(8,128)(2,1)S(1)} %get-tuple-element.50), channel_id=1, source_target_pairs={{0,24},{1,25},{2,26},{3,27},{4,28},{5,29},{6,30},{7,31},{8,0},{9,1... | collective-permute-start | bytes 589832 | tf_op jit(solution)/shard_map/ppermute | solution.py:264
  55.7 74.4 %all-to-all-start.1 = ((bf16[16,96,128]{2,1,0:T(8,128)(2,1)}), bf16[16,96,128]{2,1,0:T(8,128)(2,1)}, u32[]{:S(2)}, u32[]{:S(2)}) async-start(bf16[16,96,128]{2,1,0:T(8,128)(2,1)} %bitcast.10), calls=%async_computation.1 | async-start | bytes 786432 | tf_op jit(solution)/shard_map/all_to_all | solution.py:296
  100.8 16.3 %collective-permute-start.6 = (bf16[16,192,128]{2,1,0:T(8,128)(2,1)S(1)}, bf16[16,192,128]{2,1,0:T(8,128)(2,1)S(1)}, u32[]{:S(2)}, u32[]{:S(2)}) collective-permute-start(bf16[16,192,128]{2,1,0:T(8,128)(2,1)S(1)} %slice.12.here), channel_id=1, source_target_pairs={{0,2},{1,3},{2,4},{3,5},{4,6},{5,7},{6,0},{7,1},{8,10},{9,11},{10,... | collective-permute-start | bytes 2359304 | tf_op jit(solution)/shard_map/ppermute | solution.py:269
  102.9 16.2 %collective-permute-start.8 = (bf16[16,192,128]{2,1,0:T(8,128)(2,1)S(1)}, bf16[16,192,128]{2,1,0:T(8,128)(2,1)S(1)}, u32[]{:S(2)}, u32[]{:S(2)}) collective-permute-start(bf16[16,192,128]{2,1,0:T(8,128)(2,1)S(1)} %slice.12.here), channel_id=1, source_target_pairs={{0,6},{1,7},{2,0},{3,1},{4,2},{5,3},{6,4},{7,5},{8,14},{9,15},{10,... | collective-permute-start | bytes 2359304 | tf_op jit(solution)/shard_map/ppermute | solution.py:270
  107.3 16.4 %collective-permute-start.10 = (bf16[4,4,192,128]{3,2,1,0:T(8,128)(2,1)S(1)}, bf16[4,4,192,128]{3,2,1,0:T(8,128)(2,1)S(1)}, u32[]{:S(2)}, u32[]{:S(2)}) collective-permute-start(bf16[4,4,192,128]{3,2,1,0:T(8,128)(2,1)S(1)} %pad_maximum_fusion.1.own_ref), channel_id=1, source_target_pairs={{0,1},{1,0},{2,3},{3,2},{4,5},{5,4},{6,7},{7,6},{8,9},{9,8},{10,11... | collective-permute-start | bytes 2359304 | tf_op jit(solution)/shard_map/ppermute | solution.py:297
  117.2 10.6 %collective-permute-start.7 = (bf16[8,192,128]{2,1,0:T(8,128)(2,1)S(1)}, bf16[8,192,128]{2,1,0:T(8,128)(2,1)S(1)}, u32[]{:S(2)}, u32[]{:S(2)}) collective-permute-start(bf16[8,192,128]{2,1,0:T(8,128)(2,1)S(1)} %slice.13), channel_id=1, source_target_pairs={{0,2},{1,3},{2,4},{3,5},{4,6},{5,7},{6,0},{7,1},{8,10},{9,11},{10,... | collective-permute-start | bytes 1179656 | tf_op jit(solution)/shard_map/ppermute | solution.py:271
  119.2 10.2 %collective-permute-start.9 = (bf16[8,192,128]{2,1,0:T(8,128)(2,1)S(1)}, bf16[8,192,128]{2,1,0:T(8,128)(2,1)S(1)}, u32[]{:S(2)}, u32[]{:S(2)}) collective-permute-start(bf16[8,192,128]{2,1,0:T(8,128)(2,1)S(1)} %slice.14), channel_id=1, source_target_pairs={{0,6},{1,7},{2,0},{3,1},{4,2},{5,3},{6,4},{7,5},{8,14},{9,15},{10,... | collective-permute-start | bytes 1179656 | tf_op jit(solution)/shard_map/ppermute | solution.py:272
  130.1 10.2 %collective-permute-start.18 = (bf16[16,96,128]{2,1,0:T(8,128)(2,1)}, bf16[16,96,128]{2,1,0:T(8,128)(2,1)S(1)}, u32[]{:S(2)}, u32[]{:S(2)}) collective-permute-start(bf16[16,96,128]{2,1,0:T(8,128)(2,1)} %all-to-all-done.1), channel_id=1, source_target_pairs={{0,8},{1,9},{2,10},{3,11},{4,12},{5,13},{6,14},{7,15},{8,16},{9,17... | collective-permute-start | bytes 1179656 | tf_op jit(solution)/shard_map/ppermute | solution.py:264
  133.7 11.1 %collective-permute-start.19 = (bf16[16,96,128]{2,1,0:T(8,128)(2,1)}, bf16[16,96,128]{2,1,0:T(8,128)(2,1)S(1)}, u32[]{:S(2)}, u32[]{:S(2)}) collective-permute-start(bf16[16,96,128]{2,1,0:T(8,128)(2,1)} %all-to-all-done.1), channel_id=1, source_target_pairs={{0,16},{1,17},{2,18},{3,19},{4,20},{5,21},{6,22},{7,23},{8,24},{9,... | collective-permute-start | bytes 1179656 | tf_op jit(solution)/shard_map/ppermute | solution.py:264
  137.0 10.1 %collective-permute-start.20 = (bf16[16,96,128]{2,1,0:T(8,128)(2,1)}, bf16[16,96,128]{2,1,0:T(8,128)(2,1)S(1)}, u32[]{:S(2)}, u32[]{:S(2)}) collective-permute-start(bf16[16,96,128]{2,1,0:T(8,128)(2,1)} %all-to-all-done.1), channel_id=1, source_target_pairs={{0,24},{1,25},{2,26},{3,27},{4,28},{5,29},{6,30},{7,31},{8,0},{9,1... | collective-permute-start | bytes 1179656 | tf_op jit(solution)/shard_map/ppermute | solution.py:264
  148.3 14.1 %collective-permute-start.21 = (bf16[4,16,96,128]{3,2,1,0:T(8,128)(2,1)S(1)}, bf16[4,16,96,128]{3,2,1,0:T(8,128)(2,1)}, u32[]{:S(2)}, u32[]{:S(2)}) collective-permute-start(bf16[4,16,96,128]{3,2,1,0:T(8,128)(2,1)S(1)} %pad_maximum_fusion.own_ref), channel_id=1, source_target_pairs={{0,1},{1,0},{2,3},{3,2},{4,5},{5,4},{6,7},{7,6},{8,9},{9,8},{10,11... | collective-permute-start | bytes 4718600 | tf_op jit(solution)/shard_map/ppermute | solution.py:302
  174.9 20.8 %all-to-all-start.2 = ((bf16[8,96,768]{2,1,0:T(8,128)(2,1)}), bf16[8,96,768]{2,1,0:T(8,128)(2,1)S(1)}, u32[]{:S(2)}, u32[]{:S(2)}) async-start(bf16[8,96,768]{2,1,0:T(8,128)(2,1)} %wgrad_products.1), calls=%async_computation.2 | async-start | bytes 2359296 | tf_op jit(solution)/shard_map/all_to_all | solution.py:305
  197.4 46.2 %all-to-all-start.3 = ((bf16[16,32,512]{2,1,0:T(8,128)(2,1)}), bf16[16,32,512]{2,1,0:T(8,128)(2,1)S(1)}, u32[]{:S(2)}, u32[]{:S(2)}) async-start(bf16[16,32,512]{2,1,0:T(8,128)(2,1)} %pick_slots.1), calls=%async_computation.3 | async-start | bytes 1048576 | tf_op jit(solution)/shard_map/all_to_all | solution.py:307
  219.3 11.0 %collective-permute-start.12 = (bf16[4,192,128]{2,1,0:T(8,128)(2,1)S(1)}, bf16[4,192,128]{2,1,0:T(8,128)(2,1)S(1)}, u32[]{:S(2)}, u32[]{:S(2)}) collective-permute-start(bf16[4,192,128]{2,1,0:T(8,128)(2,1)S(1)} %get-tuple-element.32), channel_id=1, source_target_pairs={{0,2},{1,3},{2,4},{3,5},{4,6},{5,7},{6,0},{7,1},{8,10},{9,11},{10,... | collective-permute-start | bytes 589832 | tf_op jit(solution)/shard_map/ppermute | solution.py:233
  222.4 11.8 %collective-permute-start.13 = (bf16[4,192,128]{2,1,0:T(8,128)(2,1)S(1)}, bf16[4,192,128]{2,1,0:T(8,128)(2,1)S(1)}, u32[]{:S(2)}, u32[]{:S(2)}) collective-permute-start(bf16[4,192,128]{2,1,0:T(8,128)(2,1)S(1)} %get-tuple-element.33), channel_id=1, source_target_pairs={{0,4},{1,5},{2,6},{3,7},{4,0},{5,1},{6,2},{7,3},{8,12},{9,13},{10,... | collective-permute-start | bytes 589832 | tf_op jit(solution)/shard_map/ppermute | solution.py:233
  227.2 7.8 %collective-permute-start.14 = (bf16[4,192,128]{2,1,0:T(8,128)(2,1)S(1)}, bf16[4,192,128]{2,1,0:T(8,128)(2,1)S(1)}, u32[]{:S(2)}, u32[]{:S(2)}) collective-permute-start(bf16[4,192,128]{2,1,0:T(8,128)(2,1)S(1)} %get-tuple-element.34), channel_id=1, source_target_pairs={{0,6},{1,7},{2,0},{3,1},{4,2},{5,3},{6,4},{7,5},{8,14},{9,15},{10,... | collective-permute-start | bytes 589832 | tf_op jit(solution)/shard_map/ppermute | solution.py:233
  235.2 8.5 %collective-permute-start.15 = (f32[192,128]{1,0:T(8,128)S(1)}, f32[192,128]{1,0:T(8,128)S(1)}, u32[]{:S(2)}, u32[]{:S(2)}) collective-permute-start(f32[192,128]{1,0:T(8,128)S(1)} %get-tuple-element.36), channel_id=1, source_target_pairs={{0,8},{1,9},{2,10},{3,11},{4,12},{5,13},{6,14},{7,15},{8,16},{9,17... | collective-permute-start | bytes 294920 | tf_op jit(solution)/shard_map/ppermute | solution.py:235
  (15 other events, 112.9 us)
Sparse Core Ops, SparseCore 0:
  26.6 73.0 all-gather.4
  101.7 74.7 all-gather.6

commit v6 on v5

--- a/solution.py
+++ b/solution.py
@@ -11,7 +11,6 @@
 BF = jnp.bfloat16
 F32 = jnp.float32
 NX, NY, NC = 4, 4, 2
-PAD = 64
 PARAMS = pltpu.CompilerParams(vmem_limit_bytes=48 * 1024 * 1024)
 
 
@@ -31,26 +30,21 @@
     return pl.ds(pl.multiple_of(start, step), size)
 
 
-def tokens_kernel(meta, place, own_ref, oth_ref, grad_ref, w_ref, out_ref, *refs, blk):
-    (in_own, in_oth), (act, out_acc, in_acc, in_rows) = refs[:NC], refs[NC:]
+def tokens_kernel(meta, place, act_ref, grad_ref, w_ref, out_ref, *refs, blk):
+    (in_own, in_oth), (out_acc, in_acc, in_rows) = refs[:NC], refs[NC:]
     step = pl.program_id(0)
-    piece = own_ref.shape[2]
+    piece = in_own.shape[2]
     x, y, core = place[0], place[1], place[2]
 
     @pl.when(step == 0)
     def _():
         out_acc[...] = jnp.zeros_like(out_acc)
         in_acc[...] = jnp.zeros_like(in_acc)
-        for t in range(NX):
-            for s in range(NY):
-                chip = (lax.rem(x - t + NX, NX) * NY + lax.rem(y - s + NY, NY)) * NC
-                act[aligned((chip + core) * piece, piece, 64), :] = own_ref[t, s]
-                act[aligned((chip + 1 - core) * piece, piece, 64), :] = oth_ref[t, s]
 
     hid = aligned(meta[1, step] * blk, blk, blk)
     mod = aligned(meta[2, step] * blk, blk, blk)
     w = w_ref[:, 0].reshape(blk, blk)
-    out_acc[hid, :] += jnp.dot(w, act[mod, :], preferred_element_type=F32)
+    out_acc[hid, :] += jnp.dot(w, act_ref[mod, :], preferred_element_type=F32)
     in_acc[:, mod] += jnp.dot(grad_ref[:, hid], w, preferred_element_type=F32)
 
     @pl.when(step == pl.num_programs(0) - 1)
@@ -64,12 +58,11 @@
                 in_oth[s, t] = in_rows[aligned((chip + 1 - core) * piece, piece, 64), :]
 
 
-def tokens_step(meta, place, act_own, act_oth, grad, w_all):
+def tokens_step(meta, place, act, grad, w_all):
     parts, _, rows, blk = w_all.shape
-    piece, toks = act_own.shape[2:]
-    feats = NX * NY * NC * piece
+    feats, toks = act.shape
+    piece = feats // (NX * NY * NC)
     hidden = grad.shape[1]
-    lines = pl.BlockSpec((NX, NY, piece, toks), lambda k, m, p: (0, 0, 0, 0))
     whole = lambda k, m, p: (0, 0)
     return pl.pallas_call(
         functools.partial(tokens_kernel, blk=blk),
@@ -77,15 +70,13 @@
             num_scalar_prefetch=2,
             grid=(meta.shape[1],),
             in_specs=[
-                lines,
-                lines,
+                pl.BlockSpec((feats, toks), whole),
                 pl.BlockSpec((toks, hidden), whole),
                 pl.BlockSpec((parts, 1, rows, blk), lambda k, m, p: (0, k, 0, 0)),
             ],
             out_specs=[pl.BlockSpec((toks, hidden), whole)]
             + [pl.BlockSpec((NY, NX, piece, toks), lambda k, m, p: (0, 0, 0, 0))] * NC,
             scratch_shapes=[
-                pltpu.VMEM((feats, toks), BF),
                 pltpu.VMEM((hidden, toks), F32),
                 pltpu.VMEM((toks, feats), F32),
                 pltpu.VMEM((feats, toks), BF),
@@ -95,42 +86,70 @@
         + [jax.ShapeDtypeStruct((NY, NX, piece, toks), BF)] * NC,
         compiler_params=PARAMS,
         name="tokens_step",
-    )(meta, place, act_own, act_oth, grad, w_all)
-
-
-def keep_kernel(meta, parts_ref, out_ref):
-    for k in range(out_ref.shape[0]):
-        out_ref[k] = parts_ref[meta[0, k]]
-
-
-def keep_filled(meta, parts):
-    return pl.pallas_call(
-        keep_kernel,
+    )(meta, place, act, grad, w_all)
+
+
+def pack_kernel(grad_ref, w_ref, out_ref):
+    owners, rows, toks = out_ref.shape
+    blk = w_ref.shape[0]
+    chunk = blk // owners
+    hid_blocks = grad_ref.shape[1] // blk
+    for f in range(hid_blocks):
+        grad_t = grad_ref[:, f * blk : (f + 1) * blk].T
+        for z in range(owners):
+            out_ref[z, f * chunk : (f + 1) * chunk] = grad_t[z * chunk : (z + 1) * chunk]
+    for q in range(blk // toks):
+        at = (hid_blocks + q) * chunk
+        for z in range(owners):
+            out_ref[z, at : at + chunk] = w_ref[z * chunk : (z + 1) * chunk, q * toks : (q + 1) * toks]
+
+
+def pack_rows(grad, w, owners):
+    toks, hidden = grad.shape
+    blk = w.shape[0]
+    rows = (hidden + blk * blk // toks) // owners
+    return small_call(pack_kernel, "pack_rows", [jax.ShapeDtypeStruct((owners, rows, toks), BF)], grad, w)[0]
+
+
+def unpack_kernel(meta, parts_ref, grad_ref, w_ref):
+    _, rows, toks = grad_ref.shape
+    grad_ref[...] = parts_ref[:, :rows]
+    kept, chunk, blk = w_ref.shape
+    for k in range(kept):
+        for q in range(blk // toks):
+            at = rows + q * chunk
+            w_ref[k, :, q * toks : (q + 1) * toks] = parts_ref[meta[0, k], at : at + chunk]
+
+
+def unpack_rows(meta, parts, rows, chunk, blk):
+    owners, _, toks = parts.shape
+    return pl.pallas_call(
+        unpack_kernel,
         in_specs=[
             pl.BlockSpec(memory_space=pltpu.SMEM),
             pl.BlockSpec(memory_space=pltpu.VMEM),
         ],
-        out_specs=pl.BlockSpec(memory_space=pltpu.VMEM),
-        out_shape=jax.ShapeDtypeStruct((meta.shape[1], *parts.shape[1:]), BF),
-        compiler_params=PARAMS,
-        name="keep_filled",
+        out_specs=[pl.BlockSpec(memory_space=pltpu.VMEM)] * 2,
+        out_shape=[
+            jax.ShapeDtypeStruct((owners, rows, toks), BF),
+            jax.ShapeDtypeStruct((meta.shape[1], chunk, blk), BF),
+        ],
+        compiler_params=PARAMS,
+        name="unpack_rows",
     )(meta, parts)
 
 
-def wgrad_kernel(place, own_ref, oth_ref, here, before, far_lo, far_hi, after, out_ref, a_buf, b_buf, *, scale):
+def wgrad_kernel(place, own_ref, oth_ref, act_ref, out_ref, a_buf, b_buf, *, scale):
     _, n_z, rows, toks = own_ref.shape
-    piece = b_buf.shape[0] // NY
-    x, y, core = place[0], place[1], place[2]
+    n_y, _, piece, _ = act_ref.shape
+    x, core = place[0], place[2]
     step = pl.program_id(0)
-    half = n_z // 2
 
     @pl.when(step == 0)
     def _():
-        for s, parts in enumerate(((here,), (before,), (far_lo, far_hi), (after,))):
-            at = aligned(lax.rem(y - s + NY, NY) * piece, piece, 64)
+        for y in range(n_y):
             for z in range(n_z):
-                src = parts[0][z] if len(parts) == 1 else parts[z // half][z % half]
-                b_buf[at, z * toks : (z + 1) * toks] = src[:piece]
+                b_buf[y * piece : (y + 1) * piece, z * toks : (z + 1) * toks] = act_ref[y, z]
 
     for z in range(n_z):
         a_buf[:rows, z * toks : (z + 1) * toks] = own_ref[0, z]
@@ -144,15 +163,16 @@
     out_ref[line + 1 - core] = prod[rows:]
 
 
-def wgrad_products(place, grad_own, grad_oth, act_y, piece, scale):
+def wgrad_products(place, grad_own, grad_oth, act_y, scale):
     n_x, n_z, rows, toks = grad_own.shape
+    piece = act_y.shape[2]
     line = pl.BlockSpec((1, n_z, rows, toks), lambda s, p: (s, 0, 0, 0))
     return pl.pallas_call(
         functools.partial(wgrad_kernel, scale=scale),
         grid_spec=pltpu.PrefetchScalarGridSpec(
             num_scalar_prefetch=1,
             grid=(n_x,),
-            in_specs=[line, line] + [pl.BlockSpec(a.shape, lambda s, p: (0, 0, 0)) for a in act_y],
+            in_specs=[line, line, pl.BlockSpec(act_y.shape, lambda s, p: (0, 0, 0, 0))],
             out_specs=pl.BlockSpec((n_x * NC, rows, NY * piece), lambda s, p: (0, 0, 0)),
             scratch_shapes=[
                 pltpu.VMEM((NC * rows, n_z * toks), BF),
@@ -162,7 +182,7 @@
         out_shape=jax.ShapeDtypeStruct((n_x * NC, rows, NY * piece), BF),
         compiler_params=PARAMS,
         name="wgrad_products",
-    )(place, grad_own, grad_oth, *act_y)
+    )(place, grad_own, grad_oth, act_y)
 
 
 def slots_kernel(meta, prod_ref, out_ref, line_buf, *, chunk, blk):
@@ -265,48 +285,40 @@
 
 
 def share_y(x):
-    half = x.shape[0] // 2
-    before = lax.ppermute(x, "col", Y_SHIFTS[1])
-    after = lax.ppermute(x, "col", Y_SHIFTS[NY - 1])
-    far_lo = lax.ppermute(before[:half], "col", Y_SHIFTS[1])
-    far_hi = lax.ppermute(after[half:], "col", Y_SHIFTS[NY - 1])
-    return x, before, far_lo, far_hi, after
+    wide = jnp.broadcast_to(x[None], (NY, *x.shape))
+    return lax.all_to_all(wide, "col", 0, 0, tiled=True, axis_index_groups=Y_GROUPS)
 
 
 def per_device(activations, out_grad, weight_slots, block_mask, block_owner):
     blk = weight_slots.shape[2]
     owners, groups = lax.axis_size("row"), lax.axis_size("col")
-    group, at_z = lax.axis_index("col"), lax.axis_index("row")
+    group = lax.axis_index("col")
     toks, piece = activations.shape
     hidden = out_grad.shape[1]
-    hid_blocks = hidden // blk
     chunk = blk // owners
+    rows = hidden // owners
     listed, slots = layout_tables(block_mask, block_owner, group, groups, owners)
     place = jnp.stack([group // (NY * NC), group // NC % NY, group % NC]).astype(jnp.int32)
 
-    w_parts = lax.all_to_all(weight_slots[0, 0].reshape(owners, chunk, blk), "row", 0, 0, tiled=True)
     act_t = activations.T
-    act_z = lax.all_gather(jnp.pad(act_t, ((0, PAD), (0, 0))), "row", axis=0)
-    line_y = [act_t] + [lax.ppermute(act_t, "col", Y_SHIFTS[s]) for s in range(1, NY)]
-    act_own = line_x(jnp.stack(line_y))
-    grad_send = out_grad.T.reshape(hid_blocks, owners, chunk, toks).transpose(1, 0, 2, 3)
-    grad_send = grad_send.reshape(owners, hid_blocks * chunk, toks)
-    grad_send, w_parts, act_own = lax.optimization_barrier((grad_send, w_parts, act_own))
-    w_all = lax.all_gather(keep_filled(listed, w_parts), "row", axis=0)
-    grad_z = lax.all_to_all(grad_send, "row", 0, 0, tiled=True)
-    act_oth = lax.ppermute(act_own, "col", CORE_SWAP)
-    act_y = share_y(act_z[:, :piece])
-    grad_z, act_y, act_oth = lax.optimization_barrier((grad_z, act_y, act_oth))
-
+    act_all = lax.all_gather(act_t, "col", axis=0).reshape(groups * piece, toks)
+    parts = pack_rows(out_grad, weight_slots[0, 0], owners)
+    parts = lax.all_to_all(parts, "row", 0, 0, tiled=True)
+    act_z = lax.all_gather(act_t, "row", axis=0)
+    parts, act_z = lax.optimization_barrier((parts, act_z))
+    grad_z, w_parts = unpack_rows(listed, parts, rows, chunk, blk)
+    w_all = lax.all_gather(w_parts, "row", axis=0)
+
+    act_y = share_y(act_z).reshape(NY, owners, piece, toks)
     grad_own = line_x(grad_z)
     grad_oth = lax.ppermute(grad_own, "col", CORE_SWAP)
     scale = 1.0 / math.sqrt(toks * owners)
-    prods = wgrad_products(place, grad_own, grad_oth, act_y, piece, scale)
+    prods = wgrad_products(place, grad_own, grad_oth, act_y, scale)
     prods = lax.all_to_all(prods, "col", 0, 0, tiled=True, axis_index_groups=XC_GROUPS)
     slot_parts = pick_slots(slots, prods, chunk, blk)
     weight_grad = lax.all_to_all(slot_parts, "row", 0, 0, tiled=True).reshape(1, 1, blk, blk)
 
-    outputs, in_own, in_oth = tokens_step(listed, place, act_own, act_oth, out_grad, w_all)
+    outputs, in_own, in_oth = tokens_step(listed, place, act_all, out_grad, w_all)
     return outputs, sum_groups(in_own, in_oth).T, weight_grad
 
 

time: 259 us -> 236 us (0.911)
  blocking collectives: 0 us -> 63.7 us
  starting transfers between devices: 127 us -> 81.8 us
  waiting for transfers between devices: 77.8 us -> 41.1 us
  local copies, waits for them, and re-layouts: 12.4 us -> 8.28 us
    all_gather x0 -> x1, blocking collectives: none -> 63.7 us  [per_device(): act_z = lax.all_gather(act_t, 'row', axis=0)]
    ppermute x8 -> x0, starting transfers between devices: 33.5 us -> none  [the longest x3 10.7 us: per_device(): lax.ppermute(act_t, 'col', Y_SHIFTS[s])]
    all_gather x2, waiting for transfers between devices: 32 us -> 0.04 us  [the longest x1 0.02 us: per_device(): act_all = lax.all_gather(act_t, 'col', axis=0).reshape(groups * piece, toks)]
    ppermute x6 -> x3, starting transfers between devices: 20.5 us -> 10.5 us  [line_x(): lax.ppermute(x, 'col', X_SHIFTS[t])]
    all_to_all x2, starting transfers between devices: 27.8 us -> 20.4 us  [the longest x1 15.7 us: per_device(): parts = lax.all_to_all(parts, 'row', 0, 0, tiled=True)]
    all_to_all x1, starting transfers between devices: 4.29 us -> 11.5 us  [per_device(): lax.all_to_all(prods, 'col', 0, 0, tiled=True, axis_index_groups=XC_GROUPS)]
    ppermute x8 -> x0, waiting for transfers between devices: 4.85 us -> none  [the longest x1 3.09 us: share_y(): far_lo = lax.ppermute(before[:half], 'col', Y_SHIFTS[1])]
    ppermute x6 -> x3, waiting for transfers between devices: 11.1 us -> 7.64 us  [line_x(): lax.ppermute(x, 'col', X_SHIFTS[t])]
  transfers between devices with their start and end apart: 28 -> 17, of which waited for: 16 -> 11; matrix products, arithmetic and copies ran while one was open for 3% -> 2% of each run, Pallas kernels for 8% -> 9%
where the time goes in v6:
time: 236 us; the launch traced here: 234 us
  starting transfers between devices  81.8 us (35%)
  blocking collectives  63.7 us (27%)
  waiting for transfers between devices  41.1 us (17%)
  Pallas kernels  23.9 us (10%)
  between operations  14.3 us (6%)
  local copies, waits for them, and re-layouts  8.28 us (4%)
    all_gather x1, blocking collectives, per_device(): act_z = lax.all_gather(act_t, 'row', axis=0)  63.7 us
    all_to_all x1, waiting for transfers between devices, per_device(): lax.all_to_all(prods, 'col', 0, 0, tiled=True, axis_index_groups=XC_GROUPS)  16.3 us
    all_to_all x1, starting transfers between devices, per_device(): parts = lax.all_to_all(parts, 'row', 0, 0, tiled=True)  15.7 us
    all_to_all x1, starting transfers between devices, per_device(): lax.all_to_all(prods, 'col', 0, 0, tiled=True, axis_index_groups=XC_GROUPS)  11.5 us
    ppermute x3, starting transfers between devices, line_x(): lax.ppermute(x, 'col', X_SHIFTS[t])  10.5 us
    all_to_all x1, starting transfers between devices, per_device(): lax.all_to_all(slot_parts, 'row', 0, 0, tiled=True).reshape(1, 1, blk, blk)  10 us
    pallas_call x1, Pallas kernels, tokens_step(): pl.pallas_call(functools.partial(tokens_kernel, blk=blk), grid_spec=pltpu...  9.51 us
    pallas_call x1, Pallas kernels, wgrad_products(): pl.pallas_call(functools.partial(wgrad_kernel, scale=scale), grid_spec=pl...  9.31 us
  transfers between devices with their start and end apart: 17, of which 11 were waited for; matrix products, arithmetic and copies ran while one was open for 2% of the time, Pallas kernels for 9%

profile of v6, /device:TPU:1, one launch (start us, length us, event | category | flops | bytes accessed | tf_op | source)
XLA Modules:
  0.0 233.8 jit_solution(11635755258686705902)
XLA Ops:
  10.4 15.7 %all-to-all-start = ((bf16[16,224,128]{2,1,0:T(8,128)(2,1)}), bf16[16,224,128]{2,1,0:T(8,128)(2,1)S(1)}, u32[]{:S(2)}, u32[]{:S(2)}) async-start(bf16[16,224,128]{2,1,0:T(8,128)(2,1)} %pack_rows.1), calls=%async_computation | async-start | bytes 1835008 | tf_op jit(solution)/shard_map/all_to_all | solution.py:306
  27.6 63.7 %all-gather.1 = bf16[3072,128]{1,0:T(8,128)(2,1)S(1)} all-gather(bf16[192,128]{1,0:T(8,128)(2,1)S(1)} %bitcast.41), channel_id=3, replica_groups=mesh['row'=16,'col'=32] {'row'}, dimensions={0}, use_global_device_ids=true | all-gather | bytes 835584 | tf_op jit(solution)/shard_map/all_gather | solution.py:307
  92.7 2.5 %broadcast_in_dim.50 = bf16[4,16,192,128]{3,2,1,0:T(8,128)(2,1)} broadcast(bf16[16,192,128]{2,1,0:T(8,128)(2,1)S(1)} %bitcast.36), dimensions={1,2,3} | broadcast | bytes 3932160 | tf_op jit(solution)/shard_map/broadcast_in_dim | solution.py:288
  95.2 4.7 %all-to-all-start.1 = ((bf16[4,16,192,128]{3,2,1,0:T(8,128)(2,1)}), bf16[4,16,192,128]{3,2,1,0:T(8,128)(2,1)}, u32[]{:S(2)}, u32[]{:S(2)}) async-start(bf16[4,16,192,128]{3,2,1,0:T(8,128)(2,1)} %broadcast_in_dim.50), calls=%async_computation.1 | async-start | bytes 6291456 | tf_op jit(solution)/shard_map/all_to_all | solution.py:289
  99.9 3.1 %collective-permute-start.7 = (bf16[16,96,128]{2,1,0:T(8,128)(2,1)S(1)}, bf16[16,96,128]{2,1,0:T(8,128)(2,1)S(1)}, u32[]{:S(2)}, u32[]{:S(2)}) collective-permute-start(bf16[16,96,128]{2,1,0:T(8,128)(2,1)S(1)} %get-tuple-element.31), channel_id=1, source_target_pairs={{0,8},{1,9},{2,10},{3,11},{4,12},{5,13},{6,14},{7,15},{8,16},{9,17... | collective-permute-start | bytes 1179656 | tf_op jit(solution)/shard_map/ppermute | solution.py:284
  103.0 4.4 %collective-permute-start.8 = (bf16[16,96,128]{2,1,0:T(8,128)(2,1)S(1)}, bf16[16,96,128]{2,1,0:T(8,128)(2,1)S(1)}, u32[]{:S(2)}, u32[]{:S(2)}) collective-permute-start(bf16[16,96,128]{2,1,0:T(8,128)(2,1)S(1)} %get-tuple-element.31), channel_id=1, source_target_pairs={{0,16},{1,17},{2,18},{3,19},{4,20},{5,21},{6,22},{7,23},{8,24},{9,... | collective-permute-start | bytes 1179656 | tf_op jit(solution)/shard_map/ppermute | solution.py:284
  107.4 3.1 %collective-permute-start.9 = (bf16[16,96,128]{2,1,0:T(8,128)(2,1)S(1)}, bf16[16,96,128]{2,1,0:T(8,128)(2,1)S(1)}, u32[]{:S(2)}, u32[]{:S(2)}) collective-permute-start(bf16[16,96,128]{2,1,0:T(8,128)(2,1)S(1)} %get-tuple-element.31), channel_id=1, source_target_pairs={{0,24},{1,25},{2,26},{3,27},{4,28},{5,29},{6,30},{7,31},{8,0},{9,1... | collective-permute-start | bytes 1179656 | tf_op jit(solution)/shard_map/ppermute | solution.py:284
  110.5 6.0 %collective-permute-done.8 = bf16[16,96,128]{2,1,0:T(8,128)(2,1)S(1)} collective-permute-done((bf16[16,96,128]{2,1,0:T(8,128)(2,1)S(1)}, bf16[16,96,128]{2,1,0:T(8,128)(2,1)S(1)}, u32[]{:S(2)}, u32[]{:S(2)}) %collective-permute-start.8) | collective-permute-done | bytes 393248 | tf_op jit(solution)/shard_map/ppermute | solution.py:284
  118.3 9.3 %collective-permute-start.10 = (bf16[4,16,96,128]{3,2,1,0:T(8,128)(2,1)S(1)}, bf16[4,16,96,128]{3,2,1,0:T(8,128)(2,1)S(1)}, u32[]{:S(2)}, u32[]{:S(2)}) collective-permute-start(bf16[4,16,96,128]{3,2,1,0:T(8,128)(2,1)S(1)} %pad_maximum_fusion.own_ref), channel_id=1, source_target_pairs={{0,1},{1,0},{2,3},{3,2},{4,5},{5,4},{6,7},{7,6},{8,9},{9,8},{10,11... | collective-permute-start | bytes 4718600 | tf_op jit(solution)/shard_map/ppermute | solution.py:314
  127.7 2.9 %collective-permute-done.10.oth_ref = bf16[4,16,96,128]{3,2,1,0:T(8,128)(2,1)S(1)} collective-permute-done((bf16[4,16,96,128]{3,2,1,0:T(8,128)(2,1)S(1)}, bf16[4,16,96,128]{3,2,1,0:T(8,128)(2,1)S(1)}, u32[]{:S(2)}, u32[]{:S(2)}) %collective-permute-start.10) | collective-permute-done | bytes 1572896 | tf_op jit(solution)/shard_map/ppermute | solution.py:314
  131.3 9.3 %wgrad_products.1 = bf16[8,96,768]{2,1,0:T(8,128)(2,1)} custom-call(s32[3]{0:T(128)S(1)} %pad_add_fusion.2.place, bf16[4,16,96,128]{3,2,1,0:T(8,128)(2,1)S(1)} %pad_maximum_fusion.own_ref, bf16[4,16,96,128]{3,2,1,0:T(8,128)(2,1)S(1)} %collective-permute-done.10.oth_ref, bf16[4,16,192,128]{3,2,1,0:T(8,128)(2,1)} %all-to-all-done.1.act_ref), custom_call_target="tpu_custom_call" | custom-call | tf_op jit(solution)/shard_map/wgrad_products/pallas_call | solution.py:170
  140.6 11.5 %all-to-all-start.2 = ((bf16[8,96,768]{2,1,0:T(8,128)(2,1)}), bf16[8,96,768]{2,1,0:T(8,128)(2,1)S(1)}, u32[]{:S(2)}, u32[]{:S(2)}) async-start(bf16[8,96,768]{2,1,0:T(8,128)(2,1)} %wgrad_products.1), calls=%async_computation.2 | async-start | bytes 2359296 | tf_op jit(solution)/shard_map/all_to_all | solution.py:317
  152.3 16.3 %all-to-all-done.2.prod_ref = bf16[8,96,768]{2,1,0:T(8,128)(2,1)S(1)} async-done(((bf16[8,96,768]{2,1,0:T(8,128)(2,1)}), bf16[8,96,768]{2,1,0:T(8,128)(2,1)S(1)}, u32[]{:S(2)}, u32[]{:S(2)}) %all-to-all-start.2) | async-done | bytes 1179680 | tf_op jit(solution)/shard_map/all_to_all | solution.py:317
  170.3 10.0 %all-to-all-start.3 = ((bf16[16,32,512]{2,1,0:T(8,128)(2,1)}), bf16[16,32,512]{2,1,0:T(8,128)(2,1)}, u32[]{:S(2)}, u32[]{:S(2)}) async-start(bf16[16,32,512]{2,1,0:T(8,128)(2,1)} %pick_slots.1), calls=%async_computation.3 | async-start | bytes 1048576 | tf_op jit(solution)/shard_map/all_to_all | solution.py:319
  181.8 9.5 %tokens_step.1 = (bf16[128,1536]{1,0:T(8,128)(2,1)}, bf16[4,4,192,128]{3,2,1,0:T(8,128)(2,1)S(1)}, bf16[4,4,192,128]{3,2,1,0:T(8,128)(2,1)S(1)}) custom-call(s32[3,9]{1,0:T(4,128)S(1)} %pad_add_fusion.meta, s32[3]{0:T(128)S(1)} %pad_add_fusion.2.place, bf16[6144,128]{1,0:T(8,128)(2,1)S(1)} %copy-done.2, bf16[128,1536]{1,0:T(8,128)(2,1)S(1)} %copy-done.1, ...), custom_call_target="tpu_custom_call" | custom-call | tf_op jit(solution)/shard_map/tokens_step/pallas_call | solution.py:67
  191.3 3.0 %collective-permute-start = (bf16[4,4,192,128]{3,2,1,0:T(8,128)(2,1)S(1)}, bf16[4,4,192,128]{3,2,1,0:T(8,128)(2,1)S(1)}, u32[]{:S(2)}, u32[]{:S(2)}) collective-permute-start(bf16[4,4,192,128]{3,2,1,0:T(8,128)(2,1)S(1)} %get-tuple-element.22), channel_id=1, source_target_pairs={{0,1},{1,0},{2,3},{3,2},{4,5},{5,4},{6,7},{7,6},{8,9},{9,8},{10,11... | collective-permute-start | bytes 2359304 | tf_op jit(solution)/shard_map/ppermute | solution.py:250
  196.5 2.3 collective-permute-start.1
  198.7 3.7 %collective-permute-start.2 = (bf16[4,192,128]{2,1,0:T(8,128)(2,1)S(1)}, bf16[4,192,128]{2,1,0:T(8,128)(2,1)S(1)}, u32[]{:S(2)}, u32[]{:S(2)}) collective-permute-start(bf16[4,192,128]{2,1,0:T(8,128)(2,1)S(1)} %get-tuple-element.25), channel_id=1, source_target_pairs={{0,4},{1,5},{2,6},{3,7},{4,0},{5,1},{6,2},{7,3},{8,12},{9,13},{10,... | collective-permute-start | bytes 589832 | tf_op jit(solution)/shard_map/ppermute | solution.py:253
  202.4 2.6 %collective-permute-start.3 = (bf16[4,192,128]{2,1,0:T(8,128)(2,1)S(1)}, bf16[4,192,128]{2,1,0:T(8,128)(2,1)S(1)}, u32[]{:S(2)}, u32[]{:S(2)}) collective-permute-start(bf16[4,192,128]{2,1,0:T(8,128)(2,1)S(1)} %get-tuple-element.26), channel_id=1, source_target_pairs={{0,6},{1,7},{2,0},{3,1},{4,2},{5,3},{6,4},{7,5},{8,14},{9,15},{10,... | collective-permute-start | bytes 589832 | tf_op jit(solution)/shard_map/ppermute | solution.py:253
  206.4 3.1 %collective-permute-done.2.refs_2_ = bf16[4,192,128]{2,1,0:T(8,128)(2,1)S(1)} collective-permute-done((bf16[4,192,128]{2,1,0:T(8,128)(2,1)S(1)}, bf16[4,192,128]{2,1,0:T(8,128)(2,1)S(1)}, u32[]{:S(2)}, u32[]{:S(2)}) %collective-permute-start.2) | collective-permute-done | bytes 196640 | tf_op jit(solution)/shard_map/ppermute | solution.py:253
  209.5 2.6 %collective-permute-done.3.refs_3_ = bf16[4,192,128]{2,1,0:T(8,128)(2,1)S(1)} collective-permute-done((bf16[4,192,128]{2,1,0:T(8,128)(2,1)S(1)}, bf16[4,192,128]{2,1,0:T(8,128)(2,1)S(1)}, u32[]{:S(2)}, u32[]{:S(2)}) %collective-permute-start.3) | collective-permute-done | bytes 196640 | tf_op jit(solution)/shard_map/ppermute | solution.py:253
  214.4 3.7 %collective-permute-start.5 = (f32[192,128]{1,0:T(8,128)S(1)}, f32[192,128]{1,0:T(8,128)S(1)}, u32[]{:S(2)}, u32[]{:S(2)}) collective-permute-start(f32[192,128]{1,0:T(8,128)S(1)} %get-tuple-element.29), channel_id=1, source_target_pairs={{0,16},{1,17},{2,18},{3,19},{4,20},{5,21},{6,22},{7,23},{8,24},{9,... | collective-permute-start | bytes 294920 | tf_op jit(solution)/shard_map/ppermute | solution.py:255
  218.1 2.5 %collective-permute-start.6 = (f32[192,128]{1,0:T(8,128)S(1)}, f32[192,128]{1,0:T(8,128)S(1)}, u32[]{:S(2)}, u32[]{:S(2)}) collective-permute-start(f32[192,128]{1,0:T(8,128)S(1)} %get-tuple-element.30), channel_id=1, source_target_pairs={{0,24},{1,25},{2,26},{3,27},{4,28},{5,29},{6,30},{7,31},{8,0},{9,1... | collective-permute-start | bytes 294920 | tf_op jit(solution)/shard_map/ppermute | solution.py:255
  221.3 3.1 %collective-permute-done.6.refs_3_ = f32[192,128]{1,0:T(8,128)S(1)} collective-permute-done((f32[192,128]{1,0:T(8,128)S(1)}, f32[192,128]{1,0:T(8,128)S(1)}, u32[]{:S(2)}, u32[]{:S(2)}) %collective-permute-start.6) | collective-permute-done | bytes 98336 | tf_op jit(solution)/shard_map/ppermute | solution.py:255
  (52 shorter events, 20.9 us)
Async XLA Ops:
  7.2 1.0 copy-start
  8.2 1.0 copy-start.3
  9.2 17.7 %copy-start.5 = (s32[96,12]{0,1:T(8,128)S(1)}, s32[96,12]{0,1:T(8,128)}, u32[]{:S(2)}) copy-start(s32[96,12]{0,1:T(8,128)} %param.9) | copy-start | bytes 13828
  9.2 17.7 %copy-start.6 = (s32[96,12]{0,1:T(8,128)S(1)}, s32[96,12]{0,1:T(8,128)}, u32[]{:S(2)}) copy-start(s32[96,12]{0,1:T(8,128)} %param.8) | copy-start | bytes 13828
  9.2 18.4 %copy-start.4 = (bf16[128,192]{0,1:T(8,128)(2,1)S(1)}, bf16[128,192]{0,1:T(8,128)(2,1)}, u32[]{:S(2)}) copy-start(bf16[128,192]{0,1:T(8,128)(2,1)} %param.5) | copy-start | bytes 147460
  10.4 81.0 %all-to-all-start = ((bf16[16,224,128]{2,1,0:T(8,128)(2,1)}), bf16[16,224,128]{2,1,0:T(8,128)(2,1)S(1)}, u32[]{:S(2)}, u32[]{:S(2)}) async-start(bf16[16,224,128]{2,1,0:T(8,128)(2,1)} %pack_rows.1), calls=%async_computation | async-start | bytes 1835008 | tf_op jit(solution)/shard_map/all_to_all | solution.py:306
  26.1 154.3 %all-gather.6.cloned.1.call-start = ((), (), s32[]{:S(2)}) async-start(), calls=%async_computation.4 | async-start | bytes 1622016 | tf_op jit(solution)/shard_map/all_gather | solution.py:304
  26.8 153.6 %all-gather.8.cloned.1.call-start = ((), (), s32[]{:S(2)}) async-start(), calls=%async_computation.5 | async-start | bytes 5013504 | tf_op jit(solution)/shard_map/all_gather | solution.py:310
  95.2 36.1 %all-to-all-start.1 = ((bf16[4,16,192,128]{3,2,1,0:T(8,128)(2,1)}), bf16[4,16,192,128]{3,2,1,0:T(8,128)(2,1)}, u32[]{:S(2)}, u32[]{:S(2)}) async-start(bf16[4,16,192,128]{3,2,1,0:T(8,128)(2,1)} %broadcast_in_dim.50), calls=%async_computation.1 | async-start | bytes 6291456 | tf_op jit(solution)/shard_map/all_to_all | solution.py:289
  99.9 10.6 %collective-permute-start.7 = (bf16[16,96,128]{2,1,0:T(8,128)(2,1)S(1)}, bf16[16,96,128]{2,1,0:T(8,128)(2,1)S(1)}, u32[]{:S(2)}, u32[]{:S(2)}) collective-permute-start(bf16[16,96,128]{2,1,0:T(8,128)(2,1)S(1)} %get-tuple-element.31), channel_id=1, source_target_pairs={{0,8},{1,9},{2,10},{3,11},{4,12},{5,13},{6,14},{7,15},{8,16},{9,17... | collective-permute-start | bytes 1179656 | tf_op jit(solution)/shard_map/ppermute | solution.py:284
  103.0 13.4 %collective-permute-start.8 = (bf16[16,96,128]{2,1,0:T(8,128)(2,1)S(1)}, bf16[16,96,128]{2,1,0:T(8,128)(2,1)S(1)}, u32[]{:S(2)}, u32[]{:S(2)}) collective-permute-start(bf16[16,96,128]{2,1,0:T(8,128)(2,1)S(1)} %get-tuple-element.31), channel_id=1, source_target_pairs={{0,16},{1,17},{2,18},{3,19},{4,20},{5,21},{6,22},{7,23},{8,24},{9,... | collective-permute-start | bytes 1179656 | tf_op jit(solution)/shard_map/ppermute | solution.py:284
  107.4 10.7 %collective-permute-start.9 = (bf16[16,96,128]{2,1,0:T(8,128)(2,1)S(1)}, bf16[16,96,128]{2,1,0:T(8,128)(2,1)S(1)}, u32[]{:S(2)}, u32[]{:S(2)}) collective-permute-start(bf16[16,96,128]{2,1,0:T(8,128)(2,1)S(1)} %get-tuple-element.31), channel_id=1, source_target_pairs={{0,24},{1,25},{2,26},{3,27},{4,28},{5,29},{6,30},{7,31},{8,0},{9,1... | collective-permute-start | bytes 1179656 | tf_op jit(solution)/shard_map/ppermute | solution.py:284
  118.3 12.3 %collective-permute-start.10 = (bf16[4,16,96,128]{3,2,1,0:T(8,128)(2,1)S(1)}, bf16[4,16,96,128]{3,2,1,0:T(8,128)(2,1)S(1)}, u32[]{:S(2)}, u32[]{:S(2)}) collective-permute-start(bf16[4,16,96,128]{3,2,1,0:T(8,128)(2,1)S(1)} %pad_maximum_fusion.own_ref), channel_id=1, source_target_pairs={{0,1},{1,0},{2,3},{3,2},{4,5},{5,4},{6,7},{7,6},{8,9},{9,8},{10,11... | collective-permute-start | bytes 4718600 | tf_op jit(solution)/shard_map/ppermute | solution.py:314
  140.6 28.0 %all-to-all-start.2 = ((bf16[8,96,768]{2,1,0:T(8,128)(2,1)}), bf16[8,96,768]{2,1,0:T(8,128)(2,1)S(1)}, u32[]{:S(2)}, u32[]{:S(2)}) async-start(bf16[8,96,768]{2,1,0:T(8,128)(2,1)} %wgrad_products.1), calls=%async_computation.2 | async-start | bytes 2359296 | tf_op jit(solution)/shard_map/all_to_all | solution.py:317
  152.1 28.3 %copy-start.1 = (bf16[128,1536]{1,0:T(8,128)(2,1)S(1)}, bf16[128,1536]{1,0:T(8,128)(2,1)}, u32[]{:S(2)}) copy-start(bf16[128,1536]{1,0:T(8,128)(2,1)} %grad_ref.3) | copy-start | bytes 1179652
  170.3 50.3 %all-to-all-start.3 = ((bf16[16,32,512]{2,1,0:T(8,128)(2,1)}), bf16[16,32,512]{2,1,0:T(8,128)(2,1)}, u32[]{:S(2)}, u32[]{:S(2)}) async-start(bf16[16,32,512]{2,1,0:T(8,128)(2,1)} %pick_slots.1), calls=%async_computation.3 | async-start | bytes 1048576 | tf_op jit(solution)/shard_map/all_to_all | solution.py:319
  180.4 1.4 copy-start.2
  191.3 4.9 %collective-permute-start = (bf16[4,4,192,128]{3,2,1,0:T(8,128)(2,1)S(1)}, bf16[4,4,192,128]{3,2,1,0:T(8,128)(2,1)S(1)}, u32[]{:S(2)}, u32[]{:S(2)}) collective-permute-start(bf16[4,4,192,128]{3,2,1,0:T(8,128)(2,1)S(1)} %get-tuple-element.22), channel_id=1, source_target_pairs={{0,1},{1,0},{2,3},{3,2},{4,5},{5,4},{6,7},{7,6},{8,9},{9,8},{10,11... | collective-permute-start | bytes 2359304 | tf_op jit(solution)/shard_map/ppermute | solution.py:250
  196.5 9.9 %collective-permute-start.1 = (bf16[4,192,128]{2,1,0:T(8,128)(2,1)S(1)}, bf16[4,192,128]{2,1,0:T(8,128)(2,1)S(1)}, u32[]{:S(2)}, u32[]{:S(2)}) collective-permute-start(bf16[4,192,128]{2,1,0:T(8,128)(2,1)S(1)} %get-tuple-element.24), channel_id=1, source_target_pairs={{0,2},{1,3},{2,4},{3,5},{4,6},{5,7},{6,0},{7,1},{8,10},{9,11},{10,... | collective-permute-start | bytes 589832 | tf_op jit(solution)/shard_map/ppermute | solution.py:253
  198.7 10.7 %collective-permute-start.2 = (bf16[4,192,128]{2,1,0:T(8,128)(2,1)S(1)}, bf16[4,192,128]{2,1,0:T(8,128)(2,1)S(1)}, u32[]{:S(2)}, u32[]{:S(2)}) collective-permute-start(bf16[4,192,128]{2,1,0:T(8,128)(2,1)S(1)} %get-tuple-element.25), channel_id=1, source_target_pairs={{0,4},{1,5},{2,6},{3,7},{4,0},{5,1},{6,2},{7,3},{8,12},{9,13},{10,... | collective-permute-start | bytes 589832 | tf_op jit(solution)/shard_map/ppermute | solution.py:253
  202.4 9.7 %collective-permute-start.3 = (bf16[4,192,128]{2,1,0:T(8,128)(2,1)S(1)}, bf16[4,192,128]{2,1,0:T(8,128)(2,1)S(1)}, u32[]{:S(2)}, u32[]{:S(2)}) collective-permute-start(bf16[4,192,128]{2,1,0:T(8,128)(2,1)S(1)} %get-tuple-element.26), channel_id=1, source_target_pairs={{0,6},{1,7},{2,0},{3,1},{4,2},{5,3},{6,4},{7,5},{8,14},{9,15},{10,... | collective-permute-start | bytes 589832 | tf_op jit(solution)/shard_map/ppermute | solution.py:253
  212.2 8.5 %collective-permute-start.4 = (f32[192,128]{1,0:T(8,128)S(1)}, f32[192,128]{1,0:T(8,128)S(1)}, u32[]{:S(2)}, u32[]{:S(2)}) collective-permute-start(f32[192,128]{1,0:T(8,128)S(1)} %get-tuple-element.28), channel_id=1, source_target_pairs={{0,8},{1,9},{2,10},{3,11},{4,12},{5,13},{6,14},{7,15},{8,16},{9,17... | collective-permute-start | bytes 294920 | tf_op jit(solution)/shard_map/ppermute | solution.py:255
  214.4 7.0 %collective-permute-start.5 = (f32[192,128]{1,0:T(8,128)S(1)}, f32[192,128]{1,0:T(8,128)S(1)}, u32[]{:S(2)}, u32[]{:S(2)}) collective-permute-start(f32[192,128]{1,0:T(8,128)S(1)} %get-tuple-element.29), channel_id=1, source_target_pairs={{0,16},{1,17},{2,18},{3,19},{4,20},{5,21},{6,22},{7,23},{8,24},{9,... | collective-permute-start | bytes 294920 | tf_op jit(solution)/shard_map/ppermute | solution.py:255
  218.1 6.4 %collective-permute-start.6 = (f32[192,128]{1,0:T(8,128)S(1)}, f32[192,128]{1,0:T(8,128)S(1)}, u32[]{:S(2)}, u32[]{:S(2)}) collective-permute-start(f32[192,128]{1,0:T(8,128)S(1)} %get-tuple-element.30), channel_id=1, source_target_pairs={{0,24},{1,25},{2,26},{3,27},{4,28},{5,29},{6,30},{7,31},{8,0},{9,1... | collective-permute-start | bytes 294920 | tf_op jit(solution)/shard_map/ppermute | solution.py:255
Sparse Core Ops, SparseCore 0:
  30.1 60.5 all-gather.5
  93.3 76.5 all-gather.7

commit v7 on v5

--- a/solution.py
+++ b/solution.py
@@ -11,7 +11,6 @@
 BF = jnp.bfloat16
 F32 = jnp.float32
 NX, NY, NC = 4, 4, 2
-PAD = 64
 PARAMS = pltpu.CompilerParams(vmem_limit_bytes=48 * 1024 * 1024)
 
 
@@ -21,7 +20,6 @@
 
 PLANE = [(x, y, c) for x in range(NX) for y in range(NY) for c in range(NC)]
 XC_GROUPS = [[col_of(x, y, c) for x in range(NX) for c in range(NC)] for y in range(NY)]
-Y_GROUPS = [[col_of(x, y, c) for y in range(NY)] for x in range(NX) for c in range(NC)]
 CORE_SWAP = [(col_of(x, y, c), col_of(x, y, 1 - c)) for x, y, c in PLANE]
 X_SHIFTS = {s: [(col_of(x, y, c), col_of((x + s) % NX, y, c)) for x, y, c in PLANE] for s in range(1, NX)}
 Y_SHIFTS = {s: [(col_of(x, y, c), col_of(x, (y + s) % NY, c)) for x, y, c in PLANE] for s in range(1, NY)}
@@ -31,26 +29,21 @@
     return pl.ds(pl.multiple_of(start, step), size)
 
 
-def tokens_kernel(meta, place, own_ref, oth_ref, grad_ref, w_ref, out_ref, *refs, blk):
-    (in_own, in_oth), (act, out_acc, in_acc, in_rows) = refs[:NC], refs[NC:]
+def tokens_kernel(meta, place, act_ref, grad_ref, w_ref, out_ref, *refs, blk):
+    (in_own, in_oth), (out_acc, in_acc, in_rows) = refs[:NC], refs[NC:]
     step = pl.program_id(0)
-    piece = own_ref.shape[2]
+    piece = in_own.shape[2]
     x, y, core = place[0], place[1], place[2]
 
     @pl.when(step == 0)
     def _():
         out_acc[...] = jnp.zeros_like(out_acc)
         in_acc[...] = jnp.zeros_like(in_acc)
-        for t in range(NX):
-            for s in range(NY):
-                chip = (lax.rem(x - t + NX, NX) * NY + lax.rem(y - s + NY, NY)) * NC
-                act[aligned((chip + core) * piece, piece, 64), :] = own_ref[t, s]
-                act[aligned((chip + 1 - core) * piece, piece, 64), :] = oth_ref[t, s]
 
     hid = aligned(meta[1, step] * blk, blk, blk)
     mod = aligned(meta[2, step] * blk, blk, blk)
-    w = w_ref[:, 0].reshape(blk, blk)
-    out_acc[hid, :] += jnp.dot(w, act[mod, :], preferred_element_type=F32)
+    w = w_ref[0]
+    out_acc[hid, :] += jnp.dot(w, act_ref[mod, :], preferred_element_type=F32)
     in_acc[:, mod] += jnp.dot(grad_ref[:, hid], w, preferred_element_type=F32)
 
     @pl.when(step == pl.num_programs(0) - 1)
@@ -64,12 +57,11 @@
                 in_oth[s, t] = in_rows[aligned((chip + 1 - core) * piece, piece, 64), :]
 
 
-def tokens_step(meta, place, act_own, act_oth, grad, w_all):
-    parts, _, rows, blk = w_all.shape
-    piece, toks = act_own.shape[2:]
-    feats = NX * NY * NC * piece
+def tokens_step(meta, place, act, grad, w_all):
+    blk = w_all.shape[1]
+    feats, toks = act.shape
+    piece = feats // (NX * NY * NC)
     hidden = grad.shape[1]
-    lines = pl.BlockSpec((NX, NY, piece, toks), lambda k, m, p: (0, 0, 0, 0))
     whole = lambda k, m, p: (0, 0)
     return pl.pallas_call(
         functools.partial(tokens_kernel, blk=blk),
@@ -77,15 +69,13 @@
             num_scalar_prefetch=2,
             grid=(meta.shape[1],),
             in_specs=[
-                lines,
-                lines,
+                pl.BlockSpec((feats, toks), whole),
                 pl.BlockSpec((toks, hidden), whole),
-                pl.BlockSpec((parts, 1, rows, blk), lambda k, m, p: (0, k, 0, 0)),
+                pl.BlockSpec((1, blk, blk), lambda k, m, p: (m[0, k], 0, 0)),
             ],
             out_specs=[pl.BlockSpec((toks, hidden), whole)]
             + [pl.BlockSpec((NY, NX, piece, toks), lambda k, m, p: (0, 0, 0, 0))] * NC,
             scratch_shapes=[
-                pltpu.VMEM((feats, toks), BF),
                 pltpu.VMEM((hidden, toks), F32),
                 pltpu.VMEM((toks, feats), F32),
                 pltpu.VMEM((feats, toks), BF),
@@ -95,26 +85,7 @@
         + [jax.ShapeDtypeStruct((NY, NX, piece, toks), BF)] * NC,
         compiler_params=PARAMS,
         name="tokens_step",
-    )(meta, place, act_own, act_oth, grad, w_all)
-
-
-def keep_kernel(meta, parts_ref, out_ref):
-    for k in range(out_ref.shape[0]):
-        out_ref[k] = parts_ref[meta[0, k]]
-
-
-def keep_filled(meta, parts):
-    return pl.pallas_call(
-        keep_kernel,
-        in_specs=[
-            pl.BlockSpec(memory_space=pltpu.SMEM),
-            pl.BlockSpec(memory_space=pltpu.VMEM),
-        ],
-        out_specs=pl.BlockSpec(memory_space=pltpu.VMEM),
-        out_shape=jax.ShapeDtypeStruct((meta.shape[1], *parts.shape[1:]), BF),
-        compiler_params=PARAMS,
-        name="keep_filled",
-    )(meta, parts)
+    )(meta, place, act, grad, w_all)
 
 
 def wgrad_kernel(place, own_ref, oth_ref, here, before, far_lo, far_hi, after, out_ref, a_buf, b_buf, *, scale):
@@ -130,7 +101,7 @@
             at = aligned(lax.rem(y - s + NY, NY) * piece, piece, 64)
             for z in range(n_z):
                 src = parts[0][z] if len(parts) == 1 else parts[z // half][z % half]
-                b_buf[at, z * toks : (z + 1) * toks] = src[:piece]
+                b_buf[at, z * toks : (z + 1) * toks] = src
 
     for z in range(n_z):
         a_buf[:rows, z * toks : (z + 1) * toks] = own_ref[0, z]
@@ -225,11 +196,14 @@
     )(*args)
 
 
-def sum_groups(in_own, in_oth):
-    _, _, piece, toks = in_own.shape
+def sum_pair(in_own, in_oth):
+    line = lambda dtype: jax.ShapeDtypeStruct(in_own.shape[1:], dtype)
     got = lax.ppermute(in_oth, "col", CORE_SWAP)
-    line = lambda dtype: jax.ShapeDtypeStruct((NX, piece, toks), dtype)
-    by_y = small_call(sum_core_kernel, "sum_core", [line(F32)] + [line(BF)] * (NY - 1), in_own, got)
+    return small_call(sum_core_kernel, "sum_core", [line(F32)] + [line(BF)] * (NY - 1), in_own, got)
+
+
+def sum_plane(by_y):
+    _, piece, toks = by_y[0].shape
     got = [by_y[0]] + [lax.ppermute(by_y[s], "col", Y_SHIFTS[s]) for s in range(1, NY)]
     by_x = small_call(sum_y_kernel, "sum_y", [jax.ShapeDtypeStruct((piece, toks), F32)] * NX, *got)
     got = [by_x[0]] + [lax.ppermute(by_x[t], "col", X_SHIFTS[t]) for t in range(1, NX)]
@@ -276,27 +250,26 @@
 def per_device(activations, out_grad, weight_slots, block_mask, block_owner):
     blk = weight_slots.shape[2]
     owners, groups = lax.axis_size("row"), lax.axis_size("col")
-    group, at_z = lax.axis_index("col"), lax.axis_index("row")
+    group = lax.axis_index("col")
     toks, piece = activations.shape
     hidden = out_grad.shape[1]
-    hid_blocks = hidden // blk
     chunk = blk // owners
+    rows = hidden // owners
     listed, slots = layout_tables(block_mask, block_owner, group, groups, owners)
     place = jnp.stack([group // (NY * NC), group // NC % NY, group % NC]).astype(jnp.int32)
 
-    w_parts = lax.all_to_all(weight_slots[0, 0].reshape(owners, chunk, blk), "row", 0, 0, tiled=True)
+    w_all = lax.all_gather(weight_slots[0, 0], "row", axis=0)
     act_t = activations.T
-    act_z = lax.all_gather(jnp.pad(act_t, ((0, PAD), (0, 0))), "row", axis=0)
-    line_y = [act_t] + [lax.ppermute(act_t, "col", Y_SHIFTS[s]) for s in range(1, NY)]
-    act_own = line_x(jnp.stack(line_y))
-    grad_send = out_grad.T.reshape(hid_blocks, owners, chunk, toks).transpose(1, 0, 2, 3)
-    grad_send = grad_send.reshape(owners, hid_blocks * chunk, toks)
-    grad_send, w_parts, act_own = lax.optimization_barrier((grad_send, w_parts, act_own))
-    w_all = lax.all_gather(keep_filled(listed, w_parts), "row", axis=0)
+    wide = jnp.broadcast_to(act_t[None], (groups, piece, toks))
+    act_all = lax.all_to_all(wide, "col", 0, 0, tiled=True).reshape(groups * piece, toks)
+    act_z = lax.all_gather(act_t, "row", axis=0)
+
+    grad_send = out_grad.T.reshape(-1, owners, chunk, toks).transpose(1, 0, 2, 3)
+    grad_send = grad_send.reshape(owners, rows, toks)
+    grad_send, act_z, act_all = lax.optimization_barrier((grad_send, act_z, act_all))
     grad_z = lax.all_to_all(grad_send, "row", 0, 0, tiled=True)
-    act_oth = lax.ppermute(act_own, "col", CORE_SWAP)
-    act_y = share_y(act_z[:, :piece])
-    grad_z, act_y, act_oth = lax.optimization_barrier((grad_z, act_y, act_oth))
+    act_y = share_y(act_z)
+    grad_z, act_y = lax.optimization_barrier((grad_z, act_y))
 
     grad_own = line_x(grad_z)
     grad_oth = lax.ppermute(grad_own, "col", CORE_SWAP)
@@ -304,10 +277,11 @@
     prods = wgrad_products(place, grad_own, grad_oth, act_y, piece, scale)
     prods = lax.all_to_all(prods, "col", 0, 0, tiled=True, axis_index_groups=XC_GROUPS)
     slot_parts = pick_slots(slots, prods, chunk, blk)
+
+    outputs, in_own, in_oth = tokens_step(listed, place, act_all, out_grad, w_all)
+    slot_parts, by_y = lax.optimization_barrier((slot_parts, sum_pair(in_own, in_oth)))
     weight_grad = lax.all_to_all(slot_parts, "row", 0, 0, tiled=True).reshape(1, 1, blk, blk)
-
-    outputs, in_own, in_oth = tokens_step(listed, place, act_own, act_oth, out_grad, w_all)
-    return outputs, sum_groups(in_own, in_oth).T, weight_grad
+    return outputs, sum_plane(by_y).T, weight_grad
 
 
 def solution(mesh):

time: 259 us -> 219 us (0.85)
  waiting for transfers between devices: 77.8 us -> 34 us
  blocking collectives: 0 us -> 39.4 us
  starting transfers between devices: 127 us -> 88.6 us
  local copies, waits for them, and re-layouts: 12.4 us -> 16.5 us
    all_gather x0 -> x1, blocking collectives: none -> 39.4 us  [per_device(): act_z = lax.all_gather(act_t, 'row', axis=0)]
    all_gather x2 -> x1, waiting for transfers between devices: 32 us -> 0.02 us  [per_device(): w_all = lax.all_gather(weight_slots[0, 0], 'row', axis=0)]
    ppermute x11 -> x7, starting transfers between devices: 42.9 us -> 20.1 us  [the longest x3 9.62 us: sum_plane(): lax.ppermute(by_y[s], 'col', Y_SHIFTS[s])]
    all_to_all x1, waiting for transfers between devices: 16.3 us -> 3.57 us  [per_device(): lax.all_to_all(prods, 'col', 0, 0, tiled=True, axis_index_groups=XC_GROUPS)]
    ppermute x1, waiting for transfers between devices: 0.01 us -> 10.3 us  [share_y(): before = lax.ppermute(x, 'col', Y_SHIFTS[1])]
    ppermute x6 -> x3, starting transfers between devices: 20.5 us -> 10.5 us  [line_x(): lax.ppermute(x, 'col', X_SHIFTS[t])]
    all_to_all x1, starting transfers between devices: 15.9 us -> 10.6 us  [per_device(): lax.all_to_all(wide, 'col', 0, 0, tiled=True).reshape(groups * piece, toks)]
    all_to_all x1, starting transfers between devices: 11.9 us -> 7.06 us  [per_device(): grad_z = lax.all_to_all(grad_send, 'row', 0, 0, tiled=True)]
  transfers between devices with their start and end apart: 28 -> 20, of which waited for: 16 -> 10; matrix products, arithmetic and copies ran while one was open for 3% -> 4% of each run, Pallas kernels for 8% -> 9%
where the time goes in v7:
time: 219 us; the launch traced here: 215 us
  starting transfers between devices  88.6 us (40%)
  blocking collectives  39.4 us (18%)
  waiting for transfers between devices  34 us (16%)
  Pallas kernels  19.6 us (9%)
  local copies, waits for them, and re-layouts  16.5 us (8%)
  between operations  14.4 us (7%)
  other arithmetic  2.83 us (1%)
    all_gather x1, blocking collectives, per_device(): act_z = lax.all_gather(act_t, 'row', axis=0)  39.4 us
    all_to_all x1, starting transfers between devices, per_device(): lax.all_to_all(slot_parts, 'row', 0, 0, tiled=True).reshape(1, 1, blk, blk)  11.7 us
    ppermute x1, starting transfers between devices, per_device(): grad_oth = lax.ppermute(grad_own, 'col', CORE_SWAP)  11.2 us
    unnamed x36, local copies, waits for them, and re-layouts  11 us
    all_to_all x1, starting transfers between devices, per_device(): lax.all_to_all(wide, 'col', 0, 0, tiled=True).reshape(groups * piece, toks)  10.6 us
    ppermute x3, starting transfers between devices, line_x(): lax.ppermute(x, 'col', X_SHIFTS[t])  10.5 us
    ppermute x1, waiting for transfers between devices, share_y(): before = lax.ppermute(x, 'col', Y_SHIFTS[1])  10.3 us
    pallas_call x1, Pallas kernels, tokens_step(): pl.pallas_call(functools.partial(tokens_kernel, blk=blk), grid_spec=pltpu...  9.77 us
  transfers between devices with their start and end apart: 20, of which 10 were waited for; matrix products, arithmetic and copies ran while one was open for 4% of the time, Pallas kernels for 9%

profile of v7, /device:TPU:1, one launch (start us, length us, event | category | flops | bytes accessed | tf_op | source)
XLA Modules:
  0.0 215.4 jit_solution(9433880987325193001)
XLA Ops:
  7.9 2.3 %broadcast_in_dim.48 = bf16[32,192,128]{2,1,0:T(8,128)(2,1)} broadcast(bf16[192,128]{1,0:T(8,128)(2,1)} %bitcast.49), dimensions={1,2} | broadcast | bytes 1622016 | tf_op jit(solution)/shard_map/broadcast_in_dim | solution.py:263
  10.2 10.6 %all-to-all-start = ((bf16[32,192,128]{2,1,0:T(8,128)(2,1)}), bf16[32,192,128]{2,1,0:T(8,128)(2,1)S(1)}, u32[]{:S(2)}, u32[]{:S(2)}) async-start(bf16[32,192,128]{2,1,0:T(8,128)(2,1)} %broadcast_in_dim.48), calls=%async_computation | async-start | bytes 3145728 | tf_op jit(solution)/shard_map/all_to_all | solution.py:264
  21.9 39.4 %all-gather = bf16[3072,128]{1,0:T(8,128)(2,1)S(1)} all-gather(bf16[192,128]{1,0:T(8,128)(2,1)S(1)} %bitcast.50), channel_id=2, replica_groups=mesh['row'=16,'col'=32] {'row'}, dimensions={0}, use_global_device_ids=true | all-gather | bytes 835584 | tf_op jit(solution)/shard_map/all_gather | solution.py:265
  61.3 7.1 %all-to-all-start.1 = ((bf16[16,96,128]{2,1,0:T(8,128)(2,1)}), bf16[16,96,128]{2,1,0:T(8,128)(2,1)}, u32[]{:S(2)}, u32[]{:S(2)}) async-start(bf16[16,96,128]{2,1,0:T(8,128)(2,1)} %bitcast.10), calls=%async_computation.1 | async-start | bytes 786432 | tf_op jit(solution)/shard_map/all_to_all | solution.py:270
  68.4 3.3 %collective-permute-start = (bf16[16,192,128]{2,1,0:T(8,128)(2,1)S(1)}, bf16[16,192,128]{2,1,0:T(8,128)(2,1)S(1)}, u32[]{:S(2)}, u32[]{:S(2)}) collective-permute-start(bf16[16,192,128]{2,1,0:T(8,128)(2,1)S(1)} %bitcast.40), channel_id=1, source_target_pairs={{0,2},{1,3},{2,4},{3,5},{4,6},{5,7},{6,0},{7,1},{8,10},{9,11},{10,... | collective-permute-start | bytes 2359304 | tf_op jit(solution)/shard_map/ppermute | solution.py:243
  71.7 3.2 %collective-permute-start.2 = (bf16[16,192,128]{2,1,0:T(8,128)(2,1)S(1)}, bf16[16,192,128]{2,1,0:T(8,128)(2,1)S(1)}, u32[]{:S(2)}, u32[]{:S(2)}) collective-permute-start(bf16[16,192,128]{2,1,0:T(8,128)(2,1)S(1)} %bitcast.41), channel_id=1, source_target_pairs={{0,6},{1,7},{2,0},{3,1},{4,2},{5,3},{6,4},{7,5},{8,14},{9,15},{10,... | collective-permute-start | bytes 2359304 | tf_op jit(solution)/shard_map/ppermute | solution.py:244
  74.9 10.3 %collective-permute-done.before = bf16[16,192,128]{2,1,0:T(8,128)(2,1)S(1)} collective-permute-done((bf16[16,192,128]{2,1,0:T(8,128)(2,1)S(1)}, bf16[16,192,128]{2,1,0:T(8,128)(2,1)S(1)}, u32[]{:S(2)}, u32[]{:S(2)}) %collective-permute-start) | collective-permute-done | bytes 786464 | tf_op jit(solution)/shard_map/ppermute | solution.py:243
  88.1 4.5 %collective-permute-start.3 = (bf16[8,192,128]{2,1,0:T(8,128)(2,1)S(1)}, bf16[8,192,128]{2,1,0:T(8,128)(2,1)S(1)}, u32[]{:S(2)}, u32[]{:S(2)}) collective-permute-start(bf16[8,192,128]{2,1,0:T(8,128)(2,1)S(1)} %slice.9), channel_id=1, source_target_pairs={{0,6},{1,7},{2,0},{3,1},{4,2},{5,3},{6,4},{7,5},{8,14},{9,15},{10,... | collective-permute-start | bytes 1179656 | tf_op jit(solution)/shard_map/ppermute | solution.py:246
  92.7 2.7 %collective-permute-done.1.far_lo = bf16[8,192,128]{2,1,0:T(8,128)(2,1)S(1)} collective-permute-done((bf16[8,192,128]{2,1,0:T(8,128)(2,1)S(1)}, bf16[8,192,128]{2,1,0:T(8,128)(2,1)S(1)}, u32[]{:S(2)}, u32[]{:S(2)}) %collective-permute-start.1) | collective-permute-done | bytes 393248 | tf_op jit(solution)/shard_map/ppermute | solution.py:245
  98.2 3.1 %collective-permute-start.4 = (bf16[16,96,128]{2,1,0:T(8,128)(2,1)}, bf16[16,96,128]{2,1,0:T(8,128)(2,1)S(1)}, u32[]{:S(2)}, u32[]{:S(2)}) collective-permute-start(bf16[16,96,128]{2,1,0:T(8,128)(2,1)} %all-to-all-done.1), channel_id=1, source_target_pairs={{0,8},{1,9},{2,10},{3,11},{4,12},{5,13},{6,14},{7,15},{8,16},{9,17... | collective-permute-start | bytes 1179656 | tf_op jit(solution)/shard_map/ppermute | solution.py:238
  101.3 4.3 %collective-permute-start.5 = (bf16[16,96,128]{2,1,0:T(8,128)(2,1)}, bf16[16,96,128]{2,1,0:T(8,128)(2,1)S(1)}, u32[]{:S(2)}, u32[]{:S(2)}) collective-permute-start(bf16[16,96,128]{2,1,0:T(8,128)(2,1)} %all-to-all-done.1), channel_id=1, source_target_pairs={{0,16},{1,17},{2,18},{3,19},{4,20},{5,21},{6,22},{7,23},{8,24},{9,... | collective-permute-start | bytes 1179656 | tf_op jit(solution)/shard_map/ppermute | solution.py:238
  105.6 3.1 %collective-permute-start.6 = (bf16[16,96,128]{2,1,0:T(8,128)(2,1)}, bf16[16,96,128]{2,1,0:T(8,128)(2,1)S(1)}, u32[]{:S(2)}, u32[]{:S(2)}) collective-permute-start(bf16[16,96,128]{2,1,0:T(8,128)(2,1)} %all-to-all-done.1), channel_id=1, source_target_pairs={{0,24},{1,25},{2,26},{3,27},{4,28},{5,29},{6,30},{7,31},{8,0},{9,1... | collective-permute-start | bytes 1179656 | tf_op jit(solution)/shard_map/ppermute | solution.py:238
  108.7 4.8 %collective-permute-done.5 = bf16[16,96,128]{2,1,0:T(8,128)(2,1)S(1)} collective-permute-done((bf16[16,96,128]{2,1,0:T(8,128)(2,1)}, bf16[16,96,128]{2,1,0:T(8,128)(2,1)S(1)}, u32[]{:S(2)}, u32[]{:S(2)}) %collective-permute-start.5) | collective-permute-done | bytes 393248 | tf_op jit(solution)/shard_map/ppermute | solution.py:238
  116.5 11.2 %collective-permute-start.7 = (bf16[4,16,96,128]{3,2,1,0:T(8,128)(2,1)S(1)}, bf16[4,16,96,128]{3,2,1,0:T(8,128)(2,1)}, u32[]{:S(2)}, u32[]{:S(2)}) collective-permute-start(bf16[4,16,96,128]{3,2,1,0:T(8,128)(2,1)S(1)} %pad_maximum_fusion.own_ref), channel_id=1, source_target_pairs={{0,1},{1,0},{2,3},{3,2},{4,5},{5,4},{6,7},{7,6},{8,9},{9,8},{10,11... | collective-permute-start | bytes 4718600 | tf_op jit(solution)/shard_map/ppermute | solution.py:275
  137.2 7.2 %wgrad_products.1 = bf16[8,96,768]{2,1,0:T(8,128)(2,1)S(1)} custom-call(s32[3]{0:T(128)S(1)} %pad_add_fusion.2.place, bf16[4,16,96,128]{3,2,1,0:T(8,128)(2,1)S(1)} %pad_maximum_fusion.own_ref, bf16[4,16,96,128]{3,2,1,0:T(8,128)(2,1)} %collective-permute-done.7.oth_ref, bf16[16,192,128]{2,1,0:T(8,128)(2,1)S(1)} %bitcast.42, ...), custom_call_target="tpu_custom_call" | custom-call | tf_op jit(solution)/shard_map/wgrad_products/pallas_call | solution.py:121
  145.5 4.5 %all-to-all-start.2 = ((bf16[8,96,768]{2,1,0:T(8,128)(2,1)}), bf16[8,96,768]{2,1,0:T(8,128)(2,1)S(1)}, u32[]{:S(2)}, u32[]{:S(2)}) async-start(bf16[8,96,768]{2,1,0:T(8,128)(2,1)} %copy-done), calls=%async_computation.2 | async-start | bytes 2359296 | tf_op jit(solution)/shard_map/all_to_all | solution.py:278
  150.1 9.8 %tokens_step.1 = (bf16[128,1536]{1,0:T(8,128)(2,1)}, bf16[4,4,192,128]{3,2,1,0:T(8,128)(2,1)S(1)}, bf16[4,4,192,128]{3,2,1,0:T(8,128)(2,1)}) custom-call(s32[3,9]{1,0:T(4,128)S(1)} %pad_add_fusion.meta, s32[3]{0:T(128)S(1)} %pad_add_fusion.2.place, bf16[6144,128]{1,0:T(8,128)(2,1)S(1)} %bitcast.39, bf16[128,1536]{1,0:T(8,128)(2,1)S(1)} %copy-done.7, ...), custom_call_target="tpu_custom_call" | custom-call | tf_op jit(solution)/shard_map/tokens_step/pallas_call | solution.py:66
  162.9 3.6 %all-to-all-done.2.prod_ref = bf16[8,96,768]{2,1,0:T(8,128)(2,1)S(1)} async-done(((bf16[8,96,768]{2,1,0:T(8,128)(2,1)}), bf16[8,96,768]{2,1,0:T(8,128)(2,1)S(1)}, u32[]{:S(2)}, u32[]{:S(2)}) %all-to-all-start.2) | async-done | bytes 1179680 | tf_op jit(solution)/shard_map/all_to_all | solution.py:278
  168.4 11.7 %all-to-all-start.3 = ((bf16[16,32,512]{2,1,0:T(8,128)(2,1)}), bf16[16,32,512]{2,1,0:T(8,128)(2,1)S(1)}, u32[]{:S(2)}, u32[]{:S(2)}) async-start(bf16[16,32,512]{2,1,0:T(8,128)(2,1)} %pick_slots.1), calls=%async_computation.3 | async-start | bytes 1048576 | tf_op jit(solution)/shard_map/all_to_all | solution.py:283
  180.1 4.3 %collective-permute-start.10 = (bf16[4,192,128]{2,1,0:T(8,128)(2,1)S(1)}, bf16[4,192,128]{2,1,0:T(8,128)(2,1)S(1)}, u32[]{:S(2)}, u32[]{:S(2)}) collective-permute-start(bf16[4,192,128]{2,1,0:T(8,128)(2,1)S(1)} %get-tuple-element.46), channel_id=1, source_target_pairs={{0,4},{1,5},{2,6},{3,7},{4,0},{5,1},{6,2},{7,3},{8,12},{9,13},{10,... | collective-permute-start | bytes 589832 | tf_op jit(solution)/shard_map/ppermute | solution.py:207
  184.5 3.1 %collective-permute-start.11 = (bf16[4,192,128]{2,1,0:T(8,128)(2,1)S(1)}, bf16[4,192,128]{2,1,0:T(8,128)(2,1)S(1)}, u32[]{:S(2)}, u32[]{:S(2)}) collective-permute-start(bf16[4,192,128]{2,1,0:T(8,128)(2,1)S(1)} %get-tuple-element.47), channel_id=1, source_target_pairs={{0,6},{1,7},{2,0},{3,1},{4,2},{5,3},{6,4},{7,5},{8,14},{9,15},{10,... | collective-permute-start | bytes 589832 | tf_op jit(solution)/shard_map/ppermute | solution.py:207
  189.8 3.5 %collective-permute-done.11.refs_3_ = bf16[4,192,128]{2,1,0:T(8,128)(2,1)S(1)} collective-permute-done((bf16[4,192,128]{2,1,0:T(8,128)(2,1)S(1)}, bf16[4,192,128]{2,1,0:T(8,128)(2,1)S(1)}, u32[]{:S(2)}, u32[]{:S(2)}) %collective-permute-start.11) | collective-permute-done | bytes 196640 | tf_op jit(solution)/shard_map/ppermute | solution.py:207
  197.7 3.7 %collective-permute-start.13 = (f32[192,128]{1,0:T(8,128)S(1)}, f32[192,128]{1,0:T(8,128)S(1)}, u32[]{:S(2)}, u32[]{:S(2)}) collective-permute-start(f32[192,128]{1,0:T(8,128)S(1)} %get-tuple-element.50), channel_id=1, source_target_pairs={{0,16},{1,17},{2,18},{3,19},{4,20},{5,21},{6,22},{7,23},{8,24},{9,... | collective-permute-start | bytes 294920 | tf_op jit(solution)/shard_map/ppermute | solution.py:209
  201.4 2.5 %collective-permute-start.14 = (f32[192,128]{1,0:T(8,128)S(1)}, f32[192,128]{1,0:T(8,128)S(1)}, u32[]{:S(2)}, u32[]{:S(2)}) collective-permute-start(f32[192,128]{1,0:T(8,128)S(1)} %get-tuple-element.51), channel_id=1, source_target_pairs={{0,24},{1,25},{2,26},{3,27},{4,28},{5,29},{6,30},{7,31},{8,0},{9,1... | collective-permute-start | bytes 294920 | tf_op jit(solution)/shard_map/ppermute | solution.py:209
  (79 shorter events, 37.2 us)
Async XLA Ops:
  7.2 142.9 %all-gather.4.cloned.1.call-start = ((), (), s32[]{:S(2)}) async-start(), calls=%async_computation.4 | async-start | bytes 8912896 | tf_op jit(solution)/shard_map/all_gather | solution.py:261
  10.2 10.6 %copy-start.7 = (bf16[128,1536]{1,0:T(8,128)(2,1)S(1)}, bf16[128,1536]{1,0:T(8,128)(2,1)}, u32[]{:S(2)}) copy-start(bf16[128,1536]{1,0:T(8,128)(2,1)} %grad_ref.1) | copy-start | bytes 1179652
  10.2 51.1 %all-to-all-start = ((bf16[32,192,128]{2,1,0:T(8,128)(2,1)}), bf16[32,192,128]{2,1,0:T(8,128)(2,1)S(1)}, u32[]{:S(2)}, u32[]{:S(2)}) async-start(bf16[32,192,128]{2,1,0:T(8,128)(2,1)} %broadcast_in_dim.48), calls=%async_computation | async-start | bytes 3145728 | tf_op jit(solution)/shard_map/all_to_all | solution.py:264
  61.3 53.9 %copy-start.1 = (bf16[3072,128]{1,0:T(8,128)(2,1)}, bf16[3072,128]{1,0:T(8,128)(2,1)S(1)}, u32[]{:S(2)}) copy-start(bf16[3072,128]{1,0:T(8,128)(2,1)S(1)} %all-gather) | copy-start | bytes 2359300
  61.3 36.9 %all-to-all-start.1 = ((bf16[16,96,128]{2,1,0:T(8,128)(2,1)}), bf16[16,96,128]{2,1,0:T(8,128)(2,1)}, u32[]{:S(2)}, u32[]{:S(2)}) async-start(bf16[16,96,128]{2,1,0:T(8,128)(2,1)} %bitcast.10), calls=%async_computation.1 | async-start | bytes 786432 | tf_op jit(solution)/shard_map/all_to_all | solution.py:270
  68.4 16.8 %collective-permute-start = (bf16[16,192,128]{2,1,0:T(8,128)(2,1)S(1)}, bf16[16,192,128]{2,1,0:T(8,128)(2,1)S(1)}, u32[]{:S(2)}, u32[]{:S(2)}) collective-permute-start(bf16[16,192,128]{2,1,0:T(8,128)(2,1)S(1)} %bitcast.40), channel_id=1, source_target_pairs={{0,2},{1,3},{2,4},{3,5},{4,6},{5,7},{6,0},{7,1},{8,10},{9,11},{10,... | collective-permute-start | bytes 2359304 | tf_op jit(solution)/shard_map/ppermute | solution.py:243
  71.7 15.5 %collective-permute-start.2 = (bf16[16,192,128]{2,1,0:T(8,128)(2,1)S(1)}, bf16[16,192,128]{2,1,0:T(8,128)(2,1)S(1)}, u32[]{:S(2)}, u32[]{:S(2)}) collective-permute-start(bf16[16,192,128]{2,1,0:T(8,128)(2,1)S(1)} %bitcast.41), channel_id=1, source_target_pairs={{0,6},{1,7},{2,0},{3,1},{4,2},{5,3},{6,4},{7,5},{8,14},{9,15},{10,... | collective-permute-start | bytes 2359304 | tf_op jit(solution)/shard_map/ppermute | solution.py:244
  85.2 10.1 %collective-permute-start.1 = (bf16[8,192,128]{2,1,0:T(8,128)(2,1)S(1)}, bf16[8,192,128]{2,1,0:T(8,128)(2,1)S(1)}, u32[]{:S(2)}, u32[]{:S(2)}) collective-permute-start(bf16[8,192,128]{2,1,0:T(8,128)(2,1)S(1)} %slice.8), channel_id=1, source_target_pairs={{0,2},{1,3},{2,4},{3,5},{4,6},{5,7},{6,0},{7,1},{8,10},{9,11},{10,... | collective-permute-start | bytes 1179656 | tf_op jit(solution)/shard_map/ppermute | solution.py:245
  88.1 9.3 %collective-permute-start.3 = (bf16[8,192,128]{2,1,0:T(8,128)(2,1)S(1)}, bf16[8,192,128]{2,1,0:T(8,128)(2,1)S(1)}, u32[]{:S(2)}, u32[]{:S(2)}) collective-permute-start(bf16[8,192,128]{2,1,0:T(8,128)(2,1)S(1)} %slice.9), channel_id=1, source_target_pairs={{0,6},{1,7},{2,0},{3,1},{4,2},{5,3},{6,4},{7,5},{8,14},{9,15},{10,... | collective-permute-start | bytes 1179656 | tf_op jit(solution)/shard_map/ppermute | solution.py:246
  98.2 10.5 %collective-permute-start.4 = (bf16[16,96,128]{2,1,0:T(8,128)(2,1)}, bf16[16,96,128]{2,1,0:T(8,128)(2,1)S(1)}, u32[]{:S(2)}, u32[]{:S(2)}) collective-permute-start(bf16[16,96,128]{2,1,0:T(8,128)(2,1)} %all-to-all-done.1), channel_id=1, source_target_pairs={{0,8},{1,9},{2,10},{3,11},{4,12},{5,13},{6,14},{7,15},{8,16},{9,17... | collective-permute-start | bytes 1179656 | tf_op jit(solution)/shard_map/ppermute | solution.py:238
  101.3 12.2 %collective-permute-start.5 = (bf16[16,96,128]{2,1,0:T(8,128)(2,1)}, bf16[16,96,128]{2,1,0:T(8,128)(2,1)S(1)}, u32[]{:S(2)}, u32[]{:S(2)}) collective-permute-start(bf16[16,96,128]{2,1,0:T(8,128)(2,1)} %all-to-all-done.1), channel_id=1, source_target_pairs={{0,16},{1,17},{2,18},{3,19},{4,20},{5,21},{6,22},{7,23},{8,24},{9,... | collective-permute-start | bytes 1179656 | tf_op jit(solution)/shard_map/ppermute | solution.py:238
  105.6 9.6 %collective-permute-start.6 = (bf16[16,96,128]{2,1,0:T(8,128)(2,1)}, bf16[16,96,128]{2,1,0:T(8,128)(2,1)S(1)}, u32[]{:S(2)}, u32[]{:S(2)}) collective-permute-start(bf16[16,96,128]{2,1,0:T(8,128)(2,1)} %all-to-all-done.1), channel_id=1, source_target_pairs={{0,24},{1,25},{2,26},{3,27},{4,28},{5,29},{6,30},{7,31},{8,0},{9,1... | collective-permute-start | bytes 1179656 | tf_op jit(solution)/shard_map/ppermute | solution.py:238
  116.5 15.3 %collective-permute-start.7 = (bf16[4,16,96,128]{3,2,1,0:T(8,128)(2,1)S(1)}, bf16[4,16,96,128]{3,2,1,0:T(8,128)(2,1)}, u32[]{:S(2)}, u32[]{:S(2)}) collective-permute-start(bf16[4,16,96,128]{3,2,1,0:T(8,128)(2,1)S(1)} %pad_maximum_fusion.own_ref), channel_id=1, source_target_pairs={{0,1},{1,0},{2,3},{3,2},{4,5},{5,4},{6,7},{7,6},{8,9},{9,8},{10,11... | collective-permute-start | bytes 4718600 | tf_op jit(solution)/shard_map/ppermute | solution.py:275
  145.5 4.5 %copy-start.16 = (s32[9]{0:T(128)S(1)}, s32[9]{0:T(128)}, u32[]{:S(2)}) copy-start(s32[9]{0:T(128)} %get-tuple-element.56) | copy-start | bytes 112
  145.5 21.0 %all-to-all-start.2 = ((bf16[8,96,768]{2,1,0:T(8,128)(2,1)}), bf16[8,96,768]{2,1,0:T(8,128)(2,1)S(1)}, u32[]{:S(2)}, u32[]{:S(2)}) async-start(bf16[8,96,768]{2,1,0:T(8,128)(2,1)} %copy-done), calls=%async_computation.2 | async-start | bytes 2359296 | tf_op jit(solution)/shard_map/all_to_all | solution.py:278
  160.7 7.5 %copy-start.9 = (bf16[4,4,192,128]{3,2,1,0:T(8,128)(2,1)S(1)}, bf16[4,4,192,128]{3,2,1,0:T(8,128)(2,1)}, u32[]{:S(2)}) copy-start(bf16[4,4,192,128]{3,2,1,0:T(8,128)(2,1)} %copy-done.8) | copy-start | bytes 2359300
  160.7 7.5 %collective-permute-start.8 = (bf16[4,4,192,128]{3,2,1,0:T(8,128)(2,1)}, bf16[4,4,192,128]{3,2,1,0:T(8,128)(2,1)S(1)}, u32[]{:S(2)}, u32[]{:S(2)}) collective-permute-start(bf16[4,4,192,128]{3,2,1,0:T(8,128)(2,1)} %get-tuple-element.39), channel_id=1, source_target_pairs={{0,1},{1,0},{2,3},{3,2},{4,5},{5,4},{6,7},{7,6},{8,9},{9,8},{10,11... | collective-permute-start | bytes 2359304 | tf_op jit(solution)/shard_map/ppermute | solution.py:201
  168.4 39.3 %all-to-all-start.3 = ((bf16[16,32,512]{2,1,0:T(8,128)(2,1)}), bf16[16,32,512]{2,1,0:T(8,128)(2,1)S(1)}, u32[]{:S(2)}, u32[]{:S(2)}) async-start(bf16[16,32,512]{2,1,0:T(8,128)(2,1)} %pick_slots.1), calls=%async_computation.3 | async-start | bytes 1048576 | tf_op jit(solution)/shard_map/all_to_all | solution.py:283
  180.1 9.6 %collective-permute-start.10 = (bf16[4,192,128]{2,1,0:T(8,128)(2,1)S(1)}, bf16[4,192,128]{2,1,0:T(8,128)(2,1)S(1)}, u32[]{:S(2)}, u32[]{:S(2)}) collective-permute-start(bf16[4,192,128]{2,1,0:T(8,128)(2,1)S(1)} %get-tuple-element.46), channel_id=1, source_target_pairs={{0,4},{1,5},{2,6},{3,7},{4,0},{5,1},{6,2},{7,3},{8,12},{9,13},{10,... | collective-permute-start | bytes 589832 | tf_op jit(solution)/shard_map/ppermute | solution.py:207
  184.5 8.8 %collective-permute-start.11 = (bf16[4,192,128]{2,1,0:T(8,128)(2,1)S(1)}, bf16[4,192,128]{2,1,0:T(8,128)(2,1)S(1)}, u32[]{:S(2)}, u32[]{:S(2)}) collective-permute-start(bf16[4,192,128]{2,1,0:T(8,128)(2,1)S(1)} %get-tuple-element.47), channel_id=1, source_target_pairs={{0,6},{1,7},{2,0},{3,1},{4,2},{5,3},{6,4},{7,5},{8,14},{9,15},{10,... | collective-permute-start | bytes 589832 | tf_op jit(solution)/shard_map/ppermute | solution.py:207
  187.5 7.9 %collective-permute-start.9 = (bf16[4,192,128]{2,1,0:T(8,128)(2,1)S(1)}, bf16[4,192,128]{2,1,0:T(8,128)(2,1)S(1)}, u32[]{:S(2)}, u32[]{:S(2)}) collective-permute-start(bf16[4,192,128]{2,1,0:T(8,128)(2,1)S(1)} %get-tuple-element.45), channel_id=1, source_target_pairs={{0,2},{1,3},{2,4},{3,5},{4,6},{5,7},{6,0},{7,1},{8,10},{9,11},{10,... | collective-permute-start | bytes 589832 | tf_op jit(solution)/shard_map/ppermute | solution.py:207
  195.5 8.4 %collective-permute-start.12 = (f32[192,128]{1,0:T(8,128)S(1)}, f32[192,128]{1,0:T(8,128)S(1)}, u32[]{:S(2)}, u32[]{:S(2)}) collective-permute-start(f32[192,128]{1,0:T(8,128)S(1)} %get-tuple-element.49), channel_id=1, source_target_pairs={{0,8},{1,9},{2,10},{3,11},{4,12},{5,13},{6,14},{7,15},{8,16},{9,17... | collective-permute-start | bytes 294920 | tf_op jit(solution)/shard_map/ppermute | solution.py:209
  197.7 8.1 %collective-permute-start.13 = (f32[192,128]{1,0:T(8,128)S(1)}, f32[192,128]{1,0:T(8,128)S(1)}, u32[]{:S(2)}, u32[]{:S(2)}) collective-permute-start(f32[192,128]{1,0:T(8,128)S(1)} %get-tuple-element.50), channel_id=1, source_target_pairs={{0,16},{1,17},{2,18},{3,19},{4,20},{5,21},{6,22},{7,23},{8,24},{9,... | collective-permute-start | bytes 294920 | tf_op jit(solution)/shard_map/ppermute | solution.py:209
  201.4 5.7 %collective-permute-start.14 = (f32[192,128]{1,0:T(8,128)S(1)}, f32[192,128]{1,0:T(8,128)S(1)}, u32[]{:S(2)}, u32[]{:S(2)}) collective-permute-start(f32[192,128]{1,0:T(8,128)S(1)} %get-tuple-element.51), channel_id=1, source_target_pairs={{0,24},{1,25},{2,26},{3,27},{4,28},{5,29},{6,30},{7,31},{8,0},{9,1... | collective-permute-start | bytes 294920 | tf_op jit(solution)/shard_map/ppermute | solution.py:209
  (13 other events, 13.3 us)
Sparse Core Ops, SparseCore 0:
  10.1 135.0 all-gather.3

commit v8 on v7

v8 whole, which is shorter than its diff:
```python
import functools
import math

import jax
import jax.numpy as jnp
from jax import lax
from jax.experimental import pallas as pl
from jax.experimental.pallas import tpu as pltpu
from jax.sharding import PartitionSpec as P

BF = jnp.bfloat16
F32 = jnp.float32
NX, NY, NC = 4, 4, 2
MIB = 1024 * 1024


def col_of(x, y, c):
    return (x * NY + y) * NC + c


PLANE = [(x, y, c) for x in range(NX) for y in range(NY) for c in range(NC)]
XC_GROUPS = [[col_of(x, y, c) for x in range(NX) for c in range(NC)] for y in range(NY)]
CORE_SWAP = [(col_of(x, y, c), col_of(x, y, 1 - c)) for x, y, c in PLANE]
X_SHIFTS = {s: [(col_of(x, y, c), col_of((x + s) % NX, y, c)) for x, y, c in PLANE] for s in range(1, NX)}
Y_SHIFTS = {s: [(col_of(x, y, c), col_of(x, (y + s) % NY, c)) for x, y, c in PLANE] for s in range(1, NY)}


def aligned(start, size, step):
    return pl.ds(pl.multiple_of(start, step), size)


def tokens_kernel(meta, place, act_ref, grad_ref, w_ref, out_ref, in_own, in_oth, w_buf, out_acc, in_acc, in_rows, sems):
    count, blk, _ = w_buf.shape
    piece = in_own.shape[2]
    x, y, core = place[0], place[1], place[2]
    copies = [pltpu.make_async_copy(w_ref.at[meta[0, k]], w_buf.at[k], sems.at[k]) for k in range(count)]
    for copy in copies:
        copy.start()
    out_acc[...] = jnp.zeros_like(out_acc)
    in_acc[...] = jnp.zeros_like(in_acc)
    for k in range(count):
        hid = aligned(meta[1, k] * blk, blk, blk)
        mod = aligned(meta[2, k] * blk, blk, blk)
        copies[k].wait()
        w = w_buf[k]
        out_acc[hid, :] += jnp.dot(w, act_ref[mod, :], preferred_element_type=F32)
        in_acc[:, mod] += jnp.dot(grad_ref[:, hid], w, preferred_element_type=F32)
    out_ref[...] = out_acc[...].T.astype(BF)
    in_rows[...] = in_acc[...].T.astype(BF)
    for s in range(NY):
        for t in range(NX):
            chip = (lax.rem(x + t, NX) * NY + lax.rem(y + s, NY)) * NC
            in_own[s, t] = in_rows[aligned((chip + core) * piece, piece, 64), :]
            in_oth[s, t] = in_rows[aligned((chip + 1 - core) * piece, piece, 64), :]


def tokens_step(meta, place, act, grad, w_all):
    count, blk = meta.shape[1], w_all.shape[1]
    feats, toks = act.shape
    hidden = grad.shape[1]
    parts = pltpu.HBM((NY, NX, feats // (NX * NY * NC), toks), BF)
    vmem = pl.BlockSpec(memory_space=pltpu.VMEM)
    smem = pl.BlockSpec(memory_space=pltpu.SMEM)
    return pl.pallas_call(
        tokens_kernel,
        in_specs=[smem, smem, vmem, vmem, pl.BlockSpec(memory_space=pltpu.HBM)],
        out_specs=[vmem] * 3,
        out_shape=[jax.ShapeDtypeStruct((toks, hidden), BF), parts, parts],
        scratch_shapes=[
            pltpu.VMEM((count, blk, blk), BF),
            pltpu.VMEM((hidden, toks), F32),
            pltpu.VMEM((toks, feats), F32),
            pltpu.VMEM((feats, toks), BF),
            pltpu.SemaphoreType.DMA((count,)),
        ],
        compiler_params=pltpu.CompilerParams(vmem_limit_bytes=28 * MIB),
        name="tokens_step",
    )(meta, place, act, grad, in_hbm(w_all))


def wgrad_kernel(place, *refs, scale):
    n_in = 7
    in_refs, out_ref, buffers, (a_buf, b_buf, sems) = refs[:n_in], refs[n_in], refs[n_in + 1 : -3], refs[-3:]
    copies = [pltpu.make_async_copy(in_refs[i], buffers[i], sems.at[i]) for i in range(n_in)]
    for copy in copies:
        copy.start()
    here, before, far_lo, far_hi, after, own, oth = buffers
    n_x, n_z, rows, toks = own.shape
    piece = here.shape[1]
    x, y, core = place[0], place[1], place[2]
    for i, (part, s, first) in enumerate(
        ((here, 0, 0), (before, 1, 0), (far_lo, 2, 0), (far_hi, 2, n_z // 2), (after, 3, 0))
    ):
        at = aligned(lax.rem(y - s + NY, NY) * piece, piece, 64)
        copies[i].wait()
        for z in range(part.shape[0]):
            b_buf[at, (first + z) * toks : (first + z + 1) * toks] = part[z]
    for c, part in enumerate((own, oth)):
        copies[n_in - 2 + c].wait()
        for t in range(n_x):
            at = (t * NC + c) * rows
            for z in range(n_z):
                a_buf[at : at + rows, z * toks : (z + 1) * toks] = part[t, z]
    prod = lax.dot_general(
        a_buf[...], b_buf[...], (((1,), (1,)), ((), ())), preferred_element_type=F32
    )
    prod = (prod * scale).astype(BF)
    for t in range(n_x):
        line = lax.rem(x - t + n_x, n_x) * NC
        out_ref[line + core] = prod[2 * t * rows : (2 * t + 1) * rows]
        out_ref[line + 1 - core] = prod[(2 * t + 1) * rows : (2 * t + 2) * rows]


def in_hbm(x):
    return pltpu.with_memory_space_constraint(x, pltpu.HBM)


def wgrad_products(place, grad_own, grad_oth, act_y, scale):
    n_x, n_z, rows, toks = grad_own.shape
    piece = act_y[0].shape[1]
    args = [in_hbm(a) for a in (*act_y, grad_own, grad_oth)]
    return pl.pallas_call(
        functools.partial(wgrad_kernel, scale=scale),
        in_specs=[pl.BlockSpec(memory_space=pltpu.SMEM)]
        + [pl.BlockSpec(memory_space=pltpu.HBM)] * len(args),
        out_specs=pl.BlockSpec(memory_space=pltpu.VMEM),
        out_shape=pltpu.HBM((n_x * NC, rows, NY * piece), BF),
        scratch_shapes=[pltpu.VMEM(a.shape, BF) for a in args]
        + [
            pltpu.VMEM((n_x * NC * rows, n_z * toks), BF),
            pltpu.VMEM((NY * piece, n_z * toks), BF),
            pltpu.SemaphoreType.DMA((len(args),)),
        ],
        compiler_params=pltpu.CompilerParams(vmem_limit_bytes=32 * MIB),
        name="wgrad_products",
    )(place, *args)


def slots_kernel(meta, prod_ref, out_ref, line_buf, *, chunk, blk):
    piece = prod_ref.shape[2] // NY
    for x in range(NX):
        for y in range(NY):
            for c in range(NC):
                at = (y * NC + c) * piece
                line_buf[x, :, at : at + piece] = prod_ref[x * NC + c, :, y * piece : (y + 1) * piece]
    per_x = line_buf.shape[2] // blk
    for s in range(out_ref.shape[0]):
        hid, mod, full = meta[0, s], meta[1, s], meta[2, s]
        rows = aligned(hid * chunk, chunk, chunk)
        cols = aligned(lax.rem(mod, per_x) * blk, blk, blk)
        part = line_buf[lax.div(mod, per_x), rows, cols]
        out_ref[s] = jnp.where(full > 0, part, jnp.zeros_like(part))


def pick_slots(meta, prods, chunk, blk):
    owners = meta.shape[1]
    _, rows, cols = prods.shape
    return pl.pallas_call(
        functools.partial(slots_kernel, chunk=chunk, blk=blk),
        in_specs=[
            pl.BlockSpec(memory_space=pltpu.SMEM),
            pl.BlockSpec(memory_space=pltpu.VMEM),
        ],
        out_specs=pl.BlockSpec(memory_space=pltpu.VMEM),
        out_shape=jax.ShapeDtypeStruct((owners, chunk, blk), BF),
        scratch_shapes=[pltpu.VMEM((NX, rows, NC * cols), BF)],
        compiler_params=pltpu.CompilerParams(vmem_limit_bytes=12 * MIB),
        name="pick_slots",
    )(meta, prods)


def sum_core_kernel(own_ref, oth_ref, *out_refs):
    for s in range(NY):
        out_refs[s][...] = (own_ref[s].astype(F32) + oth_ref[s].astype(F32)).astype(out_refs[s].dtype)


def sum_y_kernel(*refs):
    parts, out_refs = refs[:NY], refs[NY:]
    for t in range(NX):
        out_refs[t][...] = sum(part[t].astype(F32) for part in parts)


def sum_x_kernel(*refs):
    parts, out_ref = refs[:NX], refs[NX]
    out_ref[...] = sum(part[...] for part in parts).astype(BF)


def small_call(kernel, name, outs, *args):
    return pl.pallas_call(
        kernel,
        in_specs=[pl.BlockSpec(memory_space=pltpu.VMEM)] * len(args),
        out_specs=[pl.BlockSpec(memory_space=pltpu.VMEM)] * len(outs),
        out_shape=outs,
        compiler_params=pltpu.CompilerParams(vmem_limit_bytes=12 * MIB),
        name=name,
    )(*args)


def sum_pair(in_own, in_oth):
    line = lambda dtype: jax.ShapeDtypeStruct(in_own.shape[1:], dtype)
    got = lax.ppermute(in_oth, "col", CORE_SWAP)
    return small_call(sum_core_kernel, "sum_core", [line(F32)] + [line(BF)] * (NY - 1), in_own, got)


def sum_plane(by_y):
    _, piece, toks = by_y[0].shape
    got = [by_y[0]] + [lax.ppermute(by_y[s], "col", Y_SHIFTS[s]) for s in range(1, NY)]
    by_x = small_call(sum_y_kernel, "sum_y", [jax.ShapeDtypeStruct((piece, toks), F32)] * NX, *got)
    got = [by_x[0]] + [lax.ppermute(by_x[t], "col", X_SHIFTS[t]) for t in range(1, NX)]
    return small_call(sum_x_kernel, "sum_x", [jax.ShapeDtypeStruct((piece, toks), BF)], *got)[0]


def tables_kernel(at, mask_ref, owner_ref, listed_ref, slots_ref):
    model_blocks = mask_ref.shape[0]
    count, owners = listed_ref.shape[1], slots_ref.shape[1]
    for s in range(owners):
        slots_ref[0, s] = 0
        slots_ref[1, s] = 0
        slots_ref[2, s] = 0

    def look(i, k):
        hid, mod = lax.div(i, model_blocks), lax.rem(i, model_blocks)
        full = mask_ref[mod, at[0] + hid]
        owner = owner_ref[mod, at[0] + hid]

        @pl.when(full == 1)
        def _():
            listed_ref[0, k] = owner
            listed_ref[1, k] = hid
            listed_ref[2, k] = mod
            slots_ref[0, owner] = hid
            slots_ref[1, owner] = mod
            slots_ref[2, owner] = 1

        return k + full

    lax.fori_loop(0, count * 4, look, 0)


def layout_tables(block_mask, block_owner, group, n_groups, owners):
    hidden_blocks, model_blocks = block_mask.shape
    per_group = hidden_blocks // n_groups
    smem = pl.BlockSpec(memory_space=pltpu.SMEM)
    return pl.pallas_call(
        tables_kernel,
        in_specs=[smem] * 3,
        out_specs=[smem] * 2,
        out_shape=[
            jax.ShapeDtypeStruct((3, per_group * model_blocks // 4), jnp.int32),
            jax.ShapeDtypeStruct((3, owners), jnp.int32),
        ],
        name="layout_tables",
    )((group * per_group).reshape(1).astype(jnp.int32), block_mask.T, block_owner.T)


def line_x(x):
    return jnp.stack([x] + [lax.ppermute(x, "col", X_SHIFTS[t]) for t in range(1, NX)])


def share_y(x):
    half = x.shape[0] // 2
    before = lax.ppermute(x, "col", Y_SHIFTS[1])
    after = lax.ppermute(x, "col", Y_SHIFTS[NY - 1])
    far_lo = lax.ppermute(before[:half], "col", Y_SHIFTS[1])
    far_hi = lax.ppermute(after[half:], "col", Y_SHIFTS[NY - 1])
    return x, before, far_lo, far_hi, after


def per_device(activations, out_grad, weight_slots, block_mask, block_owner):
    blk = weight_slots.shape[2]
    owners, groups = lax.axis_size("row"), lax.axis_size("col")
    group = lax.axis_index("col")
    toks, piece = activations.shape
    hidden = out_grad.shape[1]
    chunk = blk // owners
    rows = hidden // owners
    listed, slots = layout_tables(block_mask, block_owner, group, groups, owners)
    place = jnp.stack([group // (NY * NC), group // NC % NY, group % NC]).astype(jnp.int32)

    w_all = lax.all_gather(weight_slots[0, 0], "row", axis=0)
    act_t = activations.T
    wide = jnp.broadcast_to(act_t[None], (groups, piece, toks))
    act_all = lax.all_to_all(wide, "col", 0, 0, tiled=True).reshape(groups * piece, toks)
    act_z = lax.all_gather(act_t, "row", axis=0)

    grad_send = out_grad.T.reshape(-1, owners, chunk, toks).transpose(1, 0, 2, 3)
    grad_send = grad_send.reshape(owners, rows, toks)
    grad_send, act_z, act_all = lax.optimization_barrier((grad_send, act_z, act_all))
    grad_z = lax.all_to_all(grad_send, "row", 0, 0, tiled=True)
    here, before, far_lo, far_hi, after = share_y(act_z)
    grad_z, far_lo, far_hi, listed, slots = lax.optimization_barrier((grad_z, far_lo, far_hi, listed, slots))
    act_y = (here, before, far_lo, far_hi, after)

    grad_own = line_x(grad_z)
    grad_oth = lax.ppermute(grad_own, "col", CORE_SWAP)
    scale = 1.0 / math.sqrt(toks * owners)
    prods = wgrad_products(place, grad_own, grad_oth, act_y, scale)
    prods = lax.all_to_all(prods, "col", 0, 0, tiled=True, axis_index_groups=XC_GROUPS)
    slot_parts = pick_slots(slots, prods, chunk, blk)

    outputs, in_own, in_oth = tokens_step(listed, place, act_all, out_grad, w_all)
    by_y = sum_pair(in_own, in_oth)
    slot_parts, by_y = lax.optimization_barrier((slot_parts, by_y))
    weight_grad = lax.all_to_all(slot_parts, "row", 0, 0, tiled=True).reshape(1, 1, blk, blk)
    return outputs, sum_plane(by_y).T, weight_grad


def solution(mesh):
    placed = (P("row", "col"), P("row", "col"), P("col", "row", None, None), P(), P())
    return jax.shard_map(
        per_device,
        mesh=mesh,
        in_specs=placed,
        out_specs=(P("row", "col"), P("row", "col"), P("col", "row", None, None)),
        check_vma=False,
    )
```

time: 219 us -> 214 us (0.977)
  waiting for transfers between devices: 34 us -> 46.6 us
  local copies, waits for them, and re-layouts: 16.5 us -> 5.2 us
  starting transfers between devices: 88.6 us -> 85.8 us
    ppermute x1, waiting for transfers between devices: 10.3 us -> 0.01 us  [share_y(): before = lax.ppermute(x, 'col', Y_SHIFTS[1])]
    unnamed x36 -> x18, local copies, waits for them, and re-layouts: 11 us -> 1.23 us
    ppermute x1, waiting for transfers between devices: 0.01 us -> 9.33 us  [share_y(): after = lax.ppermute(x, 'col', Y_SHIFTS[NY - 1])]
    all_to_all x1, waiting for transfers between devices: 3.57 us -> 7.41 us  [per_device(): lax.all_to_all(prods, 'col', 0, 0, tiled=True, axis_index_groups=XC_GROUPS)]
    ppermute x1, waiting for transfers between devices: 2.73 us -> 6.08 us  [share_y(): far_lo = lax.ppermute(before[:half], 'col', Y_SHIFTS[1])]
    ppermute x1, waiting for transfers between devices: 0.01 us -> 3.24 us  [per_device(): grad_oth = lax.ppermute(grad_own, 'col', CORE_SWAP)]
    ppermute x3, waiting for transfers between devices: 6.53 us -> 9.76 us  [line_x(): lax.ppermute(x, 'col', X_SHIFTS[t])]
    pallas_call x2 -> x3, Pallas kernels: 17 us -> 16.4 us  [the longest x1 7.21 us: wgrad_products(): pl.pallas_call(functools.partial(wgrad_kernel, scale=scale), in_specs=[pl...]
  transfers between devices with their start and end apart: 20 -> 20, of which waited for: 10 -> 11; matrix products, arithmetic and copies ran while one was open for 4% -> 3% of each run, Pallas kernels for 9% -> 9%
where the time goes in v8:
time: 214 us; the launch traced here: 212 us
  starting transfers between devices  85.8 us (40%)
  waiting for transfers between devices  46.6 us (22%)
  blocking collectives  39.4 us (18%)
  Pallas kernels  19 us (9%)
  between operations  14.3 us (7%)
  local copies, waits for them, and re-layouts  5.2 us (2%)
    all_gather x1, blocking collectives, per_device(): act_z = lax.all_gather(act_t, 'row', axis=0)  39.4 us
    all_to_all x1, starting transfers between devices, per_device(): lax.all_to_all(slot_parts, 'row', 0, 0, tiled=True).reshape(1, 1, blk, blk)  11.6 us
    all_to_all x1, starting transfers between devices, per_device(): lax.all_to_all(wide, 'col', 0, 0, tiled=True).reshape(groups * piece, toks)  10.6 us
    ppermute x1, starting transfers between devices, per_device(): grad_oth = lax.ppermute(grad_own, 'col', CORE_SWAP)  10.6 us
    ppermute x3, waiting for transfers between devices, line_x(): lax.ppermute(x, 'col', X_SHIFTS[t])  9.76 us
    ppermute x1, waiting for transfers between devices, share_y(): after = lax.ppermute(x, 'col', Y_SHIFTS[NY - 1])  9.33 us
    ppermute x3, starting transfers between devices, line_x(): lax.ppermute(x, 'col', X_SHIFTS[t])  9.29 us
    ppermute x3, starting transfers between devices, sum_plane(): lax.ppermute(by_x[t], 'col', X_SHIFTS[t])  8.43 us
  transfers between devices with their start and end apart: 20, of which 11 were waited for; matrix products, arithmetic and copies ran while one was open for 3% of the time, Pallas kernels for 9%

profile of v8, /device:TPU:1, one launch (start us, length us, event | category | flops | bytes accessed | tf_op | source)
XLA Modules:
  0.0 211.8 jit_solution(16966171372714556927)
XLA Ops:
  10.2 10.6 %all-to-all-start = ((bf16[32,192,128]{2,1,0:T(8,128)(2,1)}), bf16[32,192,128]{2,1,0:T(8,128)(2,1)S(1)}, u32[]{:S(2)}, u32[]{:S(2)}) async-start(bf16[32,192,128]{2,1,0:T(8,128)(2,1)} %broadcast_in_dim.2), calls=%async_computation | async-start | bytes 3145728 | tf_op jit(solution)/shard_map/all_to_all | solution.py:283
  21.9 39.4 %all-gather = bf16[3072,128]{1,0:T(8,128)(2,1)S(1)} all-gather(bf16[192,128]{1,0:T(8,128)(2,1)S(1)} %bitcast.34), channel_id=2, replica_groups=mesh['row'=16,'col'=32] {'row'}, dimensions={0}, use_global_device_ids=true | all-gather | bytes 835584 | tf_op jit(solution)/shard_map/all_gather | solution.py:284
  61.3 7.0 %all-to-all-start.1 = ((bf16[16,96,128]{2,1,0:T(8,128)(2,1)}), bf16[16,96,128]{2,1,0:T(8,128)(2,1)S(1)}, u32[]{:S(2)}, u32[]{:S(2)}) async-start(bf16[16,96,128]{2,1,0:T(8,128)(2,1)} %bitcast.3), calls=%async_computation.1 | async-start | bytes 786432 | tf_op jit(solution)/shard_map/all_to_all | solution.py:289
  68.4 4.5 %collective-permute-start.2 = (bf16[16,192,128]{2,1,0:T(8,128)(2,1)S(1)}, bf16[16,192,128]{2,1,0:T(8,128)(2,1)S(1)}, u32[]{:S(2)}, u32[]{:S(2)}) collective-permute-start(bf16[16,192,128]{2,1,0:T(8,128)(2,1)S(1)} %bitcast.24), channel_id=1, source_target_pairs={{0,6},{1,7},{2,0},{3,1},{4,2},{5,3},{6,4},{7,5},{8,14},{9,15},{10,... | collective-permute-start | bytes 2359304 | tf_op jit(solution)/shard_map/ppermute | solution.py:263
  74.8 9.3 %collective-permute-done.2.refs_4_ = bf16[16,192,128]{2,1,0:T(8,128)(2,1)S(1)} collective-permute-done((bf16[16,192,128]{2,1,0:T(8,128)(2,1)S(1)}, bf16[16,192,128]{2,1,0:T(8,128)(2,1)S(1)}, u32[]{:S(2)}, u32[]{:S(2)}) %collective-permute-start.2) | collective-permute-done | bytes 786464 | tf_op jit(solution)/shard_map/ppermute | solution.py:263
  84.1 5.4 %collective-permute-start.3 = (bf16[8,192,128]{2,1,0:T(8,128)(2,1)S(1)}, bf16[8,192,128]{2,1,0:T(8,128)(2,1)}, u32[]{:S(2)}, u32[]{:S(2)}) collective-permute-start(bf16[8,192,128]{2,1,0:T(8,128)(2,1)S(1)} %slice.9), channel_id=1, source_target_pairs={{0,6},{1,7},{2,0},{3,1},{4,2},{5,3},{6,4},{7,5},{8,14},{9,15},{10,... | collective-permute-start | bytes 1179656 | tf_op jit(solution)/shard_map/ppermute | solution.py:265
  94.9 6.1 %collective-permute-done.1.refs_2_ = bf16[8,192,128]{2,1,0:T(8,128)(2,1)} collective-permute-done((bf16[8,192,128]{2,1,0:T(8,128)(2,1)}, bf16[8,192,128]{2,1,0:T(8,128)(2,1)}, u32[]{:S(2)}, u32[]{:S(2)}) %collective-permute-start.1) | collective-permute-done | bytes 393248 | tf_op jit(solution)/shard_map/ppermute | solution.py:264
  101.0 4.4 %collective-permute-start.6 = (bf16[16,96,128]{2,1,0:T(8,128)(2,1)S(1)}, bf16[16,96,128]{2,1,0:T(8,128)(2,1)S(1)}, u32[]{:S(2)}, u32[]{:S(2)}) collective-permute-start(bf16[16,96,128]{2,1,0:T(8,128)(2,1)S(1)} %all-to-all-done.1), channel_id=1, source_target_pairs={{0,24},{1,25},{2,26},{3,27},{4,28},{5,29},{6,30},{7,31},{8,0},{9,1... | collective-permute-start | bytes 1179656 | tf_op jit(solution)/shard_map/ppermute | solution.py:257
  105.3 2.4 %collective-permute-start.5 = (bf16[16,96,128]{2,1,0:T(8,128)(2,1)S(1)}, bf16[16,96,128]{2,1,0:T(8,128)(2,1)S(1)}, u32[]{:S(2)}, u32[]{:S(2)}) collective-permute-start(bf16[16,96,128]{2,1,0:T(8,128)(2,1)S(1)} %all-to-all-done.1), channel_id=1, source_target_pairs={{0,16},{1,17},{2,18},{3,19},{4,20},{5,21},{6,22},{7,23},{8,24},{9,... | collective-permute-start | bytes 1179656 | tf_op jit(solution)/shard_map/ppermute | solution.py:257
  107.8 2.5 %collective-permute-start.4 = (bf16[16,96,128]{2,1,0:T(8,128)(2,1)S(1)}, bf16[16,96,128]{2,1,0:T(8,128)(2,1)S(1)}, u32[]{:S(2)}, u32[]{:S(2)}) collective-permute-start(bf16[16,96,128]{2,1,0:T(8,128)(2,1)S(1)} %all-to-all-done.1), channel_id=1, source_target_pairs={{0,8},{1,9},{2,10},{3,11},{4,12},{5,13},{6,14},{7,15},{8,16},{9,17... | collective-permute-start | bytes 1179656 | tf_op jit(solution)/shard_map/ppermute | solution.py:257
  110.3 4.2 %collective-permute-done.6 = bf16[16,96,128]{2,1,0:T(8,128)(2,1)S(1)} collective-permute-done((bf16[16,96,128]{2,1,0:T(8,128)(2,1)S(1)}, bf16[16,96,128]{2,1,0:T(8,128)(2,1)S(1)}, u32[]{:S(2)}, u32[]{:S(2)}) %collective-permute-start.6) | collective-permute-done | bytes 393248 | tf_op jit(solution)/shard_map/ppermute | solution.py:257
  115.5 4.6 %collective-permute-done.4 = bf16[16,96,128]{2,1,0:T(8,128)(2,1)S(1)} collective-permute-done((bf16[16,96,128]{2,1,0:T(8,128)(2,1)S(1)}, bf16[16,96,128]{2,1,0:T(8,128)(2,1)S(1)}, u32[]{:S(2)}, u32[]{:S(2)}) %collective-permute-start.4) | collective-permute-done | bytes 393248 | tf_op jit(solution)/shard_map/ppermute | solution.py:257
  121.4 10.6 %collective-permute-start.7 = (bf16[4,16,96,128]{3,2,1,0:T(8,128)(2,1)}, bf16[4,16,96,128]{3,2,1,0:T(8,128)(2,1)}, u32[]{:S(2)}, u32[]{:S(2)}) collective-permute-start(bf16[4,16,96,128]{3,2,1,0:T(8,128)(2,1)} %pad_maximum_fusion.refs_5_), channel_id=1, source_target_pairs={{0,1},{1,0},{2,3},{3,2},{4,5},{5,4},{6,7},{7,6},{8,9},{9,8},{10,11... | collective-permute-start | bytes 4718600 | tf_op jit(solution)/shard_map/ppermute | solution.py:295
  132.1 3.2 %collective-permute-done.7.refs_6_ = bf16[4,16,96,128]{3,2,1,0:T(8,128)(2,1)} collective-permute-done((bf16[4,16,96,128]{3,2,1,0:T(8,128)(2,1)}, bf16[4,16,96,128]{3,2,1,0:T(8,128)(2,1)}, u32[]{:S(2)}, u32[]{:S(2)}) %collective-permute-start.7) | collective-permute-done | bytes 1572896 | tf_op jit(solution)/shard_map/ppermute | solution.py:295
  135.4 7.2 %wgrad_products.1 = bf16[8,96,768]{2,1,0:T(8,128)(2,1)} custom-call(s32[3]{0:T(128)S(1)} %pad_add_fusion.place, bf16[16,192,128]{2,1,0:T(8,128)(2,1)} %bitcast.26, bf16[16,192,128]{2,1,0:T(8,128)(2,1)} %copy-done.6, bf16[8,192,128]{2,1,0:T(8,128)(2,1)} %collective-permute-done.1.refs_2_, bf16[8,192,128]{2,1,0:T(8,128)(2,1)} %collective-permute-done.3.refs_3_, ...), custom_call_target="tpu_custom_call" | custom-call | tf_op jit(solution)/shard_map/wgrad_products/pallas_call | solution.py:122
  142.6 3.8 %all-to-all-start.2 = ((bf16[8,96,768]{2,1,0:T(8,128)(2,1)}), bf16[8,96,768]{2,1,0:T(8,128)(2,1)S(1)}, u32[]{:S(2)}, u32[]{:S(2)}) async-start(bf16[8,96,768]{2,1,0:T(8,128)(2,1)} %wgrad_products.1), calls=%async_computation.2 | async-start | bytes 2359296 | tf_op jit(solution)/shard_map/all_to_all | solution.py:298
  146.5 6.9 %tokens_step.1 = (bf16[128,1536]{1,0:T(8,128)(2,1)}, bf16[4,4,192,128]{3,2,1,0:T(8,128)(2,1)}, bf16[4,4,192,128]{3,2,1,0:T(8,128)(2,1)}) custom-call(s32[3,9]{1,0:T(4,128)S(1)} %copy-done.3, s32[3]{0:T(128)S(1)} %pad_add_fusion.place, bf16[6144,128]{1,0:T(8,128)(2,1)S(1)} %bitcast.22, bf16[128,1536]{1,0:T(8,128)(2,1)S(1)} %copy-done, ...), custom_call_target="tpu_custom_call" | custom-call | tf_op jit(solution)/shard_map/tokens_step/pallas_call | solution.py:64
  155.6 7.4 %all-to-all-done.2.prod_ref = bf16[8,96,768]{2,1,0:T(8,128)(2,1)S(1)} async-done(((bf16[8,96,768]{2,1,0:T(8,128)(2,1)}), bf16[8,96,768]{2,1,0:T(8,128)(2,1)S(1)}, u32[]{:S(2)}, u32[]{:S(2)}) %all-to-all-start.2) | async-done | bytes 1179680 | tf_op jit(solution)/shard_map/all_to_all | solution.py:298
  164.9 11.6 %all-to-all-start.3 = ((bf16[16,32,512]{2,1,0:T(8,128)(2,1)}), bf16[16,32,512]{2,1,0:T(8,128)(2,1)S(1)}, u32[]{:S(2)}, u32[]{:S(2)}) async-start(bf16[16,32,512]{2,1,0:T(8,128)(2,1)} %pick_slots.1), calls=%async_computation.3 | async-start | bytes 1048576 | tf_op jit(solution)/shard_map/all_to_all | solution.py:304
  180.7 4.1 %collective-permute-start.11 = (bf16[4,192,128]{2,1,0:T(8,128)(2,1)S(1)}, bf16[4,192,128]{2,1,0:T(8,128)(2,1)S(1)}, u32[]{:S(2)}, u32[]{:S(2)}) collective-permute-start(bf16[4,192,128]{2,1,0:T(8,128)(2,1)S(1)} %get-tuple-element.49), channel_id=1, source_target_pairs={{0,6},{1,7},{2,0},{3,1},{4,2},{5,3},{6,4},{7,5},{8,14},{9,15},{10,... | collective-permute-start | bytes 589832 | tf_op jit(solution)/shard_map/ppermute | solution.py:207
  184.9 4.1 %collective-permute-done.9.refs_1_ = bf16[4,192,128]{2,1,0:T(8,128)(2,1)S(1)} collective-permute-done((bf16[4,192,128]{2,1,0:T(8,128)(2,1)S(1)}, bf16[4,192,128]{2,1,0:T(8,128)(2,1)S(1)}, u32[]{:S(2)}, u32[]{:S(2)}) %collective-permute-start.9) | collective-permute-done | bytes 196640 | tf_op jit(solution)/shard_map/ppermute | solution.py:207
  189.0 2.4 %collective-permute-done.11.refs_3_ = bf16[4,192,128]{2,1,0:T(8,128)(2,1)S(1)} collective-permute-done((bf16[4,192,128]{2,1,0:T(8,128)(2,1)S(1)}, bf16[4,192,128]{2,1,0:T(8,128)(2,1)S(1)}, u32[]{:S(2)}, u32[]{:S(2)}) %collective-permute-start.11) | collective-permute-done | bytes 196640 | tf_op jit(solution)/shard_map/ppermute | solution.py:207
  193.7 3.7 %collective-permute-start.13 = (f32[192,128]{1,0:T(8,128)S(1)}, f32[192,128]{1,0:T(8,128)S(1)}, u32[]{:S(2)}, u32[]{:S(2)}) collective-permute-start(f32[192,128]{1,0:T(8,128)S(1)} %get-tuple-element.52), channel_id=1, source_target_pairs={{0,16},{1,17},{2,18},{3,19},{4,20},{5,21},{6,22},{7,23},{8,24},{9,... | collective-permute-start | bytes 294920 | tf_op jit(solution)/shard_map/ppermute | solution.py:209
  197.4 2.6 %collective-permute-start.14 = (f32[192,128]{1,0:T(8,128)S(1)}, f32[192,128]{1,0:T(8,128)S(1)}, u32[]{:S(2)}, u32[]{:S(2)}) collective-permute-start(f32[192,128]{1,0:T(8,128)S(1)} %get-tuple-element.53), channel_id=1, source_target_pairs={{0,24},{1,25},{2,26},{3,27},{4,28},{5,29},{6,30},{7,31},{8,0},{9,1... | collective-permute-start | bytes 294920 | tf_op jit(solution)/shard_map/ppermute | solution.py:209
  (49 shorter events, 29.3 us)
Async XLA Ops:
  7.2 139.3 %all-gather.4.cloned.1.call-start = ((), (), s32[]{:S(2)}) async-start(), calls=%async_computation.4 | async-start | bytes 8912896 | tf_op jit(solution)/shard_map/all_gather | solution.py:280
  10.2 10.6 %copy-start = (bf16[128,1536]{1,0:T(8,128)(2,1)S(1)}, bf16[128,1536]{1,0:T(8,128)(2,1)}, u32[]{:S(2)}) copy-start(bf16[128,1536]{1,0:T(8,128)(2,1)} %grad_ref.1) | copy-start | bytes 1179652
  10.2 51.1 %all-to-all-start = ((bf16[32,192,128]{2,1,0:T(8,128)(2,1)}), bf16[32,192,128]{2,1,0:T(8,128)(2,1)S(1)}, u32[]{:S(2)}, u32[]{:S(2)}) async-start(bf16[32,192,128]{2,1,0:T(8,128)(2,1)} %broadcast_in_dim.2), calls=%async_computation | async-start | bytes 3145728 | tf_op jit(solution)/shard_map/all_to_all | solution.py:283
  61.3 60.1 %copy-start.4 = (bf16[3072,128]{1,0:T(8,128)(2,1)}, bf16[3072,128]{1,0:T(8,128)(2,1)S(1)}, u32[]{:S(2)}) copy-start(bf16[3072,128]{1,0:T(8,128)(2,1)S(1)} %all-gather) | copy-start | bytes 2359300
  61.3 39.7 %all-to-all-start.1 = ((bf16[16,96,128]{2,1,0:T(8,128)(2,1)}), bf16[16,96,128]{2,1,0:T(8,128)(2,1)S(1)}, u32[]{:S(2)}, u32[]{:S(2)}) async-start(bf16[16,96,128]{2,1,0:T(8,128)(2,1)} %bitcast.3), calls=%async_computation.1 | async-start | bytes 786432 | tf_op jit(solution)/shard_map/all_to_all | solution.py:289
  68.4 15.7 %collective-permute-start.2 = (bf16[16,192,128]{2,1,0:T(8,128)(2,1)S(1)}, bf16[16,192,128]{2,1,0:T(8,128)(2,1)S(1)}, u32[]{:S(2)}, u32[]{:S(2)}) collective-permute-start(bf16[16,192,128]{2,1,0:T(8,128)(2,1)S(1)} %bitcast.24), channel_id=1, source_target_pairs={{0,6},{1,7},{2,0},{3,1},{4,2},{5,3},{6,4},{7,5},{8,14},{9,15},{10,... | collective-permute-start | bytes 2359304 | tf_op jit(solution)/shard_map/ppermute | solution.py:263
  72.8 16.7 %collective-permute-start = (bf16[16,192,128]{2,1,0:T(8,128)(2,1)S(1)}, bf16[16,192,128]{2,1,0:T(8,128)(2,1)S(1)}, u32[]{:S(2)}, u32[]{:S(2)}) collective-permute-start(bf16[16,192,128]{2,1,0:T(8,128)(2,1)S(1)} %bitcast.25), channel_id=1, source_target_pairs={{0,2},{1,3},{2,4},{3,5},{4,6},{5,7},{6,0},{7,1},{8,10},{9,11},{10,... | collective-permute-start | bytes 2359304 | tf_op jit(solution)/shard_map/ppermute | solution.py:262
  84.1 10.7 %collective-permute-start.3 = (bf16[8,192,128]{2,1,0:T(8,128)(2,1)S(1)}, bf16[8,192,128]{2,1,0:T(8,128)(2,1)}, u32[]{:S(2)}, u32[]{:S(2)}) collective-permute-start(bf16[8,192,128]{2,1,0:T(8,128)(2,1)S(1)} %slice.9), channel_id=1, source_target_pairs={{0,6},{1,7},{2,0},{3,1},{4,2},{5,3},{6,4},{7,5},{8,14},{9,15},{10,... | collective-permute-start | bytes 1179656 | tf_op jit(solution)/shard_map/ppermute | solution.py:265
  90.6 10.3 %collective-permute-start.1 = (bf16[8,192,128]{2,1,0:T(8,128)(2,1)}, bf16[8,192,128]{2,1,0:T(8,128)(2,1)}, u32[]{:S(2)}, u32[]{:S(2)}) collective-permute-start(bf16[8,192,128]{2,1,0:T(8,128)(2,1)} %slice.8), channel_id=1, source_target_pairs={{0,2},{1,3},{2,4},{3,5},{4,6},{5,7},{6,0},{7,1},{8,10},{9,11},{10,... | collective-permute-start | bytes 1179656 | tf_op jit(solution)/shard_map/ppermute | solution.py:264
  101.0 13.5 %collective-permute-start.6 = (bf16[16,96,128]{2,1,0:T(8,128)(2,1)S(1)}, bf16[16,96,128]{2,1,0:T(8,128)(2,1)S(1)}, u32[]{:S(2)}, u32[]{:S(2)}) collective-permute-start(bf16[16,96,128]{2,1,0:T(8,128)(2,1)S(1)} %all-to-all-done.1), channel_id=1, source_target_pairs={{0,24},{1,25},{2,26},{3,27},{4,28},{5,29},{6,30},{7,31},{8,0},{9,1... | collective-permute-start | bytes 1179656 | tf_op jit(solution)/shard_map/ppermute | solution.py:257
  105.3 10.1 %collective-permute-start.5 = (bf16[16,96,128]{2,1,0:T(8,128)(2,1)S(1)}, bf16[16,96,128]{2,1,0:T(8,128)(2,1)S(1)}, u32[]{:S(2)}, u32[]{:S(2)}) collective-permute-start(bf16[16,96,128]{2,1,0:T(8,128)(2,1)S(1)} %all-to-all-done.1), channel_id=1, source_target_pairs={{0,16},{1,17},{2,18},{3,19},{4,20},{5,21},{6,22},{7,23},{8,24},{9,... | collective-permute-start | bytes 1179656 | tf_op jit(solution)/shard_map/ppermute | solution.py:257
  107.8 12.3 %collective-permute-start.4 = (bf16[16,96,128]{2,1,0:T(8,128)(2,1)S(1)}, bf16[16,96,128]{2,1,0:T(8,128)(2,1)S(1)}, u32[]{:S(2)}, u32[]{:S(2)}) collective-permute-start(bf16[16,96,128]{2,1,0:T(8,128)(2,1)S(1)} %all-to-all-done.1), channel_id=1, source_target_pairs={{0,8},{1,9},{2,10},{3,11},{4,12},{5,13},{6,14},{7,15},{8,16},{9,17... | collective-permute-start | bytes 1179656 | tf_op jit(solution)/shard_map/ppermute | solution.py:257
  121.4 14.0 %collective-permute-start.7 = (bf16[4,16,96,128]{3,2,1,0:T(8,128)(2,1)}, bf16[4,16,96,128]{3,2,1,0:T(8,128)(2,1)}, u32[]{:S(2)}, u32[]{:S(2)}) collective-permute-start(bf16[4,16,96,128]{3,2,1,0:T(8,128)(2,1)} %pad_maximum_fusion.refs_5_), channel_id=1, source_target_pairs={{0,1},{1,0},{2,3},{3,2},{4,5},{5,4},{6,7},{7,6},{8,9},{9,8},{10,11... | collective-permute-start | bytes 4718600 | tf_op jit(solution)/shard_map/ppermute | solution.py:295
  142.6 20.4 %all-to-all-start.2 = ((bf16[8,96,768]{2,1,0:T(8,128)(2,1)}), bf16[8,96,768]{2,1,0:T(8,128)(2,1)S(1)}, u32[]{:S(2)}, u32[]{:S(2)}) async-start(bf16[8,96,768]{2,1,0:T(8,128)(2,1)} %wgrad_products.1), calls=%async_computation.2 | async-start | bytes 2359296 | tf_op jit(solution)/shard_map/all_to_all | solution.py:298
  146.4 16.5 %copy-start.2 = (s32[3,16]{1,0:T(4,128)S(1)}, s32[3,16]{1,0:T(4,128)}, u32[]{:S(2)}) copy-start(s32[3,16]{1,0:T(4,128)} %get-tuple-element.36.meta) | copy-start | bytes 580
  153.4 11.3 %copy-start.1 = (bf16[4,4,192,128]{3,2,1,0:T(8,128)(2,1)S(1)}, bf16[4,4,192,128]{3,2,1,0:T(8,128)(2,1)}, u32[]{:S(2)}) copy-start(bf16[4,4,192,128]{3,2,1,0:T(8,128)(2,1)} %get-tuple-element.40.own_ref) | copy-start | bytes 2359300
  153.4 11.3 %collective-permute-start.8 = (bf16[4,4,192,128]{3,2,1,0:T(8,128)(2,1)}, bf16[4,4,192,128]{3,2,1,0:T(8,128)(2,1)S(1)}, u32[]{:S(2)}, u32[]{:S(2)}) collective-permute-start(bf16[4,4,192,128]{3,2,1,0:T(8,128)(2,1)} %get-tuple-element.41), channel_id=1, source_target_pairs={{0,1},{1,0},{2,3},{3,2},{4,5},{5,4},{6,7},{7,6},{8,9},{9,8},{10,11... | collective-permute-start | bytes 2359304 | tf_op jit(solution)/shard_map/ppermute | solution.py:201
  164.9 39.3 %all-to-all-start.3 = ((bf16[16,32,512]{2,1,0:T(8,128)(2,1)}), bf16[16,32,512]{2,1,0:T(8,128)(2,1)S(1)}, u32[]{:S(2)}, u32[]{:S(2)}) async-start(bf16[16,32,512]{2,1,0:T(8,128)(2,1)} %pick_slots.1), calls=%async_computation.3 | async-start | bytes 1048576 | tf_op jit(solution)/shard_map/all_to_all | solution.py:304
  176.4 12.6 %collective-permute-start.9 = (bf16[4,192,128]{2,1,0:T(8,128)(2,1)S(1)}, bf16[4,192,128]{2,1,0:T(8,128)(2,1)S(1)}, u32[]{:S(2)}, u32[]{:S(2)}) collective-permute-start(bf16[4,192,128]{2,1,0:T(8,128)(2,1)S(1)} %get-tuple-element.47), channel_id=1, source_target_pairs={{0,2},{1,3},{2,4},{3,5},{4,6},{5,7},{6,0},{7,1},{8,10},{9,11},{10,... | collective-permute-start | bytes 589832 | tf_op jit(solution)/shard_map/ppermute | solution.py:207
  178.4 10.6 %collective-permute-start.10 = (bf16[4,192,128]{2,1,0:T(8,128)(2,1)S(1)}, bf16[4,192,128]{2,1,0:T(8,128)(2,1)S(1)}, u32[]{:S(2)}, u32[]{:S(2)}) collective-permute-start(bf16[4,192,128]{2,1,0:T(8,128)(2,1)S(1)} %get-tuple-element.48), channel_id=1, source_target_pairs={{0,4},{1,5},{2,6},{3,7},{4,0},{5,1},{6,2},{7,3},{8,12},{9,13},{10,... | collective-permute-start | bytes 589832 | tf_op jit(solution)/shard_map/ppermute | solution.py:207
  180.7 10.7 %collective-permute-start.11 = (bf16[4,192,128]{2,1,0:T(8,128)(2,1)S(1)}, bf16[4,192,128]{2,1,0:T(8,128)(2,1)S(1)}, u32[]{:S(2)}, u32[]{:S(2)}) collective-permute-start(bf16[4,192,128]{2,1,0:T(8,128)(2,1)S(1)} %get-tuple-element.49), channel_id=1, source_target_pairs={{0,6},{1,7},{2,0},{3,1},{4,2},{5,3},{6,4},{7,5},{8,14},{9,15},{10,... | collective-permute-start | bytes 589832 | tf_op jit(solution)/shard_map/ppermute | solution.py:207
  191.5 8.5 %collective-permute-start.12 = (f32[192,128]{1,0:T(8,128)S(1)}, f32[192,128]{1,0:T(8,128)S(1)}, u32[]{:S(2)}, u32[]{:S(2)}) collective-permute-start(f32[192,128]{1,0:T(8,128)S(1)} %get-tuple-element.51), channel_id=1, source_target_pairs={{0,8},{1,9},{2,10},{3,11},{4,12},{5,13},{6,14},{7,15},{8,16},{9,17... | collective-permute-start | bytes 294920 | tf_op jit(solution)/shard_map/ppermute | solution.py:209
  193.7 7.7 %collective-permute-start.13 = (f32[192,128]{1,0:T(8,128)S(1)}, f32[192,128]{1,0:T(8,128)S(1)}, u32[]{:S(2)}, u32[]{:S(2)}) collective-permute-start(f32[192,128]{1,0:T(8,128)S(1)} %get-tuple-element.52), channel_id=1, source_target_pairs={{0,16},{1,17},{2,18},{3,19},{4,20},{5,21},{6,22},{7,23},{8,24},{9,... | collective-permute-start | bytes 294920 | tf_op jit(solution)/shard_map/ppermute | solution.py:209
  197.4 6.1 %collective-permute-start.14 = (f32[192,128]{1,0:T(8,128)S(1)}, f32[192,128]{1,0:T(8,128)S(1)}, u32[]{:S(2)}, u32[]{:S(2)}) collective-permute-start(f32[192,128]{1,0:T(8,128)S(1)} %get-tuple-element.53), channel_id=1, source_target_pairs={{0,24},{1,25},{2,26},{3,27},{4,28},{5,29},{6,30},{7,31},{8,0},{9,1... | collective-permute-start | bytes 294920 | tf_op jit(solution)/shard_map/ppermute | solution.py:209
  (4 other events, 11.4 us)
Sparse Core Ops, SparseCore 0:
  10.1 134.9 all-gather.3

commit v9 on v8

--- a/solution.py
+++ b/solution.py
@@ -19,7 +19,7 @@
 
 
 PLANE = [(x, y, c) for x in range(NX) for y in range(NY) for c in range(NC)]
-XC_GROUPS = [[col_of(x, y, c) for x in range(NX) for c in range(NC)] for y in range(NY)]
+X_GROUPS = [[col_of(x, y, c) for x in range(NX)] for y in range(NY) for c in range(NC)]
 CORE_SWAP = [(col_of(x, y, c), col_of(x, y, 1 - c)) for x, y, c in PLANE]
 X_SHIFTS = {s: [(col_of(x, y, c), col_of((x + s) % NX, y, c)) for x, y, c in PLANE] for s in range(1, NX)}
 Y_SHIFTS = {s: [(col_of(x, y, c), col_of(x, (y + s) % NY, c)) for x, y, c in PLANE] for s in range(1, NY)}
@@ -78,83 +78,83 @@
     )(meta, place, act, grad, in_hbm(w_all))
 
 
-def wgrad_kernel(place, *refs, scale):
-    n_in = 7
-    in_refs, out_ref, buffers, (a_buf, b_buf, sems) = refs[:n_in], refs[n_in], refs[n_in + 1 : -3], refs[-3:]
+def in_hbm(x):
+    return pltpu.with_memory_space_constraint(x, pltpu.HBM)
+
+
+def features_kernel(place, *refs):
+    n_in = (len(refs) - 2) // 2
+    in_refs, out_ref, buffers, sems = refs[:n_in], refs[n_in], refs[n_in + 1 : -1], refs[-1]
     copies = [pltpu.make_async_copy(in_refs[i], buffers[i], sems.at[i]) for i in range(n_in)]
     for copy in copies:
         copy.start()
-    here, before, far_lo, far_hi, after, own, oth = buffers
-    n_x, n_z, rows, toks = own.shape
-    piece = here.shape[1]
-    x, y, core = place[0], place[1], place[2]
-    for i, (part, s, first) in enumerate(
-        ((here, 0, 0), (before, 1, 0), (far_lo, 2, 0), (far_hi, 2, n_z // 2), (after, 3, 0))
-    ):
-        at = aligned(lax.rem(y - s + NY, NY) * piece, piece, 64)
+    n_z, piece, toks = buffers[0].shape
+    y, core = place[1], place[2]
+    parts = ((0, 0), (1, 0), (2, 0), (2, n_z // 2), (3, 0))
+    for i in range(n_in):
+        s, first = parts[i % len(parts)]
+        side = core if i < len(parts) else 1 - core
+        at = aligned((lax.rem(y - s + NY, NY) * NC + side) * piece, piece, 64)
         copies[i].wait()
-        for z in range(part.shape[0]):
-            b_buf[at, (first + z) * toks : (first + z + 1) * toks] = part[z]
-    for c, part in enumerate((own, oth)):
-        copies[n_in - 2 + c].wait()
-        for t in range(n_x):
-            at = (t * NC + c) * rows
-            for z in range(n_z):
-                a_buf[at : at + rows, z * toks : (z + 1) * toks] = part[t, z]
-    prod = lax.dot_general(
-        a_buf[...], b_buf[...], (((1,), (1,)), ((), ())), preferred_element_type=F32
-    )
-    prod = (prod * scale).astype(BF)
-    for t in range(n_x):
-        line = lax.rem(x - t + n_x, n_x) * NC
-        out_ref[line + core] = prod[2 * t * rows : (2 * t + 1) * rows]
-        out_ref[line + 1 - core] = prod[(2 * t + 1) * rows : (2 * t + 2) * rows]
-
-
-def in_hbm(x):
-    return pltpu.with_memory_space_constraint(x, pltpu.HBM)
-
-
-def wgrad_products(place, grad_own, grad_oth, act_y, scale):
-    n_x, n_z, rows, toks = grad_own.shape
-    piece = act_y[0].shape[1]
-    args = [in_hbm(a) for a in (*act_y, grad_own, grad_oth)]
-    return pl.pallas_call(
-        functools.partial(wgrad_kernel, scale=scale),
+        for z in range(buffers[i].shape[0]):
+            out_ref[at, (first + z) * toks : (first + z + 1) * toks] = buffers[i][z]
+
+
+def line_features(place, own, oth):
+    n_z, piece, toks = own[0].shape
+    args = [in_hbm(a) for a in (*own, *oth)]
+    return pl.pallas_call(
+        features_kernel,
         in_specs=[pl.BlockSpec(memory_space=pltpu.SMEM)]
         + [pl.BlockSpec(memory_space=pltpu.HBM)] * len(args),
         out_specs=pl.BlockSpec(memory_space=pltpu.VMEM),
-        out_shape=pltpu.HBM((n_x * NC, rows, NY * piece), BF),
-        scratch_shapes=[pltpu.VMEM(a.shape, BF) for a in args]
-        + [
-            pltpu.VMEM((n_x * NC * rows, n_z * toks), BF),
-            pltpu.VMEM((NY * piece, n_z * toks), BF),
-            pltpu.SemaphoreType.DMA((len(args),)),
-        ],
-        compiler_params=pltpu.CompilerParams(vmem_limit_bytes=32 * MIB),
+        out_shape=jax.ShapeDtypeStruct((NY * NC * piece, n_z * toks), BF),
+        scratch_shapes=[pltpu.VMEM(a.shape, BF) for a in args] + [pltpu.SemaphoreType.DMA((len(args),))],
+        compiler_params=pltpu.CompilerParams(vmem_limit_bytes=20 * MIB),
+        name="line_features",
+    )(place, *args)
+
+
+def wgrad_kernel(place, *refs, scale):
+    grad_refs, (feats_ref, out_ref, a_buf) = refs[:NX], refs[NX:]
+    n_z, rows, toks = grad_refs[0].shape
+    for t in range(NX):
+        for z in range(n_z):
+            a_buf[t * rows : (t + 1) * rows, z * toks : (z + 1) * toks] = grad_refs[t][z]
+    prod = lax.dot_general(
+        a_buf[...], feats_ref[...], (((1,), (1,)), ((), ())), preferred_element_type=F32
+    )
+    prod = (prod * scale).astype(BF)
+    for t in range(NX):
+        out_ref[lax.rem(place[0] - t + NX, NX)] = prod[t * rows : (t + 1) * rows]
+
+
+def wgrad_products(place, grads, feats, scale):
+    n_z, rows, toks = grads[0].shape
+    vmem = pl.BlockSpec(memory_space=pltpu.VMEM)
+    return pl.pallas_call(
+        functools.partial(wgrad_kernel, scale=scale),
+        in_specs=[pl.BlockSpec(memory_space=pltpu.SMEM)] + [vmem] * (NX + 1),
+        out_specs=vmem,
+        out_shape=pltpu.HBM((NX, rows, feats.shape[0]), BF),
+        scratch_shapes=[pltpu.VMEM((NX * rows, n_z * toks), BF)],
+        compiler_params=pltpu.CompilerParams(vmem_limit_bytes=20 * MIB),
         name="wgrad_products",
-    )(place, *args)
-
-
-def slots_kernel(meta, prod_ref, out_ref, line_buf, *, chunk, blk):
-    piece = prod_ref.shape[2] // NY
-    for x in range(NX):
-        for y in range(NY):
-            for c in range(NC):
-                at = (y * NC + c) * piece
-                line_buf[x, :, at : at + piece] = prod_ref[x * NC + c, :, y * piece : (y + 1) * piece]
-    per_x = line_buf.shape[2] // blk
+    )(place, *grads, feats)
+
+
+def slots_kernel(meta, prod_ref, out_ref, *, chunk, blk):
+    per_x = prod_ref.shape[2] // blk
     for s in range(out_ref.shape[0]):
         hid, mod, full = meta[0, s], meta[1, s], meta[2, s]
         rows = aligned(hid * chunk, chunk, chunk)
         cols = aligned(lax.rem(mod, per_x) * blk, blk, blk)
-        part = line_buf[lax.div(mod, per_x), rows, cols]
+        part = prod_ref[lax.div(mod, per_x), rows, cols]
         out_ref[s] = jnp.where(full > 0, part, jnp.zeros_like(part))
 
 
 def pick_slots(meta, prods, chunk, blk):
     owners = meta.shape[1]
-    _, rows, cols = prods.shape
     return pl.pallas_call(
         functools.partial(slots_kernel, chunk=chunk, blk=blk),
         in_specs=[
@@ -163,7 +163,6 @@
         ],
         out_specs=pl.BlockSpec(memory_space=pltpu.VMEM),
         out_shape=jax.ShapeDtypeStruct((owners, chunk, blk), BF),
-        scratch_shapes=[pltpu.VMEM((NX, rows, NC * cols), BF)],
         compiler_params=pltpu.CompilerParams(vmem_limit_bytes=12 * MIB),
         name="pick_slots",
     )(meta, prods)
@@ -254,7 +253,7 @@
 
 
 def line_x(x):
-    return jnp.stack([x] + [lax.ppermute(x, "col", X_SHIFTS[t]) for t in range(1, NX)])
+    return [x] + [lax.ppermute(x, "col", X_SHIFTS[t]) for t in range(1, NX)]
 
 
 def share_y(x):
@@ -289,13 +288,12 @@
     grad_z = lax.all_to_all(grad_send, "row", 0, 0, tiled=True)
     here, before, far_lo, far_hi, after = share_y(act_z)
     grad_z, far_lo, far_hi, listed, slots = lax.optimization_barrier((grad_z, far_lo, far_hi, listed, slots))
-    act_y = (here, before, far_lo, far_hi, after)
-
-    grad_own = line_x(grad_z)
-    grad_oth = lax.ppermute(grad_own, "col", CORE_SWAP)
-    scale = 1.0 / math.sqrt(toks * owners)
-    prods = wgrad_products(place, grad_own, grad_oth, act_y, scale)
-    prods = lax.all_to_all(prods, "col", 0, 0, tiled=True, axis_index_groups=XC_GROUPS)
+    act_own = (here, before, far_lo, far_hi, after)
+    act_oth = [lax.ppermute(a, "col", CORE_SWAP) for a in act_own]
+
+    feats = line_features(place, act_own, act_oth)
+    prods = wgrad_products(place, line_x(grad_z), feats, 1.0 / math.sqrt(toks * owners))
+    prods = lax.all_to_all(prods, "col", 0, 0, tiled=True, axis_index_groups=X_GROUPS)
     slot_parts = pick_slots(slots, prods, chunk, blk)
 
     outputs, in_own, in_oth = tokens_step(listed, place, act_all, out_grad, w_all)

time: 214 us -> 213 us (level)
  waiting for transfers between devices: 46.6 us -> 30.5 us
  starting transfers between devices: 85.8 us -> 97.8 us
    ppermute x4 -> x8, starting transfers between devices: 19.9 us -> 32.1 us  [the longest x5 21.6 us: per_device(): act_oth = [lax.ppermute(a, 'col', CORE_SWAP) for a in act_own]]
    ppermute x1, waiting for transfers between devices: 9.33 us -> 0.01 us  [share_y(): after = lax.ppermute(x, 'col', Y_SHIFTS[NY - 1])]
    all_to_all x1, starting transfers between devices: 11.6 us -> 7.42 us  [per_device(): lax.all_to_all(slot_parts, 'row', 0, 0, tiled=True).reshape(1, 1, blk, blk)]
    pallas_call x0 -> x1, Pallas kernels: none -> 3.69 us  [line_features(): pl.pallas_call(features_kernel, in_specs=[pl.BlockSpec(memory_space=pltpu...]
    ppermute x4 -> x8, waiting for transfers between devices: 13 us -> 9.69 us  [the longest x3 9.67 us: line_x(): return [x] + [lax.ppermute(x, 'col', X_SHIFTS[t]) for t in range(1, NX)]]
    pallas_call x1, Pallas kernels: 7.21 us -> 4.24 us  [wgrad_products(): pl.pallas_call(functools.partial(wgrad_kernel, scale=scale), in_specs=[pl...]
    ppermute x1, waiting for transfers between devices: 0.01 us -> 2.83 us  [share_y(): far_hi = lax.ppermute(after[half:], 'col', Y_SHIFTS[NY - 1])]
    ppermute x3, starting transfers between devices: 8.41 us -> 11.2 us  [sum_plane(): lax.ppermute(by_y[s], 'col', Y_SHIFTS[s])]
  transfers between devices with their start and end apart: 20 -> 24, of which waited for: 11 -> 9; matrix products, arithmetic and copies ran while one was open for 3% -> 3% of each run, Pallas kernels for 9% -> 9%
where the time goes in v9:
time: 213 us; the launch traced here: 209 us
  starting transfers between devices  97.8 us (46%)
  blocking collectives  39.5 us (19%)
  waiting for transfers between devices  30.5 us (14%)
  Pallas kernels  19.5 us (9%)
  between operations  14.4 us (7%)
  local copies, waits for them, and re-layouts  6.92 us (3%)
    all_gather x1, blocking collectives, per_device(): act_z = lax.all_gather(act_t, 'row', axis=0)  39.5 us
    ppermute x5, starting transfers between devices, per_device(): act_oth = [lax.ppermute(a, 'col', CORE_SWAP) for a in act_own]  21.6 us
    ppermute x3, starting transfers between devices, sum_plane(): lax.ppermute(by_y[s], 'col', Y_SHIFTS[s])  11.2 us
    all_to_all x1, starting transfers between devices, per_device(): lax.all_to_all(wide, 'col', 0, 0, tiled=True).reshape(groups * piece, toks)  10.6 us
    ppermute x3, starting transfers between devices, line_x(): return [x] + [lax.ppermute(x, 'col', X_SHIFTS[t]) for t in range(1, NX)]  10.5 us
    ppermute x3, waiting for transfers between devices, line_x(): return [x] + [lax.ppermute(x, 'col', X_SHIFTS[t]) for t in range(1, NX)]  9.67 us
    ppermute x3, starting transfers between devices, sum_plane(): lax.ppermute(by_x[t], 'col', X_SHIFTS[t])  8.57 us
    all_to_all x1, starting transfers between devices, per_device(): lax.all_to_all(slot_parts, 'row', 0, 0, tiled=True).reshape(1, 1, blk, blk)  7.42 us
  transfers between devices with their start and end apart: 24, of which 9 were waited for; matrix products, arithmetic and copies ran while one was open for 3% of the time, Pallas kernels for 9%

profile of v9, /device:TPU:1, one launch (start us, length us, event | category | flops | bytes accessed | tf_op | source)
XLA Modules:
  0.0 208.7 jit_solution(7505927675779077330)
XLA Ops:
  10.2 10.6 %all-to-all-start = ((bf16[32,192,128]{2,1,0:T(8,128)(2,1)}), bf16[32,192,128]{2,1,0:T(8,128)(2,1)S(1)}, u32[]{:S(2)}, u32[]{:S(2)}) async-start(bf16[32,192,128]{2,1,0:T(8,128)(2,1)} %broadcast_in_dim.2), calls=%async_computation | async-start | bytes 3145728 | tf_op jit(solution)/shard_map/all_to_all | solution.py:282
  21.9 39.5 %all-gather = bf16[3072,128]{1,0:T(8,128)(2,1)S(1)} all-gather(bf16[192,128]{1,0:T(8,128)(2,1)S(1)} %bitcast.27), channel_id=2, replica_groups=mesh['row'=16,'col'=32] {'row'}, dimensions={0}, use_global_device_ids=true | all-gather | bytes 835584 | tf_op jit(solution)/shard_map/all_gather | solution.py:283
  61.3 5.0 %collective-permute-start.2 = (bf16[16,192,128]{2,1,0:T(8,128)(2,1)S(1)}, bf16[16,192,128]{2,1,0:T(8,128)(2,1)}, u32[]{:S(2)}, u32[]{:S(2)}) collective-permute-start(bf16[16,192,128]{2,1,0:T(8,128)(2,1)S(1)} %bitcast.20), channel_id=1, source_target_pairs={{0,6},{1,7},{2,0},{3,1},{4,2},{5,3},{6,4},{7,5},{8,14},{9,15},{10,... | collective-permute-start | bytes 2359304 | tf_op jit(solution)/shard_map/ppermute | solution.py:262
  68.3 6.4 %all-to-all-start.1 = ((bf16[16,96,128]{2,1,0:T(8,128)(2,1)}), bf16[16,96,128]{2,1,0:T(8,128)(2,1)S(1)}, u32[]{:S(2)}, u32[]{:S(2)}) async-start(bf16[16,96,128]{2,1,0:T(8,128)(2,1)} %bitcast.3), calls=%async_computation.1 | async-start | bytes 786432 | tf_op jit(solution)/shard_map/all_to_all | solution.py:288
  74.8 7.7 %collective-permute-start.7 = (bf16[16,192,128]{2,1,0:T(8,128)(2,1)S(1)}, bf16[16,192,128]{2,1,0:T(8,128)(2,1)}, u32[]{:S(2)}, u32[]{:S(2)}) collective-permute-start(bf16[16,192,128]{2,1,0:T(8,128)(2,1)S(1)} %bitcast.22), channel_id=1, source_target_pairs={{0,1},{1,0},{2,3},{3,2},{4,5},{5,4},{6,7},{7,6},{8,9},{9,8},{10,11... | collective-permute-start | bytes 2359304 | tf_op jit(solution)/shard_map/ppermute | solution.py:292
  82.5 3.5 %collective-permute-start.11 = (bf16[16,192,128]{2,1,0:T(8,128)(2,1)}, bf16[16,192,128]{2,1,0:T(8,128)(2,1)}, u32[]{:S(2)}, u32[]{:S(2)}) collective-permute-start(bf16[16,192,128]{2,1,0:T(8,128)(2,1)} %collective-permute-done.2.refs_4_), channel_id=1, source_target_pairs={{0,1},{1,0},{2,3},{3,2},{4,5},{5,4},{6,7},{7,6},{8,9},{9,8},{10,11... | collective-permute-start | bytes 2359304 | tf_op jit(solution)/shard_map/ppermute | solution.py:292
  86.0 5.4 %collective-permute-start.8 = (bf16[16,192,128]{2,1,0:T(8,128)(2,1)}, bf16[16,192,128]{2,1,0:T(8,128)(2,1)}, u32[]{:S(2)}, u32[]{:S(2)}) collective-permute-start(bf16[16,192,128]{2,1,0:T(8,128)(2,1)} %collective-permute-done.refs_1_), channel_id=1, source_target_pairs={{0,1},{1,0},{2,3},{3,2},{4,5},{5,4},{6,7},{7,6},{8,9},{9,8},{10,11... | collective-permute-start | bytes 2359304 | tf_op jit(solution)/shard_map/ppermute | solution.py:292
  96.2 4.6 %collective-permute-start.3 = (bf16[8,192,128]{2,1,0:T(8,128)(2,1)}, bf16[8,192,128]{2,1,0:T(8,128)(2,1)}, u32[]{:S(2)}, u32[]{:S(2)}) collective-permute-start(bf16[8,192,128]{2,1,0:T(8,128)(2,1)} %slice.9), channel_id=1, source_target_pairs={{0,6},{1,7},{2,0},{3,1},{4,2},{5,3},{6,4},{7,5},{8,14},{9,15},{10,... | collective-permute-start | bytes 1179656 | tf_op jit(solution)/shard_map/ppermute | solution.py:264
  103.1 3.4 %collective-permute-done.1.refs_2_ = bf16[8,192,128]{2,1,0:T(8,128)(2,1)} collective-permute-done((bf16[8,192,128]{2,1,0:T(8,128)(2,1)S(1)}, bf16[8,192,128]{2,1,0:T(8,128)(2,1)}, u32[]{:S(2)}, u32[]{:S(2)}) %collective-permute-start.1) | collective-permute-done | bytes 393248 | tf_op jit(solution)/shard_map/ppermute | solution.py:263
  109.3 3.0 %collective-permute-start.10 = (bf16[8,192,128]{2,1,0:T(8,128)(2,1)}, bf16[8,192,128]{2,1,0:T(8,128)(2,1)}, u32[]{:S(2)}, u32[]{:S(2)}) collective-permute-start(bf16[8,192,128]{2,1,0:T(8,128)(2,1)} %collective-permute-done.3.refs_3_), channel_id=1, source_target_pairs={{0,1},{1,0},{2,3},{3,2},{4,5},{5,4},{6,7},{7,6},{8,9},{9,8},{10,11... | collective-permute-start | bytes 1179656 | tf_op jit(solution)/shard_map/ppermute | solution.py:292
  114.2 3.1 %collective-permute-start.4 = (bf16[16,96,128]{2,1,0:T(8,128)(2,1)S(1)}, bf16[16,96,128]{2,1,0:T(8,128)(2,1)S(1)}, u32[]{:S(2)}, u32[]{:S(2)}) collective-permute-start(bf16[16,96,128]{2,1,0:T(8,128)(2,1)S(1)} %all-to-all-done.1.refs_0_), channel_id=1, source_target_pairs={{0,8},{1,9},{2,10},{3,11},{4,12},{5,13},{6,14},{7,15},{8,16},{9,17... | collective-permute-start | bytes 1179656 | tf_op jit(solution)/shard_map/ppermute | solution.py:256
  117.4 4.3 %collective-permute-start.5 = (bf16[16,96,128]{2,1,0:T(8,128)(2,1)S(1)}, bf16[16,96,128]{2,1,0:T(8,128)(2,1)S(1)}, u32[]{:S(2)}, u32[]{:S(2)}) collective-permute-start(bf16[16,96,128]{2,1,0:T(8,128)(2,1)S(1)} %all-to-all-done.1.refs_0_), channel_id=1, source_target_pairs={{0,16},{1,17},{2,18},{3,19},{4,20},{5,21},{6,22},{7,23},{8,24},{9,... | collective-permute-start | bytes 1179656 | tf_op jit(solution)/shard_map/ppermute | solution.py:256
  121.7 3.1 %collective-permute-start.6 = (bf16[16,96,128]{2,1,0:T(8,128)(2,1)S(1)}, bf16[16,96,128]{2,1,0:T(8,128)(2,1)S(1)}, u32[]{:S(2)}, u32[]{:S(2)}) collective-permute-start(bf16[16,96,128]{2,1,0:T(8,128)(2,1)S(1)} %all-to-all-done.1.refs_0_), channel_id=1, source_target_pairs={{0,24},{1,25},{2,26},{3,27},{4,28},{5,29},{6,30},{7,31},{8,0},{9,1... | collective-permute-start | bytes 1179656 | tf_op jit(solution)/shard_map/ppermute | solution.py:256
  124.9 3.7 %line_features.1.refs_4_ = bf16[1536,2048]{1,0:T(8,128)(2,1)S(1)} custom-call(s32[3]{0:T(128)S(1)} %pad_add_fusion.place, bf16[16,192,128]{2,1,0:T(8,128)(2,1)} %bitcast.23, bf16[16,192,128]{2,1,0:T(8,128)(2,1)} %collective-permute-done.refs_1_, bf16[8,192,128]{2,1,0:T(8,128)(2,1)} %collective-permute-done.1.refs_2_, ...), custom_call_target="tpu_custom_call" | custom-call | tf_op jit(solution)/shard_map/line_features/pallas_call | solution.py:106
  128.6 8.2 %collective-permute-done.5.refs_2_ = bf16[16,96,128]{2,1,0:T(8,128)(2,1)S(1)} collective-permute-done((bf16[16,96,128]{2,1,0:T(8,128)(2,1)S(1)}, bf16[16,96,128]{2,1,0:T(8,128)(2,1)S(1)}, u32[]{:S(2)}, u32[]{:S(2)}) %collective-permute-start.5) | collective-permute-done | bytes 393248 | tf_op jit(solution)/shard_map/ppermute | solution.py:256
  138.3 4.2 %wgrad_products.1 = bf16[4,96,1536]{2,1,0:T(8,128)(2,1)} custom-call(s32[3]{0:T(128)S(1)} %pad_add_fusion.place, bf16[16,96,128]{2,1,0:T(8,128)(2,1)S(1)} %all-to-all-done.1.refs_0_, bf16[16,96,128]{2,1,0:T(8,128)(2,1)S(1)} %collective-permute-done.4.refs_1_, bf16[16,96,128]{2,1,0:T(8,128)(2,1)S(1)} %collective-permute-done.5.refs_2_, ...), custom_call_target="tpu_custom_call" | custom-call | tf_op jit(solution)/shard_map/wgrad_products/pallas_call | solution.py:135
  142.5 4.9 %all-to-all-start.2 = ((bf16[4,96,1536]{2,1,0:T(8,128)(2,1)}), bf16[4,96,1536]{2,1,0:T(8,128)(2,1)S(1)}, u32[]{:S(2)}, u32[]{:S(2)}) async-start(bf16[4,96,1536]{2,1,0:T(8,128)(2,1)} %wgrad_products.1), calls=%async_computation.2 | async-start | bytes 2359296 | tf_op jit(solution)/shard_map/all_to_all | solution.py:296
  147.5 6.9 %tokens_step.1 = (bf16[128,1536]{1,0:T(8,128)(2,1)}, bf16[4,4,192,128]{3,2,1,0:T(8,128)(2,1)}, bf16[4,4,192,128]{3,2,1,0:T(8,128)(2,1)}) custom-call(s32[3,9]{1,0:T(4,128)S(1)} %copy-done.3, s32[3]{0:T(128)S(1)} %pad_add_fusion.place, bf16[6144,128]{1,0:T(8,128)(2,1)S(1)} %bitcast.18, bf16[128,1536]{1,0:T(8,128)(2,1)S(1)} %copy-done, ...), custom_call_target="tpu_custom_call" | custom-call | tf_op jit(solution)/shard_map/tokens_step/pallas_call | solution.py:64
  154.4 3.1 %collective-permute-start.12 = (bf16[4,4,192,128]{3,2,1,0:T(8,128)(2,1)}, bf16[4,4,192,128]{3,2,1,0:T(8,128)(2,1)S(1)}, u32[]{:S(2)}, u32[]{:S(2)}) collective-permute-start(bf16[4,4,192,128]{3,2,1,0:T(8,128)(2,1)} %get-tuple-element.41), channel_id=1, source_target_pairs={{0,1},{1,0},{2,3},{3,2},{4,5},{5,4},{6,7},{7,6},{8,9},{9,8},{10,11... | collective-permute-start | bytes 2359304 | tf_op jit(solution)/shard_map/ppermute | solution.py:200
  157.5 5.5 %all-to-all-done.2.prod_ref = bf16[4,96,1536]{2,1,0:T(8,128)(2,1)S(1)} async-done(((bf16[4,96,1536]{2,1,0:T(8,128)(2,1)}), bf16[4,96,1536]{2,1,0:T(8,128)(2,1)S(1)}, u32[]{:S(2)}, u32[]{:S(2)}) %all-to-all-start.2) | async-done | bytes 1179680 | tf_op jit(solution)/shard_map/all_to_all | solution.py:296
  164.6 7.4 %all-to-all-start.3 = ((bf16[16,32,512]{2,1,0:T(8,128)(2,1)}), bf16[16,32,512]{2,1,0:T(8,128)(2,1)S(1)}, u32[]{:S(2)}, u32[]{:S(2)}) async-start(bf16[16,32,512]{2,1,0:T(8,128)(2,1)} %pick_slots.1), calls=%async_computation.3 | async-start | bytes 1048576 | tf_op jit(solution)/shard_map/all_to_all | solution.py:302
  172.0 3.5 %collective-permute-start.13 = (bf16[4,192,128]{2,1,0:T(8,128)(2,1)S(1)}, bf16[4,192,128]{2,1,0:T(8,128)(2,1)S(1)}, u32[]{:S(2)}, u32[]{:S(2)}) collective-permute-start(bf16[4,192,128]{2,1,0:T(8,128)(2,1)S(1)} %get-tuple-element.47), channel_id=1, source_target_pairs={{0,2},{1,3},{2,4},{3,5},{4,6},{5,7},{6,0},{7,1},{8,10},{9,11},{10,... | collective-permute-start | bytes 589832 | tf_op jit(solution)/shard_map/ppermute | solution.py:206
  175.6 4.9 %collective-permute-start.14 = (bf16[4,192,128]{2,1,0:T(8,128)(2,1)S(1)}, bf16[4,192,128]{2,1,0:T(8,128)(2,1)S(1)}, u32[]{:S(2)}, u32[]{:S(2)}) collective-permute-start(bf16[4,192,128]{2,1,0:T(8,128)(2,1)S(1)} %get-tuple-element.48), channel_id=1, source_target_pairs={{0,4},{1,5},{2,6},{3,7},{4,0},{5,1},{6,2},{7,3},{8,12},{9,13},{10,... | collective-permute-start | bytes 589832 | tf_op jit(solution)/shard_map/ppermute | solution.py:206
  190.3 4.2 %collective-permute-start.17 = (f32[192,128]{1,0:T(8,128)S(1)}, f32[192,128]{1,0:T(8,128)S(1)}, u32[]{:S(2)}, u32[]{:S(2)}) collective-permute-start(f32[192,128]{1,0:T(8,128)S(1)} %get-tuple-element.52), channel_id=1, source_target_pairs={{0,16},{1,17},{2,18},{3,19},{4,20},{5,21},{6,22},{7,23},{8,24},{9,... | collective-permute-start | bytes 294920 | tf_op jit(solution)/shard_map/ppermute | solution.py:208
  (53 shorter events, 38.0 us)
Async XLA Ops:
  7.2 140.3 %all-gather.4.cloned.1.call-start = ((), (), s32[]{:S(2)}) async-start(), calls=%async_computation.4 | async-start | bytes 8912896 | tf_op jit(solution)/shard_map/all_gather | solution.py:279
  10.2 51.1 %all-to-all-start = ((bf16[32,192,128]{2,1,0:T(8,128)(2,1)}), bf16[32,192,128]{2,1,0:T(8,128)(2,1)S(1)}, u32[]{:S(2)}, u32[]{:S(2)}) async-start(bf16[32,192,128]{2,1,0:T(8,128)(2,1)} %broadcast_in_dim.2), calls=%async_computation | async-start | bytes 3145728 | tf_op jit(solution)/shard_map/all_to_all | solution.py:282
  61.3 21.2 %collective-permute-start.2 = (bf16[16,192,128]{2,1,0:T(8,128)(2,1)S(1)}, bf16[16,192,128]{2,1,0:T(8,128)(2,1)}, u32[]{:S(2)}, u32[]{:S(2)}) collective-permute-start(bf16[16,192,128]{2,1,0:T(8,128)(2,1)S(1)} %bitcast.20), channel_id=1, source_target_pairs={{0,6},{1,7},{2,0},{3,1},{4,2},{5,3},{6,4},{7,5},{8,14},{9,15},{10,... | collective-permute-start | bytes 2359304 | tf_op jit(solution)/shard_map/ppermute | solution.py:262
  66.4 19.6 %collective-permute-start = (bf16[16,192,128]{2,1,0:T(8,128)(2,1)S(1)}, bf16[16,192,128]{2,1,0:T(8,128)(2,1)}, u32[]{:S(2)}, u32[]{:S(2)}) collective-permute-start(bf16[16,192,128]{2,1,0:T(8,128)(2,1)S(1)} %bitcast.21), channel_id=1, source_target_pairs={{0,2},{1,3},{2,4},{3,5},{4,6},{5,7},{6,0},{7,1},{8,10},{9,11},{10,... | collective-permute-start | bytes 2359304 | tf_op jit(solution)/shard_map/ppermute | solution.py:261
  68.3 41.0 %all-to-all-start.1 = ((bf16[16,96,128]{2,1,0:T(8,128)(2,1)}), bf16[16,96,128]{2,1,0:T(8,128)(2,1)S(1)}, u32[]{:S(2)}, u32[]{:S(2)}) async-start(bf16[16,96,128]{2,1,0:T(8,128)(2,1)} %bitcast.3), calls=%async_computation.1 | async-start | bytes 786432 | tf_op jit(solution)/shard_map/all_to_all | solution.py:288
  74.8 39.5 %collective-permute-start.7 = (bf16[16,192,128]{2,1,0:T(8,128)(2,1)S(1)}, bf16[16,192,128]{2,1,0:T(8,128)(2,1)}, u32[]{:S(2)}, u32[]{:S(2)}) collective-permute-start(bf16[16,192,128]{2,1,0:T(8,128)(2,1)S(1)} %bitcast.22), channel_id=1, source_target_pairs={{0,1},{1,0},{2,3},{3,2},{4,5},{5,4},{6,7},{7,6},{8,9},{9,8},{10,11... | collective-permute-start | bytes 2359304 | tf_op jit(solution)/shard_map/ppermute | solution.py:292
  82.5 34.8 %collective-permute-start.11 = (bf16[16,192,128]{2,1,0:T(8,128)(2,1)}, bf16[16,192,128]{2,1,0:T(8,128)(2,1)}, u32[]{:S(2)}, u32[]{:S(2)}) collective-permute-start(bf16[16,192,128]{2,1,0:T(8,128)(2,1)} %collective-permute-done.2.refs_4_), channel_id=1, source_target_pairs={{0,1},{1,0},{2,3},{3,2},{4,5},{5,4},{6,7},{7,6},{8,9},{9,8},{10,11... | collective-permute-start | bytes 2359304 | tf_op jit(solution)/shard_map/ppermute | solution.py:292
  86.0 35.6 %collective-permute-start.8 = (bf16[16,192,128]{2,1,0:T(8,128)(2,1)}, bf16[16,192,128]{2,1,0:T(8,128)(2,1)}, u32[]{:S(2)}, u32[]{:S(2)}) collective-permute-start(bf16[16,192,128]{2,1,0:T(8,128)(2,1)} %collective-permute-done.refs_1_), channel_id=1, source_target_pairs={{0,1},{1,0},{2,3},{3,2},{4,5},{5,4},{6,7},{7,6},{8,9},{9,8},{10,11... | collective-permute-start | bytes 2359304 | tf_op jit(solution)/shard_map/ppermute | solution.py:292
  92.5 13.9 %collective-permute-start.1 = (bf16[8,192,128]{2,1,0:T(8,128)(2,1)S(1)}, bf16[8,192,128]{2,1,0:T(8,128)(2,1)}, u32[]{:S(2)}, u32[]{:S(2)}) collective-permute-start(bf16[8,192,128]{2,1,0:T(8,128)(2,1)S(1)} %slice.8), channel_id=1, source_target_pairs={{0,2},{1,3},{2,4},{3,5},{4,6},{5,7},{6,0},{7,1},{8,10},{9,11},{10,... | collective-permute-start | bytes 1179656 | tf_op jit(solution)/shard_map/ppermute | solution.py:263
  96.2 13.1 %collective-permute-start.3 = (bf16[8,192,128]{2,1,0:T(8,128)(2,1)}, bf16[8,192,128]{2,1,0:T(8,128)(2,1)}, u32[]{:S(2)}, u32[]{:S(2)}) collective-permute-start(bf16[8,192,128]{2,1,0:T(8,128)(2,1)} %slice.9), channel_id=1, source_target_pairs={{0,6},{1,7},{2,0},{3,1},{4,2},{5,3},{6,4},{7,5},{8,14},{9,15},{10,... | collective-permute-start | bytes 1179656 | tf_op jit(solution)/shard_map/ppermute | solution.py:264
  109.3 15.6 %collective-permute-start.10 = (bf16[8,192,128]{2,1,0:T(8,128)(2,1)}, bf16[8,192,128]{2,1,0:T(8,128)(2,1)}, u32[]{:S(2)}, u32[]{:S(2)}) collective-permute-start(bf16[8,192,128]{2,1,0:T(8,128)(2,1)} %collective-permute-done.3.refs_3_), channel_id=1, source_target_pairs={{0,1},{1,0},{2,3},{3,2},{4,5},{5,4},{6,7},{7,6},{8,9},{9,8},{10,11... | collective-permute-start | bytes 1179656 | tf_op jit(solution)/shard_map/ppermute | solution.py:292
  112.3 12.6 %collective-permute-start.9 = (bf16[8,192,128]{2,1,0:T(8,128)(2,1)}, bf16[8,192,128]{2,1,0:T(8,128)(2,1)}, u32[]{:S(2)}, u32[]{:S(2)}) collective-permute-start(bf16[8,192,128]{2,1,0:T(8,128)(2,1)} %collective-permute-done.1.refs_2_), channel_id=1, source_target_pairs={{0,1},{1,0},{2,3},{3,2},{4,5},{5,4},{6,7},{7,6},{8,9},{9,8},{10,11... | collective-permute-start | bytes 1179656 | tf_op jit(solution)/shard_map/ppermute | solution.py:292
  114.2 14.4 %collective-permute-start.4 = (bf16[16,96,128]{2,1,0:T(8,128)(2,1)S(1)}, bf16[16,96,128]{2,1,0:T(8,128)(2,1)S(1)}, u32[]{:S(2)}, u32[]{:S(2)}) collective-permute-start(bf16[16,96,128]{2,1,0:T(8,128)(2,1)S(1)} %all-to-all-done.1.refs_0_), channel_id=1, source_target_pairs={{0,8},{1,9},{2,10},{3,11},{4,12},{5,13},{6,14},{7,15},{8,16},{9,17... | collective-permute-start | bytes 1179656 | tf_op jit(solution)/shard_map/ppermute | solution.py:256
  117.4 19.5 %collective-permute-start.5 = (bf16[16,96,128]{2,1,0:T(8,128)(2,1)S(1)}, bf16[16,96,128]{2,1,0:T(8,128)(2,1)S(1)}, u32[]{:S(2)}, u32[]{:S(2)}) collective-permute-start(bf16[16,96,128]{2,1,0:T(8,128)(2,1)S(1)} %all-to-all-done.1.refs_0_), channel_id=1, source_target_pairs={{0,16},{1,17},{2,18},{3,19},{4,20},{5,21},{6,22},{7,23},{8,24},{9,... | collective-permute-start | bytes 1179656 | tf_op jit(solution)/shard_map/ppermute | solution.py:256
  121.7 16.6 %collective-permute-start.6 = (bf16[16,96,128]{2,1,0:T(8,128)(2,1)S(1)}, bf16[16,96,128]{2,1,0:T(8,128)(2,1)S(1)}, u32[]{:S(2)}, u32[]{:S(2)}) collective-permute-start(bf16[16,96,128]{2,1,0:T(8,128)(2,1)S(1)} %all-to-all-done.1.refs_0_), channel_id=1, source_target_pairs={{0,24},{1,25},{2,26},{3,27},{4,28},{5,29},{6,30},{7,31},{8,0},{9,1... | collective-permute-start | bytes 1179656 | tf_op jit(solution)/shard_map/ppermute | solution.py:256
  142.5 20.4 %all-to-all-start.2 = ((bf16[4,96,1536]{2,1,0:T(8,128)(2,1)}), bf16[4,96,1536]{2,1,0:T(8,128)(2,1)S(1)}, u32[]{:S(2)}, u32[]{:S(2)}) async-start(bf16[4,96,1536]{2,1,0:T(8,128)(2,1)} %wgrad_products.1), calls=%async_computation.2 | async-start | bytes 2359296 | tf_op jit(solution)/shard_map/all_to_all | solution.py:296
  154.4 10.0 %collective-permute-start.12 = (bf16[4,4,192,128]{3,2,1,0:T(8,128)(2,1)}, bf16[4,4,192,128]{3,2,1,0:T(8,128)(2,1)S(1)}, u32[]{:S(2)}, u32[]{:S(2)}) collective-permute-start(bf16[4,4,192,128]{3,2,1,0:T(8,128)(2,1)} %get-tuple-element.41), channel_id=1, source_target_pairs={{0,1},{1,0},{2,3},{3,2},{4,5},{5,4},{6,7},{7,6},{8,9},{9,8},{10,11... | collective-permute-start | bytes 2359304 | tf_op jit(solution)/shard_map/ppermute | solution.py:200
  164.6 36.4 %all-to-all-start.3 = ((bf16[16,32,512]{2,1,0:T(8,128)(2,1)}), bf16[16,32,512]{2,1,0:T(8,128)(2,1)S(1)}, u32[]{:S(2)}, u32[]{:S(2)}) async-start(bf16[16,32,512]{2,1,0:T(8,128)(2,1)} %pick_slots.1), calls=%async_computation.3 | async-start | bytes 1048576 | tf_op jit(solution)/shard_map/all_to_all | solution.py:302
  172.0 11.2 %collective-permute-start.13 = (bf16[4,192,128]{2,1,0:T(8,128)(2,1)S(1)}, bf16[4,192,128]{2,1,0:T(8,128)(2,1)S(1)}, u32[]{:S(2)}, u32[]{:S(2)}) collective-permute-start(bf16[4,192,128]{2,1,0:T(8,128)(2,1)S(1)} %get-tuple-element.47), channel_id=1, source_target_pairs={{0,2},{1,3},{2,4},{3,5},{4,6},{5,7},{6,0},{7,1},{8,10},{9,11},{10,... | collective-permute-start | bytes 589832 | tf_op jit(solution)/shard_map/ppermute | solution.py:206
  175.6 9.9 %collective-permute-start.14 = (bf16[4,192,128]{2,1,0:T(8,128)(2,1)S(1)}, bf16[4,192,128]{2,1,0:T(8,128)(2,1)S(1)}, u32[]{:S(2)}, u32[]{:S(2)}) collective-permute-start(bf16[4,192,128]{2,1,0:T(8,128)(2,1)S(1)} %get-tuple-element.48), channel_id=1, source_target_pairs={{0,4},{1,5},{2,6},{3,7},{4,0},{5,1},{6,2},{7,3},{8,12},{9,13},{10,... | collective-permute-start | bytes 589832 | tf_op jit(solution)/shard_map/ppermute | solution.py:206
  180.5 7.5 %collective-permute-start.15 = (bf16[4,192,128]{2,1,0:T(8,128)(2,1)S(1)}, bf16[4,192,128]{2,1,0:T(8,128)(2,1)S(1)}, u32[]{:S(2)}, u32[]{:S(2)}) collective-permute-start(bf16[4,192,128]{2,1,0:T(8,128)(2,1)S(1)} %get-tuple-element.49), channel_id=1, source_target_pairs={{0,6},{1,7},{2,0},{3,1},{4,2},{5,3},{6,4},{7,5},{8,14},{9,15},{10,... | collective-permute-start | bytes 589832 | tf_op jit(solution)/shard_map/ppermute | solution.py:206
  188.1 8.6 %collective-permute-start.16 = (f32[192,128]{1,0:T(8,128)S(1)}, f32[192,128]{1,0:T(8,128)S(1)}, u32[]{:S(2)}, u32[]{:S(2)}) collective-permute-start(f32[192,128]{1,0:T(8,128)S(1)} %get-tuple-element.51), channel_id=1, source_target_pairs={{0,8},{1,9},{2,10},{3,11},{4,12},{5,13},{6,14},{7,15},{8,16},{9,17... | collective-permute-start | bytes 294920 | tf_op jit(solution)/shard_map/ppermute | solution.py:208
  190.3 7.6 %collective-permute-start.17 = (f32[192,128]{1,0:T(8,128)S(1)}, f32[192,128]{1,0:T(8,128)S(1)}, u32[]{:S(2)}, u32[]{:S(2)}) collective-permute-start(f32[192,128]{1,0:T(8,128)S(1)} %get-tuple-element.52), channel_id=1, source_target_pairs={{0,16},{1,17},{2,18},{3,19},{4,20},{5,21},{6,22},{7,23},{8,24},{9,... | collective-permute-start | bytes 294920 | tf_op jit(solution)/shard_map/ppermute | solution.py:208
  194.5 5.9 %collective-permute-start.18 = (f32[192,128]{1,0:T(8,128)S(1)}, f32[192,128]{1,0:T(8,128)S(1)}, u32[]{:S(2)}, u32[]{:S(2)}) collective-permute-start(f32[192,128]{1,0:T(8,128)S(1)} %get-tuple-element.53), channel_id=1, source_target_pairs={{0,24},{1,25},{2,26},{3,27},{4,28},{5,29},{6,30},{7,31},{8,0},{9,1... | collective-permute-start | bytes 294920 | tf_op jit(solution)/shard_map/ppermute | solution.py:208
  (6 other events, 95.0 us)
Sparse Core Ops, SparseCore 0:
  10.1 134.9 all-gather.3

commit v10 on v9

--- a/solution.py
+++ b/solution.py
@@ -108,39 +108,49 @@
         in_specs=[pl.BlockSpec(memory_space=pltpu.SMEM)]
         + [pl.BlockSpec(memory_space=pltpu.HBM)] * len(args),
         out_specs=pl.BlockSpec(memory_space=pltpu.VMEM),
-        out_shape=jax.ShapeDtypeStruct((NY * NC * piece, n_z * toks), BF),
+        out_shape=pltpu.HBM((NY * NC * piece, n_z * toks), BF),
         scratch_shapes=[pltpu.VMEM(a.shape, BF) for a in args] + [pltpu.SemaphoreType.DMA((len(args),))],
         compiler_params=pltpu.CompilerParams(vmem_limit_bytes=20 * MIB),
         name="line_features",
     )(place, *args)
 
 
-def wgrad_kernel(place, *refs, scale):
-    grad_refs, (feats_ref, out_ref, a_buf) = refs[:NX], refs[NX:]
-    n_z, rows, toks = grad_refs[0].shape
-    for t in range(NX):
+def wgrad_kernel(grad_ref, feats_ref, out_ref, a_buf, b_buf, sems, *, scale):
+    n_x, n_z, rows, toks = grad_ref.shape
+    span = feats_ref.shape[0] // NY
+    parts = [pl.ds(y * span, span) for y in range(NY)]
+    copies = [pltpu.make_async_copy(feats_ref.at[parts[y]], b_buf.at[parts[y]], sems.at[y]) for y in range(NY)]
+    for copy in copies:
+        copy.start()
+    for x in range(n_x):
         for z in range(n_z):
-            a_buf[t * rows : (t + 1) * rows, z * toks : (z + 1) * toks] = grad_refs[t][z]
-    prod = lax.dot_general(
-        a_buf[...], feats_ref[...], (((1,), (1,)), ((), ())), preferred_element_type=F32
-    )
-    prod = (prod * scale).astype(BF)
-    for t in range(NX):
-        out_ref[lax.rem(place[0] - t + NX, NX)] = prod[t * rows : (t + 1) * rows]
-
-
-def wgrad_products(place, grads, feats, scale):
-    n_z, rows, toks = grads[0].shape
+            a_buf[x * rows : (x + 1) * rows, z * toks : (z + 1) * toks] = grad_ref[x, z]
+    for y in range(NY):
+        copies[y].wait()
+        prod = lax.dot_general(
+            a_buf[...], b_buf[parts[y]], (((1,), (1,)), ((), ())), preferred_element_type=F32
+        )
+        prod = (prod * scale).astype(BF)
+        for x in range(n_x):
+            out_ref[x, :, parts[y]] = prod[x * rows : (x + 1) * rows]
+
+
+def wgrad_products(grads, feats, scale):
+    n_x, n_z, rows, toks = grads.shape
     vmem = pl.BlockSpec(memory_space=pltpu.VMEM)
     return pl.pallas_call(
         functools.partial(wgrad_kernel, scale=scale),
-        in_specs=[pl.BlockSpec(memory_space=pltpu.SMEM)] + [vmem] * (NX + 1),
+        in_specs=[vmem, pl.BlockSpec(memory_space=pltpu.HBM)],
         out_specs=vmem,
-        out_shape=pltpu.HBM((NX, rows, feats.shape[0]), BF),
-        scratch_shapes=[pltpu.VMEM((NX * rows, n_z * toks), BF)],
+        out_shape=pltpu.HBM((n_x, rows, feats.shape[0]), BF),
+        scratch_shapes=[
+            pltpu.VMEM((n_x * rows, n_z * toks), BF),
+            pltpu.VMEM(feats.shape, BF),
+            pltpu.SemaphoreType.DMA((NY,)),
+        ],
         compiler_params=pltpu.CompilerParams(vmem_limit_bytes=20 * MIB),
         name="wgrad_products",
-    )(place, *grads, feats)
+    )(grads, in_hbm(feats))
 
 
 def slots_kernel(meta, prod_ref, out_ref, *, chunk, blk):
@@ -252,8 +262,24 @@
     )((group * per_group).reshape(1).astype(jnp.int32), block_mask.T, block_owner.T)
 
 
-def line_x(x):
-    return [x] + [lax.ppermute(x, "col", X_SHIFTS[t]) for t in range(1, NX)]
+def spread_kernel(in_ref, out_ref, sems):
+    copies = [pltpu.make_async_copy(in_ref, out_ref.at[i], sems.at[i]) for i in range(out_ref.shape[0])]
+    for copy in copies:
+        copy.start()
+    for copy in copies:
+        copy.wait()
+
+
+def spread(x, n):
+    return pl.pallas_call(
+        spread_kernel,
+        in_specs=[pl.BlockSpec(memory_space=pltpu.VMEM)],
+        out_specs=pl.BlockSpec(memory_space=pltpu.HBM),
+        out_shape=pltpu.HBM((n, *x.shape), x.dtype),
+        scratch_shapes=[pltpu.SemaphoreType.DMA((n,))],
+        compiler_params=pltpu.CompilerParams(vmem_limit_bytes=4 * MIB),
+        name="spread",
+    )(x)
 
 
 def share_y(x):
@@ -278,8 +304,7 @@
 
     w_all = lax.all_gather(weight_slots[0, 0], "row", axis=0)
     act_t = activations.T
-    wide = jnp.broadcast_to(act_t[None], (groups, piece, toks))
-    act_all = lax.all_to_all(wide, "col", 0, 0, tiled=True).reshape(groups * piece, toks)
+    act_all = lax.all_to_all(spread(act_t, groups), "col", 0, 0, tiled=True).reshape(groups * piece, toks)
     act_z = lax.all_gather(act_t, "row", axis=0)
 
     grad_send = out_grad.T.reshape(-1, owners, chunk, toks).transpose(1, 0, 2, 3)
@@ -287,12 +312,17 @@
     grad_send, act_z, act_all = lax.optimization_barrier((grad_send, act_z, act_all))
     grad_z = lax.all_to_all(grad_send, "row", 0, 0, tiled=True)
     here, before, far_lo, far_hi, after = share_y(act_z)
-    grad_z, far_lo, far_hi, listed, slots = lax.optimization_barrier((grad_z, far_lo, far_hi, listed, slots))
-    act_own = (here, before, far_lo, far_hi, after)
-    act_oth = [lax.ppermute(a, "col", CORE_SWAP) for a in act_own]
+    swap = lambda a: lax.ppermute(a, "col", CORE_SWAP)
+    near_oth = swap(here), swap(before), swap(after)
+    grad_z, far, near_oth, listed, slots = lax.optimization_barrier(
+        (grad_z, (far_lo, far_hi), near_oth, listed, slots)
+    )
+    act_own = here, before, *far, after
+    act_oth = near_oth[0], near_oth[1], swap(far[0]), swap(far[1]), near_oth[2]
+    grad_x = lax.all_to_all(spread(grad_z, NX), "col", 0, 0, tiled=True, axis_index_groups=X_GROUPS)
 
     feats = line_features(place, act_own, act_oth)
-    prods = wgrad_products(place, line_x(grad_z), feats, 1.0 / math.sqrt(toks * owners))
+    prods = wgrad_products(grad_x, feats, 1.0 / math.sqrt(toks * owners))
     prods = lax.all_to_all(prods, "col", 0, 0, tiled=True, axis_index_groups=X_GROUPS)
     slot_parts = pick_slots(slots, prods, chunk, blk)
 

time: 213 us -> 210 us (0.986)
  the two profiles are of different devices: /device:TPU:1 before, /device:TPU:8 now
where the time goes in v10:
time: 210 us; the launch traced here: 209 us
  starting transfers between devices  78.7 us (37%)
  blocking collectives  44 us (21%)
  waiting for transfers between devices  38.1 us (18%)
  Pallas kernels  27.2 us (13%)
  between operations  14.4 us (7%)
  local copies, waits for them, and re-layouts  6.21 us (3%)
    all_gather x1, blocking collectives, per_device(): act_z = lax.all_gather(act_t, 'row', axis=0)  44 us
    ppermute x3, starting transfers between devices, sum_plane(): lax.ppermute(by_y[s], 'col', Y_SHIFTS[s])  10.1 us
    ppermute x5, starting transfers between devices, per_device(): swap = lambda a: lax.ppermute(a, 'col', CORE_SWAP)  10.1 us
    all_to_all x1, starting transfers between devices, per_device(): lax.all_to_all(spread(act_t, groups), 'col', 0, 0, tiled=True)  9.6 us
    all_to_all x1, starting transfers between devices, per_device(): lax.all_to_all(slot_parts, 'row', 0, 0, tiled=True).reshape(1, 1, blk, blk)  9.57 us
    ppermute x3, starting transfers between devices, sum_plane(): lax.ppermute(by_x[t], 'col', X_SHIFTS[t])  9.2 us
    all_to_all x1, waiting for transfers between devices, per_device(): lax.all_to_all(spread(grad_z, NX), 'col', 0, 0, tiled=True, axis_index_gr...  7.84 us
    all_to_all x1, starting transfers between devices, per_device(): grad_z = lax.all_to_all(grad_send, 'row', 0, 0, tiled=True)  7.58 us
  transfers between devices with their start and end apart: 22, of which 11 were waited for; matrix products, arithmetic and copies ran while one was open for 2% of the time, Pallas kernels for 13%

profile of v10, /device:TPU:8, one launch (start us, length us, event | category | flops | bytes accessed | tf_op | source)
XLA Modules:
  0.0 208.7 jit_solution(18202421653956243036)
XLA Ops:
  10.2 9.6 %all-to-all-start = ((bf16[32,192,128]{2,1,0:T(8,128)(2,1)}), bf16[32,192,128]{2,1,0:T(8,128)(2,1)S(1)}, u32[]{:S(2)}, u32[]{:S(2)}) async-start(bf16[32,192,128]{2,1,0:T(8,128)(2,1)} %spread.2), calls=%async_computation | async-start | bytes 3145728 | tf_op jit(solution)/shard_map/all_to_all | solution.py:307
  20.8 44.0 %all-gather = bf16[3072,128]{1,0:T(8,128)(2,1)S(1)} all-gather(bf16[192,128]{1,0:T(8,128)(2,1)S(1)} %bitcast.20), channel_id=2, replica_groups=mesh['row'=16,'col'=32] {'row'}, dimensions={0}, use_global_device_ids=true | all-gather | bytes 835584 | tf_op jit(solution)/shard_map/all_gather | solution.py:308
  66.8 3.9 %collective-permute-start = (bf16[16,192,128]{2,1,0:T(8,128)(2,1)S(1)}, bf16[16,192,128]{2,1,0:T(8,128)(2,1)}, u32[]{:S(2)}, u32[]{:S(2)}) collective-permute-start(bf16[16,192,128]{2,1,0:T(8,128)(2,1)S(1)} %bitcast.23), channel_id=1, source_target_pairs={{0,2},{1,3},{2,4},{3,5},{4,6},{5,7},{6,0},{7,1},{8,10},{9,11},{10,... | collective-permute-start | bytes 2359304 | tf_op jit(solution)/shard_map/ppermute | solution.py:287
  70.7 7.6 %all-to-all-start.1 = ((bf16[16,96,128]{2,1,0:T(8,128)(2,1)}), bf16[16,96,128]{2,1,0:T(8,128)(2,1)S(1)}, u32[]{:S(2)}, u32[]{:S(2)}) async-start(bf16[16,96,128]{2,1,0:T(8,128)(2,1)} %bitcast.3), calls=%async_computation.1 | async-start | bytes 786432 | tf_op jit(solution)/shard_map/all_to_all | solution.py:313
  89.2 4.8 %collective-permute-start.3 = (bf16[8,192,128]{2,1,0:T(8,128)(2,1)}, bf16[8,192,128]{2,1,0:T(8,128)(2,1)S(1)}, u32[]{:S(2)}, u32[]{:S(2)}) collective-permute-start(bf16[8,192,128]{2,1,0:T(8,128)(2,1)} %slice.9), channel_id=1, source_target_pairs={{0,6},{1,7},{2,0},{3,1},{4,2},{5,3},{6,4},{7,5},{8,14},{9,15},{10,... | collective-permute-start | bytes 1179656 | tf_op jit(solution)/shard_map/ppermute | solution.py:290
  97.8 2.3 %layout_tables.1 = (s32[3,9]{1,0:T(4,128)}, s32[3,16]{1,0:T(4,128)}) custom-call(s32[1]{0:T(128)} %bitcast.7.at, s32[12,96]{1,0:T(8,128)} %bitcast.29, s32[12,96]{1,0:T(8,128)} %bitcast.30), custom_call_target="tpu_custom_call" | custom-call | tf_op jit(solution)/shard_map/layout_tables/pallas_call | solution.py:253
  100.1 3.3 %collective-permute-done.3.refs_3_ = bf16[8,192,128]{2,1,0:T(8,128)(2,1)S(1)} collective-permute-done((bf16[8,192,128]{2,1,0:T(8,128)(2,1)}, bf16[8,192,128]{2,1,0:T(8,128)(2,1)S(1)}, u32[]{:S(2)}, u32[]{:S(2)}) %collective-permute-start.3) | collective-permute-done | bytes 393248 | tf_op jit(solution)/shard_map/ppermute | solution.py:290
  103.4 5.9 %collective-permute-done.1.refs_2_ = bf16[8,192,128]{2,1,0:T(8,128)(2,1)} collective-permute-done((bf16[8,192,128]{2,1,0:T(8,128)(2,1)}, bf16[8,192,128]{2,1,0:T(8,128)(2,1)}, u32[]{:S(2)}, u32[]{:S(2)}) %collective-permute-start.1) | collective-permute-done | bytes 393248 | tf_op jit(solution)/shard_map/ppermute | solution.py:289
  110.5 4.3 %all-to-all-start.2 = ((bf16[4,16,96,128]{3,2,1,0:T(8,128)(2,1)}), bf16[4,16,96,128]{3,2,1,0:T(8,128)(2,1)S(1)}, u32[]{:S(2)}, u32[]{:S(2)}) async-start(bf16[4,16,96,128]{3,2,1,0:T(8,128)(2,1)} %spread.3), calls=%async_computation.2 | async-start | bytes 3145728 | tf_op jit(solution)/shard_map/all_to_all | solution.py:322
  116.7 2.4 %collective-permute-start.8 = (bf16[8,192,128]{2,1,0:T(8,128)(2,1)}, bf16[8,192,128]{2,1,0:T(8,128)(2,1)}, u32[]{:S(2)}, u32[]{:S(2)}) collective-permute-start(bf16[8,192,128]{2,1,0:T(8,128)(2,1)} %copy-done.7), channel_id=1, source_target_pairs={{0,1},{1,0},{2,3},{3,2},{4,5},{5,4},{6,7},{7,6},{8,9},{9,8},{10,11... | collective-permute-start | bytes 1179656 | tf_op jit(solution)/shard_map/ppermute | solution.py:315
  120.8 6.4 %line_features.1.feats_ref = bf16[1536,2048]{1,0:T(8,128)(2,1)} custom-call(s32[3]{0:T(128)S(1)} %pad_add_fusion.place, bf16[16,192,128]{2,1,0:T(8,128)(2,1)} %bitcast.25, bf16[16,192,128]{2,1,0:T(8,128)(2,1)} %collective-permute-done.refs_1_, bf16[8,192,128]{2,1,0:T(8,128)(2,1)} %collective-permute-done.1.refs_2_, bf16[8,192,128]{2,1,0:T(8,128)(2,1)} %copy-done.7, ...), custom_call_target="tpu_custom_call" | custom-call | tf_op jit(solution)/shard_map/line_features/pallas_call | solution.py:106
  127.2 7.8 %all-to-all-done.2.grad_ref = bf16[4,16,96,128]{3,2,1,0:T(8,128)(2,1)S(1)} async-done(((bf16[4,16,96,128]{3,2,1,0:T(8,128)(2,1)}), bf16[4,16,96,128]{3,2,1,0:T(8,128)(2,1)S(1)}, u32[]{:S(2)}, u32[]{:S(2)}) %all-to-all-start.2) | async-done | bytes 1572896 | tf_op jit(solution)/shard_map/all_to_all | solution.py:322
  135.1 6.5 %wgrad_products.1 = bf16[4,96,1536]{2,1,0:T(8,128)(2,1)} custom-call(bf16[4,16,96,128]{3,2,1,0:T(8,128)(2,1)S(1)} %all-to-all-done.2.grad_ref, bf16[1536,2048]{1,0:T(8,128)(2,1)} %line_features.1.feats_ref), custom_call_target="tpu_custom_call" | custom-call | tf_op jit(solution)/shard_map/wgrad_products/pallas_call | solution.py:141
  141.6 3.5 %all-to-all-start.3 = ((bf16[4,96,1536]{2,1,0:T(8,128)(2,1)}), bf16[4,96,1536]{2,1,0:T(8,128)(2,1)S(1)}, u32[]{:S(2)}, u32[]{:S(2)}) async-start(bf16[4,96,1536]{2,1,0:T(8,128)(2,1)} %wgrad_products.1), calls=%async_computation.3 | async-start | bytes 2359296 | tf_op jit(solution)/shard_map/all_to_all | solution.py:326
  145.2 6.9 %tokens_step.1 = (bf16[128,1536]{1,0:T(8,128)(2,1)}, bf16[4,4,192,128]{3,2,1,0:T(8,128)(2,1)}, bf16[4,4,192,128]{3,2,1,0:T(8,128)(2,1)}) custom-call(s32[3,9]{1,0:T(4,128)S(1)} %copy-done.5, s32[3]{0:T(128)S(1)} %pad_add_fusion.place, bf16[6144,128]{1,0:T(8,128)(2,1)S(1)} %bitcast.18, bf16[128,1536]{1,0:T(8,128)(2,1)S(1)} %copy-done, ...), custom_call_target="tpu_custom_call" | custom-call | tf_op jit(solution)/shard_map/tokens_step/pallas_call | solution.py:64
  154.2 6.1 %all-to-all-done.3.prod_ref = bf16[4,96,1536]{2,1,0:T(8,128)(2,1)S(1)} async-done(((bf16[4,96,1536]{2,1,0:T(8,128)(2,1)}), bf16[4,96,1536]{2,1,0:T(8,128)(2,1)S(1)}, u32[]{:S(2)}, u32[]{:S(2)}) %all-to-all-start.3) | async-done | bytes 1179680 | tf_op jit(solution)/shard_map/all_to_all | solution.py:326
  162.0 9.6 %all-to-all-start.4 = ((bf16[16,32,512]{2,1,0:T(8,128)(2,1)}), bf16[16,32,512]{2,1,0:T(8,128)(2,1)S(1)}, u32[]{:S(2)}, u32[]{:S(2)}) async-start(bf16[16,32,512]{2,1,0:T(8,128)(2,1)} %pick_slots.1), calls=%async_computation.4 | async-start | bytes 1048576 | tf_op jit(solution)/shard_map/all_to_all | solution.py:332
  173.5 6.3 %collective-permute-start.11 = (bf16[4,192,128]{2,1,0:T(8,128)(2,1)S(1)}, bf16[4,192,128]{2,1,0:T(8,128)(2,1)S(1)}, u32[]{:S(2)}, u32[]{:S(2)}) collective-permute-start(bf16[4,192,128]{2,1,0:T(8,128)(2,1)S(1)} %get-tuple-element.54), channel_id=1, source_target_pairs={{0,4},{1,5},{2,6},{3,7},{4,0},{5,1},{6,2},{7,3},{8,12},{9,13},{10,... | collective-permute-start | bytes 589832 | tf_op jit(solution)/shard_map/ppermute | solution.py:216
  181.7 2.4 %collective-permute-done.11.refs_2_ = bf16[4,192,128]{2,1,0:T(8,128)(2,1)S(1)} collective-permute-done((bf16[4,192,128]{2,1,0:T(8,128)(2,1)S(1)}, bf16[4,192,128]{2,1,0:T(8,128)(2,1)S(1)}, u32[]{:S(2)}, u32[]{:S(2)}) %collective-permute-start.11) | collective-permute-done | bytes 196640 | tf_op jit(solution)/shard_map/ppermute | solution.py:216
  184.1 3.2 %collective-permute-done.12.refs_3_ = bf16[4,192,128]{2,1,0:T(8,128)(2,1)S(1)} collective-permute-done((bf16[4,192,128]{2,1,0:T(8,128)(2,1)S(1)}, bf16[4,192,128]{2,1,0:T(8,128)(2,1)S(1)}, u32[]{:S(2)}, u32[]{:S(2)}) %collective-permute-start.12) | collective-permute-done | bytes 196640 | tf_op jit(solution)/shard_map/ppermute | solution.py:216
  187.4 2.5 %collective-permute-start.13 = (f32[192,128]{1,0:T(8,128)S(1)}, f32[192,128]{1,0:T(8,128)S(1)}, u32[]{:S(2)}, u32[]{:S(2)}) collective-permute-start(f32[192,128]{1,0:T(8,128)S(1)} %get-tuple-element.57), channel_id=1, source_target_pairs={{0,8},{1,9},{2,10},{3,11},{4,12},{5,13},{6,14},{7,15},{8,16},{9,17... | collective-permute-start | bytes 294920 | tf_op jit(solution)/shard_map/ppermute | solution.py:218
  189.9 4.0 %collective-permute-start.14 = (f32[192,128]{1,0:T(8,128)S(1)}, f32[192,128]{1,0:T(8,128)S(1)}, u32[]{:S(2)}, u32[]{:S(2)}) collective-permute-start(f32[192,128]{1,0:T(8,128)S(1)} %get-tuple-element.58), channel_id=1, source_target_pairs={{0,16},{1,17},{2,18},{3,19},{4,20},{5,21},{6,22},{7,23},{8,24},{9,... | collective-permute-start | bytes 294920 | tf_op jit(solution)/shard_map/ppermute | solution.py:218
  193.9 2.8 %collective-permute-start.15 = (f32[192,128]{1,0:T(8,128)S(1)}, f32[192,128]{1,0:T(8,128)S(1)}, u32[]{:S(2)}, u32[]{:S(2)}) collective-permute-start(f32[192,128]{1,0:T(8,128)S(1)} %get-tuple-element.59), channel_id=1, source_target_pairs={{0,24},{1,25},{2,26},{3,27},{4,28},{5,29},{6,30},{7,31},{8,0},{9,1... | collective-permute-start | bytes 294920 | tf_op jit(solution)/shard_map/ppermute | solution.py:218
  197.9 2.5 %collective-permute-done.15.refs_3_ = f32[192,128]{1,0:T(8,128)S(1)} collective-permute-done((f32[192,128]{1,0:T(8,128)S(1)}, f32[192,128]{1,0:T(8,128)S(1)}, u32[]{:S(2)}, u32[]{:S(2)}) %collective-permute-start.15) | collective-permute-done | bytes 98336 | tf_op jit(solution)/shard_map/ppermute | solution.py:218
  (54 shorter events, 35.7 us)
Async XLA Ops:
  7.2 138.0 %all-gather.4.cloned.1.call-start = ((), (), s32[]{:S(2)}) async-start(), calls=%async_computation.5 | async-start | bytes 8912896 | tf_op jit(solution)/shard_map/all_gather | solution.py:305
  10.2 54.7 %all-to-all-start = ((bf16[32,192,128]{2,1,0:T(8,128)(2,1)}), bf16[32,192,128]{2,1,0:T(8,128)(2,1)S(1)}, u32[]{:S(2)}, u32[]{:S(2)}) async-start(bf16[32,192,128]{2,1,0:T(8,128)(2,1)} %spread.2), calls=%async_computation | async-start | bytes 3145728 | tf_op jit(solution)/shard_map/all_to_all | solution.py:307
  64.8 45.7 %copy-start.6 = (bf16[3072,128]{1,0:T(8,128)(2,1)}, bf16[3072,128]{1,0:T(8,128)(2,1)S(1)}, u32[]{:S(2)}) copy-start(bf16[3072,128]{1,0:T(8,128)(2,1)S(1)} %all-gather) | copy-start | bytes 2359300
  64.9 17.5 %collective-permute-start.2 = (bf16[16,192,128]{2,1,0:T(8,128)(2,1)S(1)}, bf16[16,192,128]{2,1,0:T(8,128)(2,1)}, u32[]{:S(2)}, u32[]{:S(2)}) collective-permute-start(bf16[16,192,128]{2,1,0:T(8,128)(2,1)S(1)} %bitcast.22), channel_id=1, source_target_pairs={{0,6},{1,7},{2,0},{3,1},{4,2},{5,3},{6,4},{7,5},{8,14},{9,15},{10,... | collective-permute-start | bytes 2359304 | tf_op jit(solution)/shard_map/ppermute | solution.py:288
  66.8 18.7 %collective-permute-start = (bf16[16,192,128]{2,1,0:T(8,128)(2,1)S(1)}, bf16[16,192,128]{2,1,0:T(8,128)(2,1)}, u32[]{:S(2)}, u32[]{:S(2)}) collective-permute-start(bf16[16,192,128]{2,1,0:T(8,128)(2,1)S(1)} %bitcast.23), channel_id=1, source_target_pairs={{0,2},{1,3},{2,4},{3,5},{4,6},{5,7},{6,0},{7,1},{8,10},{9,11},{10,... | collective-permute-start | bytes 2359304 | tf_op jit(solution)/shard_map/ppermute | solution.py:287
  70.7 38.6 %all-to-all-start.1 = ((bf16[16,96,128]{2,1,0:T(8,128)(2,1)}), bf16[16,96,128]{2,1,0:T(8,128)(2,1)S(1)}, u32[]{:S(2)}, u32[]{:S(2)}) async-start(bf16[16,96,128]{2,1,0:T(8,128)(2,1)} %bitcast.3), calls=%async_computation.1 | async-start | bytes 786432 | tf_op jit(solution)/shard_map/all_to_all | solution.py:313
  78.3 21.8 %collective-permute-start.4 = (bf16[16,192,128]{2,1,0:T(8,128)(2,1)S(1)}, bf16[16,192,128]{2,1,0:T(8,128)(2,1)}, u32[]{:S(2)}, u32[]{:S(2)}) collective-permute-start(bf16[16,192,128]{2,1,0:T(8,128)(2,1)S(1)} %bitcast.24), channel_id=1, source_target_pairs={{0,1},{1,0},{2,3},{3,2},{4,5},{5,4},{6,7},{7,6},{8,9},{9,8},{10,11... | collective-permute-start | bytes 2359304 | tf_op jit(solution)/shard_map/ppermute | solution.py:315
  82.4 27.0 %collective-permute-start.6 = (bf16[16,192,128]{2,1,0:T(8,128)(2,1)}, bf16[16,192,128]{2,1,0:T(8,128)(2,1)}, u32[]{:S(2)}, u32[]{:S(2)}) collective-permute-start(bf16[16,192,128]{2,1,0:T(8,128)(2,1)} %collective-permute-done.2.refs_4_), channel_id=1, source_target_pairs={{0,1},{1,0},{2,3},{3,2},{4,5},{5,4},{6,7},{7,6},{8,9},{9,8},{10,11... | collective-permute-start | bytes 2359304 | tf_op jit(solution)/shard_map/ppermute | solution.py:315
  85.5 23.8 %collective-permute-start.5 = (bf16[16,192,128]{2,1,0:T(8,128)(2,1)}, bf16[16,192,128]{2,1,0:T(8,128)(2,1)}, u32[]{:S(2)}, u32[]{:S(2)}) collective-permute-start(bf16[16,192,128]{2,1,0:T(8,128)(2,1)} %collective-permute-done.refs_1_), channel_id=1, source_target_pairs={{0,1},{1,0},{2,3},{3,2},{4,5},{5,4},{6,7},{7,6},{8,9},{9,8},{10,11... | collective-permute-start | bytes 2359304 | tf_op jit(solution)/shard_map/ppermute | solution.py:315
  89.2 14.2 %collective-permute-start.3 = (bf16[8,192,128]{2,1,0:T(8,128)(2,1)}, bf16[8,192,128]{2,1,0:T(8,128)(2,1)S(1)}, u32[]{:S(2)}, u32[]{:S(2)}) collective-permute-start(bf16[8,192,128]{2,1,0:T(8,128)(2,1)} %slice.9), channel_id=1, source_target_pairs={{0,6},{1,7},{2,0},{3,1},{4,2},{5,3},{6,4},{7,5},{8,14},{9,15},{10,... | collective-permute-start | bytes 1179656 | tf_op jit(solution)/shard_map/ppermute | solution.py:290
  95.9 13.4 %collective-permute-start.1 = (bf16[8,192,128]{2,1,0:T(8,128)(2,1)}, bf16[8,192,128]{2,1,0:T(8,128)(2,1)}, u32[]{:S(2)}, u32[]{:S(2)}) collective-permute-start(bf16[8,192,128]{2,1,0:T(8,128)(2,1)} %slice.8), channel_id=1, source_target_pairs={{0,2},{1,3},{2,4},{3,5},{4,6},{5,7},{6,0},{7,1},{8,10},{9,11},{10,... | collective-permute-start | bytes 1179656 | tf_op jit(solution)/shard_map/ppermute | solution.py:289
  110.5 24.6 %all-to-all-start.2 = ((bf16[4,16,96,128]{3,2,1,0:T(8,128)(2,1)}), bf16[4,16,96,128]{3,2,1,0:T(8,128)(2,1)S(1)}, u32[]{:S(2)}, u32[]{:S(2)}) async-start(bf16[4,16,96,128]{3,2,1,0:T(8,128)(2,1)} %spread.3), calls=%async_computation.2 | async-start | bytes 3145728 | tf_op jit(solution)/shard_map/all_to_all | solution.py:322
  114.8 4.5 %collective-permute-start.7 = (bf16[8,192,128]{2,1,0:T(8,128)(2,1)}, bf16[8,192,128]{2,1,0:T(8,128)(2,1)}, u32[]{:S(2)}, u32[]{:S(2)}) collective-permute-start(bf16[8,192,128]{2,1,0:T(8,128)(2,1)} %collective-permute-done.1.refs_2_), channel_id=1, source_target_pairs={{0,1},{1,0},{2,3},{3,2},{4,5},{5,4},{6,7},{7,6},{8,9},{9,8},{10,11... | collective-permute-start | bytes 1179656 | tf_op jit(solution)/shard_map/ppermute | solution.py:315
  116.7 4.1 %collective-permute-start.8 = (bf16[8,192,128]{2,1,0:T(8,128)(2,1)}, bf16[8,192,128]{2,1,0:T(8,128)(2,1)}, u32[]{:S(2)}, u32[]{:S(2)}) collective-permute-start(bf16[8,192,128]{2,1,0:T(8,128)(2,1)} %copy-done.7), channel_id=1, source_target_pairs={{0,1},{1,0},{2,3},{3,2},{4,5},{5,4},{6,7},{7,6},{8,9},{9,8},{10,11... | collective-permute-start | bytes 1179656 | tf_op jit(solution)/shard_map/ppermute | solution.py:315
  141.6 18.6 %all-to-all-start.3 = ((bf16[4,96,1536]{2,1,0:T(8,128)(2,1)}), bf16[4,96,1536]{2,1,0:T(8,128)(2,1)S(1)}, u32[]{:S(2)}, u32[]{:S(2)}) async-start(bf16[4,96,1536]{2,1,0:T(8,128)(2,1)} %wgrad_products.1), calls=%async_computation.3 | async-start | bytes 2359296 | tf_op jit(solution)/shard_map/all_to_all | solution.py:326
  145.2 15.1 %copy-start.4 = (s32[3,16]{1,0:T(4,128)S(1)}, s32[3,16]{1,0:T(4,128)}, u32[]{:S(2)}) copy-start(s32[3,16]{1,0:T(4,128)} %get-tuple-element.39.meta) | copy-start | bytes 580
  152.1 9.6 %collective-permute-start.9 = (bf16[4,4,192,128]{3,2,1,0:T(8,128)(2,1)}, bf16[4,4,192,128]{3,2,1,0:T(8,128)(2,1)S(1)}, u32[]{:S(2)}, u32[]{:S(2)}) collective-permute-start(bf16[4,4,192,128]{3,2,1,0:T(8,128)(2,1)} %get-tuple-element.47), channel_id=1, source_target_pairs={{0,1},{1,0},{2,3},{3,2},{4,5},{5,4},{6,7},{7,6},{8,9},{9,8},{10,11... | collective-permute-start | bytes 2359304 | tf_op jit(solution)/shard_map/ppermute | solution.py:210
  162.0 39.1 %all-to-all-start.4 = ((bf16[16,32,512]{2,1,0:T(8,128)(2,1)}), bf16[16,32,512]{2,1,0:T(8,128)(2,1)S(1)}, u32[]{:S(2)}, u32[]{:S(2)}) async-start(bf16[16,32,512]{2,1,0:T(8,128)(2,1)} %pick_slots.1), calls=%async_computation.4 | async-start | bytes 1048576 | tf_op jit(solution)/shard_map/all_to_all | solution.py:332
  171.5 10.2 %collective-permute-start.10 = (bf16[4,192,128]{2,1,0:T(8,128)(2,1)S(1)}, bf16[4,192,128]{2,1,0:T(8,128)(2,1)S(1)}, u32[]{:S(2)}, u32[]{:S(2)}) collective-permute-start(bf16[4,192,128]{2,1,0:T(8,128)(2,1)S(1)} %get-tuple-element.53), channel_id=1, source_target_pairs={{0,2},{1,3},{2,4},{3,5},{4,6},{5,7},{6,0},{7,1},{8,10},{9,11},{10,... | collective-permute-start | bytes 589832 | tf_op jit(solution)/shard_map/ppermute | solution.py:216
  173.5 10.7 %collective-permute-start.11 = (bf16[4,192,128]{2,1,0:T(8,128)(2,1)S(1)}, bf16[4,192,128]{2,1,0:T(8,128)(2,1)S(1)}, u32[]{:S(2)}, u32[]{:S(2)}) collective-permute-start(bf16[4,192,128]{2,1,0:T(8,128)(2,1)S(1)} %get-tuple-element.54), channel_id=1, source_target_pairs={{0,4},{1,5},{2,6},{3,7},{4,0},{5,1},{6,2},{7,3},{8,12},{9,13},{10,... | collective-permute-start | bytes 589832 | tf_op jit(solution)/shard_map/ppermute | solution.py:216
  179.8 7.6 %collective-permute-start.12 = (bf16[4,192,128]{2,1,0:T(8,128)(2,1)S(1)}, bf16[4,192,128]{2,1,0:T(8,128)(2,1)S(1)}, u32[]{:S(2)}, u32[]{:S(2)}) collective-permute-start(bf16[4,192,128]{2,1,0:T(8,128)(2,1)S(1)} %get-tuple-element.55), channel_id=1, source_target_pairs={{0,6},{1,7},{2,0},{3,1},{4,2},{5,3},{6,4},{7,5},{8,14},{9,15},{10,... | collective-permute-start | bytes 589832 | tf_op jit(solution)/shard_map/ppermute | solution.py:216
  187.4 9.2 %collective-permute-start.13 = (f32[192,128]{1,0:T(8,128)S(1)}, f32[192,128]{1,0:T(8,128)S(1)}, u32[]{:S(2)}, u32[]{:S(2)}) collective-permute-start(f32[192,128]{1,0:T(8,128)S(1)} %get-tuple-element.57), channel_id=1, source_target_pairs={{0,8},{1,9},{2,10},{3,11},{4,12},{5,13},{6,14},{7,15},{8,16},{9,17... | collective-permute-start | bytes 294920 | tf_op jit(solution)/shard_map/ppermute | solution.py:218
  189.9 8.0 %collective-permute-start.14 = (f32[192,128]{1,0:T(8,128)S(1)}, f32[192,128]{1,0:T(8,128)S(1)}, u32[]{:S(2)}, u32[]{:S(2)}) collective-permute-start(f32[192,128]{1,0:T(8,128)S(1)} %get-tuple-element.58), channel_id=1, source_target_pairs={{0,16},{1,17},{2,18},{3,19},{4,20},{5,21},{6,22},{7,23},{8,24},{9,... | collective-permute-start | bytes 294920 | tf_op jit(solution)/shard_map/ppermute | solution.py:218
  193.9 6.5 %collective-permute-start.15 = (f32[192,128]{1,0:T(8,128)S(1)}, f32[192,128]{1,0:T(8,128)S(1)}, u32[]{:S(2)}, u32[]{:S(2)}) collective-permute-start(f32[192,128]{1,0:T(8,128)S(1)} %get-tuple-element.59), channel_id=1, source_target_pairs={{0,24},{1,25},{2,26},{3,27},{4,28},{5,29},{6,30},{7,31},{8,0},{9,1... | collective-permute-start | bytes 294920 | tf_op jit(solution)/shard_map/ppermute | solution.py:218
  (6 other events, 31.8 us)
Sparse Core Ops, SparseCore 0:
  10.1 134.0 all-gather.3

commit v11 on v10

--- a/solution.py
+++ b/solution.py
@@ -117,22 +117,23 @@
 
 def wgrad_kernel(grad_ref, feats_ref, out_ref, a_buf, b_buf, sems, *, scale):
     n_x, n_z, rows, toks = grad_ref.shape
-    span = feats_ref.shape[0] // NY
-    parts = [pl.ds(y * span, span) for y in range(NY)]
-    copies = [pltpu.make_async_copy(feats_ref.at[parts[y]], b_buf.at[parts[y]], sems.at[y]) for y in range(NY)]
+    steps = sems.shape[0]
+    span = feats_ref.shape[0] // steps
+    parts = [pl.ds(i * span, span) for i in range(steps)]
+    copies = [pltpu.make_async_copy(feats_ref.at[parts[i]], b_buf.at[parts[i]], sems.at[i]) for i in range(steps)]
     for copy in copies:
         copy.start()
     for x in range(n_x):
         for z in range(n_z):
             a_buf[x * rows : (x + 1) * rows, z * toks : (z + 1) * toks] = grad_ref[x, z]
-    for y in range(NY):
-        copies[y].wait()
+    for i in range(steps):
+        copies[i].wait()
         prod = lax.dot_general(
-            a_buf[...], b_buf[parts[y]], (((1,), (1,)), ((), ())), preferred_element_type=F32
+            a_buf[...], b_buf[parts[i]], (((1,), (1,)), ((), ())), preferred_element_type=F32
         )
         prod = (prod * scale).astype(BF)
         for x in range(n_x):
-            out_ref[x, :, parts[y]] = prod[x * rows : (x + 1) * rows]
+            out_ref[x, :, parts[i]] = prod[x * rows : (x + 1) * rows]
 
 
 def wgrad_products(grads, feats, scale):
@@ -146,7 +147,7 @@
         scratch_shapes=[
             pltpu.VMEM((n_x * rows, n_z * toks), BF),
             pltpu.VMEM(feats.shape, BF),
-            pltpu.SemaphoreType.DMA((NY,)),
+            pltpu.SemaphoreType.DMA((3,)),
         ],
         compiler_params=pltpu.CompilerParams(vmem_limit_bytes=20 * MIB),
         name="wgrad_products",
@@ -312,13 +313,9 @@
     grad_send, act_z, act_all = lax.optimization_barrier((grad_send, act_z, act_all))
     grad_z = lax.all_to_all(grad_send, "row", 0, 0, tiled=True)
     here, before, far_lo, far_hi, after = share_y(act_z)
-    swap = lambda a: lax.ppermute(a, "col", CORE_SWAP)
-    near_oth = swap(here), swap(before), swap(after)
-    grad_z, far, near_oth, listed, slots = lax.optimization_barrier(
-        (grad_z, (far_lo, far_hi), near_oth, listed, slots)
-    )
-    act_own = here, before, *far, after
-    act_oth = near_oth[0], near_oth[1], swap(far[0]), swap(far[1]), near_oth[2]
+    grad_z, far_lo, far_hi, listed, slots = lax.optimization_barrier((grad_z, far_lo, far_hi, listed, slots))
+    act_own = here, before, far_lo, far_hi, after
+    act_oth = [lax.ppermute(a, "col", CORE_SWAP) for a in act_own]
     grad_x = lax.all_to_all(spread(grad_z, NX), "col", 0, 0, tiled=True, axis_index_groups=X_GROUPS)
 
     feats = line_features(place, act_own, act_oth)

time: 210 us -> 209 us (level)
  the two profiles are of different devices: /device:TPU:8 before, /device:TPU:1 now
where the time goes in v11:
time: 209 us; the launch traced here: 205 us
  starting transfers between devices  90.2 us (43%)
  blocking collectives  39.5 us (19%)
  waiting for transfers between devices  30 us (14%)
  Pallas kernels  26.3 us (13%)
  between operations  14.4 us (7%)
  local copies, waits for them, and re-layouts  4.49 us (2%)
    all_gather x1, blocking collectives, per_device(): act_z = lax.all_gather(act_t, 'row', axis=0)  39.5 us
    ppermute x5, starting transfers between devices, per_device(): act_oth = [lax.ppermute(a, 'col', CORE_SWAP) for a in act_own]  18.3 us
    all_to_all x1, starting transfers between devices, per_device(): lax.all_to_all(slot_parts, 'row', 0, 0, tiled=True).reshape(1, 1, blk, blk)  11.4 us
    all_to_all x1, starting transfers between devices, per_device(): lax.all_to_all(spread(act_t, groups), 'col', 0, 0, tiled=True)  10.6 us
    ppermute x3, starting transfers between devices, sum_plane(): lax.ppermute(by_y[s], 'col', Y_SHIFTS[s])  10.3 us
    ppermute x1, waiting for transfers between devices, share_y(): before = lax.ppermute(x, 'col', Y_SHIFTS[1])  10.3 us
    ppermute x3, starting transfers between devices, sum_plane(): lax.ppermute(by_x[t], 'col', X_SHIFTS[t])  8.41 us
    all_to_all x1, starting transfers between devices, per_device(): grad_z = lax.all_to_all(grad_send, 'row', 0, 0, tiled=True)  6.92 us
  transfers between devices with their start and end apart: 22, of which 10 were waited for; matrix products, arithmetic and copies ran while one was open for 1% of the time, Pallas kernels for 13%

profile of v11, /device:TPU:1, one launch (start us, length us, event | category | flops | bytes accessed | tf_op | source)
XLA Modules:
  0.0 205.0 jit_solution(17891114497579080434)
XLA Ops:
  10.1 10.6 %all-to-all-start = ((bf16[32,192,128]{2,1,0:T(8,128)(2,1)}), bf16[32,192,128]{2,1,0:T(8,128)(2,1)S(1)}, u32[]{:S(2)}, u32[]{:S(2)}) async-start(bf16[32,192,128]{2,1,0:T(8,128)(2,1)} %spread.2), calls=%async_computation | async-start | bytes 3145728 | tf_op jit(solution)/shard_map/all_to_all | solution.py:308
  21.8 39.5 %all-gather = bf16[3072,128]{1,0:T(8,128)(2,1)S(1)} all-gather(bf16[192,128]{1,0:T(8,128)(2,1)S(1)} %bitcast.20), channel_id=2, replica_groups=mesh['row'=16,'col'=32] {'row'}, dimensions={0}, use_global_device_ids=true | all-gather | bytes 835584 | tf_op jit(solution)/shard_map/all_gather | solution.py:309
  61.4 6.9 %all-to-all-start.1 = ((bf16[16,96,128]{2,1,0:T(8,128)(2,1)}), bf16[16,96,128]{2,1,0:T(8,128)(2,1)S(1)}, u32[]{:S(2)}, u32[]{:S(2)}) async-start(bf16[16,96,128]{2,1,0:T(8,128)(2,1)} %bitcast.3), calls=%async_computation.1 | async-start | bytes 786432 | tf_op jit(solution)/shard_map/all_to_all | solution.py:314
  68.3 3.3 %collective-permute-start = (bf16[16,192,128]{2,1,0:T(8,128)(2,1)S(1)}, bf16[16,192,128]{2,1,0:T(8,128)(2,1)S(1)}, u32[]{:S(2)}, u32[]{:S(2)}) collective-permute-start(bf16[16,192,128]{2,1,0:T(8,128)(2,1)S(1)} %bitcast.22), channel_id=1, source_target_pairs={{0,2},{1,3},{2,4},{3,5},{4,6},{5,7},{6,0},{7,1},{8,10},{9,11},{10,... | collective-permute-start | bytes 2359304 | tf_op jit(solution)/shard_map/ppermute | solution.py:288
  71.6 3.2 %collective-permute-start.2 = (bf16[16,192,128]{2,1,0:T(8,128)(2,1)S(1)}, bf16[16,192,128]{2,1,0:T(8,128)(2,1)S(1)}, u32[]{:S(2)}, u32[]{:S(2)}) collective-permute-start(bf16[16,192,128]{2,1,0:T(8,128)(2,1)S(1)} %bitcast.23), channel_id=1, source_target_pairs={{0,6},{1,7},{2,0},{3,1},{4,2},{5,3},{6,4},{7,5},{8,14},{9,15},{10,... | collective-permute-start | bytes 2359304 | tf_op jit(solution)/shard_map/ppermute | solution.py:289
  74.8 10.3 %collective-permute-done.refs_1_ = bf16[16,192,128]{2,1,0:T(8,128)(2,1)S(1)} collective-permute-done((bf16[16,192,128]{2,1,0:T(8,128)(2,1)S(1)}, bf16[16,192,128]{2,1,0:T(8,128)(2,1)S(1)}, u32[]{:S(2)}, u32[]{:S(2)}) %collective-permute-start) | collective-permute-done | bytes 786464 | tf_op jit(solution)/shard_map/ppermute | solution.py:288
  88.9 4.5 %collective-permute-start.3 = (bf16[8,192,128]{2,1,0:T(8,128)(2,1)}, bf16[8,192,128]{2,1,0:T(8,128)(2,1)}, u32[]{:S(2)}, u32[]{:S(2)}) collective-permute-start(bf16[8,192,128]{2,1,0:T(8,128)(2,1)} %slice.9), channel_id=1, source_target_pairs={{0,6},{1,7},{2,0},{3,1},{4,2},{5,3},{6,4},{7,5},{8,14},{9,15},{10,... | collective-permute-start | bytes 1179656 | tf_op jit(solution)/shard_map/ppermute | solution.py:291
  93.5 2.3 %layout_tables.1 = (s32[3,9]{1,0:T(4,128)}, s32[3,16]{1,0:T(4,128)}) custom-call(s32[1]{0:T(128)} %bitcast.7.at, s32[12,96]{1,0:T(8,128)} %bitcast.29, s32[12,96]{1,0:T(8,128)} %bitcast.30), custom_call_target="tpu_custom_call" | custom-call | tf_op jit(solution)/shard_map/layout_tables/pallas_call | solution.py:254
  99.7 4.0 %all-to-all-start.2 = ((bf16[4,16,96,128]{3,2,1,0:T(8,128)(2,1)}), bf16[4,16,96,128]{3,2,1,0:T(8,128)(2,1)S(1)}, u32[]{:S(2)}, u32[]{:S(2)}) async-start(bf16[4,16,96,128]{3,2,1,0:T(8,128)(2,1)} %spread.3), calls=%async_computation.2 | async-start | bytes 3145728 | tf_op jit(solution)/shard_map/all_to_all | solution.py:319
  103.7 9.7 %collective-permute-start.4 = (bf16[16,192,128]{2,1,0:T(8,128)(2,1)}, bf16[16,192,128]{2,1,0:T(8,128)(2,1)}, u32[]{:S(2)}, u32[]{:S(2)}) collective-permute-start(bf16[16,192,128]{2,1,0:T(8,128)(2,1)} %bitcast.24), channel_id=1, source_target_pairs={{0,1},{1,0},{2,3},{3,2},{4,5},{5,4},{6,7},{7,6},{8,9},{9,8},{10,11... | collective-permute-start | bytes 2359304 | tf_op jit(solution)/shard_map/ppermute | solution.py:318
  115.4 2.4 %collective-permute-start.8 = (bf16[16,192,128]{2,1,0:T(8,128)(2,1)}, bf16[16,192,128]{2,1,0:T(8,128)(2,1)}, u32[]{:S(2)}, u32[]{:S(2)}) collective-permute-start(bf16[16,192,128]{2,1,0:T(8,128)(2,1)} %copy-done.8), channel_id=1, source_target_pairs={{0,1},{1,0},{2,3},{3,2},{4,5},{5,4},{6,7},{7,6},{8,9},{9,8},{10,11... | collective-permute-start | bytes 2359304 | tf_op jit(solution)/shard_map/ppermute | solution.py:318
  119.7 2.4 %collective-permute-start.7 = (bf16[8,192,128]{2,1,0:T(8,128)(2,1)}, bf16[8,192,128]{2,1,0:T(8,128)(2,1)}, u32[]{:S(2)}, u32[]{:S(2)}) collective-permute-start(bf16[8,192,128]{2,1,0:T(8,128)(2,1)} %collective-permute-done.3.refs_3_), channel_id=1, source_target_pairs={{0,1},{1,0},{2,3},{3,2},{4,5},{5,4},{6,7},{7,6},{8,9},{9,8},{10,11... | collective-permute-start | bytes 1179656 | tf_op jit(solution)/shard_map/ppermute | solution.py:318
  123.8 6.4 %line_features.1.feats_ref = bf16[1536,2048]{1,0:T(8,128)(2,1)} custom-call(s32[3]{0:T(128)S(1)} %pad_add_fusion.place, bf16[16,192,128]{2,1,0:T(8,128)(2,1)} %bitcast.25, bf16[16,192,128]{2,1,0:T(8,128)(2,1)} %copy-done.7, bf16[8,192,128]{2,1,0:T(8,128)(2,1)} %copy-done.9, bf16[8,192,128]{2,1,0:T(8,128)(2,1)} %collective-permute-done.3.refs_3_, ...), custom_call_target="tpu_custom_call" | custom-call | tf_op jit(solution)/shard_map/line_features/pallas_call | solution.py:106
  130.2 5.7 %wgrad_products.1 = bf16[4,96,1536]{2,1,0:T(8,128)(2,1)} custom-call(bf16[4,16,96,128]{3,2,1,0:T(8,128)(2,1)S(1)} %all-to-all-done.2.grad_ref, bf16[1536,2048]{1,0:T(8,128)(2,1)} %line_features.1.feats_ref), custom_call_target="tpu_custom_call" | custom-call | tf_op jit(solution)/shard_map/wgrad_products/pallas_call | solution.py:142
  135.9 4.6 %all-to-all-start.3 = ((bf16[4,96,1536]{2,1,0:T(8,128)(2,1)}), bf16[4,96,1536]{2,1,0:T(8,128)(2,1)S(1)}, u32[]{:S(2)}, u32[]{:S(2)}) async-start(bf16[4,96,1536]{2,1,0:T(8,128)(2,1)} %wgrad_products.1), calls=%async_computation.3 | async-start | bytes 2359296 | tf_op jit(solution)/shard_map/all_to_all | solution.py:323
  140.5 4.7 %all-gather.4.cloned.1.call-done = bf16[16,1,512,512]{3,2,1,0:T(8,128)(2,1)} async-done(((bf16[1,1,512,512]{3,2,1,0:T(8,128)(2,1)}), bf16[16,1,512,512]{3,2,1,0:T(8,128)(2,1)}) %all-gather.4.cloned.1.call-update) | async-done | bytes 8388624 | tf_op jit(solution)/shard_map/all_gather | solution.py:306
  145.2 6.9 %tokens_step.1 = (bf16[128,1536]{1,0:T(8,128)(2,1)}, bf16[4,4,192,128]{3,2,1,0:T(8,128)(2,1)}, bf16[4,4,192,128]{3,2,1,0:T(8,128)(2,1)}) custom-call(s32[3,9]{1,0:T(4,128)S(1)} %copy-done.5, s32[3]{0:T(128)S(1)} %pad_add_fusion.place, bf16[6144,128]{1,0:T(8,128)(2,1)S(1)} %bitcast.18, bf16[128,1536]{1,0:T(8,128)(2,1)S(1)} %copy-done, ...), custom_call_target="tpu_custom_call" | custom-call | tf_op jit(solution)/shard_map/tokens_step/pallas_call | solution.py:64
  152.1 2.6 %collective-permute-start.9 = (bf16[4,4,192,128]{3,2,1,0:T(8,128)(2,1)}, bf16[4,4,192,128]{3,2,1,0:T(8,128)(2,1)S(1)}, u32[]{:S(2)}, u32[]{:S(2)}) collective-permute-start(bf16[4,4,192,128]{3,2,1,0:T(8,128)(2,1)} %get-tuple-element.41), channel_id=1, source_target_pairs={{0,1},{1,0},{2,3},{3,2},{4,5},{5,4},{6,7},{7,6},{8,9},{9,8},{10,11... | collective-permute-start | bytes 2359304 | tf_op jit(solution)/shard_map/ppermute | solution.py:211
  158.1 11.4 %all-to-all-start.4 = ((bf16[16,32,512]{2,1,0:T(8,128)(2,1)}), bf16[16,32,512]{2,1,0:T(8,128)(2,1)S(1)}, u32[]{:S(2)}, u32[]{:S(2)}) async-start(bf16[16,32,512]{2,1,0:T(8,128)(2,1)} %pick_slots.1), calls=%async_computation.4 | async-start | bytes 1048576 | tf_op jit(solution)/shard_map/all_to_all | solution.py:329
  169.5 3.1 %collective-permute-start.10 = (bf16[4,192,128]{2,1,0:T(8,128)(2,1)S(1)}, bf16[4,192,128]{2,1,0:T(8,128)(2,1)S(1)}, u32[]{:S(2)}, u32[]{:S(2)}) collective-permute-start(bf16[4,192,128]{2,1,0:T(8,128)(2,1)S(1)} %get-tuple-element.47), channel_id=1, source_target_pairs={{0,2},{1,3},{2,4},{3,5},{4,6},{5,7},{6,0},{7,1},{8,10},{9,11},{10,... | collective-permute-start | bytes 589832 | tf_op jit(solution)/shard_map/ppermute | solution.py:217
  172.6 5.3 %collective-permute-start.11 = (bf16[4,192,128]{2,1,0:T(8,128)(2,1)S(1)}, bf16[4,192,128]{2,1,0:T(8,128)(2,1)S(1)}, u32[]{:S(2)}, u32[]{:S(2)}) collective-permute-start(bf16[4,192,128]{2,1,0:T(8,128)(2,1)S(1)} %get-tuple-element.48), channel_id=1, source_target_pairs={{0,4},{1,5},{2,6},{3,7},{4,0},{5,1},{6,2},{7,3},{8,12},{9,13},{10,... | collective-permute-start | bytes 589832 | tf_op jit(solution)/shard_map/ppermute | solution.py:217
  179.9 3.4 %collective-permute-done.11.refs_2_ = bf16[4,192,128]{2,1,0:T(8,128)(2,1)S(1)} collective-permute-done((bf16[4,192,128]{2,1,0:T(8,128)(2,1)S(1)}, bf16[4,192,128]{2,1,0:T(8,128)(2,1)S(1)}, u32[]{:S(2)}, u32[]{:S(2)}) %collective-permute-start.11) | collective-permute-done | bytes 196640 | tf_op jit(solution)/shard_map/ppermute | solution.py:217
  187.4 3.7 %collective-permute-start.14 = (f32[192,128]{1,0:T(8,128)S(1)}, f32[192,128]{1,0:T(8,128)S(1)}, u32[]{:S(2)}, u32[]{:S(2)}) collective-permute-start(f32[192,128]{1,0:T(8,128)S(1)} %get-tuple-element.52), channel_id=1, source_target_pairs={{0,16},{1,17},{2,18},{3,19},{4,20},{5,21},{6,22},{7,23},{8,24},{9,... | collective-permute-start | bytes 294920 | tf_op jit(solution)/shard_map/ppermute | solution.py:219
  191.1 2.5 %collective-permute-start.15 = (f32[192,128]{1,0:T(8,128)S(1)}, f32[192,128]{1,0:T(8,128)S(1)}, u32[]{:S(2)}, u32[]{:S(2)}) collective-permute-start(f32[192,128]{1,0:T(8,128)S(1)} %get-tuple-element.53), channel_id=1, source_target_pairs={{0,24},{1,25},{2,26},{3,27},{4,28},{5,29},{6,30},{7,31},{8,0},{9,1... | collective-permute-start | bytes 294920 | tf_op jit(solution)/shard_map/ppermute | solution.py:219
  (58 shorter events, 31.0 us)
Async XLA Ops:
  7.2 138.0 %all-gather.4.cloned.1.call-start = ((), (), s32[]{:S(2)}) async-start(), calls=%async_computation.5 | async-start | bytes 8912896 | tf_op jit(solution)/shard_map/all_gather | solution.py:306
  10.1 51.2 %all-to-all-start = ((bf16[32,192,128]{2,1,0:T(8,128)(2,1)}), bf16[32,192,128]{2,1,0:T(8,128)(2,1)S(1)}, u32[]{:S(2)}, u32[]{:S(2)}) async-start(bf16[32,192,128]{2,1,0:T(8,128)(2,1)} %spread.2), calls=%async_computation | async-start | bytes 3145728 | tf_op jit(solution)/shard_map/all_to_all | solution.py:308
  61.4 38.3 %copy-start.6 = (bf16[3072,128]{1,0:T(8,128)(2,1)}, bf16[3072,128]{1,0:T(8,128)(2,1)S(1)}, u32[]{:S(2)}) copy-start(bf16[3072,128]{1,0:T(8,128)(2,1)S(1)} %all-gather) | copy-start | bytes 2359300
  61.4 37.1 %all-to-all-start.1 = ((bf16[16,96,128]{2,1,0:T(8,128)(2,1)}), bf16[16,96,128]{2,1,0:T(8,128)(2,1)S(1)}, u32[]{:S(2)}, u32[]{:S(2)}) async-start(bf16[16,96,128]{2,1,0:T(8,128)(2,1)} %bitcast.3), calls=%async_computation.1 | async-start | bytes 786432 | tf_op jit(solution)/shard_map/all_to_all | solution.py:314
  68.3 16.8 %collective-permute-start = (bf16[16,192,128]{2,1,0:T(8,128)(2,1)S(1)}, bf16[16,192,128]{2,1,0:T(8,128)(2,1)S(1)}, u32[]{:S(2)}, u32[]{:S(2)}) collective-permute-start(bf16[16,192,128]{2,1,0:T(8,128)(2,1)S(1)} %bitcast.22), channel_id=1, source_target_pairs={{0,2},{1,3},{2,4},{3,5},{4,6},{5,7},{6,0},{7,1},{8,10},{9,11},{10,... | collective-permute-start | bytes 2359304 | tf_op jit(solution)/shard_map/ppermute | solution.py:288
  71.6 16.3 %collective-permute-start.2 = (bf16[16,192,128]{2,1,0:T(8,128)(2,1)S(1)}, bf16[16,192,128]{2,1,0:T(8,128)(2,1)S(1)}, u32[]{:S(2)}, u32[]{:S(2)}) collective-permute-start(bf16[16,192,128]{2,1,0:T(8,128)(2,1)S(1)} %bitcast.23), channel_id=1, source_target_pairs={{0,6},{1,7},{2,0},{3,1},{4,2},{5,3},{6,4},{7,5},{8,14},{9,15},{10,... | collective-permute-start | bytes 2359304 | tf_op jit(solution)/shard_map/ppermute | solution.py:289
  85.9 10.3 %collective-permute-start.1 = (bf16[8,192,128]{2,1,0:T(8,128)(2,1)}, bf16[8,192,128]{2,1,0:T(8,128)(2,1)S(1)}, u32[]{:S(2)}, u32[]{:S(2)}) collective-permute-start(bf16[8,192,128]{2,1,0:T(8,128)(2,1)} %slice.8), channel_id=1, source_target_pairs={{0,2},{1,3},{2,4},{3,5},{4,6},{5,7},{6,0},{7,1},{8,10},{9,11},{10,... | collective-permute-start | bytes 1179656 | tf_op jit(solution)/shard_map/ppermute | solution.py:290
  88.9 9.6 %collective-permute-start.3 = (bf16[8,192,128]{2,1,0:T(8,128)(2,1)}, bf16[8,192,128]{2,1,0:T(8,128)(2,1)}, u32[]{:S(2)}, u32[]{:S(2)}) collective-permute-start(bf16[8,192,128]{2,1,0:T(8,128)(2,1)} %slice.9), channel_id=1, source_target_pairs={{0,6},{1,7},{2,0},{3,1},{4,2},{5,3},{6,4},{7,5},{8,14},{9,15},{10,... | collective-permute-start | bytes 1179656 | tf_op jit(solution)/shard_map/ppermute | solution.py:291
  99.7 30.5 %all-to-all-start.2 = ((bf16[4,16,96,128]{3,2,1,0:T(8,128)(2,1)}), bf16[4,16,96,128]{3,2,1,0:T(8,128)(2,1)S(1)}, u32[]{:S(2)}, u32[]{:S(2)}) async-start(bf16[4,16,96,128]{3,2,1,0:T(8,128)(2,1)} %spread.3), calls=%async_computation.2 | async-start | bytes 3145728 | tf_op jit(solution)/shard_map/all_to_all | solution.py:319
  103.7 18.5 %collective-permute-start.4 = (bf16[16,192,128]{2,1,0:T(8,128)(2,1)}, bf16[16,192,128]{2,1,0:T(8,128)(2,1)}, u32[]{:S(2)}, u32[]{:S(2)}) collective-permute-start(bf16[16,192,128]{2,1,0:T(8,128)(2,1)} %bitcast.24), channel_id=1, source_target_pairs={{0,1},{1,0},{2,3},{3,2},{4,5},{5,4},{6,7},{7,6},{8,9},{9,8},{10,11... | collective-permute-start | bytes 2359304 | tf_op jit(solution)/shard_map/ppermute | solution.py:318
  113.4 8.8 %collective-permute-start.5 = (bf16[16,192,128]{2,1,0:T(8,128)(2,1)}, bf16[16,192,128]{2,1,0:T(8,128)(2,1)}, u32[]{:S(2)}, u32[]{:S(2)}) collective-permute-start(bf16[16,192,128]{2,1,0:T(8,128)(2,1)} %copy-done.7), channel_id=1, source_target_pairs={{0,1},{1,0},{2,3},{3,2},{4,5},{5,4},{6,7},{7,6},{8,9},{9,8},{10,11... | collective-permute-start | bytes 2359304 | tf_op jit(solution)/shard_map/ppermute | solution.py:318
  115.4 6.9 %collective-permute-start.8 = (bf16[16,192,128]{2,1,0:T(8,128)(2,1)}, bf16[16,192,128]{2,1,0:T(8,128)(2,1)}, u32[]{:S(2)}, u32[]{:S(2)}) collective-permute-start(bf16[16,192,128]{2,1,0:T(8,128)(2,1)} %copy-done.8), channel_id=1, source_target_pairs={{0,1},{1,0},{2,3},{3,2},{4,5},{5,4},{6,7},{7,6},{8,9},{9,8},{10,11... | collective-permute-start | bytes 2359304 | tf_op jit(solution)/shard_map/ppermute | solution.py:318
  117.8 4.5 %collective-permute-start.6 = (bf16[8,192,128]{2,1,0:T(8,128)(2,1)}, bf16[8,192,128]{2,1,0:T(8,128)(2,1)}, u32[]{:S(2)}, u32[]{:S(2)}) collective-permute-start(bf16[8,192,128]{2,1,0:T(8,128)(2,1)} %copy-done.9), channel_id=1, source_target_pairs={{0,1},{1,0},{2,3},{3,2},{4,5},{5,4},{6,7},{7,6},{8,9},{9,8},{10,11... | collective-permute-start | bytes 1179656 | tf_op jit(solution)/shard_map/ppermute | solution.py:318
  119.7 4.1 %collective-permute-start.7 = (bf16[8,192,128]{2,1,0:T(8,128)(2,1)}, bf16[8,192,128]{2,1,0:T(8,128)(2,1)}, u32[]{:S(2)}, u32[]{:S(2)}) collective-permute-start(bf16[8,192,128]{2,1,0:T(8,128)(2,1)} %collective-permute-done.3.refs_3_), channel_id=1, source_target_pairs={{0,1},{1,0},{2,3},{3,2},{4,5},{5,4},{6,7},{7,6},{8,9},{9,8},{10,11... | collective-permute-start | bytes 1179656 | tf_op jit(solution)/shard_map/ppermute | solution.py:318
  135.9 20.5 %all-to-all-start.3 = ((bf16[4,96,1536]{2,1,0:T(8,128)(2,1)}), bf16[4,96,1536]{2,1,0:T(8,128)(2,1)S(1)}, u32[]{:S(2)}, u32[]{:S(2)}) async-start(bf16[4,96,1536]{2,1,0:T(8,128)(2,1)} %wgrad_products.1), calls=%async_computation.3 | async-start | bytes 2359296 | tf_op jit(solution)/shard_map/all_to_all | solution.py:323
  145.2 11.3 %copy-start.4 = (s32[3,16]{1,0:T(4,128)S(1)}, s32[3,16]{1,0:T(4,128)}, u32[]{:S(2)}) copy-start(s32[3,16]{1,0:T(4,128)} %get-tuple-element.36.meta) | copy-start | bytes 580
  152.1 5.9 %collective-permute-start.9 = (bf16[4,4,192,128]{3,2,1,0:T(8,128)(2,1)}, bf16[4,4,192,128]{3,2,1,0:T(8,128)(2,1)S(1)}, u32[]{:S(2)}, u32[]{:S(2)}) collective-permute-start(bf16[4,4,192,128]{3,2,1,0:T(8,128)(2,1)} %get-tuple-element.41), channel_id=1, source_target_pairs={{0,1},{1,0},{2,3},{3,2},{4,5},{5,4},{6,7},{7,6},{8,9},{9,8},{10,11... | collective-permute-start | bytes 2359304 | tf_op jit(solution)/shard_map/ppermute | solution.py:211
  158.1 39.2 %all-to-all-start.4 = ((bf16[16,32,512]{2,1,0:T(8,128)(2,1)}), bf16[16,32,512]{2,1,0:T(8,128)(2,1)S(1)}, u32[]{:S(2)}, u32[]{:S(2)}) async-start(bf16[16,32,512]{2,1,0:T(8,128)(2,1)} %pick_slots.1), calls=%async_computation.4 | async-start | bytes 1048576 | tf_op jit(solution)/shard_map/all_to_all | solution.py:329
  169.5 10.4 %collective-permute-start.10 = (bf16[4,192,128]{2,1,0:T(8,128)(2,1)S(1)}, bf16[4,192,128]{2,1,0:T(8,128)(2,1)S(1)}, u32[]{:S(2)}, u32[]{:S(2)}) collective-permute-start(bf16[4,192,128]{2,1,0:T(8,128)(2,1)S(1)} %get-tuple-element.47), channel_id=1, source_target_pairs={{0,2},{1,3},{2,4},{3,5},{4,6},{5,7},{6,0},{7,1},{8,10},{9,11},{10,... | collective-permute-start | bytes 589832 | tf_op jit(solution)/shard_map/ppermute | solution.py:217
  172.6 10.6 %collective-permute-start.11 = (bf16[4,192,128]{2,1,0:T(8,128)(2,1)S(1)}, bf16[4,192,128]{2,1,0:T(8,128)(2,1)S(1)}, u32[]{:S(2)}, u32[]{:S(2)}) collective-permute-start(bf16[4,192,128]{2,1,0:T(8,128)(2,1)S(1)} %get-tuple-element.48), channel_id=1, source_target_pairs={{0,4},{1,5},{2,6},{3,7},{4,0},{5,1},{6,2},{7,3},{8,12},{9,13},{10,... | collective-permute-start | bytes 589832 | tf_op jit(solution)/shard_map/ppermute | solution.py:217
  177.9 7.1 %collective-permute-start.12 = (bf16[4,192,128]{2,1,0:T(8,128)(2,1)S(1)}, bf16[4,192,128]{2,1,0:T(8,128)(2,1)S(1)}, u32[]{:S(2)}, u32[]{:S(2)}) collective-permute-start(bf16[4,192,128]{2,1,0:T(8,128)(2,1)S(1)} %get-tuple-element.49), channel_id=1, source_target_pairs={{0,6},{1,7},{2,0},{3,1},{4,2},{5,3},{6,4},{7,5},{8,14},{9,15},{10,... | collective-permute-start | bytes 589832 | tf_op jit(solution)/shard_map/ppermute | solution.py:217
  185.2 8.4 %collective-permute-start.13 = (f32[192,128]{1,0:T(8,128)S(1)}, f32[192,128]{1,0:T(8,128)S(1)}, u32[]{:S(2)}, u32[]{:S(2)}) collective-permute-start(f32[192,128]{1,0:T(8,128)S(1)} %get-tuple-element.51), channel_id=1, source_target_pairs={{0,8},{1,9},{2,10},{3,11},{4,12},{5,13},{6,14},{7,15},{8,16},{9,17... | collective-permute-start | bytes 294920 | tf_op jit(solution)/shard_map/ppermute | solution.py:219
  187.4 7.7 %collective-permute-start.14 = (f32[192,128]{1,0:T(8,128)S(1)}, f32[192,128]{1,0:T(8,128)S(1)}, u32[]{:S(2)}, u32[]{:S(2)}) collective-permute-start(f32[192,128]{1,0:T(8,128)S(1)} %get-tuple-element.52), channel_id=1, source_target_pairs={{0,16},{1,17},{2,18},{3,19},{4,20},{5,21},{6,22},{7,23},{8,24},{9,... | collective-permute-start | bytes 294920 | tf_op jit(solution)/shard_map/ppermute | solution.py:219
  191.1 5.7 %collective-permute-start.15 = (f32[192,128]{1,0:T(8,128)S(1)}, f32[192,128]{1,0:T(8,128)S(1)}, u32[]{:S(2)}, u32[]{:S(2)}) collective-permute-start(f32[192,128]{1,0:T(8,128)S(1)} %get-tuple-element.53), channel_id=1, source_target_pairs={{0,24},{1,25},{2,26},{3,27},{4,28},{5,29},{6,30},{7,31},{8,0},{9,1... | collective-permute-start | bytes 294920 | tf_op jit(solution)/shard_map/ppermute | solution.py:219
  (8 other events, 34.9 us)
Sparse Core Ops, SparseCore 0:
  10.1 135.0 all-gather.3

commit v12 on v11

--- a/solution.py
+++ b/solution.py
@@ -82,76 +82,60 @@
     return pltpu.with_memory_space_constraint(x, pltpu.HBM)
 
 
-def features_kernel(place, *refs):
-    n_in = (len(refs) - 2) // 2
-    in_refs, out_ref, buffers, sems = refs[:n_in], refs[n_in], refs[n_in + 1 : -1], refs[-1]
-    copies = [pltpu.make_async_copy(in_refs[i], buffers[i], sems.at[i]) for i in range(n_in)]
-    for copy in copies:
-        copy.start()
-    n_z, piece, toks = buffers[0].shape
+def wgrad_kernel(place, grad_ref, *refs, scale):
+    act_refs, (out_ref, a_buf, b_buf, sems) = refs[:-4], refs[-4:]
+    n_x, n_z, rows, toks = grad_ref.shape
+    piece = act_refs[0].shape[1]
     y, core = place[1], place[2]
     parts = ((0, 0), (1, 0), (2, 0), (2, n_z // 2), (3, 0))
-    for i in range(n_in):
-        s, first = parts[i % len(parts)]
-        side = core if i < len(parts) else 1 - core
-        at = aligned((lax.rem(y - s + NY, NY) * NC + side) * piece, piece, 64)
-        copies[i].wait()
-        for z in range(buffers[i].shape[0]):
-            out_ref[at, (first + z) * toks : (first + z + 1) * toks] = buffers[i][z]
-
-
-def line_features(place, own, oth):
-    n_z, piece, toks = own[0].shape
-    args = [in_hbm(a) for a in (*own, *oth)]
-    return pl.pallas_call(
-        features_kernel,
-        in_specs=[pl.BlockSpec(memory_space=pltpu.SMEM)]
-        + [pl.BlockSpec(memory_space=pltpu.HBM)] * len(args),
-        out_specs=pl.BlockSpec(memory_space=pltpu.VMEM),
-        out_shape=pltpu.HBM((NY * NC * piece, n_z * toks), BF),
-        scratch_shapes=[pltpu.VMEM(a.shape, BF) for a in args] + [pltpu.SemaphoreType.DMA((len(args),))],
-        compiler_params=pltpu.CompilerParams(vmem_limit_bytes=20 * MIB),
-        name="line_features",
-    )(place, *args)
-
-
-def wgrad_kernel(grad_ref, feats_ref, out_ref, a_buf, b_buf, sems, *, scale):
-    n_x, n_z, rows, toks = grad_ref.shape
-    steps = sems.shape[0]
-    span = feats_ref.shape[0] // steps
-    parts = [pl.ds(i * span, span) for i in range(steps)]
-    copies = [pltpu.make_async_copy(feats_ref.at[parts[i]], b_buf.at[parts[i]], sems.at[i]) for i in range(steps)]
-    for copy in copies:
-        copy.start()
+    copies = [[] for _ in range(NY)]
+    count = 0
+    for i, (s, first) in enumerate(parts):
+        for side, ref in ((core, act_refs[i]), (1 - core, act_refs[i + len(parts)])):
+            at = aligned((s * NC + side) * piece, piece, 64)
+            for z in range(ref.shape[0]):
+                lanes = pl.ds((first + z) * toks, toks)
+                copies[s].append(pltpu.make_async_copy(ref.at[z], b_buf.at[at, lanes], sems.at[count]))
+                count += 1
+    for line in copies:
+        for copy in line:
+            copy.start()
     for x in range(n_x):
         for z in range(n_z):
             a_buf[x * rows : (x + 1) * rows, z * toks : (z + 1) * toks] = grad_ref[x, z]
-    for i in range(steps):
-        copies[i].wait()
+    span = NC * piece
+    for s in range(0, NY, 2):
+        for copy in copies[s] + copies[s + 1]:
+            copy.wait()
         prod = lax.dot_general(
-            a_buf[...], b_buf[parts[i]], (((1,), (1,)), ((), ())), preferred_element_type=F32
+            a_buf[...], b_buf[s * span : (s + 2) * span], (((1,), (1,)), ((), ())), preferred_element_type=F32
         )
         prod = (prod * scale).astype(BF)
-        for x in range(n_x):
-            out_ref[x, :, parts[i]] = prod[x * rows : (x + 1) * rows]
-
-
-def wgrad_products(grads, feats, scale):
+        for i in range(2):
+            cols = aligned(lax.rem(y - s - i + NY, NY) * span, span, span)
+            for x in range(n_x):
+                out_ref[x, :, cols] = prod[x * rows : (x + 1) * rows, i * span : (i + 1) * span]
+
+
+def wgrad_products(place, grads, own, oth, scale):
     n_x, n_z, rows, toks = grads.shape
+    feats = NY * NC * own[0].shape[1]
+    args = [in_hbm(a) for a in (*own, *oth)]
     vmem = pl.BlockSpec(memory_space=pltpu.VMEM)
     return pl.pallas_call(
         functools.partial(wgrad_kernel, scale=scale),
-        in_specs=[vmem, pl.BlockSpec(memory_space=pltpu.HBM)],
+        in_specs=[pl.BlockSpec(memory_space=pltpu.SMEM), vmem]
+        + [pl.BlockSpec(memory_space=pltpu.HBM)] * len(args),
         out_specs=vmem,
-        out_shape=pltpu.HBM((n_x, rows, feats.shape[0]), BF),
+        out_shape=pltpu.HBM((n_x, rows, feats), BF),
         scratch_shapes=[
             pltpu.VMEM((n_x * rows, n_z * toks), BF),
-            pltpu.VMEM(feats.shape, BF),
-            pltpu.SemaphoreType.DMA((3,)),
+            pltpu.VMEM((feats, n_z * toks), BF),
+            pltpu.SemaphoreType.DMA((NY * NC * n_z,)),
         ],
         compiler_params=pltpu.CompilerParams(vmem_limit_bytes=20 * MIB),
         name="wgrad_products",
-    )(grads, in_hbm(feats))
+    )(place, grads, *args)
 
 
 def slots_kernel(meta, prod_ref, out_ref, *, chunk, blk):
@@ -318,8 +302,7 @@
     act_oth = [lax.ppermute(a, "col", CORE_SWAP) for a in act_own]
     grad_x = lax.all_to_all(spread(grad_z, NX), "col", 0, 0, tiled=True, axis_index_groups=X_GROUPS)
 
-    feats = line_features(place, act_own, act_oth)
-    prods = wgrad_products(grad_x, feats, 1.0 / math.sqrt(toks * owners))
+    prods = wgrad_products(place, grad_x, act_own, act_oth, 1.0 / math.sqrt(toks * owners))
     prods = lax.all_to_all(prods, "col", 0, 0, tiled=True, axis_index_groups=X_GROUPS)
     slot_parts = pick_slots(slots, prods, chunk, blk)
 

time: 209 us -> 205 us (0.981)
  the two profiles are of different devices: /device:TPU:1 before, /device:TPU:8 now
where the time goes in v12:
time: 205 us; the launch traced here: 204 us
  starting transfers between devices  81.8 us (40%)
  blocking collectives  44.1 us (22%)
  waiting for transfers between devices  36.9 us (18%)
  Pallas kernels  22.5 us (11%)
  between operations  14.4 us (7%)
  local copies, waits for them, and re-layouts  4.45 us (2%)
    all_gather x1, blocking collectives, per_device(): act_z = lax.all_gather(act_t, 'row', axis=0)  44.1 us
    ppermute x3, starting transfers between devices, sum_plane(): lax.ppermute(by_y[s], 'col', Y_SHIFTS[s])  11.4 us
    ppermute x1, waiting for transfers between devices, share_y(): before = lax.ppermute(x, 'col', Y_SHIFTS[1])  10.7 us
    ppermute x3, starting transfers between devices, sum_plane(): lax.ppermute(by_x[t], 'col', X_SHIFTS[t])  10.7 us
    ppermute x5, starting transfers between devices, per_device(): act_oth = [lax.ppermute(a, 'col', CORE_SWAP) for a in act_own]  10.6 us
    all_to_all x1, starting transfers between devices, per_device(): lax.all_to_all(slot_parts, 'row', 0, 0, tiled=True).reshape(1, 1, blk, blk)  10.2 us
    all_to_all x1, starting transfers between devices, per_device(): lax.all_to_all(spread(act_t, groups), 'col', 0, 0, tiled=True)  9.6 us
    all_gather x1, waiting for transfers between devices, per_device(): w_all = lax.all_gather(weight_slots[0, 0], 'row', axis=0)  8.67 us
  transfers between devices with their start and end apart: 22, of which 10 were waited for; matrix products, arithmetic and copies ran while one was open for 1% of the time, Pallas kernels for 11%

profile of v12, /device:TPU:8, one launch (start us, length us, event | category | flops | bytes accessed | tf_op | source)
XLA Modules:
  0.0 204.2 jit_solution(5561793086350610623)
XLA Ops:
  10.1 9.6 %all-to-all-start = ((bf16[32,192,128]{2,1,0:T(8,128)(2,1)}), bf16[32,192,128]{2,1,0:T(8,128)(2,1)S(1)}, u32[]{:S(2)}, u32[]{:S(2)}) async-start(bf16[32,192,128]{2,1,0:T(8,128)(2,1)} %spread.2), calls=%async_computation | async-start | bytes 3145728 | tf_op jit(solution)/shard_map/all_to_all | solution.py:292
  20.8 44.1 %all-gather = bf16[3072,128]{1,0:T(8,128)(2,1)S(1)} all-gather(bf16[192,128]{1,0:T(8,128)(2,1)S(1)} %bitcast.20), channel_id=2, replica_groups=mesh['row'=16,'col'=32] {'row'}, dimensions={0}, use_global_device_ids=true | all-gather | bytes 835584 | tf_op jit(solution)/shard_map/all_gather | solution.py:293
  64.8 7.6 %all-to-all-start.1 = ((bf16[16,96,128]{2,1,0:T(8,128)(2,1)}), bf16[16,96,128]{2,1,0:T(8,128)(2,1)S(1)}, u32[]{:S(2)}, u32[]{:S(2)}) async-start(bf16[16,96,128]{2,1,0:T(8,128)(2,1)} %bitcast.3), calls=%async_computation.1 | async-start | bytes 786432 | tf_op jit(solution)/shard_map/all_to_all | solution.py:298
  72.4 3.3 %collective-permute-start = (bf16[16,192,128]{2,1,0:T(8,128)(2,1)S(1)}, bf16[16,192,128]{2,1,0:T(8,128)(2,1)S(1)}, u32[]{:S(2)}, u32[]{:S(2)}) collective-permute-start(bf16[16,192,128]{2,1,0:T(8,128)(2,1)S(1)} %bitcast.22), channel_id=1, source_target_pairs={{0,2},{1,3},{2,4},{3,5},{4,6},{5,7},{6,0},{7,1},{8,10},{9,11},{10,... | collective-permute-start | bytes 2359304 | tf_op jit(solution)/shard_map/ppermute | solution.py:272
  75.7 2.6 %collective-permute-start.2 = (bf16[16,192,128]{2,1,0:T(8,128)(2,1)S(1)}, bf16[16,192,128]{2,1,0:T(8,128)(2,1)S(1)}, u32[]{:S(2)}, u32[]{:S(2)}) collective-permute-start(bf16[16,192,128]{2,1,0:T(8,128)(2,1)S(1)} %bitcast.23), channel_id=1, source_target_pairs={{0,6},{1,7},{2,0},{3,1},{4,2},{5,3},{6,4},{7,5},{8,14},{9,15},{10,... | collective-permute-start | bytes 2359304 | tf_op jit(solution)/shard_map/ppermute | solution.py:273
  78.3 10.7 %collective-permute-done.refs_1_ = bf16[16,192,128]{2,1,0:T(8,128)(2,1)S(1)} collective-permute-done((bf16[16,192,128]{2,1,0:T(8,128)(2,1)S(1)}, bf16[16,192,128]{2,1,0:T(8,128)(2,1)S(1)}, u32[]{:S(2)}, u32[]{:S(2)}) %collective-permute-start) | collective-permute-done | bytes 786464 | tf_op jit(solution)/shard_map/ppermute | solution.py:272
  89.8 3.2 %collective-permute-start.1 = (bf16[8,192,128]{2,1,0:T(8,128)(2,1)}, bf16[8,192,128]{2,1,0:T(8,128)(2,1)S(1)}, u32[]{:S(2)}, u32[]{:S(2)}) collective-permute-start(bf16[8,192,128]{2,1,0:T(8,128)(2,1)} %slice.8), channel_id=1, source_target_pairs={{0,2},{1,3},{2,4},{3,5},{4,6},{5,7},{6,0},{7,1},{8,10},{9,11},{10,... | collective-permute-start | bytes 1179656 | tf_op jit(solution)/shard_map/ppermute | solution.py:274
  94.1 2.6 %collective-permute-start.3 = (bf16[8,192,128]{2,1,0:T(8,128)(2,1)}, bf16[8,192,128]{2,1,0:T(8,128)(2,1)}, u32[]{:S(2)}, u32[]{:S(2)}) collective-permute-start(bf16[8,192,128]{2,1,0:T(8,128)(2,1)} %slice.9), channel_id=1, source_target_pairs={{0,6},{1,7},{2,0},{3,1},{4,2},{5,3},{6,4},{7,5},{8,14},{9,15},{10,... | collective-permute-start | bytes 1179656 | tf_op jit(solution)/shard_map/ppermute | solution.py:275
  99.7 4.4 %collective-permute-done.3.refs_3_ = bf16[8,192,128]{2,1,0:T(8,128)(2,1)} collective-permute-done((bf16[8,192,128]{2,1,0:T(8,128)(2,1)}, bf16[8,192,128]{2,1,0:T(8,128)(2,1)}, u32[]{:S(2)}, u32[]{:S(2)}) %collective-permute-start.3) | collective-permute-done | bytes 393248 | tf_op jit(solution)/shard_map/ppermute | solution.py:275
  105.3 4.4 %all-to-all-start.2 = ((bf16[4,16,96,128]{3,2,1,0:T(8,128)(2,1)}), bf16[4,16,96,128]{3,2,1,0:T(8,128)(2,1)S(1)}, u32[]{:S(2)}, u32[]{:S(2)}) async-start(bf16[4,16,96,128]{3,2,1,0:T(8,128)(2,1)} %spread.3), calls=%async_computation.2 | async-start | bytes 3145728 | tf_op jit(solution)/shard_map/all_to_all | solution.py:303
  115.9 2.4 %collective-permute-start.6 = (bf16[8,192,128]{2,1,0:T(8,128)(2,1)}, bf16[8,192,128]{2,1,0:T(8,128)(2,1)}, u32[]{:S(2)}, u32[]{:S(2)}) collective-permute-start(bf16[8,192,128]{2,1,0:T(8,128)(2,1)} %copy-done.9), channel_id=1, source_target_pairs={{0,1},{1,0},{2,3},{3,2},{4,5},{5,4},{6,7},{7,6},{8,9},{9,8},{10,11... | collective-permute-start | bytes 1179656 | tf_op jit(solution)/shard_map/ppermute | solution.py:302
  123.4 8.3 %wgrad_products.1 = bf16[4,96,1536]{2,1,0:T(8,128)(2,1)} custom-call(s32[3]{0:T(128)S(1)} %pad_add_fusion.place, bf16[4,16,96,128]{3,2,1,0:T(8,128)(2,1)S(1)} %all-to-all-done.2.grad_ref, bf16[16,192,128]{2,1,0:T(8,128)(2,1)} %bitcast.25, bf16[16,192,128]{2,1,0:T(8,128)(2,1)} %copy-done.7, bf16[8,192,128]{2,1,0:T(8,128)(2,1)} %copy-done.9, ...), custom_call_target="tpu_custom_call" | custom-call | tf_op jit(solution)/shard_map/wgrad_products/pallas_call | solution.py:125
  131.7 3.7 %all-to-all-start.3 = ((bf16[4,96,1536]{2,1,0:T(8,128)(2,1)}), bf16[4,96,1536]{2,1,0:T(8,128)(2,1)S(1)}, u32[]{:S(2)}, u32[]{:S(2)}) async-start(bf16[4,96,1536]{2,1,0:T(8,128)(2,1)} %wgrad_products.1), calls=%async_computation.3 | async-start | bytes 2359296 | tf_op jit(solution)/shard_map/all_to_all | solution.py:306
  135.5 8.7 %all-gather.4.cloned.1.call-done = bf16[16,1,512,512]{3,2,1,0:T(8,128)(2,1)} async-done(((bf16[1,1,512,512]{3,2,1,0:T(8,128)(2,1)}), bf16[16,1,512,512]{3,2,1,0:T(8,128)(2,1)}) %all-gather.4.cloned.1.call-update) | async-done | bytes 8388624 | tf_op jit(solution)/shard_map/all_gather | solution.py:290
  144.1 6.9 %tokens_step.1 = (bf16[128,1536]{1,0:T(8,128)(2,1)}, bf16[4,4,192,128]{3,2,1,0:T(8,128)(2,1)}, bf16[4,4,192,128]{3,2,1,0:T(8,128)(2,1)}) custom-call(s32[3,9]{1,0:T(4,128)S(1)} %copy-done.5, s32[3]{0:T(128)S(1)} %pad_add_fusion.place, bf16[6144,128]{1,0:T(8,128)(2,1)S(1)} %bitcast.18, bf16[128,1536]{1,0:T(8,128)(2,1)S(1)} %copy-done, ...), custom_call_target="tpu_custom_call" | custom-call | tf_op jit(solution)/shard_map/tokens_step/pallas_call | solution.py:64
  155.8 10.2 %all-to-all-start.4 = ((bf16[16,32,512]{2,1,0:T(8,128)(2,1)}), bf16[16,32,512]{2,1,0:T(8,128)(2,1)S(1)}, u32[]{:S(2)}, u32[]{:S(2)}) async-start(bf16[16,32,512]{2,1,0:T(8,128)(2,1)} %pick_slots.1), calls=%async_computation.4 | async-start | bytes 1048576 | tf_op jit(solution)/shard_map/all_to_all | solution.py:312
  166.0 3.1 %collective-permute-start.10 = (bf16[4,192,128]{2,1,0:T(8,128)(2,1)S(1)}, bf16[4,192,128]{2,1,0:T(8,128)(2,1)S(1)}, u32[]{:S(2)}, u32[]{:S(2)}) collective-permute-start(bf16[4,192,128]{2,1,0:T(8,128)(2,1)S(1)} %get-tuple-element.47), channel_id=1, source_target_pairs={{0,2},{1,3},{2,4},{3,5},{4,6},{5,7},{6,0},{7,1},{8,10},{9,11},{10,... | collective-permute-start | bytes 589832 | tf_op jit(solution)/shard_map/ppermute | solution.py:201
  169.1 3.8 %collective-permute-start.11 = (bf16[4,192,128]{2,1,0:T(8,128)(2,1)S(1)}, bf16[4,192,128]{2,1,0:T(8,128)(2,1)S(1)}, u32[]{:S(2)}, u32[]{:S(2)}) collective-permute-start(bf16[4,192,128]{2,1,0:T(8,128)(2,1)S(1)} %get-tuple-element.48), channel_id=1, source_target_pairs={{0,4},{1,5},{2,6},{3,7},{4,0},{5,1},{6,2},{7,3},{8,12},{9,13},{10,... | collective-permute-start | bytes 589832 | tf_op jit(solution)/shard_map/ppermute | solution.py:201
  172.8 4.5 %collective-permute-start.12 = (bf16[4,192,128]{2,1,0:T(8,128)(2,1)S(1)}, bf16[4,192,128]{2,1,0:T(8,128)(2,1)S(1)}, u32[]{:S(2)}, u32[]{:S(2)}) collective-permute-start(bf16[4,192,128]{2,1,0:T(8,128)(2,1)S(1)} %get-tuple-element.49), channel_id=1, source_target_pairs={{0,6},{1,7},{2,0},{3,1},{4,2},{5,3},{6,4},{7,5},{8,14},{9,15},{10,... | collective-permute-start | bytes 589832 | tf_op jit(solution)/shard_map/ppermute | solution.py:201
  177.4 2.7 %collective-permute-done.11.refs_2_ = bf16[4,192,128]{2,1,0:T(8,128)(2,1)S(1)} collective-permute-done((bf16[4,192,128]{2,1,0:T(8,128)(2,1)S(1)}, bf16[4,192,128]{2,1,0:T(8,128)(2,1)S(1)}, u32[]{:S(2)}, u32[]{:S(2)}) %collective-permute-start.11) | collective-permute-done | bytes 196640 | tf_op jit(solution)/shard_map/ppermute | solution.py:201
  182.1 2.7 %collective-permute-start.13 = (f32[192,128]{1,0:T(8,128)S(1)}, f32[192,128]{1,0:T(8,128)S(1)}, u32[]{:S(2)}, u32[]{:S(2)}) collective-permute-start(f32[192,128]{1,0:T(8,128)S(1)} %get-tuple-element.51), channel_id=1, source_target_pairs={{0,8},{1,9},{2,10},{3,11},{4,12},{5,13},{6,14},{7,15},{8,16},{9,17... | collective-permute-start | bytes 294920 | tf_op jit(solution)/shard_map/ppermute | solution.py:203
  184.8 4.6 %collective-permute-start.14 = (f32[192,128]{1,0:T(8,128)S(1)}, f32[192,128]{1,0:T(8,128)S(1)}, u32[]{:S(2)}, u32[]{:S(2)}) collective-permute-start(f32[192,128]{1,0:T(8,128)S(1)} %get-tuple-element.52), channel_id=1, source_target_pairs={{0,16},{1,17},{2,18},{3,19},{4,20},{5,21},{6,22},{7,23},{8,24},{9,... | collective-permute-start | bytes 294920 | tf_op jit(solution)/shard_map/ppermute | solution.py:203
  189.4 3.4 %collective-permute-start.15 = (f32[192,128]{1,0:T(8,128)S(1)}, f32[192,128]{1,0:T(8,128)S(1)}, u32[]{:S(2)}, u32[]{:S(2)}) collective-permute-start(f32[192,128]{1,0:T(8,128)S(1)} %get-tuple-element.53), channel_id=1, source_target_pairs={{0,24},{1,25},{2,26},{3,27},{4,28},{5,29},{6,30},{7,31},{8,0},{9,1... | collective-permute-start | bytes 294920 | tf_op jit(solution)/shard_map/ppermute | solution.py:203
  192.9 3.1 %collective-permute-done.15.refs_3_ = f32[192,128]{1,0:T(8,128)S(1)} collective-permute-done((f32[192,128]{1,0:T(8,128)S(1)}, f32[192,128]{1,0:T(8,128)S(1)}, u32[]{:S(2)}, u32[]{:S(2)}) %collective-permute-start.15) | collective-permute-done | bytes 98336 | tf_op jit(solution)/shard_map/ppermute | solution.py:203
  (57 shorter events, 29.4 us)
Async XLA Ops:
  7.2 137.0 %all-gather.4.cloned.1.call-start = ((), (), s32[]{:S(2)}) async-start(), calls=%async_computation.5 | async-start | bytes 8912896 | tf_op jit(solution)/shard_map/all_gather | solution.py:290
  10.1 54.7 %all-to-all-start = ((bf16[32,192,128]{2,1,0:T(8,128)(2,1)}), bf16[32,192,128]{2,1,0:T(8,128)(2,1)S(1)}, u32[]{:S(2)}, u32[]{:S(2)}) async-start(bf16[32,192,128]{2,1,0:T(8,128)(2,1)} %spread.2), calls=%async_computation | async-start | bytes 3145728 | tf_op jit(solution)/shard_map/all_to_all | solution.py:292
  64.8 40.4 %copy-start.6 = (bf16[3072,128]{1,0:T(8,128)(2,1)}, bf16[3072,128]{1,0:T(8,128)(2,1)S(1)}, u32[]{:S(2)}) copy-start(bf16[3072,128]{1,0:T(8,128)(2,1)S(1)} %all-gather) | copy-start | bytes 2359300
  64.8 39.2 %all-to-all-start.1 = ((bf16[16,96,128]{2,1,0:T(8,128)(2,1)}), bf16[16,96,128]{2,1,0:T(8,128)(2,1)S(1)}, u32[]{:S(2)}, u32[]{:S(2)}) async-start(bf16[16,96,128]{2,1,0:T(8,128)(2,1)} %bitcast.3), calls=%async_computation.1 | async-start | bytes 786432 | tf_op jit(solution)/shard_map/all_to_all | solution.py:298
  72.4 16.6 %collective-permute-start = (bf16[16,192,128]{2,1,0:T(8,128)(2,1)S(1)}, bf16[16,192,128]{2,1,0:T(8,128)(2,1)S(1)}, u32[]{:S(2)}, u32[]{:S(2)}) collective-permute-start(bf16[16,192,128]{2,1,0:T(8,128)(2,1)S(1)} %bitcast.22), channel_id=1, source_target_pairs={{0,2},{1,3},{2,4},{3,5},{4,6},{5,7},{6,0},{7,1},{8,10},{9,11},{10,... | collective-permute-start | bytes 2359304 | tf_op jit(solution)/shard_map/ppermute | solution.py:272
  75.7 17.4 %collective-permute-start.2 = (bf16[16,192,128]{2,1,0:T(8,128)(2,1)S(1)}, bf16[16,192,128]{2,1,0:T(8,128)(2,1)S(1)}, u32[]{:S(2)}, u32[]{:S(2)}) collective-permute-start(bf16[16,192,128]{2,1,0:T(8,128)(2,1)S(1)} %bitcast.23), channel_id=1, source_target_pairs={{0,6},{1,7},{2,0},{3,1},{4,2},{5,3},{6,4},{7,5},{8,14},{9,15},{10,... | collective-permute-start | bytes 2359304 | tf_op jit(solution)/shard_map/ppermute | solution.py:273
  89.8 9.9 %collective-permute-start.1 = (bf16[8,192,128]{2,1,0:T(8,128)(2,1)}, bf16[8,192,128]{2,1,0:T(8,128)(2,1)S(1)}, u32[]{:S(2)}, u32[]{:S(2)}) collective-permute-start(bf16[8,192,128]{2,1,0:T(8,128)(2,1)} %slice.8), channel_id=1, source_target_pairs={{0,2},{1,3},{2,4},{3,5},{4,6},{5,7},{6,0},{7,1},{8,10},{9,11},{10,... | collective-permute-start | bytes 1179656 | tf_op jit(solution)/shard_map/ppermute | solution.py:274
  94.1 10.0 %collective-permute-start.3 = (bf16[8,192,128]{2,1,0:T(8,128)(2,1)}, bf16[8,192,128]{2,1,0:T(8,128)(2,1)}, u32[]{:S(2)}, u32[]{:S(2)}) collective-permute-start(bf16[8,192,128]{2,1,0:T(8,128)(2,1)} %slice.9), channel_id=1, source_target_pairs={{0,6},{1,7},{2,0},{3,1},{4,2},{5,3},{6,4},{7,5},{8,14},{9,15},{10,... | collective-permute-start | bytes 1179656 | tf_op jit(solution)/shard_map/ppermute | solution.py:275
  105.3 18.1 %all-to-all-start.2 = ((bf16[4,16,96,128]{3,2,1,0:T(8,128)(2,1)}), bf16[4,16,96,128]{3,2,1,0:T(8,128)(2,1)S(1)}, u32[]{:S(2)}, u32[]{:S(2)}) async-start(bf16[4,16,96,128]{3,2,1,0:T(8,128)(2,1)} %spread.3), calls=%async_computation.2 | async-start | bytes 3145728 | tf_op jit(solution)/shard_map/all_to_all | solution.py:303
  109.7 10.7 %collective-permute-start.4 = (bf16[16,192,128]{2,1,0:T(8,128)(2,1)}, bf16[16,192,128]{2,1,0:T(8,128)(2,1)}, u32[]{:S(2)}, u32[]{:S(2)}) collective-permute-start(bf16[16,192,128]{2,1,0:T(8,128)(2,1)} %bitcast.24), channel_id=1, source_target_pairs={{0,1},{1,0},{2,3},{3,2},{4,5},{5,4},{6,7},{7,6},{8,9},{9,8},{10,11... | collective-permute-start | bytes 2359304 | tf_op jit(solution)/shard_map/ppermute | solution.py:302
  111.6 8.8 %collective-permute-start.5 = (bf16[16,192,128]{2,1,0:T(8,128)(2,1)}, bf16[16,192,128]{2,1,0:T(8,128)(2,1)}, u32[]{:S(2)}, u32[]{:S(2)}) collective-permute-start(bf16[16,192,128]{2,1,0:T(8,128)(2,1)} %copy-done.7), channel_id=1, source_target_pairs={{0,1},{1,0},{2,3},{3,2},{4,5},{5,4},{6,7},{7,6},{8,9},{9,8},{10,11... | collective-permute-start | bytes 2359304 | tf_op jit(solution)/shard_map/ppermute | solution.py:302
  114.0 6.4 %collective-permute-start.8 = (bf16[16,192,128]{2,1,0:T(8,128)(2,1)}, bf16[16,192,128]{2,1,0:T(8,128)(2,1)}, u32[]{:S(2)}, u32[]{:S(2)}) collective-permute-start(bf16[16,192,128]{2,1,0:T(8,128)(2,1)} %copy-done.8), channel_id=1, source_target_pairs={{0,1},{1,0},{2,3},{3,2},{4,5},{5,4},{6,7},{7,6},{8,9},{9,8},{10,11... | collective-permute-start | bytes 2359304 | tf_op jit(solution)/shard_map/ppermute | solution.py:302
  115.9 4.5 %collective-permute-start.6 = (bf16[8,192,128]{2,1,0:T(8,128)(2,1)}, bf16[8,192,128]{2,1,0:T(8,128)(2,1)}, u32[]{:S(2)}, u32[]{:S(2)}) collective-permute-start(bf16[8,192,128]{2,1,0:T(8,128)(2,1)} %copy-done.9), channel_id=1, source_target_pairs={{0,1},{1,0},{2,3},{3,2},{4,5},{5,4},{6,7},{7,6},{8,9},{9,8},{10,11... | collective-permute-start | bytes 1179656 | tf_op jit(solution)/shard_map/ppermute | solution.py:302
  118.3 4.0 %collective-permute-start.7 = (bf16[8,192,128]{2,1,0:T(8,128)(2,1)}, bf16[8,192,128]{2,1,0:T(8,128)(2,1)}, u32[]{:S(2)}, u32[]{:S(2)}) collective-permute-start(bf16[8,192,128]{2,1,0:T(8,128)(2,1)} %collective-permute-done.3.refs_3_), channel_id=1, source_target_pairs={{0,1},{1,0},{2,3},{3,2},{4,5},{5,4},{6,7},{7,6},{8,9},{9,8},{10,11... | collective-permute-start | bytes 1179656 | tf_op jit(solution)/shard_map/ppermute | solution.py:302
  131.7 12.4 %copy-start.5 = (s32[3,9]{1,0:T(4,128)S(1)}, s32[3,9]{1,0:T(4,128)}, u32[]{:S(2)}) copy-start(s32[3,9]{1,0:T(4,128)} %get-tuple-element.33.meta) | copy-start | bytes 328
  131.7 21.4 %all-to-all-start.3 = ((bf16[4,96,1536]{2,1,0:T(8,128)(2,1)}), bf16[4,96,1536]{2,1,0:T(8,128)(2,1)S(1)}, u32[]{:S(2)}, u32[]{:S(2)}) async-start(bf16[4,96,1536]{2,1,0:T(8,128)(2,1)} %wgrad_products.1), calls=%async_computation.3 | async-start | bytes 2359296 | tf_op jit(solution)/shard_map/all_to_all | solution.py:306
  151.1 4.5 %collective-permute-start.9 = (bf16[4,4,192,128]{3,2,1,0:T(8,128)(2,1)}, bf16[4,4,192,128]{3,2,1,0:T(8,128)(2,1)S(1)}, u32[]{:S(2)}, u32[]{:S(2)}) collective-permute-start(bf16[4,4,192,128]{3,2,1,0:T(8,128)(2,1)} %get-tuple-element.41), channel_id=1, source_target_pairs={{0,1},{1,0},{2,3},{3,2},{4,5},{5,4},{6,7},{7,6},{8,9},{9,8},{10,11... | collective-permute-start | bytes 2359304 | tf_op jit(solution)/shard_map/ppermute | solution.py:195
  155.8 40.8 %all-to-all-start.4 = ((bf16[16,32,512]{2,1,0:T(8,128)(2,1)}), bf16[16,32,512]{2,1,0:T(8,128)(2,1)S(1)}, u32[]{:S(2)}, u32[]{:S(2)}) async-start(bf16[16,32,512]{2,1,0:T(8,128)(2,1)} %pick_slots.1), calls=%async_computation.4 | async-start | bytes 1048576 | tf_op jit(solution)/shard_map/all_to_all | solution.py:312
  166.0 11.4 %collective-permute-start.10 = (bf16[4,192,128]{2,1,0:T(8,128)(2,1)S(1)}, bf16[4,192,128]{2,1,0:T(8,128)(2,1)S(1)}, u32[]{:S(2)}, u32[]{:S(2)}) collective-permute-start(bf16[4,192,128]{2,1,0:T(8,128)(2,1)S(1)} %get-tuple-element.47), channel_id=1, source_target_pairs={{0,2},{1,3},{2,4},{3,5},{4,6},{5,7},{6,0},{7,1},{8,10},{9,11},{10,... | collective-permute-start | bytes 589832 | tf_op jit(solution)/shard_map/ppermute | solution.py:201
  169.1 11.0 %collective-permute-start.11 = (bf16[4,192,128]{2,1,0:T(8,128)(2,1)S(1)}, bf16[4,192,128]{2,1,0:T(8,128)(2,1)S(1)}, u32[]{:S(2)}, u32[]{:S(2)}) collective-permute-start(bf16[4,192,128]{2,1,0:T(8,128)(2,1)S(1)} %get-tuple-element.48), channel_id=1, source_target_pairs={{0,4},{1,5},{2,6},{3,7},{4,0},{5,1},{6,2},{7,3},{8,12},{9,13},{10,... | collective-permute-start | bytes 589832 | tf_op jit(solution)/shard_map/ppermute | solution.py:201
  172.8 9.2 %collective-permute-start.12 = (bf16[4,192,128]{2,1,0:T(8,128)(2,1)S(1)}, bf16[4,192,128]{2,1,0:T(8,128)(2,1)S(1)}, u32[]{:S(2)}, u32[]{:S(2)}) collective-permute-start(bf16[4,192,128]{2,1,0:T(8,128)(2,1)S(1)} %get-tuple-element.49), channel_id=1, source_target_pairs={{0,6},{1,7},{2,0},{3,1},{4,2},{5,3},{6,4},{7,5},{8,14},{9,15},{10,... | collective-permute-start | bytes 589832 | tf_op jit(solution)/shard_map/ppermute | solution.py:201
  182.1 10.7 %collective-permute-start.13 = (f32[192,128]{1,0:T(8,128)S(1)}, f32[192,128]{1,0:T(8,128)S(1)}, u32[]{:S(2)}, u32[]{:S(2)}) collective-permute-start(f32[192,128]{1,0:T(8,128)S(1)} %get-tuple-element.51), channel_id=1, source_target_pairs={{0,8},{1,9},{2,10},{3,11},{4,12},{5,13},{6,14},{7,15},{8,16},{9,17... | collective-permute-start | bytes 294920 | tf_op jit(solution)/shard_map/ppermute | solution.py:203
  184.8 8.0 %collective-permute-start.14 = (f32[192,128]{1,0:T(8,128)S(1)}, f32[192,128]{1,0:T(8,128)S(1)}, u32[]{:S(2)}, u32[]{:S(2)}) collective-permute-start(f32[192,128]{1,0:T(8,128)S(1)} %get-tuple-element.52), channel_id=1, source_target_pairs={{0,16},{1,17},{2,18},{3,19},{4,20},{5,21},{6,22},{7,23},{8,24},{9,... | collective-permute-start | bytes 294920 | tf_op jit(solution)/shard_map/ppermute | solution.py:203
  189.4 6.5 %collective-permute-start.15 = (f32[192,128]{1,0:T(8,128)S(1)}, f32[192,128]{1,0:T(8,128)S(1)}, u32[]{:S(2)}, u32[]{:S(2)}) collective-permute-start(f32[192,128]{1,0:T(8,128)S(1)} %get-tuple-element.53), channel_id=1, source_target_pairs={{0,24},{1,25},{2,26},{3,27},{4,28},{5,29},{6,30},{7,31},{8,0},{9,1... | collective-permute-start | bytes 294920 | tf_op jit(solution)/shard_map/ppermute | solution.py:203
  (8 other events, 35.7 us)
Sparse Core Ops, SparseCore 0:
  10.1 134.0 all-gather.3

commit v13 on v12

--- a/solution.py
+++ b/solution.py
@@ -29,23 +29,26 @@
     return pl.ds(pl.multiple_of(start, step), size)
 
 
-def tokens_kernel(meta, place, act_ref, grad_ref, w_ref, out_ref, in_own, in_oth, w_buf, out_acc, in_acc, in_rows, sems):
+def slot_copies(meta, w_ref, w_buf, sems):
+    copies = [
+        pltpu.make_async_copy(w_ref.at[meta[0, k]], w_buf.at[k], sems.at[k]) for k in range(w_buf.shape[0])
+    ]
+    for copy in copies:
+        copy.start()
+    return copies
+
+
+def in_kernel(meta, place, grad_ref, w_ref, in_own, in_oth, w_buf, in_acc, in_rows, sems):
     count, blk, _ = w_buf.shape
     piece = in_own.shape[2]
     x, y, core = place[0], place[1], place[2]
-    copies = [pltpu.make_async_copy(w_ref.at[meta[0, k]], w_buf.at[k], sems.at[k]) for k in range(count)]
-    for copy in copies:
-        copy.start()
-    out_acc[...] = jnp.zeros_like(out_acc)
+    copies = slot_copies(meta, w_ref, w_buf, sems)
     in_acc[...] = jnp.zeros_like(in_acc)
     for k in range(count):
         hid = aligned(meta[1, k] * blk, blk, blk)
         mod = aligned(meta[2, k] * blk, blk, blk)
         copies[k].wait()
-        w = w_buf[k]
-        out_acc[hid, :] += jnp.dot(w, act_ref[mod, :], preferred_element_type=F32)
-        in_acc[:, mod] += jnp.dot(grad_ref[:, hid], w, preferred_element_type=F32)
-    out_ref[...] = out_acc[...].T.astype(BF)
+        in_acc[:, mod] += jnp.dot(grad_ref[:, hid], w_buf[k], preferred_element_type=F32)
     in_rows[...] = in_acc[...].T.astype(BF)
     for s in range(NY):
         for t in range(NX):
@@ -54,28 +57,57 @@
             in_oth[s, t] = in_rows[aligned((chip + 1 - core) * piece, piece, 64), :]
 
 
-def tokens_step(meta, place, act, grad, w_all):
+def in_step(meta, place, grad, w_all, feats):
     count, blk = meta.shape[1], w_all.shape[1]
-    feats, toks = act.shape
-    hidden = grad.shape[1]
+    toks = grad.shape[0]
     parts = pltpu.HBM((NY, NX, feats // (NX * NY * NC), toks), BF)
     vmem = pl.BlockSpec(memory_space=pltpu.VMEM)
     smem = pl.BlockSpec(memory_space=pltpu.SMEM)
     return pl.pallas_call(
-        tokens_kernel,
-        in_specs=[smem, smem, vmem, vmem, pl.BlockSpec(memory_space=pltpu.HBM)],
-        out_specs=[vmem] * 3,
-        out_shape=[jax.ShapeDtypeStruct((toks, hidden), BF), parts, parts],
+        in_kernel,
+        in_specs=[smem, smem, vmem, pl.BlockSpec(memory_space=pltpu.HBM)],
+        out_specs=[vmem] * 2,
+        out_shape=[parts, parts],
+        scratch_shapes=[
+            pltpu.VMEM((count, blk, blk), BF),
+            pltpu.VMEM((toks, feats), F32),
+            pltpu.VMEM((feats, toks), BF),
+            pltpu.SemaphoreType.DMA((count,)),
+        ],
+        compiler_params=pltpu.CompilerParams(vmem_limit_bytes=24 * MIB),
+        name="in_step",
+    )(meta, place, grad, in_hbm(w_all))
+
+
+def out_kernel(meta, act_ref, w_ref, out_ref, w_buf, out_acc, sems):
+    count, blk, _ = w_buf.shape
+    copies = slot_copies(meta, w_ref, w_buf, sems)
+    out_acc[...] = jnp.zeros_like(out_acc)
+    for k in range(count):
+        hid = aligned(meta[1, k] * blk, blk, blk)
+        mod = aligned(meta[2, k] * blk, blk, blk)
+        copies[k].wait()
+        out_acc[hid, :] += jnp.dot(w_buf[k], act_ref[mod, :], preferred_element_type=F32)
+    out_ref[...] = out_acc[...].T.astype(BF)
+
+
+def out_step(meta, act, w_all, hidden):
+    count, blk = meta.shape[1], w_all.shape[1]
+    toks = act.shape[1]
+    vmem = pl.BlockSpec(memory_space=pltpu.VMEM)
+    return pl.pallas_call(
+        out_kernel,
+        in_specs=[pl.BlockSpec(memory_space=pltpu.SMEM), vmem, pl.BlockSpec(memory_space=pltpu.HBM)],
+        out_specs=vmem,
+        out_shape=jax.ShapeDtypeStruct((toks, hidden), BF),
         scratch_shapes=[
             pltpu.VMEM((count, blk, blk), BF),
             pltpu.VMEM((hidden, toks), F32),
-            pltpu.VMEM((toks, feats), F32),
-            pltpu.VMEM((feats, toks), BF),
             pltpu.SemaphoreType.DMA((count,)),
         ],
-        compiler_params=pltpu.CompilerParams(vmem_limit_bytes=28 * MIB),
-        name="tokens_step",
-    )(meta, place, act, grad, in_hbm(w_all))
+        compiler_params=pltpu.CompilerParams(vmem_limit_bytes=16 * MIB),
+        name="out_step",
+    )(meta, act, in_hbm(w_all))
 
 
 def in_hbm(x):
@@ -196,12 +228,15 @@
     return small_call(sum_core_kernel, "sum_core", [line(F32)] + [line(BF)] * (NY - 1), in_own, got)
 
 
-def sum_plane(by_y):
+def sum_line(by_y):
     _, piece, toks = by_y[0].shape
     got = [by_y[0]] + [lax.ppermute(by_y[s], "col", Y_SHIFTS[s]) for s in range(1, NY)]
-    by_x = small_call(sum_y_kernel, "sum_y", [jax.ShapeDtypeStruct((piece, toks), F32)] * NX, *got)
+    return small_call(sum_y_kernel, "sum_y", [jax.ShapeDtypeStruct((piece, toks), F32)] * NX, *got)
+
+
+def sum_plane(by_x):
     got = [by_x[0]] + [lax.ppermute(by_x[t], "col", X_SHIFTS[t]) for t in range(1, NX)]
-    return small_call(sum_x_kernel, "sum_x", [jax.ShapeDtypeStruct((piece, toks), BF)], *got)[0]
+    return small_call(sum_x_kernel, "sum_x", [jax.ShapeDtypeStruct(by_x[0].shape, BF)], *got)[0]
 
 
 def tables_kernel(at, mask_ref, owner_ref, listed_ref, slots_ref):
@@ -306,11 +341,12 @@
     prods = lax.all_to_all(prods, "col", 0, 0, tiled=True, axis_index_groups=X_GROUPS)
     slot_parts = pick_slots(slots, prods, chunk, blk)
 
-    outputs, in_own, in_oth = tokens_step(listed, place, act_all, out_grad, w_all)
+    in_own, in_oth = in_step(listed, place, out_grad, w_all, groups * piece)
     by_y = sum_pair(in_own, in_oth)
-    slot_parts, by_y = lax.optimization_barrier((slot_parts, by_y))
+    slot_parts, by_y, act_all = lax.optimization_barrier((slot_parts, by_y, act_all))
     weight_grad = lax.all_to_all(slot_parts, "row", 0, 0, tiled=True).reshape(1, 1, blk, blk)
-    return outputs, sum_plane(by_y).T, weight_grad
+    by_x, outputs = lax.optimization_barrier((sum_line(by_y), out_step(listed, act_all, w_all, hidden)))
+    return outputs, sum_plane(by_x).T, weight_grad
 
 
 def solution(mesh):

time: 205 us -> 206 us (level)
  the two profiles are of different devices: /device:TPU:8 before, /device:TPU:1 now
where the time goes in v13:
time: 206 us; the launch traced here: 202 us
  starting transfers between devices  88.9 us (43%)
  blocking collectives  39.5 us (19%)
  Pallas kernels  27.6 us (13%)
  waiting for transfers between devices  27.5 us (13%)
  between operations  14.4 us (7%)
  local copies, waits for them, and re-layouts  4.45 us (2%)
    all_gather x1, blocking collectives, per_device(): act_z = lax.all_gather(act_t, 'row', axis=0)  39.5 us
    ppermute x5, starting transfers between devices, per_device(): act_oth = [lax.ppermute(a, 'col', CORE_SWAP) for a in act_own]  18.3 us
    all_to_all x1, starting transfers between devices, per_device(): lax.all_to_all(spread(act_t, groups), 'col', 0, 0, tiled=True)  10.6 us
    ppermute x1, waiting for transfers between devices, share_y(): before = lax.ppermute(x, 'col', Y_SHIFTS[1])  10.3 us
    ppermute x3, starting transfers between devices, sum_line(): lax.ppermute(by_y[s], 'col', Y_SHIFTS[s])  10.3 us
    all_to_all x1, starting transfers between devices, per_device(): lax.all_to_all(slot_parts, 'row', 0, 0, tiled=True).reshape(1, 1, blk, blk)  10.1 us
    ppermute x3, starting transfers between devices, sum_plane(): lax.ppermute(by_x[t], 'col', X_SHIFTS[t])  8.51 us
    all_gather x1, waiting for transfers between devices, per_device(): w_all = lax.all_gather(weight_slots[0, 0], 'row', axis=0)  8.5 us
  transfers between devices with their start and end apart: 22, of which 8 were waited for; matrix products, arithmetic and copies ran while one was open for 1% of the time, Pallas kernels for 13%

profile of v13, /device:TPU:1, one launch (start us, length us, event | category | flops | bytes accessed | tf_op | source)
XLA Modules:
  0.0 202.5 jit_solution(13130971220182870173)
XLA Ops:
  10.1 10.6 %all-to-all-start = ((bf16[32,192,128]{2,1,0:T(8,128)(2,1)}), bf16[32,192,128]{2,1,0:T(8,128)(2,1)S(1)}, u32[]{:S(2)}, u32[]{:S(2)}) async-start(bf16[32,192,128]{2,1,0:T(8,128)(2,1)} %spread.2), calls=%async_computation | async-start | bytes 3145728 | tf_op jit(solution)/shard_map/all_to_all | solution.py:327
  21.8 39.5 %all-gather = bf16[3072,128]{1,0:T(8,128)(2,1)S(1)} all-gather(bf16[192,128]{1,0:T(8,128)(2,1)S(1)} %bitcast.20), channel_id=2, replica_groups=mesh['row'=16,'col'=32] {'row'}, dimensions={0}, use_global_device_ids=true | all-gather | bytes 835584 | tf_op jit(solution)/shard_map/all_gather | solution.py:328
  61.4 6.9 %all-to-all-start.1 = ((bf16[16,96,128]{2,1,0:T(8,128)(2,1)}), bf16[16,96,128]{2,1,0:T(8,128)(2,1)S(1)}, u32[]{:S(2)}, u32[]{:S(2)}) async-start(bf16[16,96,128]{2,1,0:T(8,128)(2,1)} %bitcast.3), calls=%async_computation.1 | async-start | bytes 786432 | tf_op jit(solution)/shard_map/all_to_all | solution.py:333
  68.3 3.3 %collective-permute-start = (bf16[16,192,128]{2,1,0:T(8,128)(2,1)S(1)}, bf16[16,192,128]{2,1,0:T(8,128)(2,1)S(1)}, u32[]{:S(2)}, u32[]{:S(2)}) collective-permute-start(bf16[16,192,128]{2,1,0:T(8,128)(2,1)S(1)} %bitcast.23), channel_id=1, source_target_pairs={{0,2},{1,3},{2,4},{3,5},{4,6},{5,7},{6,0},{7,1},{8,10},{9,11},{10,... | collective-permute-start | bytes 2359304 | tf_op jit(solution)/shard_map/ppermute | solution.py:307
  71.6 3.2 %collective-permute-start.2 = (bf16[16,192,128]{2,1,0:T(8,128)(2,1)S(1)}, bf16[16,192,128]{2,1,0:T(8,128)(2,1)S(1)}, u32[]{:S(2)}, u32[]{:S(2)}) collective-permute-start(bf16[16,192,128]{2,1,0:T(8,128)(2,1)S(1)} %bitcast.24), channel_id=1, source_target_pairs={{0,6},{1,7},{2,0},{3,1},{4,2},{5,3},{6,4},{7,5},{8,14},{9,15},{10,... | collective-permute-start | bytes 2359304 | tf_op jit(solution)/shard_map/ppermute | solution.py:308
  74.8 10.3 %collective-permute-done.refs_1_ = bf16[16,192,128]{2,1,0:T(8,128)(2,1)S(1)} collective-permute-done((bf16[16,192,128]{2,1,0:T(8,128)(2,1)S(1)}, bf16[16,192,128]{2,1,0:T(8,128)(2,1)S(1)}, u32[]{:S(2)}, u32[]{:S(2)}) %collective-permute-start) | collective-permute-done | bytes 786464 | tf_op jit(solution)/shard_map/ppermute | solution.py:307
  88.9 4.5 %collective-permute-start.3 = (bf16[8,192,128]{2,1,0:T(8,128)(2,1)}, bf16[8,192,128]{2,1,0:T(8,128)(2,1)}, u32[]{:S(2)}, u32[]{:S(2)}) collective-permute-start(bf16[8,192,128]{2,1,0:T(8,128)(2,1)} %slice.9), channel_id=1, source_target_pairs={{0,6},{1,7},{2,0},{3,1},{4,2},{5,3},{6,4},{7,5},{8,14},{9,15},{10,... | collective-permute-start | bytes 1179656 | tf_op jit(solution)/shard_map/ppermute | solution.py:310
  93.5 2.3 %layout_tables.1 = (s32[3,9]{1,0:T(4,128)}, s32[3,16]{1,0:T(4,128)}) custom-call(s32[1]{0:T(128)} %bitcast.7.at, s32[12,96]{1,0:T(8,128)} %bitcast.30, s32[12,96]{1,0:T(8,128)} %bitcast.31), custom_call_target="tpu_custom_call" | custom-call | tf_op jit(solution)/shard_map/layout_tables/pallas_call | solution.py:273
  96.2 2.2 %collective-permute-done.3.refs_3_ = bf16[8,192,128]{2,1,0:T(8,128)(2,1)} collective-permute-done((bf16[8,192,128]{2,1,0:T(8,128)(2,1)}, bf16[8,192,128]{2,1,0:T(8,128)(2,1)}, u32[]{:S(2)}, u32[]{:S(2)}) %collective-permute-start.3) | collective-permute-done | bytes 393248 | tf_op jit(solution)/shard_map/ppermute | solution.py:310
  99.7 4.0 %all-to-all-start.2 = ((bf16[4,16,96,128]{3,2,1,0:T(8,128)(2,1)}), bf16[4,16,96,128]{3,2,1,0:T(8,128)(2,1)S(1)}, u32[]{:S(2)}, u32[]{:S(2)}) async-start(bf16[4,16,96,128]{3,2,1,0:T(8,128)(2,1)} %spread.3), calls=%async_computation.2 | async-start | bytes 3145728 | tf_op jit(solution)/shard_map/all_to_all | solution.py:338
  103.7 9.7 %collective-permute-start.4 = (bf16[16,192,128]{2,1,0:T(8,128)(2,1)}, bf16[16,192,128]{2,1,0:T(8,128)(2,1)}, u32[]{:S(2)}, u32[]{:S(2)}) collective-permute-start(bf16[16,192,128]{2,1,0:T(8,128)(2,1)} %bitcast.25), channel_id=1, source_target_pairs={{0,1},{1,0},{2,3},{3,2},{4,5},{5,4},{6,7},{7,6},{8,9},{9,8},{10,11... | collective-permute-start | bytes 2359304 | tf_op jit(solution)/shard_map/ppermute | solution.py:337
  115.3 2.4 %collective-permute-start.8 = (bf16[16,192,128]{2,1,0:T(8,128)(2,1)}, bf16[16,192,128]{2,1,0:T(8,128)(2,1)}, u32[]{:S(2)}, u32[]{:S(2)}) collective-permute-start(bf16[16,192,128]{2,1,0:T(8,128)(2,1)} %copy-done.8), channel_id=1, source_target_pairs={{0,1},{1,0},{2,3},{3,2},{4,5},{5,4},{6,7},{7,6},{8,9},{9,8},{10,11... | collective-permute-start | bytes 2359304 | tf_op jit(solution)/shard_map/ppermute | solution.py:337
  119.7 2.4 %collective-permute-start.7 = (bf16[8,192,128]{2,1,0:T(8,128)(2,1)}, bf16[8,192,128]{2,1,0:T(8,128)(2,1)}, u32[]{:S(2)}, u32[]{:S(2)}) collective-permute-start(bf16[8,192,128]{2,1,0:T(8,128)(2,1)} %collective-permute-done.3.refs_3_), channel_id=1, source_target_pairs={{0,1},{1,0},{2,3},{3,2},{4,5},{5,4},{6,7},{7,6},{8,9},{9,8},{10,11... | collective-permute-start | bytes 1179656 | tf_op jit(solution)/shard_map/ppermute | solution.py:337
  123.8 8.3 %wgrad_products.1 = bf16[4,96,1536]{2,1,0:T(8,128)(2,1)} custom-call(s32[3]{0:T(128)S(1)} %pad_add_fusion.place, bf16[4,16,96,128]{3,2,1,0:T(8,128)(2,1)S(1)} %all-to-all-done.2.grad_ref, bf16[16,192,128]{2,1,0:T(8,128)(2,1)} %bitcast.26, bf16[16,192,128]{2,1,0:T(8,128)(2,1)} %copy-done.7, bf16[8,192,128]{2,1,0:T(8,128)(2,1)} %copy-done.9, ...), custom_call_target="tpu_custom_call" | custom-call | tf_op jit(solution)/shard_map/wgrad_products/pallas_call | solution.py:157
  132.1 4.5 %all-to-all-start.3 = ((bf16[4,96,1536]{2,1,0:T(8,128)(2,1)}), bf16[4,96,1536]{2,1,0:T(8,128)(2,1)S(1)}, u32[]{:S(2)}, u32[]{:S(2)}) async-start(bf16[4,96,1536]{2,1,0:T(8,128)(2,1)} %wgrad_products.1), calls=%async_computation.3 | async-start | bytes 2359296 | tf_op jit(solution)/shard_map/all_to_all | solution.py:341
  136.7 8.5 %all-gather.4.cloned.1.call-done = bf16[16,1,512,512]{3,2,1,0:T(8,128)(2,1)} async-done(((bf16[1,1,512,512]{3,2,1,0:T(8,128)(2,1)}), bf16[16,1,512,512]{3,2,1,0:T(8,128)(2,1)}) %all-gather.4.cloned.1.call-update) | async-done | bytes 8388624 | tf_op jit(solution)/shard_map/all_gather | solution.py:325
  145.2 5.5 %in_step.1 = (bf16[4,4,192,128]{3,2,1,0:T(8,128)(2,1)}, bf16[4,4,192,128]{3,2,1,0:T(8,128)(2,1)}) custom-call(s32[3,9]{1,0:T(4,128)S(1)} %copy-done.4, s32[3]{0:T(128)S(1)} %pad_add_fusion.place, bf16[128,1536]{1,0:T(8,128)(2,1)S(1)} %copy-done, bf16[16,512,512]{2,1,0:T(8,128)(2,1)} %bitcast.21), custom_call_target="tpu_custom_call" | custom-call | tf_op jit(solution)/shard_map/in_step/pallas_call | solution.py:66
  150.7 2.5 %collective-permute-start.9 = (bf16[4,4,192,128]{3,2,1,0:T(8,128)(2,1)}, bf16[4,4,192,128]{3,2,1,0:T(8,128)(2,1)}, u32[]{:S(2)}, u32[]{:S(2)}) collective-permute-start(bf16[4,4,192,128]{3,2,1,0:T(8,128)(2,1)} %get-tuple-element.44), channel_id=1, source_target_pairs={{0,1},{1,0},{2,3},{3,2},{4,5},{5,4},{6,7},{7,6},{8,9},{9,8},{10,11... | collective-permute-start | bytes 2359304 | tf_op jit(solution)/shard_map/ppermute | solution.py:227
  156.7 10.1 %all-to-all-start.4 = ((bf16[16,32,512]{2,1,0:T(8,128)(2,1)}), bf16[16,32,512]{2,1,0:T(8,128)(2,1)S(1)}, u32[]{:S(2)}, u32[]{:S(2)}) async-start(bf16[16,32,512]{2,1,0:T(8,128)(2,1)} %pick_slots.1), calls=%async_computation.4 | async-start | bytes 1048576 | tf_op jit(solution)/shard_map/all_to_all | solution.py:347
  166.9 3.1 %collective-permute-start.10 = (bf16[4,192,128]{2,1,0:T(8,128)(2,1)S(1)}, bf16[4,192,128]{2,1,0:T(8,128)(2,1)S(1)}, u32[]{:S(2)}, u32[]{:S(2)}) collective-permute-start(bf16[4,192,128]{2,1,0:T(8,128)(2,1)S(1)} %get-tuple-element.51), channel_id=1, source_target_pairs={{0,2},{1,3},{2,4},{3,5},{4,6},{5,7},{6,0},{7,1},{8,10},{9,11},{10,... | collective-permute-start | bytes 589832 | tf_op jit(solution)/shard_map/ppermute | solution.py:233
  170.0 5.2 %collective-permute-start.11 = (bf16[4,192,128]{2,1,0:T(8,128)(2,1)S(1)}, bf16[4,192,128]{2,1,0:T(8,128)(2,1)S(1)}, u32[]{:S(2)}, u32[]{:S(2)}) collective-permute-start(bf16[4,192,128]{2,1,0:T(8,128)(2,1)S(1)} %get-tuple-element.52), channel_id=1, source_target_pairs={{0,4},{1,5},{2,6},{3,7},{4,0},{5,1},{6,2},{7,3},{8,12},{9,13},{10,... | collective-permute-start | bytes 589832 | tf_op jit(solution)/shard_map/ppermute | solution.py:233
  177.2 5.3 %out_step.1 = bf16[128,1536]{1,0:T(8,128)(2,1)} custom-call(s32[3,9]{1,0:T(4,128)S(1)} %copy-done.4, bf16[6144,128]{1,0:T(8,128)(2,1)S(1)} %bitcast.18, bf16[16,512,512]{2,1,0:T(8,128)(2,1)} %bitcast.22), custom_call_target="tpu_custom_call" | custom-call | tf_op jit(solution)/shard_map/out_step/pallas_call | solution.py:98
  184.8 3.7 %collective-permute-start.14 = (f32[192,128]{1,0:T(8,128)S(1)}, f32[192,128]{1,0:T(8,128)S(1)}, u32[]{:S(2)}, u32[]{:S(2)}) collective-permute-start(f32[192,128]{1,0:T(8,128)S(1)} %get-tuple-element.62), channel_id=1, source_target_pairs={{0,16},{1,17},{2,18},{3,19},{4,20},{5,21},{6,22},{7,23},{8,24},{9,... | collective-permute-start | bytes 294920 | tf_op jit(solution)/shard_map/ppermute | solution.py:238
  188.5 2.6 %collective-permute-start.15 = (f32[192,128]{1,0:T(8,128)S(1)}, f32[192,128]{1,0:T(8,128)S(1)}, u32[]{:S(2)}, u32[]{:S(2)}) collective-permute-start(f32[192,128]{1,0:T(8,128)S(1)} %get-tuple-element.63), channel_id=1, source_target_pairs={{0,24},{1,25},{2,26},{3,27},{4,28},{5,29},{6,30},{7,31},{8,0},{9,1... | collective-permute-start | bytes 294920 | tf_op jit(solution)/shard_map/ppermute | solution.py:238
  (58 shorter events, 27.0 us)
Async XLA Ops:
  7.2 138.0 %all-gather.4.cloned.1.call-start = ((), (), s32[]{:S(2)}) async-start(), calls=%async_computation.5 | async-start | bytes 8912896 | tf_op jit(solution)/shard_map/all_gather | solution.py:325
  10.1 51.2 %all-to-all-start = ((bf16[32,192,128]{2,1,0:T(8,128)(2,1)}), bf16[32,192,128]{2,1,0:T(8,128)(2,1)S(1)}, u32[]{:S(2)}, u32[]{:S(2)}) async-start(bf16[32,192,128]{2,1,0:T(8,128)(2,1)} %spread.2), calls=%async_computation | async-start | bytes 3145728 | tf_op jit(solution)/shard_map/all_to_all | solution.py:327
  61.4 38.3 %copy-start.6 = (bf16[3072,128]{1,0:T(8,128)(2,1)}, bf16[3072,128]{1,0:T(8,128)(2,1)S(1)}, u32[]{:S(2)}) copy-start(bf16[3072,128]{1,0:T(8,128)(2,1)S(1)} %all-gather) | copy-start | bytes 2359300
  61.4 37.1 %all-to-all-start.1 = ((bf16[16,96,128]{2,1,0:T(8,128)(2,1)}), bf16[16,96,128]{2,1,0:T(8,128)(2,1)S(1)}, u32[]{:S(2)}, u32[]{:S(2)}) async-start(bf16[16,96,128]{2,1,0:T(8,128)(2,1)} %bitcast.3), calls=%async_computation.1 | async-start | bytes 786432 | tf_op jit(solution)/shard_map/all_to_all | solution.py:333
  68.3 16.8 %collective-permute-start = (bf16[16,192,128]{2,1,0:T(8,128)(2,1)S(1)}, bf16[16,192,128]{2,1,0:T(8,128)(2,1)S(1)}, u32[]{:S(2)}, u32[]{:S(2)}) collective-permute-start(bf16[16,192,128]{2,1,0:T(8,128)(2,1)S(1)} %bitcast.23), channel_id=1, source_target_pairs={{0,2},{1,3},{2,4},{3,5},{4,6},{5,7},{6,0},{7,1},{8,10},{9,11},{10,... | collective-permute-start | bytes 2359304 | tf_op jit(solution)/shard_map/ppermute | solution.py:307
  71.6 16.3 %collective-permute-start.2 = (bf16[16,192,128]{2,1,0:T(8,128)(2,1)S(1)}, bf16[16,192,128]{2,1,0:T(8,128)(2,1)S(1)}, u32[]{:S(2)}, u32[]{:S(2)}) collective-permute-start(bf16[16,192,128]{2,1,0:T(8,128)(2,1)S(1)} %bitcast.24), channel_id=1, source_target_pairs={{0,6},{1,7},{2,0},{3,1},{4,2},{5,3},{6,4},{7,5},{8,14},{9,15},{10,... | collective-permute-start | bytes 2359304 | tf_op jit(solution)/shard_map/ppermute | solution.py:308
  85.9 10.3 %collective-permute-start.1 = (bf16[8,192,128]{2,1,0:T(8,128)(2,1)}, bf16[8,192,128]{2,1,0:T(8,128)(2,1)S(1)}, u32[]{:S(2)}, u32[]{:S(2)}) collective-permute-start(bf16[8,192,128]{2,1,0:T(8,128)(2,1)} %slice.8), channel_id=1, source_target_pairs={{0,2},{1,3},{2,4},{3,5},{4,6},{5,7},{6,0},{7,1},{8,10},{9,11},{10,... | collective-permute-start | bytes 1179656 | tf_op jit(solution)/shard_map/ppermute | solution.py:309
  88.9 9.6 %collective-permute-start.3 = (bf16[8,192,128]{2,1,0:T(8,128)(2,1)}, bf16[8,192,128]{2,1,0:T(8,128)(2,1)}, u32[]{:S(2)}, u32[]{:S(2)}) collective-permute-start(bf16[8,192,128]{2,1,0:T(8,128)(2,1)} %slice.9), channel_id=1, source_target_pairs={{0,6},{1,7},{2,0},{3,1},{4,2},{5,3},{6,4},{7,5},{8,14},{9,15},{10,... | collective-permute-start | bytes 1179656 | tf_op jit(solution)/shard_map/ppermute | solution.py:310
  99.7 24.1 %all-to-all-start.2 = ((bf16[4,16,96,128]{3,2,1,0:T(8,128)(2,1)}), bf16[4,16,96,128]{3,2,1,0:T(8,128)(2,1)S(1)}, u32[]{:S(2)}, u32[]{:S(2)}) async-start(bf16[4,16,96,128]{3,2,1,0:T(8,128)(2,1)} %spread.3), calls=%async_computation.2 | async-start | bytes 3145728 | tf_op jit(solution)/shard_map/all_to_all | solution.py:338
  103.7 18.5 %collective-permute-start.4 = (bf16[16,192,128]{2,1,0:T(8,128)(2,1)}, bf16[16,192,128]{2,1,0:T(8,128)(2,1)}, u32[]{:S(2)}, u32[]{:S(2)}) collective-permute-start(bf16[16,192,128]{2,1,0:T(8,128)(2,1)} %bitcast.25), channel_id=1, source_target_pairs={{0,1},{1,0},{2,3},{3,2},{4,5},{5,4},{6,7},{7,6},{8,9},{9,8},{10,11... | collective-permute-start | bytes 2359304 | tf_op jit(solution)/shard_map/ppermute | solution.py:337
  113.4 8.8 %collective-permute-start.5 = (bf16[16,192,128]{2,1,0:T(8,128)(2,1)}, bf16[16,192,128]{2,1,0:T(8,128)(2,1)}, u32[]{:S(2)}, u32[]{:S(2)}) collective-permute-start(bf16[16,192,128]{2,1,0:T(8,128)(2,1)} %copy-done.7), channel_id=1, source_target_pairs={{0,1},{1,0},{2,3},{3,2},{4,5},{5,4},{6,7},{7,6},{8,9},{9,8},{10,11... | collective-permute-start | bytes 2359304 | tf_op jit(solution)/shard_map/ppermute | solution.py:337
  115.3 6.9 %collective-permute-start.8 = (bf16[16,192,128]{2,1,0:T(8,128)(2,1)}, bf16[16,192,128]{2,1,0:T(8,128)(2,1)}, u32[]{:S(2)}, u32[]{:S(2)}) collective-permute-start(bf16[16,192,128]{2,1,0:T(8,128)(2,1)} %copy-done.8), channel_id=1, source_target_pairs={{0,1},{1,0},{2,3},{3,2},{4,5},{5,4},{6,7},{7,6},{8,9},{9,8},{10,11... | collective-permute-start | bytes 2359304 | tf_op jit(solution)/shard_map/ppermute | solution.py:337
  117.7 4.5 %collective-permute-start.6 = (bf16[8,192,128]{2,1,0:T(8,128)(2,1)}, bf16[8,192,128]{2,1,0:T(8,128)(2,1)}, u32[]{:S(2)}, u32[]{:S(2)}) collective-permute-start(bf16[8,192,128]{2,1,0:T(8,128)(2,1)} %copy-done.9), channel_id=1, source_target_pairs={{0,1},{1,0},{2,3},{3,2},{4,5},{5,4},{6,7},{7,6},{8,9},{9,8},{10,11... | collective-permute-start | bytes 1179656 | tf_op jit(solution)/shard_map/ppermute | solution.py:337
  119.7 4.1 %collective-permute-start.7 = (bf16[8,192,128]{2,1,0:T(8,128)(2,1)}, bf16[8,192,128]{2,1,0:T(8,128)(2,1)}, u32[]{:S(2)}, u32[]{:S(2)}) collective-permute-start(bf16[8,192,128]{2,1,0:T(8,128)(2,1)} %collective-permute-done.3.refs_3_), channel_id=1, source_target_pairs={{0,1},{1,0},{2,3},{3,2},{4,5},{5,4},{6,7},{7,6},{8,9},{9,8},{10,11... | collective-permute-start | bytes 1179656 | tf_op jit(solution)/shard_map/ppermute | solution.py:337
  132.1 13.1 %copy-start.4 = (s32[3,9]{1,0:T(4,128)S(1)}, s32[3,9]{1,0:T(4,128)}, u32[]{:S(2)}) copy-start(s32[3,9]{1,0:T(4,128)} %get-tuple-element.42.meta) | copy-start | bytes 328
  132.1 21.1 %all-to-all-start.3 = ((bf16[4,96,1536]{2,1,0:T(8,128)(2,1)}), bf16[4,96,1536]{2,1,0:T(8,128)(2,1)S(1)}, u32[]{:S(2)}, u32[]{:S(2)}) async-start(bf16[4,96,1536]{2,1,0:T(8,128)(2,1)} %wgrad_products.1), calls=%async_computation.3 | async-start | bytes 2359296 | tf_op jit(solution)/shard_map/all_to_all | solution.py:341
  150.7 4.7 %collective-permute-start.9 = (bf16[4,4,192,128]{3,2,1,0:T(8,128)(2,1)}, bf16[4,4,192,128]{3,2,1,0:T(8,128)(2,1)}, u32[]{:S(2)}, u32[]{:S(2)}) collective-permute-start(bf16[4,4,192,128]{3,2,1,0:T(8,128)(2,1)} %get-tuple-element.44), channel_id=1, source_target_pairs={{0,1},{1,0},{2,3},{3,2},{4,5},{5,4},{6,7},{7,6},{8,9},{9,8},{10,11... | collective-permute-start | bytes 2359304 | tf_op jit(solution)/shard_map/ppermute | solution.py:227
  156.7 38.1 %all-to-all-start.4 = ((bf16[16,32,512]{2,1,0:T(8,128)(2,1)}), bf16[16,32,512]{2,1,0:T(8,128)(2,1)S(1)}, u32[]{:S(2)}, u32[]{:S(2)}) async-start(bf16[16,32,512]{2,1,0:T(8,128)(2,1)} %pick_slots.1), calls=%async_computation.4 | async-start | bytes 1048576 | tf_op jit(solution)/shard_map/all_to_all | solution.py:347
  166.9 15.6 %collective-permute-start.10 = (bf16[4,192,128]{2,1,0:T(8,128)(2,1)S(1)}, bf16[4,192,128]{2,1,0:T(8,128)(2,1)S(1)}, u32[]{:S(2)}, u32[]{:S(2)}) collective-permute-start(bf16[4,192,128]{2,1,0:T(8,128)(2,1)S(1)} %get-tuple-element.51), channel_id=1, source_target_pairs={{0,2},{1,3},{2,4},{3,5},{4,6},{5,7},{6,0},{7,1},{8,10},{9,11},{10,... | collective-permute-start | bytes 589832 | tf_op jit(solution)/shard_map/ppermute | solution.py:233
  170.0 12.5 %collective-permute-start.11 = (bf16[4,192,128]{2,1,0:T(8,128)(2,1)S(1)}, bf16[4,192,128]{2,1,0:T(8,128)(2,1)S(1)}, u32[]{:S(2)}, u32[]{:S(2)}) collective-permute-start(bf16[4,192,128]{2,1,0:T(8,128)(2,1)S(1)} %get-tuple-element.52), channel_id=1, source_target_pairs={{0,4},{1,5},{2,6},{3,7},{4,0},{5,1},{6,2},{7,3},{8,12},{9,13},{10,... | collective-permute-start | bytes 589832 | tf_op jit(solution)/shard_map/ppermute | solution.py:233
  175.2 7.3 %collective-permute-start.12 = (bf16[4,192,128]{2,1,0:T(8,128)(2,1)S(1)}, bf16[4,192,128]{2,1,0:T(8,128)(2,1)S(1)}, u32[]{:S(2)}, u32[]{:S(2)}) collective-permute-start(bf16[4,192,128]{2,1,0:T(8,128)(2,1)S(1)} %get-tuple-element.53), channel_id=1, source_target_pairs={{0,6},{1,7},{2,0},{3,1},{4,2},{5,3},{6,4},{7,5},{8,14},{9,15},{10,... | collective-permute-start | bytes 589832 | tf_op jit(solution)/shard_map/ppermute | solution.py:233
  182.6 8.5 %collective-permute-start.13 = (f32[192,128]{1,0:T(8,128)S(1)}, f32[192,128]{1,0:T(8,128)S(1)}, u32[]{:S(2)}, u32[]{:S(2)}) collective-permute-start(f32[192,128]{1,0:T(8,128)S(1)} %get-tuple-element.61), channel_id=1, source_target_pairs={{0,8},{1,9},{2,10},{3,11},{4,12},{5,13},{6,14},{7,15},{8,16},{9,17... | collective-permute-start | bytes 294920 | tf_op jit(solution)/shard_map/ppermute | solution.py:238
  184.8 7.8 %collective-permute-start.14 = (f32[192,128]{1,0:T(8,128)S(1)}, f32[192,128]{1,0:T(8,128)S(1)}, u32[]{:S(2)}, u32[]{:S(2)}) collective-permute-start(f32[192,128]{1,0:T(8,128)S(1)} %get-tuple-element.62), channel_id=1, source_target_pairs={{0,16},{1,17},{2,18},{3,19},{4,20},{5,21},{6,22},{7,23},{8,24},{9,... | collective-permute-start | bytes 294920 | tf_op jit(solution)/shard_map/ppermute | solution.py:238
  188.5 5.7 %collective-permute-start.15 = (f32[192,128]{1,0:T(8,128)S(1)}, f32[192,128]{1,0:T(8,128)S(1)}, u32[]{:S(2)}, u32[]{:S(2)}) collective-permute-start(f32[192,128]{1,0:T(8,128)S(1)} %get-tuple-element.63), channel_id=1, source_target_pairs={{0,24},{1,25},{2,26},{3,27},{4,28},{5,29},{6,30},{7,31},{8,0},{9,1... | collective-permute-start | bytes 294920 | tf_op jit(solution)/shard_map/ppermute | solution.py:238
  (8 other events, 29.9 us)
Sparse Core Ops, SparseCore 0:
  10.1 135.0 all-gather.3

commit v14 on v13

--- a/solution.py
+++ b/solution.py
@@ -115,36 +115,38 @@
 
 
 def wgrad_kernel(place, grad_ref, *refs, scale):
-    act_refs, (out_ref, a_buf, b_buf, sems) = refs[:-4], refs[-4:]
+    n_in = (len(refs) - 4) // 2
+    act_refs, out_ref, buffers, (a_buf, b_buf, sems) = refs[:n_in], refs[n_in], refs[n_in + 1 : -3], refs[-3:]
     n_x, n_z, rows, toks = grad_ref.shape
     piece = act_refs[0].shape[1]
+    span = NC * piece
     y, core = place[1], place[2]
-    parts = ((0, 0), (1, 0), (2, 0), (2, n_z // 2), (3, 0))
-    copies = [[] for _ in range(NY)]
-    count = 0
-    for i, (s, first) in enumerate(parts):
-        for side, ref in ((core, act_refs[i]), (1 - core, act_refs[i + len(parts)])):
-            at = aligned((s * NC + side) * piece, piece, 64)
-            for z in range(ref.shape[0]):
-                lanes = pl.ds((first + z) * toks, toks)
-                copies[s].append(pltpu.make_async_copy(ref.at[z], b_buf.at[at, lanes], sems.at[count]))
-                count += 1
-    for line in copies:
-        for copy in line:
-            copy.start()
+    near = ((0, 0, 0), (1, 1, 0)), ((2, 2, 0), (3, 2, n_z // 2), (4, 3, 0))
+    half = n_in // 2
+    copies = [pltpu.make_async_copy(act_refs[i], buffers[i], sems.at[i]) for i in range(n_in)]
+    for parts in near:
+        for i, _, _ in parts:
+            copies[i].start()
+            copies[i + half].start()
     for x in range(n_x):
         for z in range(n_z):
             a_buf[x * rows : (x + 1) * rows, z * toks : (z + 1) * toks] = grad_ref[x, z]
-    span = NC * piece
-    for s in range(0, NY, 2):
-        for copy in copies[s] + copies[s + 1]:
-            copy.wait()
+    for pair, parts in enumerate(near):
+        for i, s, first in parts:
+            for side, j in ((core, i), (1 - core, i + half)):
+                copies[j].wait()
+                at = aligned((s * NC + side) * piece, piece, 64)
+                for z in range(buffers[j].shape[0]):
+                    b_buf[at, (first + z) * toks : (first + z + 1) * toks] = buffers[j][z]
         prod = lax.dot_general(
-            a_buf[...], b_buf[s * span : (s + 2) * span], (((1,), (1,)), ((), ())), preferred_element_type=F32
+            a_buf[...],
+            b_buf[2 * pair * span : 2 * (pair + 1) * span],
+            (((1,), (1,)), ((), ())),
+            preferred_element_type=F32,
         )
         prod = (prod * scale).astype(BF)
         for i in range(2):
-            cols = aligned(lax.rem(y - s - i + NY, NY) * span, span, span)
+            cols = aligned(lax.rem(y - 2 * pair - i + NY, NY) * span, span, span)
             for x in range(n_x):
                 out_ref[x, :, cols] = prod[x * rows : (x + 1) * rows, i * span : (i + 1) * span]
 
@@ -160,12 +162,13 @@
         + [pl.BlockSpec(memory_space=pltpu.HBM)] * len(args),
         out_specs=vmem,
         out_shape=pltpu.HBM((n_x, rows, feats), BF),
-        scratch_shapes=[
+        scratch_shapes=[pltpu.VMEM(a.shape, BF) for a in args]
+        + [
             pltpu.VMEM((n_x * rows, n_z * toks), BF),
             pltpu.VMEM((feats, n_z * toks), BF),
-            pltpu.SemaphoreType.DMA((NY * NC * n_z,)),
-        ],
-        compiler_params=pltpu.CompilerParams(vmem_limit_bytes=20 * MIB),
+            pltpu.SemaphoreType.DMA((len(args),)),
+        ],
+        compiler_params=pltpu.CompilerParams(vmem_limit_bytes=28 * MIB),
         name="wgrad_products",
     )(place, grads, *args)
 

time: 206 us -> 206 us (level)
  no operation moved by 1% of the time
where the time goes in v14:
time: 206 us; the launch traced here: 202 us
  starting transfers between devices  88.9 us (43%)
  blocking collectives  39.5 us (19%)
  waiting for transfers between devices  27.5 us (13%)
  Pallas kernels  27.5 us (13%)
  between operations  14.4 us (7%)
  local copies, waits for them, and re-layouts  4.45 us (2%)
    all_gather x1, blocking collectives, per_device(): act_z = lax.all_gather(act_t, 'row', axis=0)  39.5 us
    ppermute x5, starting transfers between devices, per_device(): act_oth = [lax.ppermute(a, 'col', CORE_SWAP) for a in act_own]  18.3 us
    all_to_all x1, starting transfers between devices, per_device(): lax.all_to_all(spread(act_t, groups), 'col', 0, 0, tiled=True)  10.6 us
    ppermute x3, starting transfers between devices, sum_line(): lax.ppermute(by_y[s], 'col', Y_SHIFTS[s])  10.3 us
    ppermute x1, waiting for transfers between devices, share_y(): before = lax.ppermute(x, 'col', Y_SHIFTS[1])  10.3 us
    all_to_all x1, starting transfers between devices, per_device(): lax.all_to_all(slot_parts, 'row', 0, 0, tiled=True).reshape(1, 1, blk, blk)  10.1 us
    ppermute x3, starting transfers between devices, sum_plane(): lax.ppermute(by_x[t], 'col', X_SHIFTS[t])  8.58 us
    all_gather x1, waiting for transfers between devices, per_device(): w_all = lax.all_gather(weight_slots[0, 0], 'row', axis=0)  8.56 us
  transfers between devices with their start and end apart: 22, of which 8 were waited for; matrix products, arithmetic and copies ran while one was open for 1% of the time, Pallas kernels for 13%

profile of v14, /device:TPU:1, one launch (start us, length us, event | category | flops | bytes accessed | tf_op | source)
XLA Modules:
  0.0 202.4 jit_solution(8417340098733656420)
XLA Ops:
  10.1 10.6 %all-to-all-start = ((bf16[32,192,128]{2,1,0:T(8,128)(2,1)}), bf16[32,192,128]{2,1,0:T(8,128)(2,1)S(1)}, u32[]{:S(2)}, u32[]{:S(2)}) async-start(bf16[32,192,128]{2,1,0:T(8,128)(2,1)} %spread.2), calls=%async_computation | async-start | bytes 3145728 | tf_op jit(solution)/shard_map/all_to_all | solution.py:330
  21.8 39.5 %all-gather = bf16[3072,128]{1,0:T(8,128)(2,1)S(1)} all-gather(bf16[192,128]{1,0:T(8,128)(2,1)S(1)} %bitcast.20), channel_id=2, replica_groups=mesh['row'=16,'col'=32] {'row'}, dimensions={0}, use_global_device_ids=true | all-gather | bytes 835584 | tf_op jit(solution)/shard_map/all_gather | solution.py:331
  61.4 6.9 %all-to-all-start.1 = ((bf16[16,96,128]{2,1,0:T(8,128)(2,1)}), bf16[16,96,128]{2,1,0:T(8,128)(2,1)S(1)}, u32[]{:S(2)}, u32[]{:S(2)}) async-start(bf16[16,96,128]{2,1,0:T(8,128)(2,1)} %bitcast.3), calls=%async_computation.1 | async-start | bytes 786432 | tf_op jit(solution)/shard_map/all_to_all | solution.py:336
  68.3 3.3 %collective-permute-start = (bf16[16,192,128]{2,1,0:T(8,128)(2,1)S(1)}, bf16[16,192,128]{2,1,0:T(8,128)(2,1)S(1)}, u32[]{:S(2)}, u32[]{:S(2)}) collective-permute-start(bf16[16,192,128]{2,1,0:T(8,128)(2,1)S(1)} %bitcast.23), channel_id=1, source_target_pairs={{0,2},{1,3},{2,4},{3,5},{4,6},{5,7},{6,0},{7,1},{8,10},{9,11},{10,... | collective-permute-start | bytes 2359304 | tf_op jit(solution)/shard_map/ppermute | solution.py:310
  71.6 3.2 %collective-permute-start.2 = (bf16[16,192,128]{2,1,0:T(8,128)(2,1)S(1)}, bf16[16,192,128]{2,1,0:T(8,128)(2,1)S(1)}, u32[]{:S(2)}, u32[]{:S(2)}) collective-permute-start(bf16[16,192,128]{2,1,0:T(8,128)(2,1)S(1)} %bitcast.24), channel_id=1, source_target_pairs={{0,6},{1,7},{2,0},{3,1},{4,2},{5,3},{6,4},{7,5},{8,14},{9,15},{10,... | collective-permute-start | bytes 2359304 | tf_op jit(solution)/shard_map/ppermute | solution.py:311
  74.8 10.3 %collective-permute-done.refs_1_ = bf16[16,192,128]{2,1,0:T(8,128)(2,1)S(1)} collective-permute-done((bf16[16,192,128]{2,1,0:T(8,128)(2,1)S(1)}, bf16[16,192,128]{2,1,0:T(8,128)(2,1)S(1)}, u32[]{:S(2)}, u32[]{:S(2)}) %collective-permute-start) | collective-permute-done | bytes 786464 | tf_op jit(solution)/shard_map/ppermute | solution.py:310
  88.9 4.5 %collective-permute-start.3 = (bf16[8,192,128]{2,1,0:T(8,128)(2,1)}, bf16[8,192,128]{2,1,0:T(8,128)(2,1)}, u32[]{:S(2)}, u32[]{:S(2)}) collective-permute-start(bf16[8,192,128]{2,1,0:T(8,128)(2,1)} %slice.9), channel_id=1, source_target_pairs={{0,6},{1,7},{2,0},{3,1},{4,2},{5,3},{6,4},{7,5},{8,14},{9,15},{10,... | collective-permute-start | bytes 1179656 | tf_op jit(solution)/shard_map/ppermute | solution.py:313
  93.5 2.3 %layout_tables.1 = (s32[3,9]{1,0:T(4,128)}, s32[3,16]{1,0:T(4,128)}) custom-call(s32[1]{0:T(128)} %bitcast.7.at, s32[12,96]{1,0:T(8,128)} %bitcast.30, s32[12,96]{1,0:T(8,128)} %bitcast.31), custom_call_target="tpu_custom_call" | custom-call | tf_op jit(solution)/shard_map/layout_tables/pallas_call | solution.py:276
  96.2 2.2 %collective-permute-done.3.refs_3_ = bf16[8,192,128]{2,1,0:T(8,128)(2,1)} collective-permute-done((bf16[8,192,128]{2,1,0:T(8,128)(2,1)}, bf16[8,192,128]{2,1,0:T(8,128)(2,1)}, u32[]{:S(2)}, u32[]{:S(2)}) %collective-permute-start.3) | collective-permute-done | bytes 393248 | tf_op jit(solution)/shard_map/ppermute | solution.py:313
  99.7 4.0 %all-to-all-start.2 = ((bf16[4,16,96,128]{3,2,1,0:T(8,128)(2,1)}), bf16[4,16,96,128]{3,2,1,0:T(8,128)(2,1)S(1)}, u32[]{:S(2)}, u32[]{:S(2)}) async-start(bf16[4,16,96,128]{3,2,1,0:T(8,128)(2,1)} %spread.3), calls=%async_computation.2 | async-start | bytes 3145728 | tf_op jit(solution)/shard_map/all_to_all | solution.py:341
  103.7 9.7 %collective-permute-start.4 = (bf16[16,192,128]{2,1,0:T(8,128)(2,1)}, bf16[16,192,128]{2,1,0:T(8,128)(2,1)}, u32[]{:S(2)}, u32[]{:S(2)}) collective-permute-start(bf16[16,192,128]{2,1,0:T(8,128)(2,1)} %bitcast.25), channel_id=1, source_target_pairs={{0,1},{1,0},{2,3},{3,2},{4,5},{5,4},{6,7},{7,6},{8,9},{9,8},{10,11... | collective-permute-start | bytes 2359304 | tf_op jit(solution)/shard_map/ppermute | solution.py:340
  115.3 2.4 %collective-permute-start.8 = (bf16[16,192,128]{2,1,0:T(8,128)(2,1)}, bf16[16,192,128]{2,1,0:T(8,128)(2,1)}, u32[]{:S(2)}, u32[]{:S(2)}) collective-permute-start(bf16[16,192,128]{2,1,0:T(8,128)(2,1)} %copy-done.8), channel_id=1, source_target_pairs={{0,1},{1,0},{2,3},{3,2},{4,5},{5,4},{6,7},{7,6},{8,9},{9,8},{10,11... | collective-permute-start | bytes 2359304 | tf_op jit(solution)/shard_map/ppermute | solution.py:340
  119.7 2.4 %collective-permute-start.7 = (bf16[8,192,128]{2,1,0:T(8,128)(2,1)}, bf16[8,192,128]{2,1,0:T(8,128)(2,1)}, u32[]{:S(2)}, u32[]{:S(2)}) collective-permute-start(bf16[8,192,128]{2,1,0:T(8,128)(2,1)} %collective-permute-done.3.refs_3_), channel_id=1, source_target_pairs={{0,1},{1,0},{2,3},{3,2},{4,5},{5,4},{6,7},{7,6},{8,9},{9,8},{10,11... | collective-permute-start | bytes 1179656 | tf_op jit(solution)/shard_map/ppermute | solution.py:340
  123.8 8.3 %wgrad_products.1 = bf16[4,96,1536]{2,1,0:T(8,128)(2,1)} custom-call(s32[3]{0:T(128)S(1)} %pad_add_fusion.place, bf16[4,16,96,128]{3,2,1,0:T(8,128)(2,1)S(1)} %all-to-all-done.2.grad_ref, bf16[16,192,128]{2,1,0:T(8,128)(2,1)} %bitcast.26, bf16[16,192,128]{2,1,0:T(8,128)(2,1)} %copy-done.7, bf16[8,192,128]{2,1,0:T(8,128)(2,1)} %copy-done.9, ...), custom_call_target="tpu_custom_call" | custom-call | tf_op jit(solution)/shard_map/wgrad_products/pallas_call | solution.py:159
  132.0 4.6 %all-to-all-start.3 = ((bf16[4,96,1536]{2,1,0:T(8,128)(2,1)}), bf16[4,96,1536]{2,1,0:T(8,128)(2,1)S(1)}, u32[]{:S(2)}, u32[]{:S(2)}) async-start(bf16[4,96,1536]{2,1,0:T(8,128)(2,1)} %wgrad_products.1), calls=%async_computation.3 | async-start | bytes 2359296 | tf_op jit(solution)/shard_map/all_to_all | solution.py:344
  136.6 8.6 %all-gather.4.cloned.1.call-done = bf16[16,1,512,512]{3,2,1,0:T(8,128)(2,1)} async-done(((bf16[1,1,512,512]{3,2,1,0:T(8,128)(2,1)}), bf16[16,1,512,512]{3,2,1,0:T(8,128)(2,1)}) %all-gather.4.cloned.1.call-update) | async-done | bytes 8388624 | tf_op jit(solution)/shard_map/all_gather | solution.py:328
  145.2 5.5 %in_step.1 = (bf16[4,4,192,128]{3,2,1,0:T(8,128)(2,1)}, bf16[4,4,192,128]{3,2,1,0:T(8,128)(2,1)}) custom-call(s32[3,9]{1,0:T(4,128)S(1)} %copy-done.4, s32[3]{0:T(128)S(1)} %pad_add_fusion.place, bf16[128,1536]{1,0:T(8,128)(2,1)S(1)} %copy-done, bf16[16,512,512]{2,1,0:T(8,128)(2,1)} %bitcast.21), custom_call_target="tpu_custom_call" | custom-call | tf_op jit(solution)/shard_map/in_step/pallas_call | solution.py:66
  150.7 2.5 %collective-permute-start.9 = (bf16[4,4,192,128]{3,2,1,0:T(8,128)(2,1)}, bf16[4,4,192,128]{3,2,1,0:T(8,128)(2,1)}, u32[]{:S(2)}, u32[]{:S(2)}) collective-permute-start(bf16[4,4,192,128]{3,2,1,0:T(8,128)(2,1)} %get-tuple-element.44), channel_id=1, source_target_pairs={{0,1},{1,0},{2,3},{3,2},{4,5},{5,4},{6,7},{7,6},{8,9},{9,8},{10,11... | collective-permute-start | bytes 2359304 | tf_op jit(solution)/shard_map/ppermute | solution.py:230
  156.7 10.1 %all-to-all-start.4 = ((bf16[16,32,512]{2,1,0:T(8,128)(2,1)}), bf16[16,32,512]{2,1,0:T(8,128)(2,1)S(1)}, u32[]{:S(2)}, u32[]{:S(2)}) async-start(bf16[16,32,512]{2,1,0:T(8,128)(2,1)} %pick_slots.1), calls=%async_computation.4 | async-start | bytes 1048576 | tf_op jit(solution)/shard_map/all_to_all | solution.py:350
  166.8 3.2 %collective-permute-start.10 = (bf16[4,192,128]{2,1,0:T(8,128)(2,1)S(1)}, bf16[4,192,128]{2,1,0:T(8,128)(2,1)S(1)}, u32[]{:S(2)}, u32[]{:S(2)}) collective-permute-start(bf16[4,192,128]{2,1,0:T(8,128)(2,1)S(1)} %get-tuple-element.51), channel_id=1, source_target_pairs={{0,2},{1,3},{2,4},{3,5},{4,6},{5,7},{6,0},{7,1},{8,10},{9,11},{10,... | collective-permute-start | bytes 589832 | tf_op jit(solution)/shard_map/ppermute | solution.py:236
  169.9 5.2 %collective-permute-start.11 = (bf16[4,192,128]{2,1,0:T(8,128)(2,1)S(1)}, bf16[4,192,128]{2,1,0:T(8,128)(2,1)S(1)}, u32[]{:S(2)}, u32[]{:S(2)}) collective-permute-start(bf16[4,192,128]{2,1,0:T(8,128)(2,1)S(1)} %get-tuple-element.52), channel_id=1, source_target_pairs={{0,4},{1,5},{2,6},{3,7},{4,0},{5,1},{6,2},{7,3},{8,12},{9,13},{10,... | collective-permute-start | bytes 589832 | tf_op jit(solution)/shard_map/ppermute | solution.py:236
  177.1 5.3 %out_step.1 = bf16[128,1536]{1,0:T(8,128)(2,1)} custom-call(s32[3,9]{1,0:T(4,128)S(1)} %copy-done.4, bf16[6144,128]{1,0:T(8,128)(2,1)S(1)} %bitcast.18, bf16[16,512,512]{2,1,0:T(8,128)(2,1)} %bitcast.22), custom_call_target="tpu_custom_call" | custom-call | tf_op jit(solution)/shard_map/out_step/pallas_call | solution.py:98
  184.8 3.7 %collective-permute-start.14 = (f32[192,128]{1,0:T(8,128)S(1)}, f32[192,128]{1,0:T(8,128)S(1)}, u32[]{:S(2)}, u32[]{:S(2)}) collective-permute-start(f32[192,128]{1,0:T(8,128)S(1)} %get-tuple-element.62), channel_id=1, source_target_pairs={{0,16},{1,17},{2,18},{3,19},{4,20},{5,21},{6,22},{7,23},{8,24},{9,... | collective-permute-start | bytes 294920 | tf_op jit(solution)/shard_map/ppermute | solution.py:241
  188.5 2.7 %collective-permute-start.15 = (f32[192,128]{1,0:T(8,128)S(1)}, f32[192,128]{1,0:T(8,128)S(1)}, u32[]{:S(2)}, u32[]{:S(2)}) collective-permute-start(f32[192,128]{1,0:T(8,128)S(1)} %get-tuple-element.63), channel_id=1, source_target_pairs={{0,24},{1,25},{2,26},{3,27},{4,28},{5,29},{6,30},{7,31},{8,0},{9,1... | collective-permute-start | bytes 294920 | tf_op jit(solution)/shard_map/ppermute | solution.py:241
  (58 shorter events, 27.0 us)
Async XLA Ops:
  7.2 138.0 %all-gather.4.cloned.1.call-start = ((), (), s32[]{:S(2)}) async-start(), calls=%async_computation.5 | async-start | bytes 8912896 | tf_op jit(solution)/shard_map/all_gather | solution.py:328
  10.1 51.2 %all-to-all-start = ((bf16[32,192,128]{2,1,0:T(8,128)(2,1)}), bf16[32,192,128]{2,1,0:T(8,128)(2,1)S(1)}, u32[]{:S(2)}, u32[]{:S(2)}) async-start(bf16[32,192,128]{2,1,0:T(8,128)(2,1)} %spread.2), calls=%async_computation | async-start | bytes 3145728 | tf_op jit(solution)/shard_map/all_to_all | solution.py:330
  61.4 38.3 %copy-start.6 = (bf16[3072,128]{1,0:T(8,128)(2,1)}, bf16[3072,128]{1,0:T(8,128)(2,1)S(1)}, u32[]{:S(2)}) copy-start(bf16[3072,128]{1,0:T(8,128)(2,1)S(1)} %all-gather) | copy-start | bytes 2359300
  61.4 37.1 %all-to-all-start.1 = ((bf16[16,96,128]{2,1,0:T(8,128)(2,1)}), bf16[16,96,128]{2,1,0:T(8,128)(2,1)S(1)}, u32[]{:S(2)}, u32[]{:S(2)}) async-start(bf16[16,96,128]{2,1,0:T(8,128)(2,1)} %bitcast.3), calls=%async_computation.1 | async-start | bytes 786432 | tf_op jit(solution)/shard_map/all_to_all | solution.py:336
  68.3 16.8 %collective-permute-start = (bf16[16,192,128]{2,1,0:T(8,128)(2,1)S(1)}, bf16[16,192,128]{2,1,0:T(8,128)(2,1)S(1)}, u32[]{:S(2)}, u32[]{:S(2)}) collective-permute-start(bf16[16,192,128]{2,1,0:T(8,128)(2,1)S(1)} %bitcast.23), channel_id=1, source_target_pairs={{0,2},{1,3},{2,4},{3,5},{4,6},{5,7},{6,0},{7,1},{8,10},{9,11},{10,... | collective-permute-start | bytes 2359304 | tf_op jit(solution)/shard_map/ppermute | solution.py:310
  71.6 16.3 %collective-permute-start.2 = (bf16[16,192,128]{2,1,0:T(8,128)(2,1)S(1)}, bf16[16,192,128]{2,1,0:T(8,128)(2,1)S(1)}, u32[]{:S(2)}, u32[]{:S(2)}) collective-permute-start(bf16[16,192,128]{2,1,0:T(8,128)(2,1)S(1)} %bitcast.24), channel_id=1, source_target_pairs={{0,6},{1,7},{2,0},{3,1},{4,2},{5,3},{6,4},{7,5},{8,14},{9,15},{10,... | collective-permute-start | bytes 2359304 | tf_op jit(solution)/shard_map/ppermute | solution.py:311
  85.9 10.3 %collective-permute-start.1 = (bf16[8,192,128]{2,1,0:T(8,128)(2,1)}, bf16[8,192,128]{2,1,0:T(8,128)(2,1)S(1)}, u32[]{:S(2)}, u32[]{:S(2)}) collective-permute-start(bf16[8,192,128]{2,1,0:T(8,128)(2,1)} %slice.8), channel_id=1, source_target_pairs={{0,2},{1,3},{2,4},{3,5},{4,6},{5,7},{6,0},{7,1},{8,10},{9,11},{10,... | collective-permute-start | bytes 1179656 | tf_op jit(solution)/shard_map/ppermute | solution.py:312
  88.9 9.6 %collective-permute-start.3 = (bf16[8,192,128]{2,1,0:T(8,128)(2,1)}, bf16[8,192,128]{2,1,0:T(8,128)(2,1)}, u32[]{:S(2)}, u32[]{:S(2)}) collective-permute-start(bf16[8,192,128]{2,1,0:T(8,128)(2,1)} %slice.9), channel_id=1, source_target_pairs={{0,6},{1,7},{2,0},{3,1},{4,2},{5,3},{6,4},{7,5},{8,14},{9,15},{10,... | collective-permute-start | bytes 1179656 | tf_op jit(solution)/shard_map/ppermute | solution.py:313
  99.7 24.1 %all-to-all-start.2 = ((bf16[4,16,96,128]{3,2,1,0:T(8,128)(2,1)}), bf16[4,16,96,128]{3,2,1,0:T(8,128)(2,1)S(1)}, u32[]{:S(2)}, u32[]{:S(2)}) async-start(bf16[4,16,96,128]{3,2,1,0:T(8,128)(2,1)} %spread.3), calls=%async_computation.2 | async-start | bytes 3145728 | tf_op jit(solution)/shard_map/all_to_all | solution.py:341
  103.7 18.5 %collective-permute-start.4 = (bf16[16,192,128]{2,1,0:T(8,128)(2,1)}, bf16[16,192,128]{2,1,0:T(8,128)(2,1)}, u32[]{:S(2)}, u32[]{:S(2)}) collective-permute-start(bf16[16,192,128]{2,1,0:T(8,128)(2,1)} %bitcast.25), channel_id=1, source_target_pairs={{0,1},{1,0},{2,3},{3,2},{4,5},{5,4},{6,7},{7,6},{8,9},{9,8},{10,11... | collective-permute-start | bytes 2359304 | tf_op jit(solution)/shard_map/ppermute | solution.py:340
  113.4 8.8 %collective-permute-start.5 = (bf16[16,192,128]{2,1,0:T(8,128)(2,1)}, bf16[16,192,128]{2,1,0:T(8,128)(2,1)}, u32[]{:S(2)}, u32[]{:S(2)}) collective-permute-start(bf16[16,192,128]{2,1,0:T(8,128)(2,1)} %copy-done.7), channel_id=1, source_target_pairs={{0,1},{1,0},{2,3},{3,2},{4,5},{5,4},{6,7},{7,6},{8,9},{9,8},{10,11... | collective-permute-start | bytes 2359304 | tf_op jit(solution)/shard_map/ppermute | solution.py:340
  115.3 6.9 %collective-permute-start.8 = (bf16[16,192,128]{2,1,0:T(8,128)(2,1)}, bf16[16,192,128]{2,1,0:T(8,128)(2,1)}, u32[]{:S(2)}, u32[]{:S(2)}) collective-permute-start(bf16[16,192,128]{2,1,0:T(8,128)(2,1)} %copy-done.8), channel_id=1, source_target_pairs={{0,1},{1,0},{2,3},{3,2},{4,5},{5,4},{6,7},{7,6},{8,9},{9,8},{10,11... | collective-permute-start | bytes 2359304 | tf_op jit(solution)/shard_map/ppermute | solution.py:340
  117.7 4.5 %collective-permute-start.6 = (bf16[8,192,128]{2,1,0:T(8,128)(2,1)}, bf16[8,192,128]{2,1,0:T(8,128)(2,1)}, u32[]{:S(2)}, u32[]{:S(2)}) collective-permute-start(bf16[8,192,128]{2,1,0:T(8,128)(2,1)} %copy-done.9), channel_id=1, source_target_pairs={{0,1},{1,0},{2,3},{3,2},{4,5},{5,4},{6,7},{7,6},{8,9},{9,8},{10,11... | collective-permute-start | bytes 1179656 | tf_op jit(solution)/shard_map/ppermute | solution.py:340
  119.7 4.1 %collective-permute-start.7 = (bf16[8,192,128]{2,1,0:T(8,128)(2,1)}, bf16[8,192,128]{2,1,0:T(8,128)(2,1)}, u32[]{:S(2)}, u32[]{:S(2)}) collective-permute-start(bf16[8,192,128]{2,1,0:T(8,128)(2,1)} %collective-permute-done.3.refs_3_), channel_id=1, source_target_pairs={{0,1},{1,0},{2,3},{3,2},{4,5},{5,4},{6,7},{7,6},{8,9},{9,8},{10,11... | collective-permute-start | bytes 1179656 | tf_op jit(solution)/shard_map/ppermute | solution.py:340
  132.0 13.1 %copy-start.4 = (s32[3,9]{1,0:T(4,128)S(1)}, s32[3,9]{1,0:T(4,128)}, u32[]{:S(2)}) copy-start(s32[3,9]{1,0:T(4,128)} %get-tuple-element.42.meta) | copy-start | bytes 328
  132.0 21.1 %all-to-all-start.3 = ((bf16[4,96,1536]{2,1,0:T(8,128)(2,1)}), bf16[4,96,1536]{2,1,0:T(8,128)(2,1)S(1)}, u32[]{:S(2)}, u32[]{:S(2)}) async-start(bf16[4,96,1536]{2,1,0:T(8,128)(2,1)} %wgrad_products.1), calls=%async_computation.3 | async-start | bytes 2359296 | tf_op jit(solution)/shard_map/all_to_all | solution.py:344
  150.7 4.7 %collective-permute-start.9 = (bf16[4,4,192,128]{3,2,1,0:T(8,128)(2,1)}, bf16[4,4,192,128]{3,2,1,0:T(8,128)(2,1)}, u32[]{:S(2)}, u32[]{:S(2)}) collective-permute-start(bf16[4,4,192,128]{3,2,1,0:T(8,128)(2,1)} %get-tuple-element.44), channel_id=1, source_target_pairs={{0,1},{1,0},{2,3},{3,2},{4,5},{5,4},{6,7},{7,6},{8,9},{9,8},{10,11... | collective-permute-start | bytes 2359304 | tf_op jit(solution)/shard_map/ppermute | solution.py:230
  156.7 38.0 %all-to-all-start.4 = ((bf16[16,32,512]{2,1,0:T(8,128)(2,1)}), bf16[16,32,512]{2,1,0:T(8,128)(2,1)S(1)}, u32[]{:S(2)}, u32[]{:S(2)}) async-start(bf16[16,32,512]{2,1,0:T(8,128)(2,1)} %pick_slots.1), calls=%async_computation.4 | async-start | bytes 1048576 | tf_op jit(solution)/shard_map/all_to_all | solution.py:350
  166.8 15.7 %collective-permute-start.10 = (bf16[4,192,128]{2,1,0:T(8,128)(2,1)S(1)}, bf16[4,192,128]{2,1,0:T(8,128)(2,1)S(1)}, u32[]{:S(2)}, u32[]{:S(2)}) collective-permute-start(bf16[4,192,128]{2,1,0:T(8,128)(2,1)S(1)} %get-tuple-element.51), channel_id=1, source_target_pairs={{0,2},{1,3},{2,4},{3,5},{4,6},{5,7},{6,0},{7,1},{8,10},{9,11},{10,... | collective-permute-start | bytes 589832 | tf_op jit(solution)/shard_map/ppermute | solution.py:236
  169.9 12.5 %collective-permute-start.11 = (bf16[4,192,128]{2,1,0:T(8,128)(2,1)S(1)}, bf16[4,192,128]{2,1,0:T(8,128)(2,1)S(1)}, u32[]{:S(2)}, u32[]{:S(2)}) collective-permute-start(bf16[4,192,128]{2,1,0:T(8,128)(2,1)S(1)} %get-tuple-element.52), channel_id=1, source_target_pairs={{0,4},{1,5},{2,6},{3,7},{4,0},{5,1},{6,2},{7,3},{8,12},{9,13},{10,... | collective-permute-start | bytes 589832 | tf_op jit(solution)/shard_map/ppermute | solution.py:236
  175.2 7.3 %collective-permute-start.12 = (bf16[4,192,128]{2,1,0:T(8,128)(2,1)S(1)}, bf16[4,192,128]{2,1,0:T(8,128)(2,1)S(1)}, u32[]{:S(2)}, u32[]{:S(2)}) collective-permute-start(bf16[4,192,128]{2,1,0:T(8,128)(2,1)S(1)} %get-tuple-element.53), channel_id=1, source_target_pairs={{0,6},{1,7},{2,0},{3,1},{4,2},{5,3},{6,4},{7,5},{8,14},{9,15},{10,... | collective-permute-start | bytes 589832 | tf_op jit(solution)/shard_map/ppermute | solution.py:236
  182.6 8.6 %collective-permute-start.13 = (f32[192,128]{1,0:T(8,128)S(1)}, f32[192,128]{1,0:T(8,128)S(1)}, u32[]{:S(2)}, u32[]{:S(2)}) collective-permute-start(f32[192,128]{1,0:T(8,128)S(1)} %get-tuple-element.61), channel_id=1, source_target_pairs={{0,8},{1,9},{2,10},{3,11},{4,12},{5,13},{6,14},{7,15},{8,16},{9,17... | collective-permute-start | bytes 294920 | tf_op jit(solution)/shard_map/ppermute | solution.py:241
  184.8 8.2 %collective-permute-start.14 = (f32[192,128]{1,0:T(8,128)S(1)}, f32[192,128]{1,0:T(8,128)S(1)}, u32[]{:S(2)}, u32[]{:S(2)}) collective-permute-start(f32[192,128]{1,0:T(8,128)S(1)} %get-tuple-element.62), channel_id=1, source_target_pairs={{0,16},{1,17},{2,18},{3,19},{4,20},{5,21},{6,22},{7,23},{8,24},{9,... | collective-permute-start | bytes 294920 | tf_op jit(solution)/shard_map/ppermute | solution.py:241
  188.5 5.7 %collective-permute-start.15 = (f32[192,128]{1,0:T(8,128)S(1)}, f32[192,128]{1,0:T(8,128)S(1)}, u32[]{:S(2)}, u32[]{:S(2)}) collective-permute-start(f32[192,128]{1,0:T(8,128)S(1)} %get-tuple-element.63), channel_id=1, source_target_pairs={{0,24},{1,25},{2,26},{3,27},{4,28},{5,29},{6,30},{7,31},{8,0},{9,1... | collective-permute-start | bytes 294920 | tf_op jit(solution)/shard_map/ppermute | solution.py:241
  (8 other events, 29.9 us)
Sparse Core Ops, SparseCore 0:
  10.1 135.0 all-gather.3

commit v15 on v13

--- a/solution.py
+++ b/solution.py
@@ -136,17 +136,17 @@
         for z in range(n_z):
             a_buf[x * rows : (x + 1) * rows, z * toks : (z + 1) * toks] = grad_ref[x, z]
     span = NC * piece
-    for s in range(0, NY, 2):
-        for copy in copies[s] + copies[s + 1]:
+    for line in copies:
+        for copy in line:
             copy.wait()
-        prod = lax.dot_general(
-            a_buf[...], b_buf[s * span : (s + 2) * span], (((1,), (1,)), ((), ())), preferred_element_type=F32
-        )
-        prod = (prod * scale).astype(BF)
-        for i in range(2):
-            cols = aligned(lax.rem(y - s - i + NY, NY) * span, span, span)
-            for x in range(n_x):
-                out_ref[x, :, cols] = prod[x * rows : (x + 1) * rows, i * span : (i + 1) * span]
+    prod = lax.dot_general(
+        a_buf[...], b_buf[...], (((1,), (1,)), ((), ())), preferred_element_type=F32
+    )
+    prod = (prod * scale).astype(BF)
+    for s in range(NY):
+        cols = aligned(lax.rem(y - s + NY, NY) * span, span, span)
+        for x in range(n_x):
+            out_ref[x, :, cols] = prod[x * rows : (x + 1) * rows, s * span : (s + 1) * span]
 
 
 def wgrad_products(place, grads, own, oth, scale):

time: 206 us -> 206 us (level)
  no operation moved by 1% of the time
where the time goes in v15:
time: 206 us; the launch traced here: 202 us
  starting transfers between devices  88.9 us (43%)
  blocking collectives  39.5 us (19%)
  waiting for transfers between devices  27.5 us (13%)
  Pallas kernels  27.4 us (13%)
  between operations  14.4 us (7%)
  local copies, waits for them, and re-layouts  4.45 us (2%)
    all_gather x1, blocking collectives, per_device(): act_z = lax.all_gather(act_t, 'row', axis=0)  39.5 us
    ppermute x5, starting transfers between devices, per_device(): act_oth = [lax.ppermute(a, 'col', CORE_SWAP) for a in act_own]  18.3 us
    all_to_all x1, starting transfers between devices, per_device(): lax.all_to_all(spread(act_t, groups), 'col', 0, 0, tiled=True)  10.6 us
    ppermute x3, starting transfers between devices, sum_line(): lax.ppermute(by_y[s], 'col', Y_SHIFTS[s])  10.4 us
    ppermute x1, waiting for transfers between devices, share_y(): before = lax.ppermute(x, 'col', Y_SHIFTS[1])  10.3 us
    all_to_all x1, starting transfers between devices, per_device(): lax.all_to_all(slot_parts, 'row', 0, 0, tiled=True).reshape(1, 1, blk, blk)  9.98 us
    all_gather x1, waiting for transfers between devices, per_device(): w_all = lax.all_gather(weight_slots[0, 0], 'row', axis=0)  8.61 us
    ppermute x3, starting transfers between devices, sum_plane(): lax.ppermute(by_x[t], 'col', X_SHIFTS[t])  8.6 us
  transfers between devices with their start and end apart: 22, of which 8 were waited for; matrix products, arithmetic and copies ran while one was open for 1% of the time, Pallas kernels for 13%

profile of v15, /device:TPU:1, one launch (start us, length us, event | category | flops | bytes accessed | tf_op | source)
XLA Modules:
  0.0 202.4 jit_solution(14464816616851604753)
XLA Ops:
  10.1 10.6 %all-to-all-start = ((bf16[32,192,128]{2,1,0:T(8,128)(2,1)}), bf16[32,192,128]{2,1,0:T(8,128)(2,1)S(1)}, u32[]{:S(2)}, u32[]{:S(2)}) async-start(bf16[32,192,128]{2,1,0:T(8,128)(2,1)} %spread.2), calls=%async_computation | async-start | bytes 3145728 | tf_op jit(solution)/shard_map/all_to_all | solution.py:327
  21.8 39.5 %all-gather = bf16[3072,128]{1,0:T(8,128)(2,1)S(1)} all-gather(bf16[192,128]{1,0:T(8,128)(2,1)S(1)} %bitcast.20), channel_id=2, replica_groups=mesh['row'=16,'col'=32] {'row'}, dimensions={0}, use_global_device_ids=true | all-gather | bytes 835584 | tf_op jit(solution)/shard_map/all_gather | solution.py:328
  61.4 6.9 %all-to-all-start.1 = ((bf16[16,96,128]{2,1,0:T(8,128)(2,1)}), bf16[16,96,128]{2,1,0:T(8,128)(2,1)S(1)}, u32[]{:S(2)}, u32[]{:S(2)}) async-start(bf16[16,96,128]{2,1,0:T(8,128)(2,1)} %bitcast.3), calls=%async_computation.1 | async-start | bytes 786432 | tf_op jit(solution)/shard_map/all_to_all | solution.py:333
  68.3 3.3 %collective-permute-start = (bf16[16,192,128]{2,1,0:T(8,128)(2,1)S(1)}, bf16[16,192,128]{2,1,0:T(8,128)(2,1)S(1)}, u32[]{:S(2)}, u32[]{:S(2)}) collective-permute-start(bf16[16,192,128]{2,1,0:T(8,128)(2,1)S(1)} %bitcast.23), channel_id=1, source_target_pairs={{0,2},{1,3},{2,4},{3,5},{4,6},{5,7},{6,0},{7,1},{8,10},{9,11},{10,... | collective-permute-start | bytes 2359304 | tf_op jit(solution)/shard_map/ppermute | solution.py:307
  71.6 3.2 %collective-permute-start.2 = (bf16[16,192,128]{2,1,0:T(8,128)(2,1)S(1)}, bf16[16,192,128]{2,1,0:T(8,128)(2,1)S(1)}, u32[]{:S(2)}, u32[]{:S(2)}) collective-permute-start(bf16[16,192,128]{2,1,0:T(8,128)(2,1)S(1)} %bitcast.24), channel_id=1, source_target_pairs={{0,6},{1,7},{2,0},{3,1},{4,2},{5,3},{6,4},{7,5},{8,14},{9,15},{10,... | collective-permute-start | bytes 2359304 | tf_op jit(solution)/shard_map/ppermute | solution.py:308
  74.8 10.3 %collective-permute-done.refs_1_ = bf16[16,192,128]{2,1,0:T(8,128)(2,1)S(1)} collective-permute-done((bf16[16,192,128]{2,1,0:T(8,128)(2,1)S(1)}, bf16[16,192,128]{2,1,0:T(8,128)(2,1)S(1)}, u32[]{:S(2)}, u32[]{:S(2)}) %collective-permute-start) | collective-permute-done | bytes 786464 | tf_op jit(solution)/shard_map/ppermute | solution.py:307
  88.9 4.5 %collective-permute-start.3 = (bf16[8,192,128]{2,1,0:T(8,128)(2,1)}, bf16[8,192,128]{2,1,0:T(8,128)(2,1)}, u32[]{:S(2)}, u32[]{:S(2)}) collective-permute-start(bf16[8,192,128]{2,1,0:T(8,128)(2,1)} %slice.9), channel_id=1, source_target_pairs={{0,6},{1,7},{2,0},{3,1},{4,2},{5,3},{6,4},{7,5},{8,14},{9,15},{10,... | collective-permute-start | bytes 1179656 | tf_op jit(solution)/shard_map/ppermute | solution.py:310
  93.5 2.3 %layout_tables.1 = (s32[3,9]{1,0:T(4,128)}, s32[3,16]{1,0:T(4,128)}) custom-call(s32[1]{0:T(128)} %bitcast.7.at, s32[12,96]{1,0:T(8,128)} %bitcast.30, s32[12,96]{1,0:T(8,128)} %bitcast.31), custom_call_target="tpu_custom_call" | custom-call | tf_op jit(solution)/shard_map/layout_tables/pallas_call | solution.py:273
  96.2 2.2 %collective-permute-done.3.refs_3_ = bf16[8,192,128]{2,1,0:T(8,128)(2,1)} collective-permute-done((bf16[8,192,128]{2,1,0:T(8,128)(2,1)}, bf16[8,192,128]{2,1,0:T(8,128)(2,1)}, u32[]{:S(2)}, u32[]{:S(2)}) %collective-permute-start.3) | collective-permute-done | bytes 393248 | tf_op jit(solution)/shard_map/ppermute | solution.py:310
  99.7 4.0 %all-to-all-start.2 = ((bf16[4,16,96,128]{3,2,1,0:T(8,128)(2,1)}), bf16[4,16,96,128]{3,2,1,0:T(8,128)(2,1)S(1)}, u32[]{:S(2)}, u32[]{:S(2)}) async-start(bf16[4,16,96,128]{3,2,1,0:T(8,128)(2,1)} %spread.3), calls=%async_computation.2 | async-start | bytes 3145728 | tf_op jit(solution)/shard_map/all_to_all | solution.py:338
  103.7 9.7 %collective-permute-start.4 = (bf16[16,192,128]{2,1,0:T(8,128)(2,1)}, bf16[16,192,128]{2,1,0:T(8,128)(2,1)}, u32[]{:S(2)}, u32[]{:S(2)}) collective-permute-start(bf16[16,192,128]{2,1,0:T(8,128)(2,1)} %bitcast.25), channel_id=1, source_target_pairs={{0,1},{1,0},{2,3},{3,2},{4,5},{5,4},{6,7},{7,6},{8,9},{9,8},{10,11... | collective-permute-start | bytes 2359304 | tf_op jit(solution)/shard_map/ppermute | solution.py:337
  115.3 2.4 %collective-permute-start.8 = (bf16[16,192,128]{2,1,0:T(8,128)(2,1)}, bf16[16,192,128]{2,1,0:T(8,128)(2,1)}, u32[]{:S(2)}, u32[]{:S(2)}) collective-permute-start(bf16[16,192,128]{2,1,0:T(8,128)(2,1)} %copy-done.8), channel_id=1, source_target_pairs={{0,1},{1,0},{2,3},{3,2},{4,5},{5,4},{6,7},{7,6},{8,9},{9,8},{10,11... | collective-permute-start | bytes 2359304 | tf_op jit(solution)/shard_map/ppermute | solution.py:337
  119.7 2.4 %collective-permute-start.7 = (bf16[8,192,128]{2,1,0:T(8,128)(2,1)}, bf16[8,192,128]{2,1,0:T(8,128)(2,1)}, u32[]{:S(2)}, u32[]{:S(2)}) collective-permute-start(bf16[8,192,128]{2,1,0:T(8,128)(2,1)} %collective-permute-done.3.refs_3_), channel_id=1, source_target_pairs={{0,1},{1,0},{2,3},{3,2},{4,5},{5,4},{6,7},{7,6},{8,9},{9,8},{10,11... | collective-permute-start | bytes 1179656 | tf_op jit(solution)/shard_map/ppermute | solution.py:337
  123.8 8.2 %wgrad_products.1 = bf16[4,96,1536]{2,1,0:T(8,128)(2,1)} custom-call(s32[3]{0:T(128)S(1)} %pad_add_fusion.place, bf16[4,16,96,128]{3,2,1,0:T(8,128)(2,1)S(1)} %all-to-all-done.2.grad_ref, bf16[16,192,128]{2,1,0:T(8,128)(2,1)} %bitcast.26, bf16[16,192,128]{2,1,0:T(8,128)(2,1)} %copy-done.7, bf16[8,192,128]{2,1,0:T(8,128)(2,1)} %copy-done.9, ...), custom_call_target="tpu_custom_call" | custom-call | tf_op jit(solution)/shard_map/wgrad_products/pallas_call | solution.py:157
  132.0 4.6 %all-to-all-start.3 = ((bf16[4,96,1536]{2,1,0:T(8,128)(2,1)}), bf16[4,96,1536]{2,1,0:T(8,128)(2,1)S(1)}, u32[]{:S(2)}, u32[]{:S(2)}) async-start(bf16[4,96,1536]{2,1,0:T(8,128)(2,1)} %wgrad_products.1), calls=%async_computation.3 | async-start | bytes 2359296 | tf_op jit(solution)/shard_map/all_to_all | solution.py:341
  136.5 8.6 %all-gather.4.cloned.1.call-done = bf16[16,1,512,512]{3,2,1,0:T(8,128)(2,1)} async-done(((bf16[1,1,512,512]{3,2,1,0:T(8,128)(2,1)}), bf16[16,1,512,512]{3,2,1,0:T(8,128)(2,1)}) %all-gather.4.cloned.1.call-update) | async-done | bytes 8388624 | tf_op jit(solution)/shard_map/all_gather | solution.py:325
  145.2 5.5 %in_step.1 = (bf16[4,4,192,128]{3,2,1,0:T(8,128)(2,1)}, bf16[4,4,192,128]{3,2,1,0:T(8,128)(2,1)}) custom-call(s32[3,9]{1,0:T(4,128)S(1)} %copy-done.4, s32[3]{0:T(128)S(1)} %pad_add_fusion.place, bf16[128,1536]{1,0:T(8,128)(2,1)S(1)} %copy-done, bf16[16,512,512]{2,1,0:T(8,128)(2,1)} %bitcast.21), custom_call_target="tpu_custom_call" | custom-call | tf_op jit(solution)/shard_map/in_step/pallas_call | solution.py:66
  150.7 2.5 %collective-permute-start.9 = (bf16[4,4,192,128]{3,2,1,0:T(8,128)(2,1)}, bf16[4,4,192,128]{3,2,1,0:T(8,128)(2,1)}, u32[]{:S(2)}, u32[]{:S(2)}) collective-permute-start(bf16[4,4,192,128]{3,2,1,0:T(8,128)(2,1)} %get-tuple-element.44), channel_id=1, source_target_pairs={{0,1},{1,0},{2,3},{3,2},{4,5},{5,4},{6,7},{7,6},{8,9},{9,8},{10,11... | collective-permute-start | bytes 2359304 | tf_op jit(solution)/shard_map/ppermute | solution.py:227
  156.7 10.0 %all-to-all-start.4 = ((bf16[16,32,512]{2,1,0:T(8,128)(2,1)}), bf16[16,32,512]{2,1,0:T(8,128)(2,1)S(1)}, u32[]{:S(2)}, u32[]{:S(2)}) async-start(bf16[16,32,512]{2,1,0:T(8,128)(2,1)} %pick_slots.1), calls=%async_computation.4 | async-start | bytes 1048576 | tf_op jit(solution)/shard_map/all_to_all | solution.py:347
  166.7 3.1 %collective-permute-start.10 = (bf16[4,192,128]{2,1,0:T(8,128)(2,1)S(1)}, bf16[4,192,128]{2,1,0:T(8,128)(2,1)S(1)}, u32[]{:S(2)}, u32[]{:S(2)}) collective-permute-start(bf16[4,192,128]{2,1,0:T(8,128)(2,1)S(1)} %get-tuple-element.51), channel_id=1, source_target_pairs={{0,2},{1,3},{2,4},{3,5},{4,6},{5,7},{6,0},{7,1},{8,10},{9,11},{10,... | collective-permute-start | bytes 589832 | tf_op jit(solution)/shard_map/ppermute | solution.py:233
  169.9 5.3 %collective-permute-start.11 = (bf16[4,192,128]{2,1,0:T(8,128)(2,1)S(1)}, bf16[4,192,128]{2,1,0:T(8,128)(2,1)S(1)}, u32[]{:S(2)}, u32[]{:S(2)}) collective-permute-start(bf16[4,192,128]{2,1,0:T(8,128)(2,1)S(1)} %get-tuple-element.52), channel_id=1, source_target_pairs={{0,4},{1,5},{2,6},{3,7},{4,0},{5,1},{6,2},{7,3},{8,12},{9,13},{10,... | collective-permute-start | bytes 589832 | tf_op jit(solution)/shard_map/ppermute | solution.py:233
  177.1 5.3 %out_step.1 = bf16[128,1536]{1,0:T(8,128)(2,1)} custom-call(s32[3,9]{1,0:T(4,128)S(1)} %copy-done.4, bf16[6144,128]{1,0:T(8,128)(2,1)S(1)} %bitcast.18, bf16[16,512,512]{2,1,0:T(8,128)(2,1)} %bitcast.22), custom_call_target="tpu_custom_call" | custom-call | tf_op jit(solution)/shard_map/out_step/pallas_call | solution.py:98
  184.7 3.7 %collective-permute-start.14 = (f32[192,128]{1,0:T(8,128)S(1)}, f32[192,128]{1,0:T(8,128)S(1)}, u32[]{:S(2)}, u32[]{:S(2)}) collective-permute-start(f32[192,128]{1,0:T(8,128)S(1)} %get-tuple-element.62), channel_id=1, source_target_pairs={{0,16},{1,17},{2,18},{3,19},{4,20},{5,21},{6,22},{7,23},{8,24},{9,... | collective-permute-start | bytes 294920 | tf_op jit(solution)/shard_map/ppermute | solution.py:238
  188.4 2.7 %collective-permute-start.15 = (f32[192,128]{1,0:T(8,128)S(1)}, f32[192,128]{1,0:T(8,128)S(1)}, u32[]{:S(2)}, u32[]{:S(2)}) collective-permute-start(f32[192,128]{1,0:T(8,128)S(1)} %get-tuple-element.63), channel_id=1, source_target_pairs={{0,24},{1,25},{2,26},{3,27},{4,28},{5,29},{6,30},{7,31},{8,0},{9,1... | collective-permute-start | bytes 294920 | tf_op jit(solution)/shard_map/ppermute | solution.py:238
  (58 shorter events, 26.9 us)
Async XLA Ops:
  7.2 138.0 %all-gather.4.cloned.1.call-start = ((), (), s32[]{:S(2)}) async-start(), calls=%async_computation.5 | async-start | bytes 8912896 | tf_op jit(solution)/shard_map/all_gather | solution.py:325
  10.1 51.2 %all-to-all-start = ((bf16[32,192,128]{2,1,0:T(8,128)(2,1)}), bf16[32,192,128]{2,1,0:T(8,128)(2,1)S(1)}, u32[]{:S(2)}, u32[]{:S(2)}) async-start(bf16[32,192,128]{2,1,0:T(8,128)(2,1)} %spread.2), calls=%async_computation | async-start | bytes 3145728 | tf_op jit(solution)/shard_map/all_to_all | solution.py:327
  61.4 38.3 %copy-start.6 = (bf16[3072,128]{1,0:T(8,128)(2,1)}, bf16[3072,128]{1,0:T(8,128)(2,1)S(1)}, u32[]{:S(2)}) copy-start(bf16[3072,128]{1,0:T(8,128)(2,1)S(1)} %all-gather) | copy-start | bytes 2359300
  61.4 37.1 %all-to-all-start.1 = ((bf16[16,96,128]{2,1,0:T(8,128)(2,1)}), bf16[16,96,128]{2,1,0:T(8,128)(2,1)S(1)}, u32[]{:S(2)}, u32[]{:S(2)}) async-start(bf16[16,96,128]{2,1,0:T(8,128)(2,1)} %bitcast.3), calls=%async_computation.1 | async-start | bytes 786432 | tf_op jit(solution)/shard_map/all_to_all | solution.py:333
  68.3 16.8 %collective-permute-start = (bf16[16,192,128]{2,1,0:T(8,128)(2,1)S(1)}, bf16[16,192,128]{2,1,0:T(8,128)(2,1)S(1)}, u32[]{:S(2)}, u32[]{:S(2)}) collective-permute-start(bf16[16,192,128]{2,1,0:T(8,128)(2,1)S(1)} %bitcast.23), channel_id=1, source_target_pairs={{0,2},{1,3},{2,4},{3,5},{4,6},{5,7},{6,0},{7,1},{8,10},{9,11},{10,... | collective-permute-start | bytes 2359304 | tf_op jit(solution)/shard_map/ppermute | solution.py:307
  71.6 16.3 %collective-permute-start.2 = (bf16[16,192,128]{2,1,0:T(8,128)(2,1)S(1)}, bf16[16,192,128]{2,1,0:T(8,128)(2,1)S(1)}, u32[]{:S(2)}, u32[]{:S(2)}) collective-permute-start(bf16[16,192,128]{2,1,0:T(8,128)(2,1)S(1)} %bitcast.24), channel_id=1, source_target_pairs={{0,6},{1,7},{2,0},{3,1},{4,2},{5,3},{6,4},{7,5},{8,14},{9,15},{10,... | collective-permute-start | bytes 2359304 | tf_op jit(solution)/shard_map/ppermute | solution.py:308
  85.9 10.3 %collective-permute-start.1 = (bf16[8,192,128]{2,1,0:T(8,128)(2,1)}, bf16[8,192,128]{2,1,0:T(8,128)(2,1)S(1)}, u32[]{:S(2)}, u32[]{:S(2)}) collective-permute-start(bf16[8,192,128]{2,1,0:T(8,128)(2,1)} %slice.8), channel_id=1, source_target_pairs={{0,2},{1,3},{2,4},{3,5},{4,6},{5,7},{6,0},{7,1},{8,10},{9,11},{10,... | collective-permute-start | bytes 1179656 | tf_op jit(solution)/shard_map/ppermute | solution.py:309
  88.9 9.6 %collective-permute-start.3 = (bf16[8,192,128]{2,1,0:T(8,128)(2,1)}, bf16[8,192,128]{2,1,0:T(8,128)(2,1)}, u32[]{:S(2)}, u32[]{:S(2)}) collective-permute-start(bf16[8,192,128]{2,1,0:T(8,128)(2,1)} %slice.9), channel_id=1, source_target_pairs={{0,6},{1,7},{2,0},{3,1},{4,2},{5,3},{6,4},{7,5},{8,14},{9,15},{10,... | collective-permute-start | bytes 1179656 | tf_op jit(solution)/shard_map/ppermute | solution.py:310
  99.7 24.1 %all-to-all-start.2 = ((bf16[4,16,96,128]{3,2,1,0:T(8,128)(2,1)}), bf16[4,16,96,128]{3,2,1,0:T(8,128)(2,1)S(1)}, u32[]{:S(2)}, u32[]{:S(2)}) async-start(bf16[4,16,96,128]{3,2,1,0:T(8,128)(2,1)} %spread.3), calls=%async_computation.2 | async-start | bytes 3145728 | tf_op jit(solution)/shard_map/all_to_all | solution.py:338
  103.7 18.5 %collective-permute-start.4 = (bf16[16,192,128]{2,1,0:T(8,128)(2,1)}, bf16[16,192,128]{2,1,0:T(8,128)(2,1)}, u32[]{:S(2)}, u32[]{:S(2)}) collective-permute-start(bf16[16,192,128]{2,1,0:T(8,128)(2,1)} %bitcast.25), channel_id=1, source_target_pairs={{0,1},{1,0},{2,3},{3,2},{4,5},{5,4},{6,7},{7,6},{8,9},{9,8},{10,11... | collective-permute-start | bytes 2359304 | tf_op jit(solution)/shard_map/ppermute | solution.py:337
  113.4 8.8 %collective-permute-start.5 = (bf16[16,192,128]{2,1,0:T(8,128)(2,1)}, bf16[16,192,128]{2,1,0:T(8,128)(2,1)}, u32[]{:S(2)}, u32[]{:S(2)}) collective-permute-start(bf16[16,192,128]{2,1,0:T(8,128)(2,1)} %copy-done.7), channel_id=1, source_target_pairs={{0,1},{1,0},{2,3},{3,2},{4,5},{5,4},{6,7},{7,6},{8,9},{9,8},{10,11... | collective-permute-start | bytes 2359304 | tf_op jit(solution)/shard_map/ppermute | solution.py:337
  115.3 6.9 %collective-permute-start.8 = (bf16[16,192,128]{2,1,0:T(8,128)(2,1)}, bf16[16,192,128]{2,1,0:T(8,128)(2,1)}, u32[]{:S(2)}, u32[]{:S(2)}) collective-permute-start(bf16[16,192,128]{2,1,0:T(8,128)(2,1)} %copy-done.8), channel_id=1, source_target_pairs={{0,1},{1,0},{2,3},{3,2},{4,5},{5,4},{6,7},{7,6},{8,9},{9,8},{10,11... | collective-permute-start | bytes 2359304 | tf_op jit(solution)/shard_map/ppermute | solution.py:337
  117.7 4.5 %collective-permute-start.6 = (bf16[8,192,128]{2,1,0:T(8,128)(2,1)}, bf16[8,192,128]{2,1,0:T(8,128)(2,1)}, u32[]{:S(2)}, u32[]{:S(2)}) collective-permute-start(bf16[8,192,128]{2,1,0:T(8,128)(2,1)} %copy-done.9), channel_id=1, source_target_pairs={{0,1},{1,0},{2,3},{3,2},{4,5},{5,4},{6,7},{7,6},{8,9},{9,8},{10,11... | collective-permute-start | bytes 1179656 | tf_op jit(solution)/shard_map/ppermute | solution.py:337
  119.7 4.1 %collective-permute-start.7 = (bf16[8,192,128]{2,1,0:T(8,128)(2,1)}, bf16[8,192,128]{2,1,0:T(8,128)(2,1)}, u32[]{:S(2)}, u32[]{:S(2)}) collective-permute-start(bf16[8,192,128]{2,1,0:T(8,128)(2,1)} %collective-permute-done.3.refs_3_), channel_id=1, source_target_pairs={{0,1},{1,0},{2,3},{3,2},{4,5},{5,4},{6,7},{7,6},{8,9},{9,8},{10,11... | collective-permute-start | bytes 1179656 | tf_op jit(solution)/shard_map/ppermute | solution.py:337
  132.0 13.2 %copy-start.4 = (s32[3,9]{1,0:T(4,128)S(1)}, s32[3,9]{1,0:T(4,128)}, u32[]{:S(2)}) copy-start(s32[3,9]{1,0:T(4,128)} %get-tuple-element.42.meta) | copy-start | bytes 328
  132.0 21.2 %all-to-all-start.3 = ((bf16[4,96,1536]{2,1,0:T(8,128)(2,1)}), bf16[4,96,1536]{2,1,0:T(8,128)(2,1)S(1)}, u32[]{:S(2)}, u32[]{:S(2)}) async-start(bf16[4,96,1536]{2,1,0:T(8,128)(2,1)} %wgrad_products.1), calls=%async_computation.3 | async-start | bytes 2359296 | tf_op jit(solution)/shard_map/all_to_all | solution.py:341
  150.7 4.7 %collective-permute-start.9 = (bf16[4,4,192,128]{3,2,1,0:T(8,128)(2,1)}, bf16[4,4,192,128]{3,2,1,0:T(8,128)(2,1)}, u32[]{:S(2)}, u32[]{:S(2)}) collective-permute-start(bf16[4,4,192,128]{3,2,1,0:T(8,128)(2,1)} %get-tuple-element.44), channel_id=1, source_target_pairs={{0,1},{1,0},{2,3},{3,2},{4,5},{5,4},{6,7},{7,6},{8,9},{9,8},{10,11... | collective-permute-start | bytes 2359304 | tf_op jit(solution)/shard_map/ppermute | solution.py:227
  156.7 38.0 %all-to-all-start.4 = ((bf16[16,32,512]{2,1,0:T(8,128)(2,1)}), bf16[16,32,512]{2,1,0:T(8,128)(2,1)S(1)}, u32[]{:S(2)}, u32[]{:S(2)}) async-start(bf16[16,32,512]{2,1,0:T(8,128)(2,1)} %pick_slots.1), calls=%async_computation.4 | async-start | bytes 1048576 | tf_op jit(solution)/shard_map/all_to_all | solution.py:347
  166.7 15.7 %collective-permute-start.10 = (bf16[4,192,128]{2,1,0:T(8,128)(2,1)S(1)}, bf16[4,192,128]{2,1,0:T(8,128)(2,1)S(1)}, u32[]{:S(2)}, u32[]{:S(2)}) collective-permute-start(bf16[4,192,128]{2,1,0:T(8,128)(2,1)S(1)} %get-tuple-element.51), channel_id=1, source_target_pairs={{0,2},{1,3},{2,4},{3,5},{4,6},{5,7},{6,0},{7,1},{8,10},{9,11},{10,... | collective-permute-start | bytes 589832 | tf_op jit(solution)/shard_map/ppermute | solution.py:233
  169.9 12.6 %collective-permute-start.11 = (bf16[4,192,128]{2,1,0:T(8,128)(2,1)S(1)}, bf16[4,192,128]{2,1,0:T(8,128)(2,1)S(1)}, u32[]{:S(2)}, u32[]{:S(2)}) collective-permute-start(bf16[4,192,128]{2,1,0:T(8,128)(2,1)S(1)} %get-tuple-element.52), channel_id=1, source_target_pairs={{0,4},{1,5},{2,6},{3,7},{4,0},{5,1},{6,2},{7,3},{8,12},{9,13},{10,... | collective-permute-start | bytes 589832 | tf_op jit(solution)/shard_map/ppermute | solution.py:233
  175.2 7.3 %collective-permute-start.12 = (bf16[4,192,128]{2,1,0:T(8,128)(2,1)S(1)}, bf16[4,192,128]{2,1,0:T(8,128)(2,1)S(1)}, u32[]{:S(2)}, u32[]{:S(2)}) collective-permute-start(bf16[4,192,128]{2,1,0:T(8,128)(2,1)S(1)} %get-tuple-element.53), channel_id=1, source_target_pairs={{0,6},{1,7},{2,0},{3,1},{4,2},{5,3},{6,4},{7,5},{8,14},{9,15},{10,... | collective-permute-start | bytes 589832 | tf_op jit(solution)/shard_map/ppermute | solution.py:233
  182.5 8.6 %collective-permute-start.13 = (f32[192,128]{1,0:T(8,128)S(1)}, f32[192,128]{1,0:T(8,128)S(1)}, u32[]{:S(2)}, u32[]{:S(2)}) collective-permute-start(f32[192,128]{1,0:T(8,128)S(1)} %get-tuple-element.61), channel_id=1, source_target_pairs={{0,8},{1,9},{2,10},{3,11},{4,12},{5,13},{6,14},{7,15},{8,16},{9,17... | collective-permute-start | bytes 294920 | tf_op jit(solution)/shard_map/ppermute | solution.py:238
  184.7 8.2 %collective-permute-start.14 = (f32[192,128]{1,0:T(8,128)S(1)}, f32[192,128]{1,0:T(8,128)S(1)}, u32[]{:S(2)}, u32[]{:S(2)}) collective-permute-start(f32[192,128]{1,0:T(8,128)S(1)} %get-tuple-element.62), channel_id=1, source_target_pairs={{0,16},{1,17},{2,18},{3,19},{4,20},{5,21},{6,22},{7,23},{8,24},{9,... | collective-permute-start | bytes 294920 | tf_op jit(solution)/shard_map/ppermute | solution.py:238
  188.4 5.7 %collective-permute-start.15 = (f32[192,128]{1,0:T(8,128)S(1)}, f32[192,128]{1,0:T(8,128)S(1)}, u32[]{:S(2)}, u32[]{:S(2)}) collective-permute-start(f32[192,128]{1,0:T(8,128)S(1)} %get-tuple-element.63), channel_id=1, source_target_pairs={{0,24},{1,25},{2,26},{3,27},{4,28},{5,29},{6,30},{7,31},{8,0},{9,1... | collective-permute-start | bytes 294920 | tf_op jit(solution)/shard_map/ppermute | solution.py:238
  (8 other events, 29.9 us)
Sparse Core Ops, SparseCore 0:
  10.1 135.0 all-gather.3

commit v16 on v12

--- a/solution.py
+++ b/solution.py
@@ -104,17 +104,17 @@
         for z in range(n_z):
             a_buf[x * rows : (x + 1) * rows, z * toks : (z + 1) * toks] = grad_ref[x, z]
     span = NC * piece
-    for s in range(0, NY, 2):
-        for copy in copies[s] + copies[s + 1]:
+    for line in copies:
+        for copy in line:
             copy.wait()
-        prod = lax.dot_general(
-            a_buf[...], b_buf[s * span : (s + 2) * span], (((1,), (1,)), ((), ())), preferred_element_type=F32
-        )
-        prod = (prod * scale).astype(BF)
-        for i in range(2):
-            cols = aligned(lax.rem(y - s - i + NY, NY) * span, span, span)
-            for x in range(n_x):
-                out_ref[x, :, cols] = prod[x * rows : (x + 1) * rows, i * span : (i + 1) * span]
+    prod = lax.dot_general(
+        a_buf[...], b_buf[...], (((1,), (1,)), ((), ())), preferred_element_type=F32
+    )
+    prod = (prod * scale).astype(BF)
+    for s in range(NY):
+        cols = aligned(lax.rem(y - s + NY, NY) * span, span, span)
+        for x in range(n_x):
+            out_ref[x, :, cols] = prod[x * rows : (x + 1) * rows, s * span : (s + 1) * span]
 
 
 def wgrad_products(place, grads, own, oth, scale):

time: 205 us -> 205 us (level)
  no operation moved by 1% of the time
where the time goes in v16:
time: 205 us; the launch traced here: 204 us
  starting transfers between devices  81.8 us (40%)
  blocking collectives  44.1 us (22%)
  waiting for transfers between devices  37 us (18%)
  Pallas kernels  22.4 us (11%)
  between operations  14.4 us (7%)
  local copies, waits for them, and re-layouts  4.45 us (2%)
    all_gather x1, blocking collectives, per_device(): act_z = lax.all_gather(act_t, 'row', axis=0)  44.1 us
    ppermute x3, starting transfers between devices, sum_plane(): lax.ppermute(by_y[s], 'col', Y_SHIFTS[s])  11.4 us
    ppermute x3, starting transfers between devices, sum_plane(): lax.ppermute(by_x[t], 'col', X_SHIFTS[t])  10.8 us
    ppermute x1, waiting for transfers between devices, share_y(): before = lax.ppermute(x, 'col', Y_SHIFTS[1])  10.7 us
    ppermute x5, starting transfers between devices, per_device(): act_oth = [lax.ppermute(a, 'col', CORE_SWAP) for a in act_own]  10.6 us
    all_to_all x1, starting transfers between devices, per_device(): lax.all_to_all(slot_parts, 'row', 0, 0, tiled=True).reshape(1, 1, blk, blk)  10.1 us
    all_to_all x1, starting transfers between devices, per_device(): lax.all_to_all(spread(act_t, groups), 'col', 0, 0, tiled=True)  9.6 us
    all_gather x1, waiting for transfers between devices, per_device(): w_all = lax.all_gather(weight_slots[0, 0], 'row', axis=0)  8.8 us
  transfers between devices with their start and end apart: 22, of which 10 were waited for; matrix products, arithmetic and copies ran while one was open for 1% of the time, Pallas kernels for 11%

profile of v16, /device:TPU:8, one launch (start us, length us, event | category | flops | bytes accessed | tf_op | source)
XLA Modules:
  0.0 204.2 jit_solution(10698218536824809109)
XLA Ops:
  10.1 9.6 %all-to-all-start = ((bf16[32,192,128]{2,1,0:T(8,128)(2,1)}), bf16[32,192,128]{2,1,0:T(8,128)(2,1)S(1)}, u32[]{:S(2)}, u32[]{:S(2)}) async-start(bf16[32,192,128]{2,1,0:T(8,128)(2,1)} %spread.2), calls=%async_computation | async-start | bytes 3145728 | tf_op jit(solution)/shard_map/all_to_all | solution.py:292
  20.8 44.1 %all-gather = bf16[3072,128]{1,0:T(8,128)(2,1)S(1)} all-gather(bf16[192,128]{1,0:T(8,128)(2,1)S(1)} %bitcast.20), channel_id=2, replica_groups=mesh['row'=16,'col'=32] {'row'}, dimensions={0}, use_global_device_ids=true | all-gather | bytes 835584 | tf_op jit(solution)/shard_map/all_gather | solution.py:293
  64.8 7.6 %all-to-all-start.1 = ((bf16[16,96,128]{2,1,0:T(8,128)(2,1)}), bf16[16,96,128]{2,1,0:T(8,128)(2,1)S(1)}, u32[]{:S(2)}, u32[]{:S(2)}) async-start(bf16[16,96,128]{2,1,0:T(8,128)(2,1)} %bitcast.3), calls=%async_computation.1 | async-start | bytes 786432 | tf_op jit(solution)/shard_map/all_to_all | solution.py:298
  72.4 3.3 %collective-permute-start = (bf16[16,192,128]{2,1,0:T(8,128)(2,1)S(1)}, bf16[16,192,128]{2,1,0:T(8,128)(2,1)S(1)}, u32[]{:S(2)}, u32[]{:S(2)}) collective-permute-start(bf16[16,192,128]{2,1,0:T(8,128)(2,1)S(1)} %bitcast.22), channel_id=1, source_target_pairs={{0,2},{1,3},{2,4},{3,5},{4,6},{5,7},{6,0},{7,1},{8,10},{9,11},{10,... | collective-permute-start | bytes 2359304 | tf_op jit(solution)/shard_map/ppermute | solution.py:272
  75.7 2.6 %collective-permute-start.2 = (bf16[16,192,128]{2,1,0:T(8,128)(2,1)S(1)}, bf16[16,192,128]{2,1,0:T(8,128)(2,1)S(1)}, u32[]{:S(2)}, u32[]{:S(2)}) collective-permute-start(bf16[16,192,128]{2,1,0:T(8,128)(2,1)S(1)} %bitcast.23), channel_id=1, source_target_pairs={{0,6},{1,7},{2,0},{3,1},{4,2},{5,3},{6,4},{7,5},{8,14},{9,15},{10,... | collective-permute-start | bytes 2359304 | tf_op jit(solution)/shard_map/ppermute | solution.py:273
  78.3 10.7 %collective-permute-done.refs_1_ = bf16[16,192,128]{2,1,0:T(8,128)(2,1)S(1)} collective-permute-done((bf16[16,192,128]{2,1,0:T(8,128)(2,1)S(1)}, bf16[16,192,128]{2,1,0:T(8,128)(2,1)S(1)}, u32[]{:S(2)}, u32[]{:S(2)}) %collective-permute-start) | collective-permute-done | bytes 786464 | tf_op jit(solution)/shard_map/ppermute | solution.py:272
  89.8 3.2 %collective-permute-start.1 = (bf16[8,192,128]{2,1,0:T(8,128)(2,1)}, bf16[8,192,128]{2,1,0:T(8,128)(2,1)S(1)}, u32[]{:S(2)}, u32[]{:S(2)}) collective-permute-start(bf16[8,192,128]{2,1,0:T(8,128)(2,1)} %slice.8), channel_id=1, source_target_pairs={{0,2},{1,3},{2,4},{3,5},{4,6},{5,7},{6,0},{7,1},{8,10},{9,11},{10,... | collective-permute-start | bytes 1179656 | tf_op jit(solution)/shard_map/ppermute | solution.py:274
  94.1 2.6 %collective-permute-start.3 = (bf16[8,192,128]{2,1,0:T(8,128)(2,1)}, bf16[8,192,128]{2,1,0:T(8,128)(2,1)}, u32[]{:S(2)}, u32[]{:S(2)}) collective-permute-start(bf16[8,192,128]{2,1,0:T(8,128)(2,1)} %slice.9), channel_id=1, source_target_pairs={{0,6},{1,7},{2,0},{3,1},{4,2},{5,3},{6,4},{7,5},{8,14},{9,15},{10,... | collective-permute-start | bytes 1179656 | tf_op jit(solution)/shard_map/ppermute | solution.py:275
  99.7 4.4 %collective-permute-done.3.refs_3_ = bf16[8,192,128]{2,1,0:T(8,128)(2,1)} collective-permute-done((bf16[8,192,128]{2,1,0:T(8,128)(2,1)}, bf16[8,192,128]{2,1,0:T(8,128)(2,1)}, u32[]{:S(2)}, u32[]{:S(2)}) %collective-permute-start.3) | collective-permute-done | bytes 393248 | tf_op jit(solution)/shard_map/ppermute | solution.py:275
  105.3 4.4 %all-to-all-start.2 = ((bf16[4,16,96,128]{3,2,1,0:T(8,128)(2,1)}), bf16[4,16,96,128]{3,2,1,0:T(8,128)(2,1)S(1)}, u32[]{:S(2)}, u32[]{:S(2)}) async-start(bf16[4,16,96,128]{3,2,1,0:T(8,128)(2,1)} %spread.3), calls=%async_computation.2 | async-start | bytes 3145728 | tf_op jit(solution)/shard_map/all_to_all | solution.py:303
  115.9 2.4 %collective-permute-start.6 = (bf16[8,192,128]{2,1,0:T(8,128)(2,1)}, bf16[8,192,128]{2,1,0:T(8,128)(2,1)}, u32[]{:S(2)}, u32[]{:S(2)}) collective-permute-start(bf16[8,192,128]{2,1,0:T(8,128)(2,1)} %copy-done.9), channel_id=1, source_target_pairs={{0,1},{1,0},{2,3},{3,2},{4,5},{5,4},{6,7},{7,6},{8,9},{9,8},{10,11... | collective-permute-start | bytes 1179656 | tf_op jit(solution)/shard_map/ppermute | solution.py:302
  123.4 8.2 %wgrad_products.1 = bf16[4,96,1536]{2,1,0:T(8,128)(2,1)} custom-call(s32[3]{0:T(128)S(1)} %pad_add_fusion.place, bf16[4,16,96,128]{3,2,1,0:T(8,128)(2,1)S(1)} %all-to-all-done.2.grad_ref, bf16[16,192,128]{2,1,0:T(8,128)(2,1)} %bitcast.25, bf16[16,192,128]{2,1,0:T(8,128)(2,1)} %copy-done.7, bf16[8,192,128]{2,1,0:T(8,128)(2,1)} %copy-done.9, ...), custom_call_target="tpu_custom_call" | custom-call | tf_op jit(solution)/shard_map/wgrad_products/pallas_call | solution.py:125
  131.6 3.7 %all-to-all-start.3 = ((bf16[4,96,1536]{2,1,0:T(8,128)(2,1)}), bf16[4,96,1536]{2,1,0:T(8,128)(2,1)S(1)}, u32[]{:S(2)}, u32[]{:S(2)}) async-start(bf16[4,96,1536]{2,1,0:T(8,128)(2,1)} %wgrad_products.1), calls=%async_computation.3 | async-start | bytes 2359296 | tf_op jit(solution)/shard_map/all_to_all | solution.py:306
  135.3 8.8 %all-gather.4.cloned.1.call-done = bf16[16,1,512,512]{3,2,1,0:T(8,128)(2,1)} async-done(((bf16[1,1,512,512]{3,2,1,0:T(8,128)(2,1)}), bf16[16,1,512,512]{3,2,1,0:T(8,128)(2,1)}) %all-gather.4.cloned.1.call-update) | async-done | bytes 8388624 | tf_op jit(solution)/shard_map/all_gather | solution.py:290
  144.1 6.9 %tokens_step.1 = (bf16[128,1536]{1,0:T(8,128)(2,1)}, bf16[4,4,192,128]{3,2,1,0:T(8,128)(2,1)}, bf16[4,4,192,128]{3,2,1,0:T(8,128)(2,1)}) custom-call(s32[3,9]{1,0:T(4,128)S(1)} %copy-done.5, s32[3]{0:T(128)S(1)} %pad_add_fusion.place, bf16[6144,128]{1,0:T(8,128)(2,1)S(1)} %bitcast.18, bf16[128,1536]{1,0:T(8,128)(2,1)S(1)} %copy-done, ...), custom_call_target="tpu_custom_call" | custom-call | tf_op jit(solution)/shard_map/tokens_step/pallas_call | solution.py:64
  155.8 10.1 %all-to-all-start.4 = ((bf16[16,32,512]{2,1,0:T(8,128)(2,1)}), bf16[16,32,512]{2,1,0:T(8,128)(2,1)S(1)}, u32[]{:S(2)}, u32[]{:S(2)}) async-start(bf16[16,32,512]{2,1,0:T(8,128)(2,1)} %pick_slots.1), calls=%async_computation.4 | async-start | bytes 1048576 | tf_op jit(solution)/shard_map/all_to_all | solution.py:312
  165.8 3.1 %collective-permute-start.10 = (bf16[4,192,128]{2,1,0:T(8,128)(2,1)S(1)}, bf16[4,192,128]{2,1,0:T(8,128)(2,1)S(1)}, u32[]{:S(2)}, u32[]{:S(2)}) collective-permute-start(bf16[4,192,128]{2,1,0:T(8,128)(2,1)S(1)} %get-tuple-element.47), channel_id=1, source_target_pairs={{0,2},{1,3},{2,4},{3,5},{4,6},{5,7},{6,0},{7,1},{8,10},{9,11},{10,... | collective-permute-start | bytes 589832 | tf_op jit(solution)/shard_map/ppermute | solution.py:201
  168.9 3.8 %collective-permute-start.11 = (bf16[4,192,128]{2,1,0:T(8,128)(2,1)S(1)}, bf16[4,192,128]{2,1,0:T(8,128)(2,1)S(1)}, u32[]{:S(2)}, u32[]{:S(2)}) collective-permute-start(bf16[4,192,128]{2,1,0:T(8,128)(2,1)S(1)} %get-tuple-element.48), channel_id=1, source_target_pairs={{0,4},{1,5},{2,6},{3,7},{4,0},{5,1},{6,2},{7,3},{8,12},{9,13},{10,... | collective-permute-start | bytes 589832 | tf_op jit(solution)/shard_map/ppermute | solution.py:201
  172.7 4.5 %collective-permute-start.12 = (bf16[4,192,128]{2,1,0:T(8,128)(2,1)S(1)}, bf16[4,192,128]{2,1,0:T(8,128)(2,1)S(1)}, u32[]{:S(2)}, u32[]{:S(2)}) collective-permute-start(bf16[4,192,128]{2,1,0:T(8,128)(2,1)S(1)} %get-tuple-element.49), channel_id=1, source_target_pairs={{0,6},{1,7},{2,0},{3,1},{4,2},{5,3},{6,4},{7,5},{8,14},{9,15},{10,... | collective-permute-start | bytes 589832 | tf_op jit(solution)/shard_map/ppermute | solution.py:201
  177.3 2.7 %collective-permute-done.11.refs_2_ = bf16[4,192,128]{2,1,0:T(8,128)(2,1)S(1)} collective-permute-done((bf16[4,192,128]{2,1,0:T(8,128)(2,1)S(1)}, bf16[4,192,128]{2,1,0:T(8,128)(2,1)S(1)}, u32[]{:S(2)}, u32[]{:S(2)}) %collective-permute-start.11) | collective-permute-done | bytes 196640 | tf_op jit(solution)/shard_map/ppermute | solution.py:201
  182.0 2.8 %collective-permute-start.13 = (f32[192,128]{1,0:T(8,128)S(1)}, f32[192,128]{1,0:T(8,128)S(1)}, u32[]{:S(2)}, u32[]{:S(2)}) collective-permute-start(f32[192,128]{1,0:T(8,128)S(1)} %get-tuple-element.51), channel_id=1, source_target_pairs={{0,8},{1,9},{2,10},{3,11},{4,12},{5,13},{6,14},{7,15},{8,16},{9,17... | collective-permute-start | bytes 294920 | tf_op jit(solution)/shard_map/ppermute | solution.py:203
  184.8 4.6 %collective-permute-start.14 = (f32[192,128]{1,0:T(8,128)S(1)}, f32[192,128]{1,0:T(8,128)S(1)}, u32[]{:S(2)}, u32[]{:S(2)}) collective-permute-start(f32[192,128]{1,0:T(8,128)S(1)} %get-tuple-element.52), channel_id=1, source_target_pairs={{0,16},{1,17},{2,18},{3,19},{4,20},{5,21},{6,22},{7,23},{8,24},{9,... | collective-permute-start | bytes 294920 | tf_op jit(solution)/shard_map/ppermute | solution.py:203
  189.4 3.4 %collective-permute-start.15 = (f32[192,128]{1,0:T(8,128)S(1)}, f32[192,128]{1,0:T(8,128)S(1)}, u32[]{:S(2)}, u32[]{:S(2)}) collective-permute-start(f32[192,128]{1,0:T(8,128)S(1)} %get-tuple-element.53), channel_id=1, source_target_pairs={{0,24},{1,25},{2,26},{3,27},{4,28},{5,29},{6,30},{7,31},{8,0},{9,1... | collective-permute-start | bytes 294920 | tf_op jit(solution)/shard_map/ppermute | solution.py:203
  192.9 3.1 %collective-permute-done.15.refs_3_ = f32[192,128]{1,0:T(8,128)S(1)} collective-permute-done((f32[192,128]{1,0:T(8,128)S(1)}, f32[192,128]{1,0:T(8,128)S(1)}, u32[]{:S(2)}, u32[]{:S(2)}) %collective-permute-start.15) | collective-permute-done | bytes 98336 | tf_op jit(solution)/shard_map/ppermute | solution.py:203
  (57 shorter events, 29.4 us)
Async XLA Ops:
  7.2 137.0 %all-gather.4.cloned.1.call-start = ((), (), s32[]{:S(2)}) async-start(), calls=%async_computation.5 | async-start | bytes 8912896 | tf_op jit(solution)/shard_map/all_gather | solution.py:290
  10.1 54.7 %all-to-all-start = ((bf16[32,192,128]{2,1,0:T(8,128)(2,1)}), bf16[32,192,128]{2,1,0:T(8,128)(2,1)S(1)}, u32[]{:S(2)}, u32[]{:S(2)}) async-start(bf16[32,192,128]{2,1,0:T(8,128)(2,1)} %spread.2), calls=%async_computation | async-start | bytes 3145728 | tf_op jit(solution)/shard_map/all_to_all | solution.py:292
  64.8 40.4 %copy-start.6 = (bf16[3072,128]{1,0:T(8,128)(2,1)}, bf16[3072,128]{1,0:T(8,128)(2,1)S(1)}, u32[]{:S(2)}) copy-start(bf16[3072,128]{1,0:T(8,128)(2,1)S(1)} %all-gather) | copy-start | bytes 2359300
  64.8 39.2 %all-to-all-start.1 = ((bf16[16,96,128]{2,1,0:T(8,128)(2,1)}), bf16[16,96,128]{2,1,0:T(8,128)(2,1)S(1)}, u32[]{:S(2)}, u32[]{:S(2)}) async-start(bf16[16,96,128]{2,1,0:T(8,128)(2,1)} %bitcast.3), calls=%async_computation.1 | async-start | bytes 786432 | tf_op jit(solution)/shard_map/all_to_all | solution.py:298
  72.4 16.6 %collective-permute-start = (bf16[16,192,128]{2,1,0:T(8,128)(2,1)S(1)}, bf16[16,192,128]{2,1,0:T(8,128)(2,1)S(1)}, u32[]{:S(2)}, u32[]{:S(2)}) collective-permute-start(bf16[16,192,128]{2,1,0:T(8,128)(2,1)S(1)} %bitcast.22), channel_id=1, source_target_pairs={{0,2},{1,3},{2,4},{3,5},{4,6},{5,7},{6,0},{7,1},{8,10},{9,11},{10,... | collective-permute-start | bytes 2359304 | tf_op jit(solution)/shard_map/ppermute | solution.py:272
  75.7 17.4 %collective-permute-start.2 = (bf16[16,192,128]{2,1,0:T(8,128)(2,1)S(1)}, bf16[16,192,128]{2,1,0:T(8,128)(2,1)S(1)}, u32[]{:S(2)}, u32[]{:S(2)}) collective-permute-start(bf16[16,192,128]{2,1,0:T(8,128)(2,1)S(1)} %bitcast.23), channel_id=1, source_target_pairs={{0,6},{1,7},{2,0},{3,1},{4,2},{5,3},{6,4},{7,5},{8,14},{9,15},{10,... | collective-permute-start | bytes 2359304 | tf_op jit(solution)/shard_map/ppermute | solution.py:273
  89.8 9.9 %collective-permute-start.1 = (bf16[8,192,128]{2,1,0:T(8,128)(2,1)}, bf16[8,192,128]{2,1,0:T(8,128)(2,1)S(1)}, u32[]{:S(2)}, u32[]{:S(2)}) collective-permute-start(bf16[8,192,128]{2,1,0:T(8,128)(2,1)} %slice.8), channel_id=1, source_target_pairs={{0,2},{1,3},{2,4},{3,5},{4,6},{5,7},{6,0},{7,1},{8,10},{9,11},{10,... | collective-permute-start | bytes 1179656 | tf_op jit(solution)/shard_map/ppermute | solution.py:274
  94.1 10.0 %collective-permute-start.3 = (bf16[8,192,128]{2,1,0:T(8,128)(2,1)}, bf16[8,192,128]{2,1,0:T(8,128)(2,1)}, u32[]{:S(2)}, u32[]{:S(2)}) collective-permute-start(bf16[8,192,128]{2,1,0:T(8,128)(2,1)} %slice.9), channel_id=1, source_target_pairs={{0,6},{1,7},{2,0},{3,1},{4,2},{5,3},{6,4},{7,5},{8,14},{9,15},{10,... | collective-permute-start | bytes 1179656 | tf_op jit(solution)/shard_map/ppermute | solution.py:275
  105.3 18.1 %all-to-all-start.2 = ((bf16[4,16,96,128]{3,2,1,0:T(8,128)(2,1)}), bf16[4,16,96,128]{3,2,1,0:T(8,128)(2,1)S(1)}, u32[]{:S(2)}, u32[]{:S(2)}) async-start(bf16[4,16,96,128]{3,2,1,0:T(8,128)(2,1)} %spread.3), calls=%async_computation.2 | async-start | bytes 3145728 | tf_op jit(solution)/shard_map/all_to_all | solution.py:303
  109.7 10.7 %collective-permute-start.4 = (bf16[16,192,128]{2,1,0:T(8,128)(2,1)}, bf16[16,192,128]{2,1,0:T(8,128)(2,1)}, u32[]{:S(2)}, u32[]{:S(2)}) collective-permute-start(bf16[16,192,128]{2,1,0:T(8,128)(2,1)} %bitcast.24), channel_id=1, source_target_pairs={{0,1},{1,0},{2,3},{3,2},{4,5},{5,4},{6,7},{7,6},{8,9},{9,8},{10,11... | collective-permute-start | bytes 2359304 | tf_op jit(solution)/shard_map/ppermute | solution.py:302
  111.6 8.8 %collective-permute-start.5 = (bf16[16,192,128]{2,1,0:T(8,128)(2,1)}, bf16[16,192,128]{2,1,0:T(8,128)(2,1)}, u32[]{:S(2)}, u32[]{:S(2)}) collective-permute-start(bf16[16,192,128]{2,1,0:T(8,128)(2,1)} %copy-done.7), channel_id=1, source_target_pairs={{0,1},{1,0},{2,3},{3,2},{4,5},{5,4},{6,7},{7,6},{8,9},{9,8},{10,11... | collective-permute-start | bytes 2359304 | tf_op jit(solution)/shard_map/ppermute | solution.py:302
  114.0 6.4 %collective-permute-start.8 = (bf16[16,192,128]{2,1,0:T(8,128)(2,1)}, bf16[16,192,128]{2,1,0:T(8,128)(2,1)}, u32[]{:S(2)}, u32[]{:S(2)}) collective-permute-start(bf16[16,192,128]{2,1,0:T(8,128)(2,1)} %copy-done.8), channel_id=1, source_target_pairs={{0,1},{1,0},{2,3},{3,2},{4,5},{5,4},{6,7},{7,6},{8,9},{9,8},{10,11... | collective-permute-start | bytes 2359304 | tf_op jit(solution)/shard_map/ppermute | solution.py:302
  115.9 4.5 %collective-permute-start.6 = (bf16[8,192,128]{2,1,0:T(8,128)(2,1)}, bf16[8,192,128]{2,1,0:T(8,128)(2,1)}, u32[]{:S(2)}, u32[]{:S(2)}) collective-permute-start(bf16[8,192,128]{2,1,0:T(8,128)(2,1)} %copy-done.9), channel_id=1, source_target_pairs={{0,1},{1,0},{2,3},{3,2},{4,5},{5,4},{6,7},{7,6},{8,9},{9,8},{10,11... | collective-permute-start | bytes 1179656 | tf_op jit(solution)/shard_map/ppermute | solution.py:302
  118.3 4.0 %collective-permute-start.7 = (bf16[8,192,128]{2,1,0:T(8,128)(2,1)}, bf16[8,192,128]{2,1,0:T(8,128)(2,1)}, u32[]{:S(2)}, u32[]{:S(2)}) collective-permute-start(bf16[8,192,128]{2,1,0:T(8,128)(2,1)} %collective-permute-done.3.refs_3_), channel_id=1, source_target_pairs={{0,1},{1,0},{2,3},{3,2},{4,5},{5,4},{6,7},{7,6},{8,9},{9,8},{10,11... | collective-permute-start | bytes 1179656 | tf_op jit(solution)/shard_map/ppermute | solution.py:302
  131.6 12.5 %copy-start.5 = (s32[3,9]{1,0:T(4,128)S(1)}, s32[3,9]{1,0:T(4,128)}, u32[]{:S(2)}) copy-start(s32[3,9]{1,0:T(4,128)} %get-tuple-element.33.meta) | copy-start | bytes 328
  131.6 21.5 %all-to-all-start.3 = ((bf16[4,96,1536]{2,1,0:T(8,128)(2,1)}), bf16[4,96,1536]{2,1,0:T(8,128)(2,1)S(1)}, u32[]{:S(2)}, u32[]{:S(2)}) async-start(bf16[4,96,1536]{2,1,0:T(8,128)(2,1)} %wgrad_products.1), calls=%async_computation.3 | async-start | bytes 2359296 | tf_op jit(solution)/shard_map/all_to_all | solution.py:306
  151.1 4.5 %collective-permute-start.9 = (bf16[4,4,192,128]{3,2,1,0:T(8,128)(2,1)}, bf16[4,4,192,128]{3,2,1,0:T(8,128)(2,1)S(1)}, u32[]{:S(2)}, u32[]{:S(2)}) collective-permute-start(bf16[4,4,192,128]{3,2,1,0:T(8,128)(2,1)} %get-tuple-element.41), channel_id=1, source_target_pairs={{0,1},{1,0},{2,3},{3,2},{4,5},{5,4},{6,7},{7,6},{8,9},{9,8},{10,11... | collective-permute-start | bytes 2359304 | tf_op jit(solution)/shard_map/ppermute | solution.py:195
  155.8 40.8 %all-to-all-start.4 = ((bf16[16,32,512]{2,1,0:T(8,128)(2,1)}), bf16[16,32,512]{2,1,0:T(8,128)(2,1)S(1)}, u32[]{:S(2)}, u32[]{:S(2)}) async-start(bf16[16,32,512]{2,1,0:T(8,128)(2,1)} %pick_slots.1), calls=%async_computation.4 | async-start | bytes 1048576 | tf_op jit(solution)/shard_map/all_to_all | solution.py:312
  165.8 11.4 %collective-permute-start.10 = (bf16[4,192,128]{2,1,0:T(8,128)(2,1)S(1)}, bf16[4,192,128]{2,1,0:T(8,128)(2,1)S(1)}, u32[]{:S(2)}, u32[]{:S(2)}) collective-permute-start(bf16[4,192,128]{2,1,0:T(8,128)(2,1)S(1)} %get-tuple-element.47), channel_id=1, source_target_pairs={{0,2},{1,3},{2,4},{3,5},{4,6},{5,7},{6,0},{7,1},{8,10},{9,11},{10,... | collective-permute-start | bytes 589832 | tf_op jit(solution)/shard_map/ppermute | solution.py:201
  168.9 11.0 %collective-permute-start.11 = (bf16[4,192,128]{2,1,0:T(8,128)(2,1)S(1)}, bf16[4,192,128]{2,1,0:T(8,128)(2,1)S(1)}, u32[]{:S(2)}, u32[]{:S(2)}) collective-permute-start(bf16[4,192,128]{2,1,0:T(8,128)(2,1)S(1)} %get-tuple-element.48), channel_id=1, source_target_pairs={{0,4},{1,5},{2,6},{3,7},{4,0},{5,1},{6,2},{7,3},{8,12},{9,13},{10,... | collective-permute-start | bytes 589832 | tf_op jit(solution)/shard_map/ppermute | solution.py:201
  172.7 9.2 %collective-permute-start.12 = (bf16[4,192,128]{2,1,0:T(8,128)(2,1)S(1)}, bf16[4,192,128]{2,1,0:T(8,128)(2,1)S(1)}, u32[]{:S(2)}, u32[]{:S(2)}) collective-permute-start(bf16[4,192,128]{2,1,0:T(8,128)(2,1)S(1)} %get-tuple-element.49), channel_id=1, source_target_pairs={{0,6},{1,7},{2,0},{3,1},{4,2},{5,3},{6,4},{7,5},{8,14},{9,15},{10,... | collective-permute-start | bytes 589832 | tf_op jit(solution)/shard_map/ppermute | solution.py:201
  182.0 10.8 %collective-permute-start.13 = (f32[192,128]{1,0:T(8,128)S(1)}, f32[192,128]{1,0:T(8,128)S(1)}, u32[]{:S(2)}, u32[]{:S(2)}) collective-permute-start(f32[192,128]{1,0:T(8,128)S(1)} %get-tuple-element.51), channel_id=1, source_target_pairs={{0,8},{1,9},{2,10},{3,11},{4,12},{5,13},{6,14},{7,15},{8,16},{9,17... | collective-permute-start | bytes 294920 | tf_op jit(solution)/shard_map/ppermute | solution.py:203
  184.8 8.0 %collective-permute-start.14 = (f32[192,128]{1,0:T(8,128)S(1)}, f32[192,128]{1,0:T(8,128)S(1)}, u32[]{:S(2)}, u32[]{:S(2)}) collective-permute-start(f32[192,128]{1,0:T(8,128)S(1)} %get-tuple-element.52), channel_id=1, source_target_pairs={{0,16},{1,17},{2,18},{3,19},{4,20},{5,21},{6,22},{7,23},{8,24},{9,... | collective-permute-start | bytes 294920 | tf_op jit(solution)/shard_map/ppermute | solution.py:203
  189.4 6.5 %collective-permute-start.15 = (f32[192,128]{1,0:T(8,128)S(1)}, f32[192,128]{1,0:T(8,128)S(1)}, u32[]{:S(2)}, u32[]{:S(2)}) collective-permute-start(f32[192,128]{1,0:T(8,128)S(1)} %get-tuple-element.53), channel_id=1, source_target_pairs={{0,24},{1,25},{2,26},{3,27},{4,28},{5,29},{6,30},{7,31},{8,0},{9,1... | collective-permute-start | bytes 294920 | tf_op jit(solution)/shard_map/ppermute | solution.py:203
  (8 other events, 35.7 us)
Sparse Core Ops, SparseCore 0:
  10.1 134.0 all-gather.3
